TPU v7x, 32 devices: a whole 2x2x4 slice. The times are simulated.
32 devices in a mesh: space: 8 (over y, x, core), tm: 4 (over z).
Axes of the slice: x: 2, y: 2, z: 4, core: 2. Of those that a mesh axis runs over, the one named last changes fastest.
Arguments:
- velocity: bfloat16 [3, 3072, 1024], P(None, 'space', 'tm'), may hold values from -6 to 6
- metric: float32 [3072], P('space'), may hold values from 0.5 to 2
Outputs:
- tiles: float32 [1024, 1024], P('tm', 'space')
All inputs are finite; a program needn't handle non-finite values.
Results may differ from a plain program's by a relative error of at most 0.0016.
Values may be sent and summed in bfloat16 or wider, within the bound.
No kernel may reach another device: no remote copies, remote signals or barrier semaphores. Data moves between devices by JAX's collectives and lax.ppermute only.
A program may use at most 64 MiB of HBM per device.

v0:
```python
import jax
import jax.numpy as jnp
from jax import lax
from jax.sharding import PartitionSpec as P


def padded_2(cells, sides, width):
    for axis, dim in sides:
        count = lax.axis_size(axis)
        ends = count - 1
        head = lax.slice_in_dim(cells, 0, width, axis=dim)
        tail = lax.slice_in_dim(cells, cells.shape[dim] - width, cells.shape[dim], axis=dim)
        cells = jnp.concatenate(
            [
                lax.ppermute(tail, axis, [(i, (i + 1) % count) for i in range(ends)]),
                cells,
                lax.ppermute(head, axis, [((i + 1) % count, i) for i in range(ends)]),
            ],
            axis=dim,
        )
    return cells


def from_behind(value, axis, steps):
    count = lax.axis_size(axis)
    pairs = [(source, (source + steps) % count) for source in range(count)]
    return lax.ppermute(value, axis, pairs)


def cross_product(left, right):
    return lax.dot_general(
        left, right, (((0,), (0,)), ((), ())), preferred_element_type=jnp.float32
    )


def body(velocity, metric):
    padded = padded_2(velocity, (("space", 1),), 1)
    field = padded.astype(jnp.float32)
    center = field[:, 1:-1]
    gradient = metric[None, :, None] * (field[:, 2:] - field[:, :-2]) * 0.5
    helical = gradient[2] + center[0] * gradient[1] - center[1] * gradient[0]
    snapshot_panel = jnp.stack([gradient[0], gradient[1], helical]).astype(jnp.bfloat16)
    snapshot_panel = snapshot_panel.reshape(3 * velocity.shape[1], velocity.shape[2])
    gram_matrix = lax.psum(cross_product(snapshot_panel, snapshot_panel), "space")
    following = from_behind(snapshot_panel[:, :1], "tm", -1)
    shifted = jnp.concatenate([snapshot_panel[:, 1:], following], axis=1)
    partial_value = cross_product(snapshot_panel, lax.all_gather(shifted, "tm", axis=1, tiled=True))
    summed = lax.psum_scatter(partial_value, "space", scatter_dimension=1, tiled=True)
    factor = jnp.linalg.cholesky(gram_matrix)
    return lax.linalg.triangular_solve(factor, summed, left_side=True, lower=True)


def solution(mesh):
    in_specs = (P(None, "space", "tm"), P("space"))
    out_specs = P("tm", "space")
    return jax.shard_map(body, mesh=mesh, in_specs=in_specs, out_specs=out_specs, check_vma=False)
```

profile of v0, /device:TPU:0, one launch (start us, length us, event | category | flops | bytes accessed | tf_op | source)
XLA Modules:
  0.0 151.9 jit_solution(11855367174585819543)
XLA Ops:
  7.4 0.7 fusion.13
  8.1 1.3 collective-permute-start.1
  9.4 3.0 %collective-permute-start = (bf16[3,1,256]{2,1,0:T(2,128)(2,1)S(1)}, bf16[3,1,256]{2,1,0:T(2,128)(2,1)S(1)}, u32[]{:S(2)}, u32[]{:S(2)}) collective-permute-start(bf16[3,1,256]{2,1,0:T(2,128)(2,1)S(1)} %get-tuple-element.23), channel_id=1, source_target_pairs={{0,4},{4,8},{8,12},{12,16},{16,20},{20,24},{24,28},{1,5},{5,9},{9,... | collective-permute-start | bytes 4616 | tf_op jit(solution)/shard_map/ppermute | solution.py:15
  12.5 0.8 collective-permute-done
  13.2 1.2 maximum_convert_fusion.1
  14.4 0.2 fusion.1
  14.7 0.2 fusion.2
  15.0 5.1 %collective-permute-start.2 = (bf16[1152,1]{1,0:T(8,128)(2,1)S(1)}, bf16[1152,1]{1,0:T(8,128)(2,1)S(1)}, u32[]{:S(2)}, u32[]{:S(2)}) collective-permute-start(bf16[1152,1]{1,0:T(8,128)(2,1)S(1)} %slice.115), channel_id=1, source_target_pairs={{0,3},{1,0},{2,1},{3,2},{4,7},{5,4},{6,5},{7,6},{8,11},{9,8},{10,9... | collective-permute-start | bytes 6920 | tf_op jit(solution)/shard_map/ppermute | solution.py:27
  20.1 1.1 convolution_bitcast_fusion
  21.2 0.3 slice.114
  21.5 5.9 %collective-permute-done.2 = bf16[1152,1]{1,0:T(8,128)(2,1)S(1)} collective-permute-done((bf16[1152,1]{1,0:T(8,128)(2,1)S(1)}, bf16[1152,1]{1,0:T(8,128)(2,1)S(1)}, u32[]{:S(2)}, u32[]{:S(2)}) %collective-permute-start.2) | collective-permute-done | bytes 2336 | tf_op jit(solution)/shard_map/ppermute | solution.py:27
  27.5 1.0 pad_maximum_fusion
  28.5 47.4 %all-reduce.3.cloned.1.call-done = f32[256,256]{0,1:T(8,128)} async-done(((f32[256,256]{0,1:T(8,128)}), f32[256,256]{0,1:T(8,128)}) %all-reduce.3.cloned.1.call-update) | async-done | bytes 262160 | tf_op jit(solution)/shard_map/psum | solution.py:44
  75.9 1.1 copy.5
  77.0 1.0 fusion.4
  78.0 11.7 %cholesky.50 = f32[128,128]{1,0:T(8,128)S(1)} custom-call(f32[128,128]{1,0:T(8,128)S(1)} %cholesky.118), custom_call_target="Cholesky" | custom-call | tf_op jit(solution)/shard_map/jit(cholesky)/cholesky | solution.py:49
  89.8 9.8 %custom-call.14 = f32[1,128,128]{1,2,0:T(8,128)S(1)} custom-call(f32[1,128,128]{2,1,0:T(8,128)S(1)} %get-tuple-element.28), custom_call_target="InvertDiagBlocksLowerTriangular" | custom-call | tf_op jit(solution)/shard_map/jit(cholesky)/cholesky | solution.py:49
  99.6 3.5 %fusion.14 = f32[256,1024]{1,0:T(8,128)} fusion(bf16[1152,256]{1,0:T(8,128)(2,1)S(1)} %bitcast.40, bf16[1152,1024]{1,0:T(8,128)(2,1)} %all-gather.2.cloned.1.call-done), kind=kOutput, calls=%fused_computation.41 | convolution fusion | flops 603979776 | bytes 3997696 | tf_op jit(solution)/shard_map/dot_general | solution.py:31
  103.2 0.2 constant_dynamic-update-slice_fusion.1
  103.4 0.3 convolution_subtract_fusion.1
  103.7 11.7 %cholesky.105 = f32[128,128]{1,0:T(8,128)S(1)} custom-call(f32[128,128]{1,0:T(8,128)S(1)} %convolution_subtract_fusion.1), custom_call_target="Cholesky" | custom-call | tf_op jit(solution)/shard_map/jit(cholesky)/cholesky | solution.py:49
  115.4 0.7 compare_reduce_fusion
  117.5 4.1 %while.1 = (s32[]{:T(128)}, f32[256,256]{1,0:T(8,128)S(1)}, s32[2,2]{1,0:T(2,128)S(1)}, f32[2,128,128]{2,1,0:T(8,128)S(1)}, s32[]{:T(128)}) while((s32[]{:T(128)}, f32[256,256]{1,0:T(8,128)S(1)}, s32[2,2]{1,0:T(2,128)S(1)}, f32[2,128,128]{2,1,0:T(8,128)S(1)}, s32[]{:T(128)}) %tuple.24), condition=%wide.while_cond, body=%wide.while_body.sunk | while | flops 2 | bytes 131189 | solution.py:50
  117.6 0.6 fusion.24
  118.2 1.3 bitcast_dynamic-update-slice_fusion.2
  119.6 0.6 fusion.24
  120.2 1.3 bitcast_dynamic-update-slice_fusion.2
  121.6 19.7 %custom-call.15 = f32[2,128,128]{1,2,0:T(8,128)S(1)} custom-call(f32[2,128,128]{2,1,0:T(8,128)S(1)} %get-tuple-element.12), custom_call_target="InvertDiagBlocksLowerTriangular" | custom-call | tf_op jit(solution)/shard_map/triangular_solve | solution.py:50
  141.3 1.1 fusion.7
  142.4 1.0 convolution_subtract_fusion
  143.5 0.3 fusion.6
  143.8 0.7 pad_maximum_fusion.1
  (24 shorter events, 0.5 us)
Async XLA Ops:
  7.4 7.1 %copy-start = (f32[384]{0:T(512)S(1)}, f32[384]{0:T(512)}, u32[]{:S(2)}) copy-start(f32[384]{0:T(512)} %param.3) | copy-start | bytes 4612
  7.4 68.6 %all-reduce.3.cloned.1.call-start = ((), (), s32[]{:S(2)}) async-start(), calls=%async_computation.1 | async-start | bytes 524288 | tf_op jit(solution)/shard_map/psum | solution.py:44
  8.1 4.3 %collective-permute-start.1 = (bf16[3,1,256]{2,1,0:T(2,128)(2,1)S(1)}, bf16[3,1,256]{2,1,0:T(2,128)(2,1)S(1)}, u32[]{:S(2)}, u32[]{:S(2)}) collective-permute-start(bf16[3,1,256]{2,1,0:T(2,128)(2,1)S(1)} %get-tuple-element.24), channel_id=1, source_target_pairs={{4,0},{8,4},{12,8},{16,12},{20,16},{24,20},{28,24},{5,1},{9,5},{13... | collective-permute-start | bytes 4616 | tf_op jit(solution)/shard_map/ppermute | solution.py:17
  9.4 3.8 %collective-permute-start = (bf16[3,1,256]{2,1,0:T(2,128)(2,1)S(1)}, bf16[3,1,256]{2,1,0:T(2,128)(2,1)S(1)}, u32[]{:S(2)}, u32[]{:S(2)}) collective-permute-start(bf16[3,1,256]{2,1,0:T(2,128)(2,1)S(1)} %get-tuple-element.23), channel_id=1, source_target_pairs={{0,4},{4,8},{8,12},{12,16},{16,20},{20,24},{24,28},{1,5},{5,9},{9,... | collective-permute-start | bytes 4616 | tf_op jit(solution)/shard_map/ppermute | solution.py:15
  15.0 12.4 %collective-permute-start.2 = (bf16[1152,1]{1,0:T(8,128)(2,1)S(1)}, bf16[1152,1]{1,0:T(8,128)(2,1)S(1)}, u32[]{:S(2)}, u32[]{:S(2)}) collective-permute-start(bf16[1152,1]{1,0:T(8,128)(2,1)S(1)} %slice.115), channel_id=1, source_target_pairs={{0,3},{1,0},{2,1},{3,2},{4,7},{5,4},{6,5},{7,6},{8,11},{9,8},{10,9... | collective-permute-start | bytes 6920 | tf_op jit(solution)/shard_map/ppermute | solution.py:27
  21.5 78.1 %all-gather.2.cloned.1.call-start = ((), (), s32[]{:S(2)}) async-start(), calls=%async_computation.2 | async-start | bytes 2949120 | tf_op jit(solution)/shard_map/all_gather | solution.py:47
  28.5 112.8 %reduce-scatter.2.cloned.1.call-start = ((), (), s32[]{:S(2)}) async-start(), calls=%async_computation.3 | async-start | bytes 1179648 | tf_op jit(solution)/shard_map/reduce_scatter | solution.py:48
Sparse Core Ops, SparseCore 0:
  21.6 54.2 all-reduce.2
  103.3 35.7 reduce-scatter.1
Sparse Core Ops, SparseCore 1:
  28.6 52.4 all-gather.1
where the time goes:
time: 152 us
  other arithmetic  58 us (38%)
  waiting for transfers between devices  54.2 us (36%)
  between operations  16.3 us (11%)
  starting transfers between devices  9.5 us (6%)
  matrix products  7.52 us (5%)
  local copies, waits for them, and re-layouts  6.15 us (4%)
    psum x1, waiting for transfers between devices, body(): lax.psum(cross_product(snapshot_panel, snapshot_panel), 'space')  47.4 us
    another operation x6, other arithmetic, body(): factor = jnp.linalg.cholesky(gram_matrix)  34 us
    another operation x4, other arithmetic, body(): lax.linalg.triangular_solve(factor, summed, left_side=True, lower=True)  20.4 us
    ppermute x1, waiting for transfers between devices, from_behind(): return lax.ppermute(value, axis, pairs)  5.92 us
    ppermute x1, starting transfers between devices, from_behind(): return lax.ppermute(value, axis, pairs)  5.1 us
    dot_general x2, matrix products, cross_product(): lax.dot_general(left, right, (((0,), (0,)), ((), ())), preferred_element_...  4.6 us
    another operation x6, local copies, waits for them, and re-layouts  3.92 us
  transfers between devices with their start and end apart: 6, of which 3 were waited for; matrix products, arithmetic and copies ran while one was open for 41% of the time, Pallas kernels for 0%

commit v1 on v0

v1 whole, which is shorter than its diff:
```python
import functools

import jax
import jax.numpy as jnp
from jax import lax
from jax.experimental import pallas as pl
from jax.experimental.pallas import tpu as pltpu
from jax.sharding import PartitionSpec as P

F32 = jnp.float32
BF16 = jnp.bfloat16
HIGHEST = lax.Precision.HIGHEST
VMEM = pl.BlockSpec(memory_space=pltpu.VMEM)
SMEM = pl.BlockSpec(memory_space=pltpu.SMEM)
LEAF = 64
PIVOTS = 4


def params(mib=40):
    return pltpu.CompilerParams(vmem_limit_bytes=mib * 1024 * 1024)


def cost(flops, moved):
    return pl.CostEstimate(flops=flops, bytes_accessed=moved, transcendentals=0)


def panel_kernel(vel_ref, lo_ref, hi_ref, met_ref, x_ref, xt_ref, g_ref):
    rows, cols = vel_ref.shape[1:]
    row = lax.broadcasted_iota(jnp.int32, (rows, cols), 0)
    metric = met_ref[...]

    def gradient(k):
        field = vel_ref[k].astype(F32)
        up = jnp.where(row == rows - 1, hi_ref[k].astype(F32), pltpu.roll(field, rows - 1, 0))
        down = jnp.where(row == 0, lo_ref[k].astype(F32), pltpu.roll(field, 1, 0))
        return metric * (up - down) * 0.5

    first = gradient(0)
    x_ref[0:rows] = first.astype(BF16)
    second = gradient(1)
    x_ref[rows : 2 * rows] = second.astype(BF16)
    third = gradient(2) + vel_ref[0].astype(F32) * second - vel_ref[1].astype(F32) * first
    x_ref[2 * rows :] = third.astype(BF16)
    xt_ref[...] = x_ref[...].T
    g_ref[...] = jnp.dot(xt_ref[...], x_ref[...], preferred_element_type=F32)


def panel(velocity, lo, hi, metric):
    _, rows, cols = velocity.shape
    return pl.pallas_call(
        panel_kernel,
        out_shape=(
            jax.ShapeDtypeStruct((3 * rows, cols), BF16),
            jax.ShapeDtypeStruct((cols, 3 * rows), BF16),
            jax.ShapeDtypeStruct((cols, cols), F32),
        ),
        in_specs=[VMEM] * 4,
        out_specs=(VMEM,) * 3,
        compiler_params=params(),
        cost_estimate=cost(2 * 3 * rows * cols * cols, 12 * rows * cols),
        name="panel",
    )(velocity, lo, hi, metric.reshape(rows, 1))


def leaf_inverse(block):
    n = block.shape[0]
    row = lax.broadcasted_iota(jnp.int32, (n, 2 * n), 0)
    lane = lax.broadcasted_iota(jnp.int32, (n, 2 * n), 1)
    eye = (row == lane).astype(F32)
    right = (lane == row + n).astype(F32)
    m = jnp.concatenate([block, right[:, n:]], axis=1)
    for j in range(0, n, PIVOTS):
        columns = [jnp.broadcast_to(m[:, j + b : j + b + 1], (n, 2 * n)) for b in range(PIVOTS)]
        pivot_rows = [m[j + a : j + a + 1, :] for a in range(PIVOTS)]
        splat = [[columns[b][j + a : j + a + 1, :] for b in range(PIVOTS)] for a in range(PIVOTS)]
        update = None
        inverses = []
        for a in range(PIVOTS):
            inverse = 1.0 / splat[a][a]
            for b in range(a + 1, PIVOTS):
                ratio = splat[a][b] * inverse
                for c in range(b, PIVOTS):
                    splat[b][c] = splat[b][c] - ratio * splat[a][c]
                pivot_rows[b] = pivot_rows[b] - ratio * pivot_rows[a]
            inverses.append(inverse)
        for a in range(PIVOTS):
            multiplier = jnp.where(row > j + a, columns[a] * inverses[a], 0.0)
            for b in range(a + 1, PIVOTS):
                columns[b] = columns[b] - multiplier * splat[a][b]
            term = multiplier * pivot_rows[a]
            update = term if update is None else update + term
        m = m - update
    diagonal = jnp.sum(m * eye, axis=1, keepdims=True)
    return m[:, n:] * lax.rsqrt(diagonal)


def mm(left, right, dims=((1,), (0,))):
    return lax.dot_general(left, right, (dims, ((), ())), precision=HIGHEST, preferred_element_type=F32)


def factor_kernel(g_ref, w_ref, a_ref, b_ref):
    n = g_ref.shape[0]
    a_ref[...] = g_ref[...]
    row = lax.broadcasted_iota(jnp.int32, (n, n), 0)
    lane = lax.broadcasted_iota(jnp.int32, (n, n), 1)
    b_ref[...] = (row == lane).astype(F32)
    for j in range(0, n, LEAF):
        k = j + LEAF
        own = slice(j, k)
        w = leaf_inverse(a_ref[own, own])
        done = mm(w, b_ref[own, :])
        w_ref[own, :] = done
        if k < n:
            u = mm(w, a_ref[own, :])
            a_ref[k:, :] -= mm(u[:, k:], u, ((0,), (0,)))
            b_ref[k:, :] -= mm(u[:, k:], done, ((0,), (0,)))


def inverse_factor(gram):
    n = gram.shape[0]
    return pl.pallas_call(
        factor_kernel,
        out_shape=jax.ShapeDtypeStruct((n, n), F32),
        in_specs=[VMEM],
        out_specs=VMEM,
        scratch_shapes=[pltpu.VMEM((n, n), F32)] * 2,
        compiler_params=params(),
        cost_estimate=cost(2 * n * n * n, 8 * n * n),
        name="factor",
    )(gram)


def blocks_kernel(count, pos_ref, xt_ref, *refs):
    panels, outs = refs[: count - 1], refs[count - 1 :]
    chip, group, core = pos_ref[0], pos_ref[1], pos_ref[2]
    for r in range(1, count):
        block = jnp.dot(xt_ref[...], panels[r - 1][...], preferred_element_type=F32)
        owner = group + jnp.where(core == 0, -r, r)
        for m in range(count):

            @pl.when(jnp.bitwise_xor(chip, m) == owner)
            def _(m=m, block=block):
                outs[m][...] = block


def blocks(pos, xt, panels):
    n = xt.shape[0]
    count = len(panels) + 1
    return pl.pallas_call(
        functools.partial(blocks_kernel, count),
        out_shape=(jax.ShapeDtypeStruct((n, n), F32),) * count,
        in_specs=[SMEM] + [VMEM] * count,
        out_specs=(VMEM,) * count,
        compiler_params=params(),
        cost_estimate=cost(2 * (count - 1) * n * n * xt.shape[1], 4 * count * n * n),
        name="blocks",
    )(pos, xt, *panels)


def total_kernel(pos_ref, *refs):
    count = len(refs) - 7
    parts = refs[:count]
    own_ref, sib_ref, low_ref, high_ref, top_t_ref, top_ref, st_ref = refs[count:]
    n = parts[0].shape[0]
    half = n // 2
    total = parts[0][...]
    for part in parts[1:]:
        total = total + part[...]
    low_ref[...] = total[: half + 8]
    high_ref[...] = total[half:]
    top_ref[...] = total[:8]
    st_ref[0:n] = total.T
    top_t_ref[...] = st_ref[0:8]
    core = pos_ref[2]
    own_ref[...] = st_ref[pl.ds(pl.multiple_of(core * half, 8), half + 8)]
    sib_ref[...] = st_ref[pl.ds(pl.multiple_of((1 - core) * half, 8), half + 8)]


def total(pos, parts):
    n = parts[0].shape[0]
    half = n // 2
    rows = (half + 8, half + 8, half + 8, half, 8, 8)
    return pl.pallas_call(
        total_kernel,
        out_shape=tuple(jax.ShapeDtypeStruct((r, n), F32) for r in rows),
        in_specs=[SMEM] + [VMEM] * len(parts),
        out_specs=(VMEM,) * 6,
        scratch_shapes=[pltpu.VMEM((n + 8, n), F32)],
        compiler_params=params(),
        name="total",
    )(pos, *parts)


def tiles_kernel(pos_ref, w_ref, g_ref, own_ref, sib_ref, low_ref, high_ref, top_t_ref, top_ref, out_ref, p_ref):
    count = pos_ref[3]
    chip, group, core = pos_ref[0], pos_ref[1], pos_ref[2]
    half = high_ref.shape[0]
    following = jnp.where(chip + 1 == count, 0, chip + 1)
    owner = jnp.where(chip < group, 0, 1)

    @pl.when(chip == group)
    def _():
        p_ref[0:half] = g_ref[pl.ds(pl.multiple_of(core * half, 8), half)]
        p_ref[half:] = g_ref[half : half + 8]

    @pl.when(chip != group)
    def _():
        slab = jnp.where(core == owner, own_ref[...], sib_ref[...])

        @pl.when(core == 0)
        def _():
            p_ref[...] = slab + low_ref[...]

        @pl.when(core != 0)
        def _():
            p_ref[0:half] = slab[:half] + high_ref[...]

    @pl.when(core != 0)
    def _():
        p_ref[half:] = jnp.where(following == group, g_ref[0:8], top_t_ref[...] + top_ref[...])

    shifted = pltpu.roll(p_ref[...], half + 7, 0)[:half]
    out_ref[...] = mm(w_ref[...], shifted, ((1,), (1,)))


def tiles(pos, w, gram, slabs):
    n = w.shape[0]
    half = n // 2
    return pl.pallas_call(
        tiles_kernel,
        out_shape=jax.ShapeDtypeStruct((n, half), F32),
        in_specs=[SMEM] + [VMEM] * 8,
        out_specs=VMEM,
        scratch_shapes=[pltpu.VMEM((half + 8, n), F32)],
        compiler_params=params(),
        name="tiles",
    )(pos, w, gram, *slabs)


def halos(velocity):
    count = lax.axis_size("space")
    head, tail = velocity[:, :1], velocity[:, -1:]
    lo = lax.ppermute(tail, "space", [(i, i + 1) for i in range(count - 1)])
    hi = lax.ppermute(head, "space", [(i + 1, i) for i in range(count - 1)])
    return lo, hi


def paired_body(velocity, metric):
    groups = lax.axis_size("tm")
    axes = ("space", "tm")
    every = range(groups)
    cores = (0, 1)

    def at(chip, group, core):
        return (2 * chip + core) * groups + group

    def send(value, pairs):
        return lax.ppermute(value, axes, pairs)

    space, group = lax.axis_index("space"), lax.axis_index("tm")
    core = space % 2
    pos = jnp.stack([space // 2, group, core, jnp.int32(groups)]).astype(jnp.int32)

    lo, hi = halos(velocity)
    x, xt, gram = panel(velocity, lo, hi, metric)

    n = gram.shape[0]
    half = n // 2
    siblings = [(at(k, z, c), at(k, z, 1 - c)) for k in every for z in every for c in cores]
    away = lax.dynamic_slice_in_dim(gram, (1 - core) * half, half, 0)
    mine = lax.dynamic_slice_in_dim(gram, core * half, half, 0)
    mine = mine + send(away, siblings)
    others = [
        send(mine, [(at(k, z, c), at(k ^ m, z, c)) for k in every for z in every for c in cores])
        for m in range(1, groups)
    ]
    for other in others:
        mine = mine + other
    theirs = send(mine, siblings)
    gram = jnp.where(core == 0, jnp.concatenate([mine, theirs]), jnp.concatenate([theirs, mine]))
    w = inverse_factor(gram)

    panels = []
    for r in range(1, groups):
        pairs = [(at(k, z, 0), at(k, z + r, 0)) for k in every for z in range(groups - r)]
        pairs += [(at(k, z, 1), at(k, z - r, 1)) for k in every for z in range(r, groups)]
        panels.append(send(x, pairs))
    parts = list(blocks(pos, xt, panels))
    for m in range(1, groups):
        pairs = []
        for z in every:
            for j in every:
                k = j ^ m
                if k != z:
                    c = 0 if k < z else 1
                    pairs.append((at(j, z, c), at(k, z, c)))
        parts[m] = send(parts[m], pairs)
    own, sib, low, high, top_t, top = total(pos, parts)

    owners = [(k, z, 0 if k < z else 1) for k in every for z in every if k != z]
    slabs = [
        own,
        send(sib, [(at(k, z, c), at(k, z, 1 - c)) for k, z, c in owners]),
        send(low, [(at(k, z, c), at(z, k, 0)) for k, z, c in owners]),
        send(high, [(at(k, z, c), at(z, k, 1)) for k, z, c in owners]),
        send(top_t, [(at(k, z, c), at((k - 1) % groups, z, 1)) for k, z, c in owners]),
        send(top, [(at(k, z, c), at((z - 1) % groups, k, 1)) for k, z, c in owners]),
    ]
    return tiles(pos, w, gram, slabs)


def general_body(velocity, metric):
    lo, hi = halos(velocity)
    x, xt, gram = panel(velocity, lo, hi, metric)
    w = inverse_factor(lax.psum(gram, "space"))
    count = lax.axis_size("tm")
    following = lax.ppermute(x[:, :1], "tm", [(i, (i - 1) % count) for i in range(count)])
    shifted = jnp.concatenate([x[:, 1:], following], axis=1)
    gathered = lax.all_gather(shifted, "tm", axis=1, tiled=True)
    partial = jnp.dot(xt, gathered, preferred_element_type=F32)
    summed = lax.psum_scatter(partial, "space", scatter_dimension=1, tiled=True)
    return mm(w, summed)


def solution(mesh):
    groups = mesh.shape["tm"]
    paired = mesh.shape["space"] == 2 * groups and groups & (groups - 1) == 0
    return jax.shard_map(
        paired_body if paired else general_body,
        mesh=mesh,
        in_specs=(P(None, "space", "tm"), P("space")),
        out_specs=P("tm", "space"),
        check_vma=False,
    )
```

time: 152 us -> 85.1 us (0.56)
  the two profiles are of different devices: /device:TPU:0 before, /device:TPU:5 now
where the time goes in v1:
time: 85.1 us; the launch traced here: 84.6 us
  starting transfers between devices  41.2 us (48%)
  waiting for transfers between devices  24.9 us (29%)
  Pallas kernels  16.1 us (19%)
  local copies, waits for them, and re-layouts  1.92 us (2%)
    ppermute x16, starting transfers between devices, send(): return lax.ppermute(value, axes, pairs)  35.6 us
    ppermute x16, waiting for transfers between devices, send(): return lax.ppermute(value, axes, pairs)  22.1 us
    pallas_call x1, Pallas kernels, inverse_factor(): pl.pallas_call(factor_kernel, out_shape=jax.ShapeDtypeStruct((n, n), F32)...  11.1 us
    ppermute x1, starting transfers between devices, halos(): lo = lax.ppermute(tail, 'space', [(i, i + 1) for i in range(count - 1)])  3.68 us
    ppermute x1, waiting for transfers between devices, halos(): hi = lax.ppermute(head, 'space', [(i + 1, i) for i in range(count - 1)])  2.85 us
    ppermute x1, starting transfers between devices, halos(): hi = lax.ppermute(head, 'space', [(i + 1, i) for i in range(count - 1)])  1.92 us
    pallas_call x1, Pallas kernels, blocks(): pl.pallas_call(functools.partial(blocks_kernel, count), out_shape=(jax.Sh...  1.9 us
  transfers between devices with their start and end apart: 18, of which 5 were waited for; matrix products, arithmetic and copies ran while one was open for 0% of the time, Pallas kernels for 16%

profile of v1, /device:TPU:5, one launch (start us, length us, event | category | flops | bytes accessed | tf_op | source)
XLA Modules:
  0.0 84.6 jit_solution(14357496150559588525)
XLA Ops:
  0.0 0.7 fusion
  0.7 3.7 %collective-permute-start = (bf16[3,1,256]{2,1,0:T(2,128)(2,1)S(1)}, bf16[3,1,256]{2,1,0:T(2,128)(2,1)S(1)}, u32[]{:S(2)}, u32[]{:S(2)}) collective-permute-start(bf16[3,1,256]{2,1,0:T(2,128)(2,1)S(1)} %get-tuple-element.32), channel_id=1, source_target_pairs={{0,4},{4,8},{8,12},{12,16},{16,20},{20,24},{24,28},{1,5},{5,9},{9,... | collective-permute-start | bytes 4616 | tf_op jit(solution)/shard_map/ppermute | solution.py:243
  4.4 1.9 %collective-permute-start.1 = (bf16[3,1,256]{2,1,0:T(2,128)(2,1)S(1)}, bf16[3,1,256]{2,1,0:T(2,128)(2,1)S(1)}, u32[]{:S(2)}, u32[]{:S(2)}) collective-permute-start(bf16[3,1,256]{2,1,0:T(2,128)(2,1)S(1)} %get-tuple-element.31), channel_id=1, source_target_pairs={{4,0},{8,4},{12,8},{16,12},{20,16},{24,20},{28,24},{5,1},{9,5},{13... | collective-permute-start | bytes 4616 | tf_op jit(solution)/shard_map/ppermute | solution.py:244
  6.4 0.1 reshape.4.met_ref
  6.5 2.9 %collective-permute-done.1.hi_ref = bf16[3,1,256]{2,1,0:T(2,128)(2,1)S(1)} collective-permute-done((bf16[3,1,256]{2,1,0:T(2,128)(2,1)S(1)}, bf16[3,1,256]{2,1,0:T(2,128)(2,1)S(1)}, u32[]{:S(2)}, u32[]{:S(2)}) %collective-permute-start.1) | collective-permute-done | bytes 1568 | tf_op jit(solution)/shard_map/ppermute | solution.py:244
  9.3 1.1 %copy-done = bf16[3,384,256]{2,1,0:T(8,128)(2,1)S(1)} copy-done((bf16[3,384,256]{2,1,0:T(8,128)(2,1)S(1)}, bf16[3,384,256]{2,1,0:T(8,128)(2,1)}, u32[]{:S(2)}) %copy-start) | copy-done | bytes 589848
  10.4 0.8 panel.1
  11.2 1.3 %collective-permute-start.7 = (bf16[1152,256]{1,0:T(8,128)(2,1)S(1)}, bf16[1152,256]{1,0:T(8,128)(2,1)S(1)}, u32[]{:S(2)}, u32[]{:S(2)}) collective-permute-start(bf16[1152,256]{1,0:T(8,128)(2,1)S(1)} %get-tuple-element.20), channel_id=1, source_target_pairs={{0,1},{1,2},{2,3},{8,9},{9,10},{10,11},{16,17},{17,18},{18,19},{24... | collective-permute-start | bytes 1769480 | tf_op jit(solution)/shard_map/ppermute | solution.py:258
  12.6 1.3 %collective-permute-start.8 = (bf16[1152,256]{1,0:T(8,128)(2,1)S(1)}, bf16[1152,256]{1,0:T(8,128)(2,1)S(1)}, u32[]{:S(2)}, u32[]{:S(2)}) collective-permute-start(bf16[1152,256]{1,0:T(8,128)(2,1)S(1)} %get-tuple-element.20), channel_id=1, source_target_pairs={{0,2},{1,3},{8,10},{9,11},{16,18},{17,19},{24,26},{25,27},{6,4},{7... | collective-permute-start | bytes 1769480 | tf_op jit(solution)/shard_map/ppermute | solution.py:258
  13.9 1.3 %collective-permute-start.9 = (bf16[1152,256]{1,0:T(8,128)(2,1)S(1)}, bf16[1152,256]{1,0:T(8,128)(2,1)S(1)}, u32[]{:S(2)}, u32[]{:S(2)}) collective-permute-start(bf16[1152,256]{1,0:T(8,128)(2,1)S(1)} %get-tuple-element.20), channel_id=1, source_target_pairs={{0,3},{8,11},{16,19},{24,27},{7,4},{15,12},{23,20},{31,28}} | collective-permute-start | bytes 1769480 | tf_op jit(solution)/shard_map/ppermute | solution.py:258
  15.2 5.4 %collective-permute-start.2 = (f32[128,256]{1,0:T(8,128)S(1)}, f32[128,256]{1,0:T(8,128)S(1)}, u32[]{:S(2)}, u32[]{:S(2)}) collective-permute-start(f32[128,256]{1,0:T(8,128)S(1)} %constant_dynamic-slice_fusion), channel_id=1, source_target_pairs={{0,4},{4,0},{1,5},{5,1},{2,6},{6,2},{3,7},{7,3},{8,12},{12,8},{9,1... | collective-permute-start | bytes 393224 | tf_op jit(solution)/shard_map/ppermute | solution.py:258
  20.6 1.0 %collective-permute-done.2 = f32[128,256]{1,0:T(8,128)S(1)} collective-permute-done((f32[128,256]{1,0:T(8,128)S(1)}, f32[128,256]{1,0:T(8,128)S(1)}, u32[]{:S(2)}, u32[]{:S(2)}) %collective-permute-start.2) | collective-permute-done | bytes 131104 | tf_op jit(solution)/shard_map/ppermute | solution.py:258
  21.6 0.4 collective-permute-start.3
  21.9 0.2 collective-permute-start.4
  22.2 2.1 %collective-permute-start.5 = (f32[128,256]{1,0:T(8,128)S(1)}, f32[128,256]{1,0:T(8,128)S(1)}, u32[]{:S(2)}, u32[]{:S(2)}) collective-permute-start(f32[128,256]{1,0:T(8,128)S(1)} %dynamic-slice_add_fusion), channel_id=1, source_target_pairs={{0,24},{4,28},{1,25},{5,29},{2,26},{6,30},{3,27},{7,31},{8,16},{12... | collective-permute-start | bytes 393224 | tf_op jit(solution)/shard_map/ppermute | solution.py:258
  24.3 0.1 pad_add_fusion.pos_ref
  24.4 17.5 %collective-permute-done.8.refs_1_ = bf16[1152,256]{1,0:T(8,128)(2,1)S(1)} collective-permute-done((bf16[1152,256]{1,0:T(8,128)(2,1)S(1)}, bf16[1152,256]{1,0:T(8,128)(2,1)S(1)}, u32[]{:S(2)}, u32[]{:S(2)}) %collective-permute-start.8) | collective-permute-done | bytes 589856 | tf_op jit(solution)/shard_map/ppermute | solution.py:258
  41.8 1.9 %blocks.1 = (f32[256,256]{1,0:T(8,128)S(1)}, f32[256,256]{1,0:T(8,128)S(1)}, f32[256,256]{1,0:T(8,128)S(1)}, f32[256,256]{1,0:T(8,128)S(1)}) custom-call(s32[4]{0:T(128)S(1)} %pad_add_fusion.pos_ref, bf16[256,1152]{1,0:T(8,128)(2,1)S(1)} %get-tuple-element.19.xt_ref, bf16[1152,256]{1,0:T(8,128)(2,1)S(1)} %collective-permute-done.7.refs_0_, ...), custom_call_target="tpu_custom_call" | custom-call | flops 452984832 | bytes 1048576 | tf_op jit(solution)/shard_map/blocks/pallas_call | solution.py:149
  43.8 1.9 %collective-permute-start.10 = (f32[256,256]{1,0:T(8,128)S(1)}, f32[256,256]{1,0:T(8,128)S(1)}, u32[]{:S(2)}, u32[]{:S(2)}) collective-permute-start(f32[256,256]{1,0:T(8,128)S(1)} %get-tuple-element.22), channel_id=1, source_target_pairs={{4,12},{20,28},{28,20},{9,1},{21,29},{29,21},{2,10},{10,2},{22,30}... | collective-permute-start | bytes 786440 | tf_op jit(solution)/shard_map/ppermute | solution.py:258
  45.7 1.3 %collective-permute-start.11 = (f32[256,256]{1,0:T(8,128)S(1)}, f32[256,256]{1,0:T(8,128)S(1)}, u32[]{:S(2)}, u32[]{:S(2)}) collective-permute-start(f32[256,256]{1,0:T(8,128)S(1)} %get-tuple-element.23), channel_id=1, source_target_pairs={{4,20},{12,28},{28,12},{5,21},{13,29},{17,1},{14,30},{18,2},{26,10... | collective-permute-start | bytes 786440 | tf_op jit(solution)/shard_map/ppermute | solution.py:258
  47.0 5.2 %collective-permute-start.12 = (f32[256,256]{1,0:T(8,128)S(1)}, f32[256,256]{1,0:T(8,128)S(1)}, u32[]{:S(2)}, u32[]{:S(2)}) collective-permute-start(f32[256,256]{1,0:T(8,128)S(1)} %get-tuple-element.24), channel_id=1, source_target_pairs={{4,28},{12,20},{20,12},{5,29},{13,21},{25,1},{6,30},{18,10},{26,2}... | collective-permute-start | bytes 786440 | tf_op jit(solution)/shard_map/ppermute | solution.py:258
  52.2 0.1 collective-permute-start.6
  52.3 0.7 collective-permute-done.11.refs_2_
  53.1 2.9 %collective-permute-done.12.refs_3_ = f32[256,256]{1,0:T(8,128)S(1)} collective-permute-done((f32[256,256]{1,0:T(8,128)S(1)}, f32[256,256]{1,0:T(8,128)S(1)}, u32[]{:S(2)}, u32[]{:S(2)}) %collective-permute-start.12) | collective-permute-done | bytes 262176 | tf_op jit(solution)/shard_map/ppermute | solution.py:258
  55.9 0.7 total.1
  56.6 1.3 %collective-permute-start.13 = (f32[136,256]{1,0:T(8,128)S(1)}, f32[136,256]{1,0:T(8,128)S(1)}, u32[]{:S(2)}, u32[]{:S(2)}) collective-permute-start(f32[136,256]{1,0:T(8,128)S(1)} %get-tuple-element.26), channel_id=1, source_target_pairs={{1,5},{2,6},{3,7},{12,8},{10,14},{11,15},{20,16},{21,17},{19,23},{... | collective-permute-start | bytes 417800 | tf_op jit(solution)/shard_map/ppermute | solution.py:258
  57.9 1.6 %collective-permute-start.14 = (f32[136,256]{1,0:T(8,128)S(1)}, f32[136,256]{1,0:T(8,128)S(1)}, u32[]{:S(2)}, u32[]{:S(2)}) collective-permute-start(f32[136,256]{1,0:T(8,128)S(1)} %get-tuple-element.27), channel_id=1, source_target_pairs={{1,8},{2,16},{3,24},{12,1},{10,17},{11,25},{20,2},{21,10},{19,26},... | collective-permute-start | bytes 417800 | tf_op jit(solution)/shard_map/ppermute | solution.py:258
  59.5 1.9 %collective-permute-start.15 = (f32[128,256]{1,0:T(8,128)S(1)}, f32[128,256]{1,0:T(8,128)S(1)}, u32[]{:S(2)}, u32[]{:S(2)}) collective-permute-start(f32[128,256]{1,0:T(8,128)S(1)} %get-tuple-element.28), channel_id=1, source_target_pairs={{1,12},{2,20},{3,28},{12,5},{10,21},{11,29},{20,6},{21,14},{19,30}... | collective-permute-start | bytes 393224 | tf_op jit(solution)/shard_map/ppermute | solution.py:258
  61.5 4.0 %collective-permute-start.16 = (f32[8,256]{1,0:T(8,128)S(1)}, f32[8,256]{1,0:T(8,128)S(1)}, u32[]{:S(2)}, u32[]{:S(2)}) collective-permute-start(f32[8,256]{1,0:T(8,128)S(1)} %get-tuple-element.29), channel_id=1, source_target_pairs={{1,29},{2,30},{3,31},{12,4},{10,6},{11,7},{20,12},{21,13},{19,15},... | collective-permute-start | bytes 24584 | tf_op jit(solution)/shard_map/ppermute | solution.py:258
  65.4 6.4 %collective-permute-start.17 = (f32[8,256]{1,0:T(8,128)S(1)}, f32[8,256]{1,0:T(8,128)S(1)}, u32[]{:S(2)}, u32[]{:S(2)}) collective-permute-start(f32[8,256]{1,0:T(8,128)S(1)} %get-tuple-element.30), channel_id=1, source_target_pairs={{1,4},{2,12},{3,20},{12,29},{10,13},{11,21},{20,30},{21,6},{19,22}... | collective-permute-start | bytes 24584 | tf_op jit(solution)/shard_map/ppermute | solution.py:258
  71.9 11.1 %factor.1.w_ref = f32[256,256]{1,0:T(8,128)S(1)} custom-call(f32[256,256]{1,0:T(8,128)S(1)} %maximum_select_fusion.g_ref), custom_call_target="tpu_custom_call" | custom-call | flops 33554432 | bytes 524288 | tf_op jit(solution)/shard_map/factor/pallas_call | solution.py:121
  83.0 1.6 %tiles.1 = f32[256,128]{1,0:T(8,128)} custom-call(s32[4]{0:T(128)S(1)} %pad_add_fusion.pos_ref, f32[256,256]{1,0:T(8,128)S(1)} %factor.1.w_ref, f32[256,256]{1,0:T(8,128)S(1)} %maximum_select_fusion.g_ref, f32[136,256]{1,0:T(8,128)S(1)} %get-tuple-element.25.own_ref, f32[136,256]{1,0:T(8,128)S(1)} %collective-permute-done.13.sib_ref, ...), custom_call_target="tpu_custom_call" | custom-call | tf_op jit(solution)/shard_map/tiles/pallas_call | solution.py:229
  (20 shorter events, 0.1 us)
Async XLA Ops:
  0.7 5.6 %copy-start.1 = (f32[384]{0:T(512)S(1)}, f32[384]{0:T(512)}, u32[]{:S(2)}) copy-start(f32[384]{0:T(512)} %param.3) | copy-start | bytes 4612
  0.7 5.7 %collective-permute-start = (bf16[3,1,256]{2,1,0:T(2,128)(2,1)S(1)}, bf16[3,1,256]{2,1,0:T(2,128)(2,1)S(1)}, u32[]{:S(2)}, u32[]{:S(2)}) collective-permute-start(bf16[3,1,256]{2,1,0:T(2,128)(2,1)S(1)} %get-tuple-element.32), channel_id=1, source_target_pairs={{0,4},{4,8},{8,12},{12,16},{16,20},{20,24},{24,28},{1,5},{5,9},{9,... | collective-permute-start | bytes 4616 | tf_op jit(solution)/shard_map/ppermute | solution.py:243
  4.4 4.9 %collective-permute-start.1 = (bf16[3,1,256]{2,1,0:T(2,128)(2,1)S(1)}, bf16[3,1,256]{2,1,0:T(2,128)(2,1)S(1)}, u32[]{:S(2)}, u32[]{:S(2)}) collective-permute-start(bf16[3,1,256]{2,1,0:T(2,128)(2,1)S(1)} %get-tuple-element.31), channel_id=1, source_target_pairs={{4,0},{8,4},{12,8},{16,12},{20,16},{24,20},{28,24},{5,1},{9,5},{13... | collective-permute-start | bytes 4616 | tf_op jit(solution)/shard_map/ppermute | solution.py:244
  9.3 1.1 %copy-start = (bf16[3,384,256]{2,1,0:T(8,128)(2,1)S(1)}, bf16[3,384,256]{2,1,0:T(8,128)(2,1)}, u32[]{:S(2)}) copy-start(bf16[3,384,256]{2,1,0:T(8,128)(2,1)} %vel_ref.1) | copy-start | bytes 1769476
  11.2 10.9 %collective-permute-start.7 = (bf16[1152,256]{1,0:T(8,128)(2,1)S(1)}, bf16[1152,256]{1,0:T(8,128)(2,1)S(1)}, u32[]{:S(2)}, u32[]{:S(2)}) collective-permute-start(bf16[1152,256]{1,0:T(8,128)(2,1)S(1)} %get-tuple-element.20), channel_id=1, source_target_pairs={{0,1},{1,2},{2,3},{8,9},{9,10},{10,11},{16,17},{17,18},{18,19},{24... | collective-permute-start | bytes 1769480 | tf_op jit(solution)/shard_map/ppermute | solution.py:258
  12.6 29.3 %collective-permute-start.8 = (bf16[1152,256]{1,0:T(8,128)(2,1)S(1)}, bf16[1152,256]{1,0:T(8,128)(2,1)S(1)}, u32[]{:S(2)}, u32[]{:S(2)}) collective-permute-start(bf16[1152,256]{1,0:T(8,128)(2,1)S(1)} %get-tuple-element.20), channel_id=1, source_target_pairs={{0,2},{1,3},{8,10},{9,11},{16,18},{17,19},{24,26},{25,27},{6,4},{7... | collective-permute-start | bytes 1769480 | tf_op jit(solution)/shard_map/ppermute | solution.py:258
  13.9 28.0 %collective-permute-start.9 = (bf16[1152,256]{1,0:T(8,128)(2,1)S(1)}, bf16[1152,256]{1,0:T(8,128)(2,1)S(1)}, u32[]{:S(2)}, u32[]{:S(2)}) collective-permute-start(bf16[1152,256]{1,0:T(8,128)(2,1)S(1)} %get-tuple-element.20), channel_id=1, source_target_pairs={{0,3},{8,11},{16,19},{24,27},{7,4},{15,12},{23,20},{31,28}} | collective-permute-start | bytes 1769480 | tf_op jit(solution)/shard_map/ppermute | solution.py:258
  15.2 6.4 %collective-permute-start.2 = (f32[128,256]{1,0:T(8,128)S(1)}, f32[128,256]{1,0:T(8,128)S(1)}, u32[]{:S(2)}, u32[]{:S(2)}) collective-permute-start(f32[128,256]{1,0:T(8,128)S(1)} %constant_dynamic-slice_fusion), channel_id=1, source_target_pairs={{0,4},{4,0},{1,5},{5,1},{2,6},{6,2},{3,7},{7,3},{8,12},{12,8},{9,1... | collective-permute-start | bytes 393224 | tf_op jit(solution)/shard_map/ppermute | solution.py:258
  21.6 25.4 %collective-permute-start.3 = (f32[128,256]{1,0:T(8,128)S(1)}, f32[128,256]{1,0:T(8,128)S(1)}, u32[]{:S(2)}, u32[]{:S(2)}) collective-permute-start(f32[128,256]{1,0:T(8,128)S(1)} %dynamic-slice_add_fusion), channel_id=1, source_target_pairs={{0,8},{4,12},{1,9},{5,13},{2,10},{6,14},{3,11},{7,15},{8,0},{12,4}... | collective-permute-start | bytes 393224 | tf_op jit(solution)/shard_map/ppermute | solution.py:258
  21.9 30.2 %collective-permute-start.4 = (f32[128,256]{1,0:T(8,128)S(1)}, f32[128,256]{1,0:T(8,128)S(1)}, u32[]{:S(2)}, u32[]{:S(2)}) collective-permute-start(f32[128,256]{1,0:T(8,128)S(1)} %dynamic-slice_add_fusion), channel_id=1, source_target_pairs={{0,16},{4,20},{1,17},{5,21},{2,18},{6,22},{3,19},{7,23},{8,24},{12... | collective-permute-start | bytes 393224 | tf_op jit(solution)/shard_map/ppermute | solution.py:258
  22.2 30.0 %collective-permute-start.5 = (f32[128,256]{1,0:T(8,128)S(1)}, f32[128,256]{1,0:T(8,128)S(1)}, u32[]{:S(2)}, u32[]{:S(2)}) collective-permute-start(f32[128,256]{1,0:T(8,128)S(1)} %dynamic-slice_add_fusion), channel_id=1, source_target_pairs={{0,24},{4,28},{1,25},{5,29},{2,26},{6,30},{3,27},{7,31},{8,16},{12... | collective-permute-start | bytes 393224 | tf_op jit(solution)/shard_map/ppermute | solution.py:258
  43.8 8.6 %collective-permute-start.10 = (f32[256,256]{1,0:T(8,128)S(1)}, f32[256,256]{1,0:T(8,128)S(1)}, u32[]{:S(2)}, u32[]{:S(2)}) collective-permute-start(f32[256,256]{1,0:T(8,128)S(1)} %get-tuple-element.22), channel_id=1, source_target_pairs={{4,12},{20,28},{28,20},{9,1},{21,29},{29,21},{2,10},{10,2},{22,30}... | collective-permute-start | bytes 786440 | tf_op jit(solution)/shard_map/ppermute | solution.py:258
  45.7 7.4 %collective-permute-start.11 = (f32[256,256]{1,0:T(8,128)S(1)}, f32[256,256]{1,0:T(8,128)S(1)}, u32[]{:S(2)}, u32[]{:S(2)}) collective-permute-start(f32[256,256]{1,0:T(8,128)S(1)} %get-tuple-element.23), channel_id=1, source_target_pairs={{4,20},{12,28},{28,12},{5,21},{13,29},{17,1},{14,30},{18,2},{26,10... | collective-permute-start | bytes 786440 | tf_op jit(solution)/shard_map/ppermute | solution.py:258
  47.0 8.9 %collective-permute-start.12 = (f32[256,256]{1,0:T(8,128)S(1)}, f32[256,256]{1,0:T(8,128)S(1)}, u32[]{:S(2)}, u32[]{:S(2)}) collective-permute-start(f32[256,256]{1,0:T(8,128)S(1)} %get-tuple-element.24), channel_id=1, source_target_pairs={{4,28},{12,20},{20,12},{5,29},{13,21},{25,1},{6,30},{18,10},{26,2}... | collective-permute-start | bytes 786440 | tf_op jit(solution)/shard_map/ppermute | solution.py:258
  52.2 13.2 %collective-permute-start.6 = (f32[128,256]{1,0:T(8,128)S(1)}, f32[128,256]{1,0:T(8,128)S(1)}, u32[]{:S(2)}, u32[]{:S(2)}) collective-permute-start(f32[128,256]{1,0:T(8,128)S(1)} %add_add_fusion), channel_id=1, source_target_pairs={{0,4},{4,0},{1,5},{5,1},{2,6},{6,2},{3,7},{7,3},{8,12},{12,8},{9,1... | collective-permute-start | bytes 393224 | tf_op jit(solution)/shard_map/ppermute | solution.py:258
  56.6 26.4 %collective-permute-start.13 = (f32[136,256]{1,0:T(8,128)S(1)}, f32[136,256]{1,0:T(8,128)S(1)}, u32[]{:S(2)}, u32[]{:S(2)}) collective-permute-start(f32[136,256]{1,0:T(8,128)S(1)} %get-tuple-element.26), channel_id=1, source_target_pairs={{1,5},{2,6},{3,7},{12,8},{10,14},{11,15},{20,16},{21,17},{19,23},{... | collective-permute-start | bytes 417800 | tf_op jit(solution)/shard_map/ppermute | solution.py:258
  57.9 25.1 %collective-permute-start.14 = (f32[136,256]{1,0:T(8,128)S(1)}, f32[136,256]{1,0:T(8,128)S(1)}, u32[]{:S(2)}, u32[]{:S(2)}) collective-permute-start(f32[136,256]{1,0:T(8,128)S(1)} %get-tuple-element.27), channel_id=1, source_target_pairs={{1,8},{2,16},{3,24},{12,1},{10,17},{11,25},{20,2},{21,10},{19,26},... | collective-permute-start | bytes 417800 | tf_op jit(solution)/shard_map/ppermute | solution.py:258
  59.5 23.4 %collective-permute-start.15 = (f32[128,256]{1,0:T(8,128)S(1)}, f32[128,256]{1,0:T(8,128)S(1)}, u32[]{:S(2)}, u32[]{:S(2)}) collective-permute-start(f32[128,256]{1,0:T(8,128)S(1)} %get-tuple-element.28), channel_id=1, source_target_pairs={{1,12},{2,20},{3,28},{12,5},{10,21},{11,29},{20,6},{21,14},{19,30}... | collective-permute-start | bytes 393224 | tf_op jit(solution)/shard_map/ppermute | solution.py:258
  61.5 21.5 %collective-permute-start.16 = (f32[8,256]{1,0:T(8,128)S(1)}, f32[8,256]{1,0:T(8,128)S(1)}, u32[]{:S(2)}, u32[]{:S(2)}) collective-permute-start(f32[8,256]{1,0:T(8,128)S(1)} %get-tuple-element.29), channel_id=1, source_target_pairs={{1,29},{2,30},{3,31},{12,4},{10,6},{11,7},{20,12},{21,13},{19,15},... | collective-permute-start | bytes 24584 | tf_op jit(solution)/shard_map/ppermute | solution.py:258
  65.4 17.5 %collective-permute-start.17 = (f32[8,256]{1,0:T(8,128)S(1)}, f32[8,256]{1,0:T(8,128)S(1)}, u32[]{:S(2)}, u32[]{:S(2)}) collective-permute-start(f32[8,256]{1,0:T(8,128)S(1)} %get-tuple-element.30), channel_id=1, source_target_pairs={{1,4},{2,12},{3,20},{12,29},{10,13},{11,21},{20,30},{21,6},{19,22}... | collective-permute-start | bytes 24584 | tf_op jit(solution)/shard_map/ppermute | solution.py:258

commit v2 on v1

--- a/solution.py
+++ b/solution.py
@@ -130,7 +130,8 @@
     )(gram)
 
 
-def blocks_kernel(count, pos_ref, xt_ref, *refs):
+def blocks_kernel(count, pos_ref, after_ref, xt_ref, *refs):
+    del after_ref
     panels, outs = refs[: count - 1], refs[count - 1 :]
     chip, group, core = pos_ref[0], pos_ref[1], pos_ref[2]
     for r in range(1, count):
@@ -143,18 +144,18 @@
                 outs[m][...] = block
 
 
-def blocks(pos, xt, panels):
+def blocks(pos, after, xt, panels):
     n = xt.shape[0]
     count = len(panels) + 1
     return pl.pallas_call(
         functools.partial(blocks_kernel, count),
         out_shape=(jax.ShapeDtypeStruct((n, n), F32),) * count,
-        in_specs=[SMEM] + [VMEM] * count,
+        in_specs=[SMEM, pl.BlockSpec(memory_space=pl.ANY)] + [VMEM] * count,
         out_specs=(VMEM,) * count,
         compiler_params=params(),
         cost_estimate=cost(2 * (count - 1) * n * n * xt.shape[1], 4 * count * n * n),
         name="blocks",
-    )(pos, xt, *panels)
+    )(pos, after, xt, *panels)
 
 
 def total_kernel(pos_ref, *refs):
@@ -285,7 +286,7 @@
         pairs = [(at(k, z, 0), at(k, z + r, 0)) for k in every for z in range(groups - r)]
         pairs += [(at(k, z, 1), at(k, z - r, 1)) for k in every for z in range(r, groups)]
         panels.append(send(x, pairs))
-    parts = list(blocks(pos, xt, panels))
+    parts = list(blocks(pos, w, xt, panels))
     for m in range(1, groups):
         pairs = []
         for z in every:

time: 85.1 us -> 84.3 us (level)
  waiting for transfers between devices: 24.9 us -> 14.8 us
  starting transfers between devices: 41.2 us -> 50 us
    ppermute x16, starting transfers between devices: 35.6 us -> 44.4 us  [send(): return lax.ppermute(value, axes, pairs)]
    ppermute x16, waiting for transfers between devices: 22.1 us -> 14.8 us  [send(): return lax.ppermute(value, axes, pairs)]
    ppermute x1, waiting for transfers between devices: 2.85 us -> 0.01 us  [halos(): hi = lax.ppermute(head, 'space', [(i + 1, i) for i in range(count - 1)])]
  transfers between devices with their start and end apart: 18 -> 18, of which waited for: 5 -> 9; matrix products, arithmetic and copies ran while one was open for 0% -> 0% of each run, Pallas kernels for 16% -> 13%
where the time goes in v2:
time: 84.3 us; the launch traced here: 83.9 us
  starting transfers between devices  50 us (59%)
  Pallas kernels  16.1 us (19%)
  waiting for transfers between devices  14.8 us (18%)
  local copies, waits for them, and re-layouts  2.59 us (3%)
    ppermute x16, starting transfers between devices, send(): return lax.ppermute(value, axes, pairs)  44.4 us
    ppermute x16, waiting for transfers between devices, send(): return lax.ppermute(value, axes, pairs)  14.8 us
    pallas_call x1, Pallas kernels, inverse_factor(): pl.pallas_call(factor_kernel, out_shape=jax.ShapeDtypeStruct((n, n), F32)...  11.1 us
    ppermute x1, starting transfers between devices, halos(): lo = lax.ppermute(tail, 'space', [(i, i + 1) for i in range(count - 1)])  3.02 us
    ppermute x1, starting transfers between devices, halos(): hi = lax.ppermute(head, 'space', [(i + 1, i) for i in range(count - 1)])  2.57 us
    pallas_call x1, Pallas kernels, blocks(): pl.pallas_call(functools.partial(blocks_kernel, count), out_shape=(jax.Sh...  1.9 us
    unnamed x4, local copies, waits for them, and re-layouts  1.73 us
  transfers between devices with their start and end apart: 18, of which 9 were waited for; matrix products, arithmetic and copies ran while one was open for 0% of the time, Pallas kernels for 13%

profile of v2, /device:TPU:5, one launch (start us, length us, event | category | flops | bytes accessed | tf_op | source)
XLA Modules:
  0.0 83.9 jit_solution(16059316055769954844)
XLA Ops:
  0.0 0.7 fusion
  0.7 2.6 %collective-permute-start.1 = (bf16[3,1,256]{2,1,0:T(2,128)(2,1)S(1)}, bf16[3,1,256]{2,1,0:T(2,128)(2,1)S(1)}, u32[]{:S(2)}, u32[]{:S(2)}) collective-permute-start(bf16[3,1,256]{2,1,0:T(2,128)(2,1)S(1)} %get-tuple-element.31), channel_id=1, source_target_pairs={{4,0},{8,4},{12,8},{16,12},{20,16},{24,20},{28,24},{5,1},{9,5},{13... | collective-permute-start | bytes 4616 | tf_op jit(solution)/shard_map/ppermute | solution.py:245
  3.3 3.0 %collective-permute-start = (bf16[3,1,256]{2,1,0:T(2,128)(2,1)S(1)}, bf16[3,1,256]{2,1,0:T(2,128)(2,1)S(1)}, u32[]{:S(2)}, u32[]{:S(2)}) collective-permute-start(bf16[3,1,256]{2,1,0:T(2,128)(2,1)S(1)} %get-tuple-element.32), channel_id=1, source_target_pairs={{0,4},{4,8},{8,12},{12,16},{16,20},{20,24},{24,28},{1,5},{5,9},{9,... | collective-permute-start | bytes 4616 | tf_op jit(solution)/shard_map/ppermute | solution.py:244
  6.4 0.7 copy-done.1
  7.2 1.1 %copy-done = bf16[3,384,256]{2,1,0:T(8,128)(2,1)S(1)} copy-done((bf16[3,384,256]{2,1,0:T(8,128)(2,1)S(1)}, bf16[3,384,256]{2,1,0:T(8,128)(2,1)}, u32[]{:S(2)}) %copy-start) | copy-done | bytes 589848
  8.2 0.8 panel.1
  9.1 2.9 %collective-permute-start.2 = (f32[128,256]{1,0:T(8,128)S(1)}, f32[128,256]{1,0:T(8,128)S(1)}, u32[]{:S(2)}, u32[]{:S(2)}) collective-permute-start(f32[128,256]{1,0:T(8,128)S(1)} %constant_dynamic-slice_fusion), channel_id=1, source_target_pairs={{0,4},{4,0},{1,5},{5,1},{2,6},{6,2},{3,7},{7,3},{8,12},{12,8},{9,1... | collective-permute-start | bytes 393224 | tf_op jit(solution)/shard_map/ppermute | solution.py:259
  12.0 1.0 %collective-permute-done.2 = f32[128,256]{1,0:T(8,128)S(1)} collective-permute-done((f32[128,256]{1,0:T(8,128)S(1)}, f32[128,256]{1,0:T(8,128)S(1)}, u32[]{:S(2)}, u32[]{:S(2)}) %collective-permute-start.2) | collective-permute-done | bytes 131104 | tf_op jit(solution)/shard_map/ppermute | solution.py:259
  13.1 0.6 collective-permute-start.4
  13.7 2.0 %collective-permute-start.3 = (f32[128,256]{1,0:T(8,128)S(1)}, f32[128,256]{1,0:T(8,128)S(1)}, u32[]{:S(2)}, u32[]{:S(2)}) collective-permute-start(f32[128,256]{1,0:T(8,128)S(1)} %dynamic-slice_add_fusion), channel_id=1, source_target_pairs={{0,8},{4,12},{1,9},{5,13},{2,10},{6,14},{3,11},{7,15},{8,0},{12,4}... | collective-permute-start | bytes 393224 | tf_op jit(solution)/shard_map/ppermute | solution.py:259
  15.7 1.3 %collective-permute-start.9 = (bf16[1152,256]{1,0:T(8,128)(2,1)S(1)}, bf16[1152,256]{1,0:T(8,128)(2,1)S(1)}, u32[]{:S(2)}, u32[]{:S(2)}) collective-permute-start(bf16[1152,256]{1,0:T(8,128)(2,1)S(1)} %get-tuple-element.20), channel_id=1, source_target_pairs={{0,3},{8,11},{16,19},{24,27},{7,4},{15,12},{23,20},{31,28}} | collective-permute-start | bytes 1769480 | tf_op jit(solution)/shard_map/ppermute | solution.py:259
  17.0 1.3 %collective-permute-start.8 = (bf16[1152,256]{1,0:T(8,128)(2,1)S(1)}, bf16[1152,256]{1,0:T(8,128)(2,1)S(1)}, u32[]{:S(2)}, u32[]{:S(2)}) collective-permute-start(bf16[1152,256]{1,0:T(8,128)(2,1)S(1)} %get-tuple-element.20), channel_id=1, source_target_pairs={{0,2},{1,3},{8,10},{9,11},{16,18},{17,19},{24,26},{25,27},{6,4},{7... | collective-permute-start | bytes 1769480 | tf_op jit(solution)/shard_map/ppermute | solution.py:259
  18.7 1.3 %collective-permute-start.7 = (bf16[1152,256]{1,0:T(8,128)(2,1)S(1)}, bf16[1152,256]{1,0:T(8,128)(2,1)S(1)}, u32[]{:S(2)}, u32[]{:S(2)}) collective-permute-start(bf16[1152,256]{1,0:T(8,128)(2,1)S(1)} %get-tuple-element.20), channel_id=1, source_target_pairs={{0,1},{1,2},{2,3},{8,9},{9,10},{10,11},{16,17},{17,18},{18,19},{24... | collective-permute-start | bytes 1769480 | tf_op jit(solution)/shard_map/ppermute | solution.py:259
  20.0 0.7 collective-permute-done.4
  20.7 5.7 %collective-permute-start.6 = (f32[128,256]{1,0:T(8,128)S(1)}, f32[128,256]{1,0:T(8,128)S(1)}, u32[]{:S(2)}, u32[]{:S(2)}) collective-permute-start(f32[128,256]{1,0:T(8,128)S(1)} %add_add_fusion), channel_id=1, source_target_pairs={{0,4},{4,0},{1,5},{5,1},{2,6},{6,2},{3,7},{7,3},{8,12},{12,8},{9,1... | collective-permute-start | bytes 393224 | tf_op jit(solution)/shard_map/ppermute | solution.py:259
  26.5 0.9 %collective-permute-done.6 = f32[128,256]{1,0:T(8,128)S(1)} collective-permute-done((f32[128,256]{1,0:T(8,128)S(1)}, f32[128,256]{1,0:T(8,128)S(1)}, u32[]{:S(2)}, u32[]{:S(2)}) %collective-permute-start.6) | collective-permute-done | bytes 131104 | tf_op jit(solution)/shard_map/ppermute | solution.py:259
  27.4 11.1 %factor.1.after_ref.w_ref = f32[256,256]{1,0:T(8,128)S(1)} custom-call(f32[256,256]{1,0:T(8,128)S(1)} %maximum_select_fusion.g_ref), custom_call_target="tpu_custom_call" | custom-call | flops 33554432 | bytes 524288 | tf_op jit(solution)/shard_map/factor/pallas_call | solution.py:121
  38.5 2.3 %collective-permute-done.8.refs_1_ = bf16[1152,256]{1,0:T(8,128)(2,1)S(1)} collective-permute-done((bf16[1152,256]{1,0:T(8,128)(2,1)S(1)}, bf16[1152,256]{1,0:T(8,128)(2,1)S(1)}, u32[]{:S(2)}, u32[]{:S(2)}) %collective-permute-start.8) | collective-permute-done | bytes 589856 | tf_op jit(solution)/shard_map/ppermute | solution.py:259
  40.8 1.9 %blocks.1 = (f32[256,256]{1,0:T(8,128)S(1)}, f32[256,256]{1,0:T(8,128)S(1)}, f32[256,256]{1,0:T(8,128)S(1)}, f32[256,256]{1,0:T(8,128)S(1)}) custom-call(s32[4]{0:T(128)S(1)} %pad_add_fusion.pos_ref, f32[256,256]{1,0:T(8,128)S(1)} %factor.1.after_ref.w_ref, bf16[256,1152]{1,0:T(8,128)(2,1)S(1)} %get-tuple-element.19.xt_ref, ...), custom_call_target="tpu_custom_call" | custom-call | flops 452984832 | bytes 1048576 | tf_op jit(solution)/shard_map/blocks/pallas_call | solution.py:150
  42.7 1.9 %collective-permute-start.10 = (f32[256,256]{1,0:T(8,128)S(1)}, f32[256,256]{1,0:T(8,128)S(1)}, u32[]{:S(2)}, u32[]{:S(2)}) collective-permute-start(f32[256,256]{1,0:T(8,128)S(1)} %get-tuple-element.22), channel_id=1, source_target_pairs={{4,12},{20,28},{28,20},{9,1},{21,29},{29,21},{2,10},{10,2},{22,30}... | collective-permute-start | bytes 786440 | tf_op jit(solution)/shard_map/ppermute | solution.py:259
  44.6 1.3 %collective-permute-start.11 = (f32[256,256]{1,0:T(8,128)S(1)}, f32[256,256]{1,0:T(8,128)S(1)}, u32[]{:S(2)}, u32[]{:S(2)}) collective-permute-start(f32[256,256]{1,0:T(8,128)S(1)} %get-tuple-element.23), channel_id=1, source_target_pairs={{4,20},{12,28},{28,12},{5,21},{13,29},{17,1},{14,30},{18,2},{26,10... | collective-permute-start | bytes 786440 | tf_op jit(solution)/shard_map/ppermute | solution.py:259
  45.9 5.2 %collective-permute-start.12 = (f32[256,256]{1,0:T(8,128)S(1)}, f32[256,256]{1,0:T(8,128)S(1)}, u32[]{:S(2)}, u32[]{:S(2)}) collective-permute-start(f32[256,256]{1,0:T(8,128)S(1)} %get-tuple-element.24), channel_id=1, source_target_pairs={{4,28},{12,20},{20,12},{5,29},{13,21},{25,1},{6,30},{18,10},{26,2}... | collective-permute-start | bytes 786440 | tf_op jit(solution)/shard_map/ppermute | solution.py:259
  51.1 0.6 collective-permute-done.11.refs_2_
  51.8 3.1 %collective-permute-done.12.refs_3_ = f32[256,256]{1,0:T(8,128)S(1)} collective-permute-done((f32[256,256]{1,0:T(8,128)S(1)}, f32[256,256]{1,0:T(8,128)S(1)}, u32[]{:S(2)}, u32[]{:S(2)}) %collective-permute-start.12) | collective-permute-done | bytes 262176 | tf_op jit(solution)/shard_map/ppermute | solution.py:259
  54.9 0.7 total.1
  55.6 1.3 %collective-permute-start.13 = (f32[136,256]{1,0:T(8,128)S(1)}, f32[136,256]{1,0:T(8,128)S(1)}, u32[]{:S(2)}, u32[]{:S(2)}) collective-permute-start(f32[136,256]{1,0:T(8,128)S(1)} %get-tuple-element.26), channel_id=1, source_target_pairs={{1,5},{2,6},{3,7},{12,8},{10,14},{11,15},{20,16},{21,17},{19,23},{... | collective-permute-start | bytes 417800 | tf_op jit(solution)/shard_map/ppermute | solution.py:259
  56.9 13.8 %collective-permute-start.14 = (f32[136,256]{1,0:T(8,128)S(1)}, f32[136,256]{1,0:T(8,128)S(1)}, u32[]{:S(2)}, u32[]{:S(2)}) collective-permute-start(f32[136,256]{1,0:T(8,128)S(1)} %get-tuple-element.27), channel_id=1, source_target_pairs={{1,8},{2,16},{3,24},{12,1},{10,17},{11,25},{20,2},{21,10},{19,26},... | collective-permute-start | bytes 417800 | tf_op jit(solution)/shard_map/ppermute | solution.py:259
  70.7 1.9 %collective-permute-start.15 = (f32[128,256]{1,0:T(8,128)S(1)}, f32[128,256]{1,0:T(8,128)S(1)}, u32[]{:S(2)}, u32[]{:S(2)}) collective-permute-start(f32[128,256]{1,0:T(8,128)S(1)} %get-tuple-element.28), channel_id=1, source_target_pairs={{1,12},{2,20},{3,28},{12,5},{10,21},{11,29},{20,6},{21,14},{19,30}... | collective-permute-start | bytes 393224 | tf_op jit(solution)/shard_map/ppermute | solution.py:259
  72.6 1.9 %collective-permute-start.16 = (f32[8,256]{1,0:T(8,128)S(1)}, f32[8,256]{1,0:T(8,128)S(1)}, u32[]{:S(2)}, u32[]{:S(2)}) collective-permute-start(f32[8,256]{1,0:T(8,128)S(1)} %get-tuple-element.29), channel_id=1, source_target_pairs={{1,29},{2,30},{3,31},{12,4},{10,6},{11,7},{20,12},{21,13},{19,15},... | collective-permute-start | bytes 24584 | tf_op jit(solution)/shard_map/ppermute | solution.py:259
  74.6 1.9 %collective-permute-start.17 = (f32[8,256]{1,0:T(8,128)S(1)}, f32[8,256]{1,0:T(8,128)S(1)}, u32[]{:S(2)}, u32[]{:S(2)}) collective-permute-start(f32[8,256]{1,0:T(8,128)S(1)} %get-tuple-element.30), channel_id=1, source_target_pairs={{1,4},{2,12},{3,20},{12,29},{10,13},{11,21},{20,30},{21,6},{19,22}... | collective-permute-start | bytes 24584 | tf_op jit(solution)/shard_map/ppermute | solution.py:259
  77.0 5.2 %collective-permute-done.17.top_ref = f32[8,256]{1,0:T(8,128)S(1)} collective-permute-done((f32[8,256]{1,0:T(8,128)S(1)}, f32[8,256]{1,0:T(8,128)S(1)}, u32[]{:S(2)}, u32[]{:S(2)}) %collective-permute-start.17) | collective-permute-done | bytes 8224 | tf_op jit(solution)/shard_map/ppermute | solution.py:259
  82.2 1.6 %tiles.1 = f32[256,128]{1,0:T(8,128)} custom-call(s32[4]{0:T(128)S(1)} %pad_add_fusion.pos_ref, f32[256,256]{1,0:T(8,128)S(1)} %factor.1.after_ref.w_ref, f32[256,256]{1,0:T(8,128)S(1)} %maximum_select_fusion.g_ref, f32[136,256]{1,0:T(8,128)S(1)} %get-tuple-element.25.own_ref, f32[136,256]{1,0:T(8,128)S(1)} %collective-permute-done.13.sib_ref, ...), custom_call_target="tpu_custom_call" | custom-call | tf_op jit(solution)/shard_map/tiles/pallas_call | solution.py:230
  (20 shorter events, 1.3 us)
Async XLA Ops:
  0.7 6.4 %collective-permute-start.1 = (bf16[3,1,256]{2,1,0:T(2,128)(2,1)S(1)}, bf16[3,1,256]{2,1,0:T(2,128)(2,1)S(1)}, u32[]{:S(2)}, u32[]{:S(2)}) collective-permute-start(bf16[3,1,256]{2,1,0:T(2,128)(2,1)S(1)} %get-tuple-element.31), channel_id=1, source_target_pairs={{4,0},{8,4},{12,8},{16,12},{20,16},{24,20},{28,24},{5,1},{9,5},{13... | collective-permute-start | bytes 4616 | tf_op jit(solution)/shard_map/ppermute | solution.py:245
  3.3 3.9 %collective-permute-start = (bf16[3,1,256]{2,1,0:T(2,128)(2,1)S(1)}, bf16[3,1,256]{2,1,0:T(2,128)(2,1)S(1)}, u32[]{:S(2)}, u32[]{:S(2)}) collective-permute-start(bf16[3,1,256]{2,1,0:T(2,128)(2,1)S(1)} %get-tuple-element.32), channel_id=1, source_target_pairs={{0,4},{4,8},{8,12},{12,16},{16,20},{20,24},{24,28},{1,5},{5,9},{9,... | collective-permute-start | bytes 4616 | tf_op jit(solution)/shard_map/ppermute | solution.py:244
  6.4 0.7 copy-start.1
  7.2 1.1 %copy-start = (bf16[3,384,256]{2,1,0:T(8,128)(2,1)S(1)}, bf16[3,384,256]{2,1,0:T(8,128)(2,1)}, u32[]{:S(2)}) copy-start(bf16[3,384,256]{2,1,0:T(8,128)(2,1)} %vel_ref.1) | copy-start | bytes 1769476
  9.1 3.9 %collective-permute-start.2 = (f32[128,256]{1,0:T(8,128)S(1)}, f32[128,256]{1,0:T(8,128)S(1)}, u32[]{:S(2)}, u32[]{:S(2)}) collective-permute-start(f32[128,256]{1,0:T(8,128)S(1)} %constant_dynamic-slice_fusion), channel_id=1, source_target_pairs={{0,4},{4,0},{1,5},{5,1},{2,6},{6,2},{3,7},{7,3},{8,12},{12,8},{9,1... | collective-permute-start | bytes 393224 | tf_op jit(solution)/shard_map/ppermute | solution.py:259
  13.0 5.7 %collective-permute-start.5 = (f32[128,256]{1,0:T(8,128)S(1)}, f32[128,256]{1,0:T(8,128)S(1)}, u32[]{:S(2)}, u32[]{:S(2)}) collective-permute-start(f32[128,256]{1,0:T(8,128)S(1)} %dynamic-slice_add_fusion), channel_id=1, source_target_pairs={{0,24},{4,28},{1,25},{5,29},{2,26},{6,30},{3,27},{7,31},{8,16},{12... | collective-permute-start | bytes 393224 | tf_op jit(solution)/shard_map/ppermute | solution.py:259
  13.1 7.6 %collective-permute-start.4 = (f32[128,256]{1,0:T(8,128)S(1)}, f32[128,256]{1,0:T(8,128)S(1)}, u32[]{:S(2)}, u32[]{:S(2)}) collective-permute-start(f32[128,256]{1,0:T(8,128)S(1)} %dynamic-slice_add_fusion), channel_id=1, source_target_pairs={{0,16},{4,20},{1,17},{5,21},{2,18},{6,22},{3,19},{7,23},{8,24},{12... | collective-permute-start | bytes 393224 | tf_op jit(solution)/shard_map/ppermute | solution.py:259
  13.7 7.0 %collective-permute-start.3 = (f32[128,256]{1,0:T(8,128)S(1)}, f32[128,256]{1,0:T(8,128)S(1)}, u32[]{:S(2)}, u32[]{:S(2)}) collective-permute-start(f32[128,256]{1,0:T(8,128)S(1)} %dynamic-slice_add_fusion), channel_id=1, source_target_pairs={{0,8},{4,12},{1,9},{5,13},{2,10},{6,14},{3,11},{7,15},{8,0},{12,4}... | collective-permute-start | bytes 393224 | tf_op jit(solution)/shard_map/ppermute | solution.py:259
  15.7 22.8 %collective-permute-start.9 = (bf16[1152,256]{1,0:T(8,128)(2,1)S(1)}, bf16[1152,256]{1,0:T(8,128)(2,1)S(1)}, u32[]{:S(2)}, u32[]{:S(2)}) collective-permute-start(bf16[1152,256]{1,0:T(8,128)(2,1)S(1)} %get-tuple-element.20), channel_id=1, source_target_pairs={{0,3},{8,11},{16,19},{24,27},{7,4},{15,12},{23,20},{31,28}} | collective-permute-start | bytes 1769480 | tf_op jit(solution)/shard_map/ppermute | solution.py:259
  17.0 23.8 %collective-permute-start.8 = (bf16[1152,256]{1,0:T(8,128)(2,1)S(1)}, bf16[1152,256]{1,0:T(8,128)(2,1)S(1)}, u32[]{:S(2)}, u32[]{:S(2)}) collective-permute-start(bf16[1152,256]{1,0:T(8,128)(2,1)S(1)} %get-tuple-element.20), channel_id=1, source_target_pairs={{0,2},{1,3},{8,10},{9,11},{16,18},{17,19},{24,26},{25,27},{6,4},{7... | collective-permute-start | bytes 1769480 | tf_op jit(solution)/shard_map/ppermute | solution.py:259
  18.7 22.1 %collective-permute-start.7 = (bf16[1152,256]{1,0:T(8,128)(2,1)S(1)}, bf16[1152,256]{1,0:T(8,128)(2,1)S(1)}, u32[]{:S(2)}, u32[]{:S(2)}) collective-permute-start(bf16[1152,256]{1,0:T(8,128)(2,1)S(1)} %get-tuple-element.20), channel_id=1, source_target_pairs={{0,1},{1,2},{2,3},{8,9},{9,10},{10,11},{16,17},{17,18},{18,19},{24... | collective-permute-start | bytes 1769480 | tf_op jit(solution)/shard_map/ppermute | solution.py:259
  20.7 6.7 %collective-permute-start.6 = (f32[128,256]{1,0:T(8,128)S(1)}, f32[128,256]{1,0:T(8,128)S(1)}, u32[]{:S(2)}, u32[]{:S(2)}) collective-permute-start(f32[128,256]{1,0:T(8,128)S(1)} %add_add_fusion), channel_id=1, source_target_pairs={{0,4},{4,0},{1,5},{5,1},{2,6},{6,2},{3,7},{7,3},{8,12},{12,8},{9,1... | collective-permute-start | bytes 393224 | tf_op jit(solution)/shard_map/ppermute | solution.py:259
  42.7 8.4 %collective-permute-start.10 = (f32[256,256]{1,0:T(8,128)S(1)}, f32[256,256]{1,0:T(8,128)S(1)}, u32[]{:S(2)}, u32[]{:S(2)}) collective-permute-start(f32[256,256]{1,0:T(8,128)S(1)} %get-tuple-element.22), channel_id=1, source_target_pairs={{4,12},{20,28},{28,20},{9,1},{21,29},{29,21},{2,10},{10,2},{22,30}... | collective-permute-start | bytes 786440 | tf_op jit(solution)/shard_map/ppermute | solution.py:259
  44.6 7.1 %collective-permute-start.11 = (f32[256,256]{1,0:T(8,128)S(1)}, f32[256,256]{1,0:T(8,128)S(1)}, u32[]{:S(2)}, u32[]{:S(2)}) collective-permute-start(f32[256,256]{1,0:T(8,128)S(1)} %get-tuple-element.23), channel_id=1, source_target_pairs={{4,20},{12,28},{28,12},{5,21},{13,29},{17,1},{14,30},{18,2},{26,10... | collective-permute-start | bytes 786440 | tf_op jit(solution)/shard_map/ppermute | solution.py:259
  45.9 8.9 %collective-permute-start.12 = (f32[256,256]{1,0:T(8,128)S(1)}, f32[256,256]{1,0:T(8,128)S(1)}, u32[]{:S(2)}, u32[]{:S(2)}) collective-permute-start(f32[256,256]{1,0:T(8,128)S(1)} %get-tuple-element.24), channel_id=1, source_target_pairs={{4,28},{12,20},{20,12},{5,29},{13,21},{25,1},{6,30},{18,10},{26,2}... | collective-permute-start | bytes 786440 | tf_op jit(solution)/shard_map/ppermute | solution.py:259
  55.6 26.7 %collective-permute-start.13 = (f32[136,256]{1,0:T(8,128)S(1)}, f32[136,256]{1,0:T(8,128)S(1)}, u32[]{:S(2)}, u32[]{:S(2)}) collective-permute-start(f32[136,256]{1,0:T(8,128)S(1)} %get-tuple-element.26), channel_id=1, source_target_pairs={{1,5},{2,6},{3,7},{12,8},{10,14},{11,15},{20,16},{21,17},{19,23},{... | collective-permute-start | bytes 417800 | tf_op jit(solution)/shard_map/ppermute | solution.py:259
  56.9 25.4 %collective-permute-start.14 = (f32[136,256]{1,0:T(8,128)S(1)}, f32[136,256]{1,0:T(8,128)S(1)}, u32[]{:S(2)}, u32[]{:S(2)}) collective-permute-start(f32[136,256]{1,0:T(8,128)S(1)} %get-tuple-element.27), channel_id=1, source_target_pairs={{1,8},{2,16},{3,24},{12,1},{10,17},{11,25},{20,2},{21,10},{19,26},... | collective-permute-start | bytes 417800 | tf_op jit(solution)/shard_map/ppermute | solution.py:259
  70.7 11.5 %collective-permute-start.15 = (f32[128,256]{1,0:T(8,128)S(1)}, f32[128,256]{1,0:T(8,128)S(1)}, u32[]{:S(2)}, u32[]{:S(2)}) collective-permute-start(f32[128,256]{1,0:T(8,128)S(1)} %get-tuple-element.28), channel_id=1, source_target_pairs={{1,12},{2,20},{3,28},{12,5},{10,21},{11,29},{20,6},{21,14},{19,30}... | collective-permute-start | bytes 393224 | tf_op jit(solution)/shard_map/ppermute | solution.py:259
  72.6 4.4 %collective-permute-start.16 = (f32[8,256]{1,0:T(8,128)S(1)}, f32[8,256]{1,0:T(8,128)S(1)}, u32[]{:S(2)}, u32[]{:S(2)}) collective-permute-start(f32[8,256]{1,0:T(8,128)S(1)} %get-tuple-element.29), channel_id=1, source_target_pairs={{1,29},{2,30},{3,31},{12,4},{10,6},{11,7},{20,12},{21,13},{19,15},... | collective-permute-start | bytes 24584 | tf_op jit(solution)/shard_map/ppermute | solution.py:259
  74.6 7.7 %collective-permute-start.17 = (f32[8,256]{1,0:T(8,128)S(1)}, f32[8,256]{1,0:T(8,128)S(1)}, u32[]{:S(2)}, u32[]{:S(2)}) collective-permute-start(f32[8,256]{1,0:T(8,128)S(1)} %get-tuple-element.30), channel_id=1, source_target_pairs={{1,4},{2,12},{3,20},{12,29},{10,13},{11,21},{20,30},{21,6},{19,22}... | collective-permute-start | bytes 24584 | tf_op jit(solution)/shard_map/ppermute | solution.py:259

commit v3 on v2

--- a/solution.py
+++ b/solution.py
@@ -98,67 +98,92 @@
     return lax.dot_general(left, right, (dims, ((), ())), precision=HIGHEST, preferred_element_type=F32)
 
 
-def factor_kernel(g_ref, w_ref, a_ref, b_ref):
+def factor_kernel(first, leaves, *refs):
+    g_ref, w_in_ref = (refs[0], None) if first == 0 else refs[:2]
+    a_ref, w_ref = refs[-2:]
     n = g_ref.shape[0]
     a_ref[...] = g_ref[...]
-    row = lax.broadcasted_iota(jnp.int32, (n, n), 0)
-    lane = lax.broadcasted_iota(jnp.int32, (n, n), 1)
-    b_ref[...] = (row == lane).astype(F32)
-    for j in range(0, n, LEAF):
+    if first == 0:
+        row = lax.broadcasted_iota(jnp.int32, (n, n), 0)
+        lane = lax.broadcasted_iota(jnp.int32, (n, n), 1)
+        w_ref[...] = (row == lane).astype(F32)
+    else:
+        w_ref[...] = w_in_ref[...]
+    for leaf in range(first, first + leaves):
+        j = leaf * LEAF
         k = j + LEAF
         own = slice(j, k)
         w = leaf_inverse(a_ref[own, own])
-        done = mm(w, b_ref[own, :])
+        done = mm(w, w_ref[own, :])
         w_ref[own, :] = done
         if k < n:
             u = mm(w, a_ref[own, :])
             a_ref[k:, :] -= mm(u[:, k:], u, ((0,), (0,)))
-            b_ref[k:, :] -= mm(u[:, k:], done, ((0,), (0,)))
-
-
-def inverse_factor(gram):
-    n = gram.shape[0]
-    return pl.pallas_call(
-        factor_kernel,
-        out_shape=jax.ShapeDtypeStruct((n, n), F32),
-        in_specs=[VMEM],
-        out_specs=VMEM,
-        scratch_shapes=[pltpu.VMEM((n, n), F32)] * 2,
+            w_ref[k:, :] -= mm(u[:, k:], done, ((0,), (0,)))
+
+
+def factor_part(first, leaves, state, after=()):
+    n = state[0].shape[0]
+    skip = len(after)
+
+    def kernel(*refs):
+        factor_kernel(first, leaves, *refs[: len(state)], *refs[len(state) + skip :])
+
+    return pl.pallas_call(
+        kernel,
+        out_shape=(jax.ShapeDtypeStruct((n, n), F32),) * 2,
+        in_specs=[VMEM] * len(state) + [pl.BlockSpec(memory_space=pl.ANY)] * skip,
+        out_specs=(VMEM,) * 2,
         compiler_params=params(),
         cost_estimate=cost(2 * n * n * n, 8 * n * n),
         name="factor",
-    )(gram)
-
-
-def blocks_kernel(count, pos_ref, after_ref, xt_ref, *refs):
+    )(*state, *after)
+
+
+def inverse_factor(gram):
+    return factor_part(0, gram.shape[0] // LEAF, (gram,))[1]
+
+
+def blocks_kernel(pos_ref, after_ref, xt_ref, near_ref, far_ref, swap_ref, *outs):
     del after_ref
-    panels, outs = refs[: count - 1], refs[count - 1 :]
     chip, group, core = pos_ref[0], pos_ref[1], pos_ref[2]
-    for r in range(1, count):
-        block = jnp.dot(xt_ref[...], panels[r - 1][...], preferred_element_type=F32)
+    count = len(outs)
+
+    def store(block, owner):
+        for m in range(count):
+
+            @pl.when(jnp.bitwise_xor(chip, m) == owner)
+            def _(m=m):
+                outs[m][...] = block
+
+    for r, panel_ref in ((1, near_ref), (2, far_ref)):
         owner = group + jnp.where(core == 0, -r, r)
-        for m in range(count):
-
-            @pl.when(jnp.bitwise_xor(chip, m) == owner)
-            def _(m=m, block=block):
-                outs[m][...] = block
-
-
-def blocks(pos, after, xt, panels):
+
+        @pl.when((owner >= 0) & (owner < count))
+        def _(panel_ref=panel_ref, owner=owner):
+            store(jnp.dot(xt_ref[...], panel_ref[...], preferred_element_type=F32), owner)
+
+    @pl.when(group == jnp.where(core == 0, 2, 1))
+    def _():
+        dims = (((0,), (0,)), ((), ()))
+        store(lax.dot_general(swap_ref[...], far_ref[...], dims, preferred_element_type=F32), group)
+
+
+def blocks(pos, after, xt, near, far, swap, count):
     n = xt.shape[0]
-    count = len(panels) + 1
-    return pl.pallas_call(
-        functools.partial(blocks_kernel, count),
+    return pl.pallas_call(
+        blocks_kernel,
         out_shape=(jax.ShapeDtypeStruct((n, n), F32),) * count,
-        in_specs=[SMEM, pl.BlockSpec(memory_space=pl.ANY)] + [VMEM] * count,
+        in_specs=[SMEM, pl.BlockSpec(memory_space=pl.ANY)] + [VMEM] * 4,
         out_specs=(VMEM,) * count,
         compiler_params=params(),
-        cost_estimate=cost(2 * (count - 1) * n * n * xt.shape[1], 4 * count * n * n),
+        cost_estimate=cost(2 * 3 * n * n * xt.shape[1], 4 * count * n * n),
         name="blocks",
-    )(pos, after, xt, *panels)
-
-
-def total_kernel(pos_ref, *refs):
+    )(pos, after, xt, near, far, swap)
+
+
+def total_kernel(pos_ref, after_ref, *refs):
+    del after_ref
     count = len(refs) - 7
     parts = refs[:count]
     own_ref, sib_ref, low_ref, high_ref, top_t_ref, top_ref, st_ref = refs[count:]
@@ -177,22 +202,22 @@
     sib_ref[...] = st_ref[pl.ds(pl.multiple_of((1 - core) * half, 8), half + 8)]
 
 
-def total(pos, parts):
+def total(pos, after, parts):
     n = parts[0].shape[0]
     half = n // 2
     rows = (half + 8, half + 8, half + 8, half, 8, 8)
     return pl.pallas_call(
         total_kernel,
         out_shape=tuple(jax.ShapeDtypeStruct((r, n), F32) for r in rows),
-        in_specs=[SMEM] + [VMEM] * len(parts),
+        in_specs=[SMEM, pl.BlockSpec(memory_space=pl.ANY)] + [VMEM] * len(parts),
         out_specs=(VMEM,) * 6,
         scratch_shapes=[pltpu.VMEM((n + 8, n), F32)],
         compiler_params=params(),
         name="total",
-    )(pos, *parts)
-
-
-def tiles_kernel(pos_ref, w_ref, g_ref, own_ref, sib_ref, low_ref, high_ref, top_t_ref, top_ref, out_ref, p_ref):
+    )(pos, after, *parts)
+
+
+def tiles_kernel(pos_ref, w_ref, g_ref, own_ref, moved_ref, sib_ref, low_ref, high_ref, top_t_ref, top_ref, out_ref, p_ref):
     count = pos_ref[3]
     chip, group, core = pos_ref[0], pos_ref[1], pos_ref[2]
     half = high_ref.shape[0]
@@ -206,7 +231,8 @@
 
     @pl.when(chip != group)
     def _():
-        slab = jnp.where(core == owner, own_ref[...], sib_ref[...])
+        direct = jnp.where(jnp.abs(chip - group) == 3, moved_ref[...], own_ref[...])
+        slab = jnp.where(core == owner, direct, sib_ref[...])
 
         @pl.when(core == 0)
         def _():
@@ -230,7 +256,7 @@
     return pl.pallas_call(
         tiles_kernel,
         out_shape=jax.ShapeDtypeStruct((n, half), F32),
-        in_specs=[SMEM] + [VMEM] * 8,
+        in_specs=[SMEM] + [VMEM] * 9,
         out_specs=VMEM,
         scratch_shapes=[pltpu.VMEM((half + 8, n), F32)],
         compiler_params=params(),
@@ -279,33 +305,39 @@
         mine = mine + other
     theirs = send(mine, siblings)
     gram = jnp.where(core == 0, jnp.concatenate([mine, theirs]), jnp.concatenate([theirs, mine]))
-    w = inverse_factor(gram)
-
-    panels = []
-    for r in range(1, groups):
-        pairs = [(at(k, z, 0), at(k, z + r, 0)) for k in every for z in range(groups - r)]
-        pairs += [(at(k, z, 1), at(k, z - r, 1)) for k in every for z in range(r, groups)]
-        panels.append(send(x, pairs))
-    parts = list(blocks(pos, w, xt, panels))
+    state = factor_part(0, n // LEAF // 2, (gram,))
+
+    def hops(group_pairs):
+        pairs = [(at(k, z, 0), at(k, t, 0)) for k in every for z, t in group_pairs]
+        return pairs + [(at(k, 3 - z, 1), at(k, 3 - t, 1)) for k in every for z, t in group_pairs]
+
+    near = send(x, hops([(0, 1), (1, 2), (2, 3)]))
+    far = send(near, hops([(1, 2), (2, 3)]))
+    swap = send(x, hops([(3, 2)]))
+    parts = list(blocks(pos, state[0], xt, near, far, swap, groups))
+    w = factor_part(n // LEAF // 2, n // LEAF - n // LEAF // 2, state, (parts[0],))[1]
+
+    owners = {(k, z): (k, z, 0 if k < z else 1) for k in every for z in every if k != z}
+    owners[0, 3] = (2, 2, 0)
+    owners[3, 0] = (1, 1, 1)
     for m in range(1, groups):
-        pairs = []
-        for z in every:
-            for j in every:
-                k = j ^ m
-                if k != z:
-                    c = 0 if k < z else 1
-                    pairs.append((at(j, z, c), at(k, z, c)))
-        parts[m] = send(parts[m], pairs)
-    own, sib, low, high, top_t, top = total(pos, parts)
-
-    owners = [(k, z, 0 if k < z else 1) for k in every for z in every if k != z]
+        parts[m] = send(parts[m], [(at(k ^ m, z, c), at(k, z, c)) for k, z, c in owners.values()])
+    own, sib, low, high, top_t, top = total(pos, w, parts)
+
+    def deliver(value, target):
+        return send(value, [(at(*o), at(*target(k, z))) for (k, z), o in owners.items()])
+
+    def first_core(k, z):
+        return 0 if k < z else 1
+
     slabs = [
         own,
-        send(sib, [(at(k, z, c), at(k, z, 1 - c)) for k, z, c in owners]),
-        send(low, [(at(k, z, c), at(z, k, 0)) for k, z, c in owners]),
-        send(high, [(at(k, z, c), at(z, k, 1)) for k, z, c in owners]),
-        send(top_t, [(at(k, z, c), at((k - 1) % groups, z, 1)) for k, z, c in owners]),
-        send(top, [(at(k, z, c), at((z - 1) % groups, k, 1)) for k, z, c in owners]),
+        send(own, [(at(*owners[p]), at(*p, first_core(*p))) for p in ((0, 3), (3, 0))]),
+        deliver(sib, lambda k, z: (k, z, 1 - first_core(k, z))),
+        deliver(low, lambda k, z: (z, k, 0)),
+        deliver(high, lambda k, z: (z, k, 1)),
+        deliver(top_t, lambda k, z: ((k - 1) % groups, z, 1)),
+        deliver(top, lambda k, z: ((z - 1) % groups, k, 1)),
     ]
     return tiles(pos, w, gram, slabs)
 
@@ -325,7 +357,7 @@
 
 def solution(mesh):
     groups = mesh.shape["tm"]
-    paired = mesh.shape["space"] == 2 * groups and groups & (groups - 1) == 0
+    paired = groups == 4 and mesh.shape["space"] == 8
     return jax.shard_map(
         paired_body if paired else general_body,
         mesh=mesh,

time: 84.3 us -> 74 us (0.88)
  starting transfers between devices: 50 us -> 43.8 us
  waiting for transfers between devices: 14.8 us -> 11.2 us
    ppermute x16 -> x17, starting transfers between devices: 44.4 us -> 38.2 us  [send(): return lax.ppermute(value, axes, pairs)]
    ppermute x16 -> x17, waiting for transfers between devices: 14.8 us -> 10.6 us  [send(): return lax.ppermute(value, axes, pairs)]
    pallas_call x2 -> x3, Pallas kernels: 13 us -> 13 us  [the longest x2 11.8 us: factor_part(): pl.pallas_call(kernel, out_shape=(jax.ShapeDtypeStruct((n, n), F32),) * 2...]
  transfers between devices with their start and end apart: 18 -> 19, of which waited for: 9 -> 8; matrix products, arithmetic and copies ran while one was open for 0% -> 0% of each run, Pallas kernels for 13% -> 16%
where the time goes in v3:
time: 74 us; the launch traced here: 73.5 us
  starting transfers between devices  43.8 us (59%)
  Pallas kernels  16.2 us (22%)
  waiting for transfers between devices  11.2 us (15%)
  local copies, waits for them, and re-layouts  1.92 us (3%)
    ppermute x17, starting transfers between devices, send(): return lax.ppermute(value, axes, pairs)  38.2 us
    pallas_call x2, Pallas kernels, factor_part(): pl.pallas_call(kernel, out_shape=(jax.ShapeDtypeStruct((n, n), F32),) * 2...  11.8 us
    ppermute x17, waiting for transfers between devices, send(): return lax.ppermute(value, axes, pairs)  10.6 us
    ppermute x1, starting transfers between devices, halos(): lo = lax.ppermute(tail, 'space', [(i, i + 1) for i in range(count - 1)])  3.02 us
    ppermute x1, starting transfers between devices, halos(): hi = lax.ppermute(head, 'space', [(i + 1, i) for i in range(count - 1)])  2.58 us
    pallas_call x1, Pallas kernels, tiles(): pl.pallas_call(tiles_kernel, out_shape=jax.ShapeDtypeStruct((n, half), F3...  1.63 us
  transfers between devices with their start and end apart: 19, of which 8 were waited for; matrix products, arithmetic and copies ran while one was open for 0% of the time, Pallas kernels for 16%

profile of v3, /device:TPU:5, one launch (start us, length us, event | category | flops | bytes accessed | tf_op | source)
XLA Modules:
  0.0 73.5 jit_solution(5504263883575921258)
XLA Ops:
  0.0 0.7 fusion
  0.7 2.6 %collective-permute-start.1 = (bf16[3,1,256]{2,1,0:T(2,128)(2,1)S(1)}, bf16[3,1,256]{2,1,0:T(2,128)(2,1)S(1)}, u32[]{:S(2)}, u32[]{:S(2)}) collective-permute-start(bf16[3,1,256]{2,1,0:T(2,128)(2,1)S(1)} %get-tuple-element.37), channel_id=1, source_target_pairs={{4,0},{8,4},{12,8},{16,12},{20,16},{24,20},{28,24},{5,1},{9,5},{13... | collective-permute-start | bytes 4616 | tf_op jit(solution)/shard_map/ppermute | solution.py:271
  3.3 3.0 %collective-permute-start = (bf16[3,1,256]{2,1,0:T(2,128)(2,1)S(1)}, bf16[3,1,256]{2,1,0:T(2,128)(2,1)S(1)}, u32[]{:S(2)}, u32[]{:S(2)}) collective-permute-start(bf16[3,1,256]{2,1,0:T(2,128)(2,1)S(1)} %get-tuple-element.38), channel_id=1, source_target_pairs={{0,4},{4,8},{8,12},{12,16},{16,20},{20,24},{24,28},{1,5},{5,9},{9,... | collective-permute-start | bytes 4616 | tf_op jit(solution)/shard_map/ppermute | solution.py:270
  7.1 1.1 %copy-done = bf16[3,384,256]{2,1,0:T(8,128)(2,1)S(1)} copy-done((bf16[3,384,256]{2,1,0:T(8,128)(2,1)S(1)}, bf16[3,384,256]{2,1,0:T(8,128)(2,1)}, u32[]{:S(2)}) %copy-start) | copy-done | bytes 589848
  8.1 0.8 %panel.1 = (bf16[1152,256]{1,0:T(8,128)(2,1)S(1)}, bf16[256,1152]{1,0:T(8,128)(2,1)S(1)}, f32[256,256]{1,0:T(8,128)S(1)}) custom-call(bf16[3,384,256]{2,1,0:T(8,128)(2,1)S(1)} %copy-done, bf16[3,1,256]{2,1,0:T(2,128)(2,1)S(1)} %collective-permute-done.lo_ref, bf16[3,1,256]{2,1,0:T(2,128)(2,1)S(1)} %collective-permute-done.1.hi_ref, f32[384,1]{1,0:T(8,128)S(1)} %reshape.4.met_ref), custom_call_target="tpu_custom_call" | custom-call | flops 150994944 | bytes 1179648 | tf_op jit(solution)/shard_map/panel/pallas_call | solution.py:50
  9.0 1.3 %collective-permute-start.7 = (bf16[1152,256]{1,0:T(8,128)(2,1)S(1)}, bf16[1152,256]{1,0:T(8,128)(2,1)S(1)}, u32[]{:S(2)}, u32[]{:S(2)}) collective-permute-start(bf16[1152,256]{1,0:T(8,128)(2,1)S(1)} %get-tuple-element.25), channel_id=1, source_target_pairs={{0,1},{1,2},{2,3},{8,9},{9,10},{10,11},{16,17},{17,18},{18,19},{24... | collective-permute-start | bytes 1769480 | tf_op jit(solution)/shard_map/ppermute | solution.py:285
  10.3 5.2 %collective-permute-start.2 = (f32[128,256]{1,0:T(8,128)S(1)}, f32[128,256]{1,0:T(8,128)S(1)}, u32[]{:S(2)}, u32[]{:S(2)}) collective-permute-start(f32[128,256]{1,0:T(8,128)S(1)} %constant_dynamic-slice_fusion), channel_id=1, source_target_pairs={{0,4},{4,0},{1,5},{5,1},{2,6},{6,2},{3,7},{7,3},{8,12},{12,8},{9,1... | collective-permute-start | bytes 393224 | tf_op jit(solution)/shard_map/ppermute | solution.py:285
  15.6 1.0 %collective-permute-done.2 = f32[128,256]{1,0:T(8,128)S(1)} collective-permute-done((f32[128,256]{1,0:T(8,128)S(1)}, f32[128,256]{1,0:T(8,128)S(1)}, u32[]{:S(2)}, u32[]{:S(2)}) %collective-permute-start.2) | collective-permute-done | bytes 131104 | tf_op jit(solution)/shard_map/ppermute | solution.py:285
  16.6 0.6 collective-permute-start.4
  17.3 2.0 %collective-permute-start.3 = (f32[128,256]{1,0:T(8,128)S(1)}, f32[128,256]{1,0:T(8,128)S(1)}, u32[]{:S(2)}, u32[]{:S(2)}) collective-permute-start(f32[128,256]{1,0:T(8,128)S(1)} %dynamic-slice_add_fusion), channel_id=1, source_target_pairs={{0,8},{4,12},{1,9},{5,13},{2,10},{6,14},{3,11},{7,15},{8,0},{12,4}... | collective-permute-start | bytes 393224 | tf_op jit(solution)/shard_map/ppermute | solution.py:285
  19.3 3.2 %collective-permute-start.9 = (bf16[1152,256]{1,0:T(8,128)(2,1)S(1)}, bf16[1152,256]{1,0:T(8,128)(2,1)S(1)}, u32[]{:S(2)}, u32[]{:S(2)}) collective-permute-start(bf16[1152,256]{1,0:T(8,128)(2,1)S(1)} %get-tuple-element.25), channel_id=1, source_target_pairs={{3,2},{11,10},{19,18},{27,26},{4,5},{12,13},{20,21},{28,29}} | collective-permute-start | bytes 1769480 | tf_op jit(solution)/shard_map/ppermute | solution.py:285
  22.5 1.3 %collective-permute-start.8 = (bf16[1152,256]{1,0:T(8,128)(2,1)S(1)}, bf16[1152,256]{1,0:T(8,128)(2,1)S(1)}, u32[]{:S(2)}, u32[]{:S(2)}) collective-permute-start(bf16[1152,256]{1,0:T(8,128)(2,1)S(1)} %collective-permute-done.7.near_ref), channel_id=1, source_target_pairs={{1,2},{2,3},{9,10},{10,11},{17,18},{18,19},{25,26},{26,27},{6,5},{... | collective-permute-start | bytes 1769480 | tf_op jit(solution)/shard_map/ppermute | solution.py:285
  24.3 1.3 %collective-permute-start.6 = (f32[128,256]{1,0:T(8,128)S(1)}, f32[128,256]{1,0:T(8,128)S(1)}, u32[]{:S(2)}, u32[]{:S(2)}) collective-permute-start(f32[128,256]{1,0:T(8,128)S(1)} %add_add_fusion), channel_id=1, source_target_pairs={{0,4},{4,0},{1,5},{5,1},{2,6},{6,2},{3,7},{7,3},{8,12},{12,8},{9,1... | collective-permute-start | bytes 393224 | tf_op jit(solution)/shard_map/ppermute | solution.py:285
  25.6 0.9 %collective-permute-done.6 = f32[128,256]{1,0:T(8,128)S(1)} collective-permute-done((f32[128,256]{1,0:T(8,128)S(1)}, f32[128,256]{1,0:T(8,128)S(1)}, u32[]{:S(2)}, u32[]{:S(2)}) %collective-permute-start.6) | collective-permute-done | bytes 131104 | tf_op jit(solution)/shard_map/ppermute | solution.py:285
  26.6 5.8 %factor.2 = (f32[256,256]{1,0:T(8,128)S(1)}, f32[256,256]{1,0:T(8,128)S(1)}) custom-call(f32[256,256]{1,0:T(8,128)S(1)} %maximum_select_fusion.refs_0_.g_ref), custom_call_target="tpu_custom_call" | custom-call | flops 33554432 | bytes 524288 | tf_op jit(solution)/shard_map/factor/pallas_call | solution.py:132
  32.4 0.7 collective-permute-done.8.far_ref
  33.1 1.3 %blocks.1 = (f32[256,256]{1,0:T(8,128)S(1)}, f32[256,256]{1,0:T(8,128)S(1)}, f32[256,256]{1,0:T(8,128)S(1)}, f32[256,256]{1,0:T(8,128)S(1)}) custom-call(s32[4]{0:T(128)S(1)} %pad_add_fusion.pos_ref, f32[256,256]{1,0:T(8,128)S(1)} %get-tuple-element.22.after_ref.refs_0_, bf16[256,1152]{1,0:T(8,128)(2,1)S(1)} %get-tuple-element.24.xt_ref, ...), custom_call_target="tpu_custom_call" | custom-call | flops 452984832 | bytes 1048576 | tf_op jit(solution)/shard_map/blocks/pallas_call | solution.py:174
  34.4 1.3 %collective-permute-start.10 = (f32[256,256]{1,0:T(8,128)S(1)}, f32[256,256]{1,0:T(8,128)S(1)}, u32[]{:S(2)}, u32[]{:S(2)}) collective-permute-start(f32[256,256]{1,0:T(8,128)S(1)} %get-tuple-element.28), channel_id=1, source_target_pairs={{9,1},{10,2},{26,18},{4,12},{2,10},{3,11},{28,20},{29,21},{27,19},... | collective-permute-start | bytes 786440 | tf_op jit(solution)/shard_map/ppermute | solution.py:285
  35.7 1.3 %collective-permute-start.11 = (f32[256,256]{1,0:T(8,128)S(1)}, f32[256,256]{1,0:T(8,128)S(1)}, u32[]{:S(2)}, u32[]{:S(2)}) collective-permute-start(f32[256,256]{1,0:T(8,128)S(1)} %get-tuple-element.29), channel_id=1, source_target_pairs={{17,1},{18,2},{2,18},{28,12},{26,10},{27,11},{4,20},{5,21},{3,19},... | collective-permute-start | bytes 786440 | tf_op jit(solution)/shard_map/ppermute | solution.py:285
  37.0 2.1 %collective-permute-start.12 = (f32[256,256]{1,0:T(8,128)S(1)}, f32[256,256]{1,0:T(8,128)S(1)}, u32[]{:S(2)}, u32[]{:S(2)}) collective-permute-start(f32[256,256]{1,0:T(8,128)S(1)} %get-tuple-element.30), channel_id=1, source_target_pairs={{25,1},{26,2},{10,18},{20,12},{18,10},{19,11},{12,20},{13,21},{11,... | collective-permute-start | bytes 786440 | tf_op jit(solution)/shard_map/ppermute | solution.py:285
  39.1 5.9 %factor.3 = (f32[256,256]{1,0:T(8,128)}, f32[256,256]{1,0:T(8,128)S(1)}) custom-call(f32[256,256]{1,0:T(8,128)S(1)} %get-tuple-element.22.after_ref.refs_0_, f32[256,256]{1,0:T(8,128)S(1)} %get-tuple-element.23.refs_1_, f32[256,256]{1,0:T(8,128)S(1)} %get-tuple-element.26.refs_2_.refs_0_), custom_call_target="tpu_custom_call" | custom-call | flops 33554432 | bytes 524288 | tf_op jit(solution)/shard_map/factor/pallas_call | solution.py:132
  45.0 0.6 collective-permute-done.11.refs_2_
  45.6 0.7 total.1
  46.3 1.3 %collective-permute-start.14 = (f32[136,256]{1,0:T(8,128)S(1)}, f32[136,256]{1,0:T(8,128)S(1)}, u32[]{:S(2)}, u32[]{:S(2)}) collective-permute-start(f32[136,256]{1,0:T(8,128)S(1)} %get-tuple-element.32), channel_id=1, source_target_pairs={{1,5},{2,6},{18,7},{12,8},{10,14},{11,15},{20,16},{21,17},{19,23},... | collective-permute-start | bytes 417800 | tf_op jit(solution)/shard_map/ppermute | solution.py:285
  47.6 9.5 %collective-permute-start.15 = (f32[136,256]{1,0:T(8,128)S(1)}, f32[136,256]{1,0:T(8,128)S(1)}, u32[]{:S(2)}, u32[]{:S(2)}) collective-permute-start(f32[136,256]{1,0:T(8,128)S(1)} %get-tuple-element.33), channel_id=1, source_target_pairs={{1,8},{2,16},{18,24},{12,1},{10,17},{11,25},{20,2},{21,10},{19,26}... | collective-permute-start | bytes 417800 | tf_op jit(solution)/shard_map/ppermute | solution.py:285
  57.1 0.7 collective-permute-start.13
  57.8 1.9 %collective-permute-start.16 = (f32[128,256]{1,0:T(8,128)S(1)}, f32[128,256]{1,0:T(8,128)S(1)}, u32[]{:S(2)}, u32[]{:S(2)}) collective-permute-start(f32[128,256]{1,0:T(8,128)S(1)} %get-tuple-element.34), channel_id=1, source_target_pairs={{1,12},{2,20},{18,28},{12,5},{10,21},{11,29},{20,6},{21,14},{19,30... | collective-permute-start | bytes 393224 | tf_op jit(solution)/shard_map/ppermute | solution.py:285
  59.7 2.2 %collective-permute-start.17 = (f32[8,256]{1,0:T(8,128)S(1)}, f32[8,256]{1,0:T(8,128)S(1)}, u32[]{:S(2)}, u32[]{:S(2)}) collective-permute-start(f32[8,256]{1,0:T(8,128)S(1)} %get-tuple-element.35), channel_id=1, source_target_pairs={{1,29},{2,30},{18,31},{12,4},{10,6},{11,7},{20,12},{21,13},{19,15}... | collective-permute-start | bytes 24584 | tf_op jit(solution)/shard_map/ppermute | solution.py:285
  61.9 4.0 %collective-permute-done.17.top_t_ref = f32[8,256]{1,0:T(8,128)S(1)} collective-permute-done((f32[8,256]{1,0:T(8,128)S(1)}, f32[8,256]{1,0:T(8,128)S(1)}, u32[]{:S(2)}, u32[]{:S(2)}) %collective-permute-start.17) | collective-permute-done | bytes 8224 | tf_op jit(solution)/shard_map/ppermute | solution.py:285
  66.0 3.0 %collective-permute-start.18 = (f32[8,256]{1,0:T(8,128)S(1)}, f32[8,256]{1,0:T(8,128)S(1)}, u32[]{:S(2)}, u32[]{:S(2)}) collective-permute-start(f32[8,256]{1,0:T(8,128)S(1)} %get-tuple-element.36), channel_id=1, source_target_pairs={{1,4},{2,12},{18,20},{12,29},{10,13},{11,21},{20,30},{21,6},{19,22... | collective-permute-start | bytes 24584 | tf_op jit(solution)/shard_map/ppermute | solution.py:285
  68.9 2.9 %collective-permute-done.18.top_ref = f32[8,256]{1,0:T(8,128)S(1)} collective-permute-done((f32[8,256]{1,0:T(8,128)S(1)}, f32[8,256]{1,0:T(8,128)S(1)}, u32[]{:S(2)}, u32[]{:S(2)}) %collective-permute-start.18) | collective-permute-done | bytes 8224 | tf_op jit(solution)/shard_map/ppermute | solution.py:285
  71.8 1.6 %tiles.1 = f32[256,128]{1,0:T(8,128)} custom-call(s32[4]{0:T(128)S(1)} %pad_add_fusion.pos_ref, f32[256,256]{1,0:T(8,128)S(1)} %get-tuple-element.27.after_ref.w_ref, f32[256,256]{1,0:T(8,128)S(1)} %maximum_select_fusion.refs_0_.g_ref, f32[136,256]{1,0:T(8,128)S(1)} %get-tuple-element.31.own_ref, f32[136,256]{1,0:T(8,128)S(1)} %collective-permute-done.13.moved_ref, ...), custom_call_target="tpu_custom_call" | custom-call | tf_op jit(solution)/shard_map/tiles/pallas_call | solution.py:256
  (23 shorter events, 1.4 us)
Async XLA Ops:
  0.7 5.6 %copy-start.1 = (f32[384]{0:T(512)S(1)}, f32[384]{0:T(512)}, u32[]{:S(2)}) copy-start(f32[384]{0:T(512)} %param.3) | copy-start | bytes 4612
  0.7 5.7 %collective-permute-start.1 = (bf16[3,1,256]{2,1,0:T(2,128)(2,1)S(1)}, bf16[3,1,256]{2,1,0:T(2,128)(2,1)S(1)}, u32[]{:S(2)}, u32[]{:S(2)}) collective-permute-start(bf16[3,1,256]{2,1,0:T(2,128)(2,1)S(1)} %get-tuple-element.37), channel_id=1, source_target_pairs={{4,0},{8,4},{12,8},{16,12},{20,16},{24,20},{28,24},{5,1},{9,5},{13... | collective-permute-start | bytes 4616 | tf_op jit(solution)/shard_map/ppermute | solution.py:271
  3.3 3.7 %collective-permute-start = (bf16[3,1,256]{2,1,0:T(2,128)(2,1)S(1)}, bf16[3,1,256]{2,1,0:T(2,128)(2,1)S(1)}, u32[]{:S(2)}, u32[]{:S(2)}) collective-permute-start(bf16[3,1,256]{2,1,0:T(2,128)(2,1)S(1)} %get-tuple-element.38), channel_id=1, source_target_pairs={{0,4},{4,8},{8,12},{12,16},{16,20},{20,24},{24,28},{1,5},{5,9},{9,... | collective-permute-start | bytes 4616 | tf_op jit(solution)/shard_map/ppermute | solution.py:270
  7.1 1.1 %copy-start = (bf16[3,384,256]{2,1,0:T(8,128)(2,1)S(1)}, bf16[3,384,256]{2,1,0:T(8,128)(2,1)}, u32[]{:S(2)}) copy-start(bf16[3,384,256]{2,1,0:T(8,128)(2,1)} %vel_ref.1) | copy-start | bytes 1769476
  9.0 13.5 %collective-permute-start.7 = (bf16[1152,256]{1,0:T(8,128)(2,1)S(1)}, bf16[1152,256]{1,0:T(8,128)(2,1)S(1)}, u32[]{:S(2)}, u32[]{:S(2)}) collective-permute-start(bf16[1152,256]{1,0:T(8,128)(2,1)S(1)} %get-tuple-element.25), channel_id=1, source_target_pairs={{0,1},{1,2},{2,3},{8,9},{9,10},{10,11},{16,17},{17,18},{18,19},{24... | collective-permute-start | bytes 1769480 | tf_op jit(solution)/shard_map/ppermute | solution.py:285
  10.3 6.2 %collective-permute-start.2 = (f32[128,256]{1,0:T(8,128)S(1)}, f32[128,256]{1,0:T(8,128)S(1)}, u32[]{:S(2)}, u32[]{:S(2)}) collective-permute-start(f32[128,256]{1,0:T(8,128)S(1)} %constant_dynamic-slice_fusion), channel_id=1, source_target_pairs={{0,4},{4,0},{1,5},{5,1},{2,6},{6,2},{3,7},{7,3},{8,12},{12,8},{9,1... | collective-permute-start | bytes 393224 | tf_op jit(solution)/shard_map/ppermute | solution.py:285
  16.6 7.2 %collective-permute-start.5 = (f32[128,256]{1,0:T(8,128)S(1)}, f32[128,256]{1,0:T(8,128)S(1)}, u32[]{:S(2)}, u32[]{:S(2)}) collective-permute-start(f32[128,256]{1,0:T(8,128)S(1)} %dynamic-slice_add_fusion), channel_id=1, source_target_pairs={{0,24},{4,28},{1,25},{5,29},{2,26},{6,30},{3,27},{7,31},{8,16},{12... | collective-permute-start | bytes 393224 | tf_op jit(solution)/shard_map/ppermute | solution.py:285
  16.6 7.6 %collective-permute-start.4 = (f32[128,256]{1,0:T(8,128)S(1)}, f32[128,256]{1,0:T(8,128)S(1)}, u32[]{:S(2)}, u32[]{:S(2)}) collective-permute-start(f32[128,256]{1,0:T(8,128)S(1)} %dynamic-slice_add_fusion), channel_id=1, source_target_pairs={{0,16},{4,20},{1,17},{5,21},{2,18},{6,22},{3,19},{7,23},{8,24},{12... | collective-permute-start | bytes 393224 | tf_op jit(solution)/shard_map/ppermute | solution.py:285
  17.3 7.0 %collective-permute-start.3 = (f32[128,256]{1,0:T(8,128)S(1)}, f32[128,256]{1,0:T(8,128)S(1)}, u32[]{:S(2)}, u32[]{:S(2)}) collective-permute-start(f32[128,256]{1,0:T(8,128)S(1)} %dynamic-slice_add_fusion), channel_id=1, source_target_pairs={{0,8},{4,12},{1,9},{5,13},{2,10},{6,14},{3,11},{7,15},{8,0},{12,4}... | collective-permute-start | bytes 393224 | tf_op jit(solution)/shard_map/ppermute | solution.py:285
  19.3 13.1 %collective-permute-start.9 = (bf16[1152,256]{1,0:T(8,128)(2,1)S(1)}, bf16[1152,256]{1,0:T(8,128)(2,1)S(1)}, u32[]{:S(2)}, u32[]{:S(2)}) collective-permute-start(bf16[1152,256]{1,0:T(8,128)(2,1)S(1)} %get-tuple-element.25), channel_id=1, source_target_pairs={{3,2},{11,10},{19,18},{27,26},{4,5},{12,13},{20,21},{28,29}} | collective-permute-start | bytes 1769480 | tf_op jit(solution)/shard_map/ppermute | solution.py:285
  22.5 10.6 %collective-permute-start.8 = (bf16[1152,256]{1,0:T(8,128)(2,1)S(1)}, bf16[1152,256]{1,0:T(8,128)(2,1)S(1)}, u32[]{:S(2)}, u32[]{:S(2)}) collective-permute-start(bf16[1152,256]{1,0:T(8,128)(2,1)S(1)} %collective-permute-done.7.near_ref), channel_id=1, source_target_pairs={{1,2},{2,3},{9,10},{10,11},{17,18},{18,19},{25,26},{26,27},{6,5},{... | collective-permute-start | bytes 1769480 | tf_op jit(solution)/shard_map/ppermute | solution.py:285
  24.3 2.2 %collective-permute-start.6 = (f32[128,256]{1,0:T(8,128)S(1)}, f32[128,256]{1,0:T(8,128)S(1)}, u32[]{:S(2)}, u32[]{:S(2)}) collective-permute-start(f32[128,256]{1,0:T(8,128)S(1)} %add_add_fusion), channel_id=1, source_target_pairs={{0,4},{4,0},{1,5},{5,1},{2,6},{6,2},{3,7},{7,3},{8,12},{12,8},{9,1... | collective-permute-start | bytes 393224 | tf_op jit(solution)/shard_map/ppermute | solution.py:285
  34.4 10.6 %collective-permute-start.10 = (f32[256,256]{1,0:T(8,128)S(1)}, f32[256,256]{1,0:T(8,128)S(1)}, u32[]{:S(2)}, u32[]{:S(2)}) collective-permute-start(f32[256,256]{1,0:T(8,128)S(1)} %get-tuple-element.28), channel_id=1, source_target_pairs={{9,1},{10,2},{26,18},{4,12},{2,10},{3,11},{28,20},{29,21},{27,19},... | collective-permute-start | bytes 786440 | tf_op jit(solution)/shard_map/ppermute | solution.py:285
  35.7 9.9 %collective-permute-start.11 = (f32[256,256]{1,0:T(8,128)S(1)}, f32[256,256]{1,0:T(8,128)S(1)}, u32[]{:S(2)}, u32[]{:S(2)}) collective-permute-start(f32[256,256]{1,0:T(8,128)S(1)} %get-tuple-element.29), channel_id=1, source_target_pairs={{17,1},{18,2},{2,18},{28,12},{26,10},{27,11},{4,20},{5,21},{3,19},... | collective-permute-start | bytes 786440 | tf_op jit(solution)/shard_map/ppermute | solution.py:285
  37.0 8.6 %collective-permute-start.12 = (f32[256,256]{1,0:T(8,128)S(1)}, f32[256,256]{1,0:T(8,128)S(1)}, u32[]{:S(2)}, u32[]{:S(2)}) collective-permute-start(f32[256,256]{1,0:T(8,128)S(1)} %get-tuple-element.30), channel_id=1, source_target_pairs={{25,1},{26,2},{10,18},{20,12},{18,10},{19,11},{12,20},{13,21},{11,... | collective-permute-start | bytes 786440 | tf_op jit(solution)/shard_map/ppermute | solution.py:285
  46.3 25.5 %collective-permute-start.14 = (f32[136,256]{1,0:T(8,128)S(1)}, f32[136,256]{1,0:T(8,128)S(1)}, u32[]{:S(2)}, u32[]{:S(2)}) collective-permute-start(f32[136,256]{1,0:T(8,128)S(1)} %get-tuple-element.32), channel_id=1, source_target_pairs={{1,5},{2,6},{18,7},{12,8},{10,14},{11,15},{20,16},{21,17},{19,23},... | collective-permute-start | bytes 417800 | tf_op jit(solution)/shard_map/ppermute | solution.py:285
  47.6 24.2 %collective-permute-start.15 = (f32[136,256]{1,0:T(8,128)S(1)}, f32[136,256]{1,0:T(8,128)S(1)}, u32[]{:S(2)}, u32[]{:S(2)}) collective-permute-start(f32[136,256]{1,0:T(8,128)S(1)} %get-tuple-element.33), channel_id=1, source_target_pairs={{1,8},{2,16},{18,24},{12,1},{10,17},{11,25},{20,2},{21,10},{19,26}... | collective-permute-start | bytes 417800 | tf_op jit(solution)/shard_map/ppermute | solution.py:285
  57.1 14.7 %collective-permute-start.13 = (f32[136,256]{1,0:T(8,128)S(1)}, f32[136,256]{1,0:T(8,128)S(1)}, u32[]{:S(2)}, u32[]{:S(2)}) collective-permute-start(f32[136,256]{1,0:T(8,128)S(1)} %get-tuple-element.31.own_ref), channel_id=1, source_target_pairs={{18,3},{13,28}} | collective-permute-start | bytes 417800 | tf_op jit(solution)/shard_map/ppermute | solution.py:285
  57.8 14.0 %collective-permute-start.16 = (f32[128,256]{1,0:T(8,128)S(1)}, f32[128,256]{1,0:T(8,128)S(1)}, u32[]{:S(2)}, u32[]{:S(2)}) collective-permute-start(f32[128,256]{1,0:T(8,128)S(1)} %get-tuple-element.34), channel_id=1, source_target_pairs={{1,12},{2,20},{18,28},{12,5},{10,21},{11,29},{20,6},{21,14},{19,30... | collective-permute-start | bytes 393224 | tf_op jit(solution)/shard_map/ppermute | solution.py:285
  59.7 6.2 %collective-permute-start.17 = (f32[8,256]{1,0:T(8,128)S(1)}, f32[8,256]{1,0:T(8,128)S(1)}, u32[]{:S(2)}, u32[]{:S(2)}) collective-permute-start(f32[8,256]{1,0:T(8,128)S(1)} %get-tuple-element.35), channel_id=1, source_target_pairs={{1,29},{2,30},{18,31},{12,4},{10,6},{11,7},{20,12},{21,13},{19,15}... | collective-permute-start | bytes 24584 | tf_op jit(solution)/shard_map/ppermute | solution.py:285
  66.0 5.9 %collective-permute-start.18 = (f32[8,256]{1,0:T(8,128)S(1)}, f32[8,256]{1,0:T(8,128)S(1)}, u32[]{:S(2)}, u32[]{:S(2)}) collective-permute-start(f32[8,256]{1,0:T(8,128)S(1)} %get-tuple-element.36), channel_id=1, source_target_pairs={{1,4},{2,12},{18,20},{12,29},{10,13},{11,21},{20,30},{21,6},{19,22... | collective-permute-start | bytes 24584 | tf_op jit(solution)/shard_map/ppermute | solution.py:285

commit v4 on v3

--- a/solution.py
+++ b/solution.py
@@ -292,19 +292,10 @@
     x, xt, gram = panel(velocity, lo, hi, metric)
 
     n = gram.shape[0]
-    half = n // 2
-    siblings = [(at(k, z, c), at(k, z, 1 - c)) for k in every for z in every for c in cores]
-    away = lax.dynamic_slice_in_dim(gram, (1 - core) * half, half, 0)
-    mine = lax.dynamic_slice_in_dim(gram, core * half, half, 0)
-    mine = mine + send(away, siblings)
-    others = [
-        send(mine, [(at(k, z, c), at(k ^ m, z, c)) for k in every for z in every for c in cores])
-        for m in range(1, groups)
-    ]
-    for other in others:
-        mine = mine + other
-    theirs = send(mine, siblings)
-    gram = jnp.where(core == 0, jnp.concatenate([mine, theirs]), jnp.concatenate([theirs, mine]))
+    devices = 2 * groups
+    shares = lax.all_to_all(gram, "space", 0, 0, tiled=True)
+    mine = jnp.sum(shares.reshape(devices, n // devices, n), axis=0)
+    gram = lax.all_to_all(jnp.tile(mine, (devices, 1)), "space", 0, 0, tiled=True)
     state = factor_part(0, n // LEAF // 2, (gram,))
 
     def hops(group_pairs):

time: 74 us -> 93.5 us (1.26)
  the two profiles are of different devices: /device:TPU:5 before, /device:TPU:3 now
where the time goes in v4:
time: 93.5 us; the launch traced here: 92.8 us
  starting transfers between devices  40.2 us (43%)
  waiting for transfers between devices  18.5 us (20%)
  Pallas kernels  16.2 us (17%)
  blocking collectives  15 us (16%)
  local copies, waits for them, and re-layouts  2.62 us (3%)
    ppermute x12, starting transfers between devices, send(): return lax.ppermute(value, axes, pairs)  28.7 us
    all_to_all x1, blocking collectives, paired_body(): shares = lax.all_to_all(gram, 'space', 0, 0, tiled=True)  15 us
    ppermute x12, waiting for transfers between devices, send(): return lax.ppermute(value, axes, pairs)  12.8 us
    pallas_call x2, Pallas kernels, factor_part(): pl.pallas_call(kernel, out_shape=(jax.ShapeDtypeStruct((n, n), F32),) * 2...  11.8 us
    all_to_all x1, waiting for transfers between devices, paired_body(): lax.all_to_all(jnp.tile(mine, (devices, 1)), 'space', 0, 0, tiled=True)  5.19 us
    all_to_all x1, starting transfers between devices, paired_body(): lax.all_to_all(jnp.tile(mine, (devices, 1)), 'space', 0, 0, tiled=True)  5.01 us
    ppermute x1, starting transfers between devices, halos(): lo = lax.ppermute(tail, 'space', [(i, i + 1) for i in range(count - 1)])  3.88 us
    ppermute x1, starting transfers between devices, halos(): hi = lax.ppermute(head, 'space', [(i + 1, i) for i in range(count - 1)])  2.58 us
  transfers between devices with their start and end apart: 15, of which 6 were waited for; matrix products, arithmetic and copies ran while one was open for 1% of the time, Pallas kernels for 13%

profile of v4, /device:TPU:3, one launch (start us, length us, event | category | flops | bytes accessed | tf_op | source)
XLA Modules:
  0.0 92.8 jit_solution(11508317147957380065)
XLA Ops:
  0.0 0.7 fusion
  0.7 2.6 %collective-permute-start.1 = (bf16[3,1,256]{2,1,0:T(2,128)(2,1)S(1)}, bf16[3,1,256]{2,1,0:T(2,128)(2,1)S(1)}, u32[]{:S(2)}, u32[]{:S(2)}) collective-permute-start(bf16[3,1,256]{2,1,0:T(2,128)(2,1)S(1)} %get-tuple-element.37), channel_id=1, source_target_pairs={{4,0},{8,4},{12,8},{16,12},{20,16},{24,20},{28,24},{5,1},{9,5},{13... | collective-permute-start | bytes 4616 | tf_op jit(solution)/shard_map/ppermute | solution.py:271
  3.3 3.9 %collective-permute-start = (bf16[3,1,256]{2,1,0:T(2,128)(2,1)S(1)}, bf16[3,1,256]{2,1,0:T(2,128)(2,1)S(1)}, u32[]{:S(2)}, u32[]{:S(2)}) collective-permute-start(bf16[3,1,256]{2,1,0:T(2,128)(2,1)S(1)} %get-tuple-element.38), channel_id=1, source_target_pairs={{0,4},{4,8},{8,12},{12,16},{16,20},{20,24},{24,28},{1,5},{5,9},{9,... | collective-permute-start | bytes 4616 | tf_op jit(solution)/shard_map/ppermute | solution.py:270
  7.2 0.1 reshape.15.met_ref
  7.3 0.6 collective-permute-done.lo_ref
  7.9 1.1 %copy-done = bf16[3,384,256]{2,1,0:T(8,128)(2,1)S(1)} copy-done((bf16[3,384,256]{2,1,0:T(8,128)(2,1)S(1)}, bf16[3,384,256]{2,1,0:T(8,128)(2,1)}, u32[]{:S(2)}) %copy-start) | copy-done | bytes 589848
  9.0 0.8 panel.1
  9.9 1.3 %collective-permute-start.2 = (bf16[1152,256]{1,0:T(8,128)(2,1)S(1)}, bf16[1152,256]{1,0:T(8,128)(2,1)S(1)}, u32[]{:S(2)}, u32[]{:S(2)}) collective-permute-start(bf16[1152,256]{1,0:T(8,128)(2,1)S(1)} %get-tuple-element.25), channel_id=1, source_target_pairs={{0,1},{1,2},{2,3},{8,9},{9,10},{10,11},{16,17},{17,18},{18,19},{24... | collective-permute-start | bytes 1769480 | tf_op jit(solution)/shard_map/ppermute | solution.py:285
  11.2 4.0 %collective-permute-start.4 = (bf16[1152,256]{1,0:T(8,128)(2,1)S(1)}, bf16[1152,256]{1,0:T(8,128)(2,1)S(1)}, u32[]{:S(2)}, u32[]{:S(2)}) collective-permute-start(bf16[1152,256]{1,0:T(8,128)(2,1)S(1)} %get-tuple-element.25), channel_id=1, source_target_pairs={{3,2},{11,10},{19,18},{27,26},{4,5},{12,13},{20,21},{28,29}} | collective-permute-start | bytes 1769480 | tf_op jit(solution)/shard_map/ppermute | solution.py:285
  15.2 5.3 %collective-permute-done.2.near_ref = bf16[1152,256]{1,0:T(8,128)(2,1)S(1)} collective-permute-done((bf16[1152,256]{1,0:T(8,128)(2,1)S(1)}, bf16[1152,256]{1,0:T(8,128)(2,1)S(1)}, u32[]{:S(2)}, u32[]{:S(2)}) %collective-permute-start.2) | collective-permute-done | bytes 589856 | tf_op jit(solution)/shard_map/ppermute | solution.py:285
  20.5 1.3 %collective-permute-start.3 = (bf16[1152,256]{1,0:T(8,128)(2,1)S(1)}, bf16[1152,256]{1,0:T(8,128)(2,1)S(1)}, u32[]{:S(2)}, u32[]{:S(2)}) collective-permute-start(bf16[1152,256]{1,0:T(8,128)(2,1)S(1)} %collective-permute-done.2.near_ref), channel_id=1, source_target_pairs={{1,2},{2,3},{9,10},{10,11},{17,18},{18,19},{25,26},{26,27},{6,5},{... | collective-permute-start | bytes 1769480 | tf_op jit(solution)/shard_map/ppermute | solution.py:285
  21.8 15.0 %all_to_all.17 = f32[8,32,256]{2,1,0:T(8,128)S(1)} all-to-all(f32[8,32,256]{2,1,0:T(8,128)S(1)} %bitcast.7), channel_id=1, replica_groups=mesh['space'=8,'tm'=4] {'space'}, dimensions={0} | all-to-all | bytes 524288 | tf_op jit(solution)/shard_map/all_to_all | solution.py:296
  36.8 0.7 tile.2
  37.5 5.0 %all-to-all-start.1 = ((f32[8,32,256]{2,1,0:T(8,128)}), f32[8,32,256]{2,1,0:T(8,128)S(1)}, u32[]{:S(2)}, u32[]{:S(2)}) async-start(f32[8,32,256]{2,1,0:T(8,128)} %tile.2), calls=%async_computation.1 | async-start | bytes 524288 | tf_op jit(solution)/shard_map/all_to_all | solution.py:298
  42.6 5.2 %all-to-all-done.1 = f32[8,32,256]{2,1,0:T(8,128)S(1)} async-done(((f32[8,32,256]{2,1,0:T(8,128)}), f32[8,32,256]{2,1,0:T(8,128)S(1)}, u32[]{:S(2)}, u32[]{:S(2)}) %all-to-all-start.1) | async-done | bytes 262176 | tf_op jit(solution)/shard_map/all_to_all | solution.py:298
  47.8 5.9 %factor.2 = (f32[256,256]{1,0:T(8,128)S(1)}, f32[256,256]{1,0:T(8,128)S(1)}) custom-call(f32[256,256]{1,0:T(8,128)S(1)} %bitcast.5), custom_call_target="tpu_custom_call" | custom-call | flops 33554432 | bytes 524288 | tf_op jit(solution)/shard_map/factor/pallas_call | solution.py:132
  53.6 1.3 %blocks.1 = (f32[256,256]{1,0:T(8,128)S(1)}, f32[256,256]{1,0:T(8,128)S(1)}, f32[256,256]{1,0:T(8,128)S(1)}, f32[256,256]{1,0:T(8,128)S(1)}) custom-call(s32[4]{0:T(128)S(1)} %pad_add_fusion.pos_ref, f32[256,256]{1,0:T(8,128)S(1)} %get-tuple-element.22.after_ref.refs_0_, bf16[256,1152]{1,0:T(8,128)(2,1)S(1)} %get-tuple-element.24.xt_ref, ...), custom_call_target="tpu_custom_call" | custom-call | flops 452984832 | bytes 1048576 | tf_op jit(solution)/shard_map/blocks/pallas_call | solution.py:174
  54.9 1.3 %collective-permute-start.5 = (f32[256,256]{1,0:T(8,128)S(1)}, f32[256,256]{1,0:T(8,128)S(1)}, u32[]{:S(2)}, u32[]{:S(2)}) collective-permute-start(f32[256,256]{1,0:T(8,128)S(1)} %get-tuple-element.28), channel_id=1, source_target_pairs={{9,1},{10,2},{26,18},{4,12},{2,10},{3,11},{28,20},{29,21},{27,19},... | collective-permute-start | bytes 786440 | tf_op jit(solution)/shard_map/ppermute | solution.py:285
  56.2 1.3 %collective-permute-start.6 = (f32[256,256]{1,0:T(8,128)S(1)}, f32[256,256]{1,0:T(8,128)S(1)}, u32[]{:S(2)}, u32[]{:S(2)}) collective-permute-start(f32[256,256]{1,0:T(8,128)S(1)} %get-tuple-element.29), channel_id=1, source_target_pairs={{17,1},{18,2},{2,18},{28,12},{26,10},{27,11},{4,20},{5,21},{3,19},... | collective-permute-start | bytes 786440 | tf_op jit(solution)/shard_map/ppermute | solution.py:285
  57.5 2.3 %collective-permute-start.7 = (f32[256,256]{1,0:T(8,128)S(1)}, f32[256,256]{1,0:T(8,128)S(1)}, u32[]{:S(2)}, u32[]{:S(2)}) collective-permute-start(f32[256,256]{1,0:T(8,128)S(1)} %get-tuple-element.30), channel_id=1, source_target_pairs={{25,1},{26,2},{10,18},{20,12},{18,10},{19,11},{12,20},{13,21},{11,... | collective-permute-start | bytes 786440 | tf_op jit(solution)/shard_map/ppermute | solution.py:285
  59.9 5.9 %factor.3 = (f32[256,256]{1,0:T(8,128)}, f32[256,256]{1,0:T(8,128)S(1)}) custom-call(f32[256,256]{1,0:T(8,128)S(1)} %get-tuple-element.22.after_ref.refs_0_, f32[256,256]{1,0:T(8,128)S(1)} %get-tuple-element.23.refs_1_, f32[256,256]{1,0:T(8,128)S(1)} %get-tuple-element.26.refs_2_.refs_0_), custom_call_target="tpu_custom_call" | custom-call | flops 33554432 | bytes 524288 | tf_op jit(solution)/shard_map/factor/pallas_call | solution.py:132
  65.8 0.4 collective-permute-done.6.refs_2_
  66.1 0.7 total.1
  66.9 1.3 %collective-permute-start.9 = (f32[136,256]{1,0:T(8,128)S(1)}, f32[136,256]{1,0:T(8,128)S(1)}, u32[]{:S(2)}, u32[]{:S(2)}) collective-permute-start(f32[136,256]{1,0:T(8,128)S(1)} %get-tuple-element.32), channel_id=1, source_target_pairs={{1,5},{2,6},{18,7},{12,8},{10,14},{11,15},{20,16},{21,17},{19,23},... | collective-permute-start | bytes 417800 | tf_op jit(solution)/shard_map/ppermute | solution.py:285
  68.2 8.4 %collective-permute-start.10 = (f32[136,256]{1,0:T(8,128)S(1)}, f32[136,256]{1,0:T(8,128)S(1)}, u32[]{:S(2)}, u32[]{:S(2)}) collective-permute-start(f32[136,256]{1,0:T(8,128)S(1)} %get-tuple-element.33), channel_id=1, source_target_pairs={{1,8},{2,16},{18,24},{12,1},{10,17},{11,25},{20,2},{21,10},{19,26}... | collective-permute-start | bytes 417800 | tf_op jit(solution)/shard_map/ppermute | solution.py:285
  76.5 0.7 collective-permute-start.8
  77.2 1.9 %collective-permute-start.11 = (f32[128,256]{1,0:T(8,128)S(1)}, f32[128,256]{1,0:T(8,128)S(1)}, u32[]{:S(2)}, u32[]{:S(2)}) collective-permute-start(f32[128,256]{1,0:T(8,128)S(1)} %get-tuple-element.34), channel_id=1, source_target_pairs={{1,12},{2,20},{18,28},{12,5},{10,21},{11,29},{20,6},{21,14},{19,30... | collective-permute-start | bytes 393224 | tf_op jit(solution)/shard_map/ppermute | solution.py:285
  79.1 1.9 %collective-permute-start.12 = (f32[8,256]{1,0:T(8,128)S(1)}, f32[8,256]{1,0:T(8,128)S(1)}, u32[]{:S(2)}, u32[]{:S(2)}) collective-permute-start(f32[8,256]{1,0:T(8,128)S(1)} %get-tuple-element.35), channel_id=1, source_target_pairs={{1,29},{2,30},{18,31},{12,4},{10,6},{11,7},{20,12},{21,13},{19,15}... | collective-permute-start | bytes 24584 | tf_op jit(solution)/shard_map/ppermute | solution.py:285
  81.1 3.4 %collective-permute-done.12.top_t_ref = f32[8,256]{1,0:T(8,128)S(1)} collective-permute-done((f32[8,256]{1,0:T(8,128)S(1)}, f32[8,256]{1,0:T(8,128)S(1)}, u32[]{:S(2)}, u32[]{:S(2)}) %collective-permute-start.12) | collective-permute-done | bytes 8224 | tf_op jit(solution)/shard_map/ppermute | solution.py:285
  84.4 3.0 %collective-permute-start.13 = (f32[8,256]{1,0:T(8,128)S(1)}, f32[8,256]{1,0:T(8,128)S(1)}, u32[]{:S(2)}, u32[]{:S(2)}) collective-permute-start(f32[8,256]{1,0:T(8,128)S(1)} %get-tuple-element.36), channel_id=1, source_target_pairs={{1,4},{2,12},{18,20},{12,29},{10,13},{11,21},{20,30},{21,6},{19,22... | collective-permute-start | bytes 24584 | tf_op jit(solution)/shard_map/ppermute | solution.py:285
  87.5 3.7 %collective-permute-done.13.top_ref = f32[8,256]{1,0:T(8,128)S(1)} collective-permute-done((f32[8,256]{1,0:T(8,128)S(1)}, f32[8,256]{1,0:T(8,128)S(1)}, u32[]{:S(2)}, u32[]{:S(2)}) %collective-permute-start.13) | collective-permute-done | bytes 8224 | tf_op jit(solution)/shard_map/ppermute | solution.py:285
  91.2 1.6 %tiles.1 = f32[256,128]{1,0:T(8,128)} custom-call(s32[4]{0:T(128)S(1)} %pad_add_fusion.pos_ref, f32[256,256]{1,0:T(8,128)S(1)} %get-tuple-element.27.after_ref.w_ref, f32[256,256]{1,0:T(8,128)S(1)} %bitcast.6, f32[136,256]{1,0:T(8,128)S(1)} %get-tuple-element.31.own_ref, f32[136,256]{1,0:T(8,128)S(1)} %collective-permute-done.8.moved_ref, ...), custom_call_target="tpu_custom_call" | custom-call | tf_op jit(solution)/shard_map/tiles/pallas_call | solution.py:256
  (14 shorter events, 0.1 us)
Async XLA Ops:
  0.7 6.5 %copy-start.1 = (f32[384]{0:T(512)S(1)}, f32[384]{0:T(512)}, u32[]{:S(2)}) copy-start(f32[384]{0:T(512)} %param.3) | copy-start | bytes 4612
  0.7 6.6 %collective-permute-start.1 = (bf16[3,1,256]{2,1,0:T(2,128)(2,1)S(1)}, bf16[3,1,256]{2,1,0:T(2,128)(2,1)S(1)}, u32[]{:S(2)}, u32[]{:S(2)}) collective-permute-start(bf16[3,1,256]{2,1,0:T(2,128)(2,1)S(1)} %get-tuple-element.37), channel_id=1, source_target_pairs={{4,0},{8,4},{12,8},{16,12},{20,16},{24,20},{28,24},{5,1},{9,5},{13... | collective-permute-start | bytes 4616 | tf_op jit(solution)/shard_map/ppermute | solution.py:271
  3.3 4.6 %collective-permute-start = (bf16[3,1,256]{2,1,0:T(2,128)(2,1)S(1)}, bf16[3,1,256]{2,1,0:T(2,128)(2,1)S(1)}, u32[]{:S(2)}, u32[]{:S(2)}) collective-permute-start(bf16[3,1,256]{2,1,0:T(2,128)(2,1)S(1)} %get-tuple-element.38), channel_id=1, source_target_pairs={{0,4},{4,8},{8,12},{12,16},{16,20},{20,24},{24,28},{1,5},{5,9},{9,... | collective-permute-start | bytes 4616 | tf_op jit(solution)/shard_map/ppermute | solution.py:270
  7.9 1.1 %copy-start = (bf16[3,384,256]{2,1,0:T(8,128)(2,1)S(1)}, bf16[3,384,256]{2,1,0:T(8,128)(2,1)}, u32[]{:S(2)}) copy-start(bf16[3,384,256]{2,1,0:T(8,128)(2,1)} %vel_ref.1) | copy-start | bytes 1769476
  9.9 10.6 %collective-permute-start.2 = (bf16[1152,256]{1,0:T(8,128)(2,1)S(1)}, bf16[1152,256]{1,0:T(8,128)(2,1)S(1)}, u32[]{:S(2)}, u32[]{:S(2)}) collective-permute-start(bf16[1152,256]{1,0:T(8,128)(2,1)S(1)} %get-tuple-element.25), channel_id=1, source_target_pairs={{0,1},{1,2},{2,3},{8,9},{9,10},{10,11},{16,17},{17,18},{18,19},{24... | collective-permute-start | bytes 1769480 | tf_op jit(solution)/shard_map/ppermute | solution.py:285
  11.2 42.5 %collective-permute-start.4 = (bf16[1152,256]{1,0:T(8,128)(2,1)S(1)}, bf16[1152,256]{1,0:T(8,128)(2,1)S(1)}, u32[]{:S(2)}, u32[]{:S(2)}) collective-permute-start(bf16[1152,256]{1,0:T(8,128)(2,1)S(1)} %get-tuple-element.25), channel_id=1, source_target_pairs={{3,2},{11,10},{19,18},{27,26},{4,5},{12,13},{20,21},{28,29}} | collective-permute-start | bytes 1769480 | tf_op jit(solution)/shard_map/ppermute | solution.py:285
  20.5 33.1 %collective-permute-start.3 = (bf16[1152,256]{1,0:T(8,128)(2,1)S(1)}, bf16[1152,256]{1,0:T(8,128)(2,1)S(1)}, u32[]{:S(2)}, u32[]{:S(2)}) collective-permute-start(bf16[1152,256]{1,0:T(8,128)(2,1)S(1)} %collective-permute-done.2.near_ref), channel_id=1, source_target_pairs={{1,2},{2,3},{9,10},{10,11},{17,18},{18,19},{25,26},{26,27},{6,5},{... | collective-permute-start | bytes 1769480 | tf_op jit(solution)/shard_map/ppermute | solution.py:285
  37.5 10.3 %all-to-all-start.1 = ((f32[8,32,256]{2,1,0:T(8,128)}), f32[8,32,256]{2,1,0:T(8,128)S(1)}, u32[]{:S(2)}, u32[]{:S(2)}) async-start(f32[8,32,256]{2,1,0:T(8,128)} %tile.2), calls=%async_computation.1 | async-start | bytes 524288 | tf_op jit(solution)/shard_map/all_to_all | solution.py:298
  54.9 10.9 %collective-permute-start.5 = (f32[256,256]{1,0:T(8,128)S(1)}, f32[256,256]{1,0:T(8,128)S(1)}, u32[]{:S(2)}, u32[]{:S(2)}) collective-permute-start(f32[256,256]{1,0:T(8,128)S(1)} %get-tuple-element.28), channel_id=1, source_target_pairs={{9,1},{10,2},{26,18},{4,12},{2,10},{3,11},{28,20},{29,21},{27,19},... | collective-permute-start | bytes 786440 | tf_op jit(solution)/shard_map/ppermute | solution.py:285
  56.2 9.9 %collective-permute-start.6 = (f32[256,256]{1,0:T(8,128)S(1)}, f32[256,256]{1,0:T(8,128)S(1)}, u32[]{:S(2)}, u32[]{:S(2)}) collective-permute-start(f32[256,256]{1,0:T(8,128)S(1)} %get-tuple-element.29), channel_id=1, source_target_pairs={{17,1},{18,2},{2,18},{28,12},{26,10},{27,11},{4,20},{5,21},{3,19},... | collective-permute-start | bytes 786440 | tf_op jit(solution)/shard_map/ppermute | solution.py:285
  57.5 8.6 %collective-permute-start.7 = (f32[256,256]{1,0:T(8,128)S(1)}, f32[256,256]{1,0:T(8,128)S(1)}, u32[]{:S(2)}, u32[]{:S(2)}) collective-permute-start(f32[256,256]{1,0:T(8,128)S(1)} %get-tuple-element.30), channel_id=1, source_target_pairs={{25,1},{26,2},{10,18},{20,12},{18,10},{19,11},{12,20},{13,21},{11,... | collective-permute-start | bytes 786440 | tf_op jit(solution)/shard_map/ppermute | solution.py:285
  66.9 24.3 %collective-permute-start.9 = (f32[136,256]{1,0:T(8,128)S(1)}, f32[136,256]{1,0:T(8,128)S(1)}, u32[]{:S(2)}, u32[]{:S(2)}) collective-permute-start(f32[136,256]{1,0:T(8,128)S(1)} %get-tuple-element.32), channel_id=1, source_target_pairs={{1,5},{2,6},{18,7},{12,8},{10,14},{11,15},{20,16},{21,17},{19,23},... | collective-permute-start | bytes 417800 | tf_op jit(solution)/shard_map/ppermute | solution.py:285
  68.2 23.0 %collective-permute-start.10 = (f32[136,256]{1,0:T(8,128)S(1)}, f32[136,256]{1,0:T(8,128)S(1)}, u32[]{:S(2)}, u32[]{:S(2)}) collective-permute-start(f32[136,256]{1,0:T(8,128)S(1)} %get-tuple-element.33), channel_id=1, source_target_pairs={{1,8},{2,16},{18,24},{12,1},{10,17},{11,25},{20,2},{21,10},{19,26}... | collective-permute-start | bytes 417800 | tf_op jit(solution)/shard_map/ppermute | solution.py:285
  76.5 14.7 %collective-permute-start.8 = (f32[136,256]{1,0:T(8,128)S(1)}, f32[136,256]{1,0:T(8,128)S(1)}, u32[]{:S(2)}, u32[]{:S(2)}) collective-permute-start(f32[136,256]{1,0:T(8,128)S(1)} %get-tuple-element.31.own_ref), channel_id=1, source_target_pairs={{18,3},{13,28}} | collective-permute-start | bytes 417800 | tf_op jit(solution)/shard_map/ppermute | solution.py:285
  77.2 14.0 %collective-permute-start.11 = (f32[128,256]{1,0:T(8,128)S(1)}, f32[128,256]{1,0:T(8,128)S(1)}, u32[]{:S(2)}, u32[]{:S(2)}) collective-permute-start(f32[128,256]{1,0:T(8,128)S(1)} %get-tuple-element.34), channel_id=1, source_target_pairs={{1,12},{2,20},{18,28},{12,5},{10,21},{11,29},{20,6},{21,14},{19,30... | collective-permute-start | bytes 393224 | tf_op jit(solution)/shard_map/ppermute | solution.py:285
  79.1 5.3 %collective-permute-start.12 = (f32[8,256]{1,0:T(8,128)S(1)}, f32[8,256]{1,0:T(8,128)S(1)}, u32[]{:S(2)}, u32[]{:S(2)}) collective-permute-start(f32[8,256]{1,0:T(8,128)S(1)} %get-tuple-element.35), channel_id=1, source_target_pairs={{1,29},{2,30},{18,31},{12,4},{10,6},{11,7},{20,12},{21,13},{19,15}... | collective-permute-start | bytes 24584 | tf_op jit(solution)/shard_map/ppermute | solution.py:285
  84.4 6.8 %collective-permute-start.13 = (f32[8,256]{1,0:T(8,128)S(1)}, f32[8,256]{1,0:T(8,128)S(1)}, u32[]{:S(2)}, u32[]{:S(2)}) collective-permute-start(f32[8,256]{1,0:T(8,128)S(1)} %get-tuple-element.36), channel_id=1, source_target_pairs={{1,4},{2,12},{18,20},{12,29},{10,13},{11,21},{20,30},{21,6},{19,22... | collective-permute-start | bytes 24584 | tf_op jit(solution)/shard_map/ppermute | solution.py:285

commit v5 on v4

--- a/solution.py
+++ b/solution.py
@@ -24,42 +24,132 @@
     return pl.CostEstimate(flops=flops, bytes_accessed=moved, transcendentals=0)
 
 
-def panel_kernel(vel_ref, lo_ref, hi_ref, met_ref, x_ref, xt_ref, g_ref):
+EDGE = 16
+
+
+def combine(first, second, third, center0, center1):
+    return third + center0 * second - center1 * first
+
+
+def interior_kernel(vel_ref, met_ref, x_ref, head_ref, tail_ref):
     rows, cols = vel_ref.shape[1:]
     row = lax.broadcasted_iota(jnp.int32, (rows, cols), 0)
     metric = met_ref[...]
 
     def gradient(k):
         field = vel_ref[k].astype(F32)
-        up = jnp.where(row == rows - 1, hi_ref[k].astype(F32), pltpu.roll(field, rows - 1, 0))
-        down = jnp.where(row == 0, lo_ref[k].astype(F32), pltpu.roll(field, 1, 0))
+        head_ref[k] = field[:8]
+        tail_ref[k] = field[rows - 8 :]
+        up = jnp.where(row == rows - 1, 0.0, pltpu.roll(field, rows - 1, 0))
+        down = jnp.where(row == 0, 0.0, pltpu.roll(field, 1, 0))
         return metric * (up - down) * 0.5
 
     first = gradient(0)
     x_ref[0:rows] = first.astype(BF16)
     second = gradient(1)
     x_ref[rows : 2 * rows] = second.astype(BF16)
-    third = gradient(2) + vel_ref[0].astype(F32) * second - vel_ref[1].astype(F32) * first
+    third = combine(first, second, gradient(2), vel_ref[0].astype(F32), vel_ref[1].astype(F32))
     x_ref[2 * rows :] = third.astype(BF16)
-    xt_ref[...] = x_ref[...].T
-    g_ref[...] = jnp.dot(xt_ref[...], x_ref[...], preferred_element_type=F32)
-
-
-def panel(velocity, lo, hi, metric):
+
+
+def interior(velocity, metric):
     _, rows, cols = velocity.shape
     return pl.pallas_call(
-        panel_kernel,
+        interior_kernel,
         out_shape=(
             jax.ShapeDtypeStruct((3 * rows, cols), BF16),
-            jax.ShapeDtypeStruct((cols, 3 * rows), BF16),
-            jax.ShapeDtypeStruct((cols, cols), F32),
+            jax.ShapeDtypeStruct((3, 8, cols), F32),
+            jax.ShapeDtypeStruct((3, 8, cols), F32),
         ),
-        in_specs=[VMEM] * 4,
+        in_specs=[VMEM] * 2,
         out_specs=(VMEM,) * 3,
         compiler_params=params(),
-        cost_estimate=cost(2 * 3 * rows * cols * cols, 12 * rows * cols),
+        cost_estimate=cost(30 * rows * cols, 12 * rows * cols),
+        name="interior",
+    )(velocity, metric)
+
+
+def panel_kernel(pos_ref, x_in_ref, head_ref, tail_ref, near_ref, far_ref, met_ref, x_ref, xt_ref, *g_refs):
+    cols = x_ref.shape[1]
+    rows = x_ref.shape[0] // 3
+    even = pos_ref[2] == 0
+    row = lax.broadcasted_iota(jnp.int32, (EDGE, cols), 0)
+
+    def edge(start, gradient, heads, at):
+        first, second, third = [gradient(k) for k in range(3)]
+        third = combine(first, second, third, heads[0], heads[1])
+        for k, value in enumerate((first, second, third)):
+            span = slice(k * rows + start, k * rows + start + EDGE)
+            kept = x_in_ref[span].astype(F32)
+            x_ref[span] = jnp.where(row == at, value, kept).astype(BF16)
+
+    x_ref[...] = x_in_ref[...]
+    lo = [jnp.where(even, far_ref[k].astype(F32), near_ref[k].astype(F32)) for k in range(3)]
+    hi = [jnp.where(even, near_ref[k].astype(F32), far_ref[k].astype(F32)) for k in range(3)]
+    low = met_ref[0:1]
+    edge(0, lambda k: low * (head_ref[k, 1:2] - lo[k]) * 0.5, [head_ref[k, 0:1] for k in range(2)], 0)
+    high = met_ref[rows - 1 : rows]
+    edge(rows - EDGE, lambda k: high * (hi[k] - tail_ref[k, 6:7]) * 0.5, [tail_ref[k, 7:8] for k in range(2)], EDGE - 1)
+    xt_ref[...] = x_ref[...].T
+    gram = jnp.dot(xt_ref[...], x_ref[...], preferred_element_type=F32)
+    if len(g_refs) == 1:
+        g_refs[0][...] = gram
+        return
+    away_ref, mine_ref, g_ref = g_refs
+    g_ref[...] = gram
+    half = cols // 2
+    for ref, core in ((mine_ref, pos_ref[2]), (away_ref, 1 - pos_ref[2])):
+        ref[0:half] = jnp.where(core == 0, g_ref[0:half, 0:half], g_ref[half:, half:])
+        ref[half:] = jnp.where(core == 0, g_ref[half : half + half // 2, 0:half], g_ref[half + half // 2 :, 0:half])
+
+
+def panel(pos, inner, near, far, metric, packed):
+    x, head, tail = inner
+    height, cols = x.shape
+    share = jax.ShapeDtypeStruct((3 * cols // 4, cols // 2), F32)
+    whole = jax.ShapeDtypeStruct((cols, cols), F32)
+    grams = (share, share) if packed else (whole,)
+    return pl.pallas_call(
+        panel_kernel,
+        out_shape=(jax.ShapeDtypeStruct((height, cols), BF16), jax.ShapeDtypeStruct((cols, height), BF16)) + grams,
+        in_specs=[SMEM] + [VMEM] * 6,
+        out_specs=(VMEM,) * (2 + len(grams)),
+        scratch_shapes=[pltpu.VMEM((cols, cols), F32)] if packed else [],
+        compiler_params=params(),
+        cost_estimate=cost(2 * height * cols * cols, 6 * height * cols),
         name="panel",
-    )(velocity, lo, hi, metric.reshape(rows, 1))
+    )(pos, x, head, tail, near, far, metric)
+
+
+def gather_kernel(pos_ref, mine_ref, theirs_ref, x_in_ref, near_in_ref, g_ref, x_ref, near_ref):
+    del x_in_ref, near_in_ref, x_ref, near_ref
+    half = mine_ref.shape[1]
+    even = pos_ref[2] == 0
+    first = jnp.where(even, mine_ref[...], theirs_ref[...])
+    second = jnp.where(even, theirs_ref[...], mine_ref[...])
+    g_ref[0:half, 0:half] = first[:half]
+    g_ref[half:, half:] = second[:half]
+    across = jnp.concatenate([first[half:], second[half:]], axis=0)
+    g_ref[half:, 0:half] = across
+    g_ref[0:half, half:] = across.T
+
+
+def gather_gram(pos, mine, theirs, x, near):
+    n = 2 * mine.shape[1]
+    anywhere = pl.BlockSpec(memory_space=pl.ANY)
+    return pl.pallas_call(
+        gather_kernel,
+        out_shape=(
+            jax.ShapeDtypeStruct((n, n), F32),
+            jax.ShapeDtypeStruct(x.shape, x.dtype),
+            jax.ShapeDtypeStruct(near.shape, near.dtype),
+        ),
+        in_specs=[SMEM, VMEM, VMEM, anywhere, anywhere],
+        out_specs=(VMEM, anywhere, anywhere),
+        input_output_aliases={3: 1, 4: 2},
+        compiler_params=params(),
+        name="gather",
+    )(pos, mine, theirs, x, near)
 
 
 def leaf_inverse(block):
@@ -182,45 +272,56 @@
     )(pos, after, xt, near, far, swap)
 
 
-def total_kernel(pos_ref, after_ref, *refs):
+def total_kernel(after_ref, *refs):
     del after_ref
-    count = len(refs) - 7
-    parts = refs[:count]
-    own_ref, sib_ref, low_ref, high_ref, top_t_ref, top_ref, st_ref = refs[count:]
+    value = refs[0][...]
+    for ref in refs[1:-1]:
+        value = value + ref[...]
+    refs[-1][...] = value
+
+
+def total(after, parts):
     n = parts[0].shape[0]
+    return pl.pallas_call(
+        total_kernel,
+        out_shape=jax.ShapeDtypeStruct((n, n), F32),
+        in_specs=[pl.BlockSpec(memory_space=pl.ANY)] + [VMEM] * len(parts),
+        out_specs=VMEM,
+        compiler_params=params(),
+        name="total",
+    )(after, *parts)
+
+
+def merge_kernel(pos_ref, after_ref, own_ref, moved_ref, cross_ref, mine_ref, sib_ref, top_ref, t_ref):
+    del after_ref
+    n = own_ref.shape[0]
     half = n // 2
-    total = parts[0][...]
-    for part in parts[1:]:
-        total = total + part[...]
-    low_ref[...] = total[: half + 8]
-    high_ref[...] = total[half:]
-    top_ref[...] = total[:8]
-    st_ref[0:n] = total.T
-    top_t_ref[...] = st_ref[0:8]
+    moved = jnp.abs(pos_ref[0] - pos_ref[1]) == 3
+    own = jnp.where(moved, moved_ref[...], own_ref[...])
+    t_ref[0:n] = own.T + cross_ref[...]
     core = pos_ref[2]
-    own_ref[...] = st_ref[pl.ds(pl.multiple_of(core * half, 8), half + 8)]
-    sib_ref[...] = st_ref[pl.ds(pl.multiple_of((1 - core) * half, 8), half + 8)]
-
-
-def total(pos, after, parts):
-    n = parts[0].shape[0]
+    top_ref[...] = t_ref[0:8]
+    mine_ref[...] = t_ref[pl.ds(pl.multiple_of(core * half, 8), half + 8)]
+    sib_ref[...] = t_ref[pl.ds(pl.multiple_of((1 - core) * half, 8), half + 8)]
+
+
+def merge(pos, after, own, moved, cross):
+    n = own.shape[0]
     half = n // 2
-    rows = (half + 8, half + 8, half + 8, half, 8, 8)
-    return pl.pallas_call(
-        total_kernel,
-        out_shape=tuple(jax.ShapeDtypeStruct((r, n), F32) for r in rows),
-        in_specs=[SMEM, pl.BlockSpec(memory_space=pl.ANY)] + [VMEM] * len(parts),
-        out_specs=(VMEM,) * 6,
+    return pl.pallas_call(
+        merge_kernel,
+        out_shape=tuple(jax.ShapeDtypeStruct((r, n), F32) for r in (half + 8, half + 8, 8)),
+        in_specs=[SMEM, pl.BlockSpec(memory_space=pl.ANY)] + [VMEM] * 3,
+        out_specs=(VMEM,) * 3,
         scratch_shapes=[pltpu.VMEM((n + 8, n), F32)],
         compiler_params=params(),
-        name="total",
-    )(pos, after, *parts)
-
-
-def tiles_kernel(pos_ref, w_ref, g_ref, own_ref, moved_ref, sib_ref, low_ref, high_ref, top_t_ref, top_ref, out_ref, p_ref):
-    count = pos_ref[3]
-    chip, group, core = pos_ref[0], pos_ref[1], pos_ref[2]
-    half = high_ref.shape[0]
+        name="merge",
+    )(pos, after, own, moved, cross)
+
+
+def tiles_kernel(pos_ref, w_ref, g_ref, own_ref, sib_ref, top_ref, out_ref, p_ref):
+    chip, group, core, count = pos_ref[0], pos_ref[1], pos_ref[2], pos_ref[3]
+    half = out_ref.shape[1]
     following = jnp.where(chip + 1 == count, 0, chip + 1)
     owner = jnp.where(chip < group, 0, 1)
 
@@ -231,20 +332,11 @@
 
     @pl.when(chip != group)
     def _():
-        direct = jnp.where(jnp.abs(chip - group) == 3, moved_ref[...], own_ref[...])
-        slab = jnp.where(core == owner, direct, sib_ref[...])
-
-        @pl.when(core == 0)
-        def _():
-            p_ref[...] = slab + low_ref[...]
-
-        @pl.when(core != 0)
-        def _():
-            p_ref[0:half] = slab[:half] + high_ref[...]
+        p_ref[...] = jnp.where(core == owner, own_ref[...], sib_ref[...])
 
     @pl.when(core != 0)
     def _():
-        p_ref[half:] = jnp.where(following == group, g_ref[0:8], top_t_ref[...] + top_ref[...])
+        p_ref[half:] = jnp.where(following == group, g_ref[0:8], top_ref[...])
 
     shifted = pltpu.roll(p_ref[...], half + 7, 0)[:half]
     out_ref[...] = mm(w_ref[...], shifted, ((1,), (1,)))
@@ -256,7 +348,7 @@
     return pl.pallas_call(
         tiles_kernel,
         out_shape=jax.ShapeDtypeStruct((n, half), F32),
-        in_specs=[SMEM] + [VMEM] * 9,
+        in_specs=[SMEM] + [VMEM] * 5,
         out_specs=VMEM,
         scratch_shapes=[pltpu.VMEM((half + 8, n), F32)],
         compiler_params=params(),
@@ -264,12 +356,19 @@
     )(pos, w, gram, *slabs)
 
 
-def halos(velocity):
+def start(velocity, metric, packed):
     count = lax.axis_size("space")
+    space, group = lax.axis_index("space"), lax.axis_index("tm")
+    odd = space % 2
+    pos = jnp.stack([space // 2, group, odd, lax.axis_size("tm")]).astype(jnp.int32)
     head, tail = velocity[:, :1], velocity[:, -1:]
-    lo = lax.ppermute(tail, "space", [(i, i + 1) for i in range(count - 1)])
-    hi = lax.ppermute(head, "space", [(i + 1, i) for i in range(count - 1)])
-    return lo, hi
+    inside = [(i, i ^ 1) for i in range(count)]
+    outside = [(i, i + 1) for i in range(1, count - 1, 2)]
+    outside += [(j, i) for i, j in outside]
+    far = lax.ppermute(jnp.where(odd == 0, head, tail), "space", outside)
+    near = lax.ppermute(jnp.where(odd == 0, tail, head), "space", inside)
+    column = metric.reshape(-1, 1)
+    return pos, panel(pos, interior(velocity, column), near, far, column, packed)
 
 
 def paired_body(velocity, metric):
@@ -284,58 +383,49 @@
     def send(value, pairs):
         return lax.ppermute(value, axes, pairs)
 
-    space, group = lax.axis_index("space"), lax.axis_index("tm")
-    core = space % 2
-    pos = jnp.stack([space // 2, group, core, jnp.int32(groups)]).astype(jnp.int32)
-
-    lo, hi = halos(velocity)
-    x, xt, gram = panel(velocity, lo, hi, metric)
-
-    n = gram.shape[0]
-    devices = 2 * groups
-    shares = lax.all_to_all(gram, "space", 0, 0, tiled=True)
-    mine = jnp.sum(shares.reshape(devices, n // devices, n), axis=0)
-    gram = lax.all_to_all(jnp.tile(mine, (devices, 1)), "space", 0, 0, tiled=True)
-    state = factor_part(0, n // LEAF // 2, (gram,))
+    pos, (x, xt, away, mine) = start(velocity, metric, True)
 
     def hops(group_pairs):
         pairs = [(at(k, z, 0), at(k, t, 0)) for k in every for z, t in group_pairs]
         return pairs + [(at(k, 3 - z, 1), at(k, 3 - t, 1)) for k in every for z, t in group_pairs]
 
     near = send(x, hops([(0, 1), (1, 2), (2, 3)]))
+
+    siblings = [(at(k, z, c), at(k, z, 1 - c)) for k in every for z in every for c in cores]
+    mine = mine + send(away, siblings)
+    others = [
+        send(mine, [(at(k, z, c), at(k ^ m, z, c)) for k in every for z in every for c in cores])
+        for m in range(1, groups)
+    ]
+    for other in others:
+        mine = mine + other
+    gram, x, near = gather_gram(pos, mine, send(mine, siblings), x, near)
+    state = factor_part(0, 2, (gram,))
+
     far = send(near, hops([(1, 2), (2, 3)]))
     swap = send(x, hops([(3, 2)]))
     parts = list(blocks(pos, state[0], xt, near, far, swap, groups))
-    w = factor_part(n // LEAF // 2, n // LEAF - n // LEAF // 2, state, (parts[0],))[1]
+    state = factor_part(2, 1, state, (parts[0],))
 
     owners = {(k, z): (k, z, 0 if k < z else 1) for k in every for z in every if k != z}
     owners[0, 3] = (2, 2, 0)
     owners[3, 0] = (1, 1, 1)
     for m in range(1, groups):
         parts[m] = send(parts[m], [(at(k ^ m, z, c), at(k, z, c)) for k, z, c in owners.values()])
-    own, sib, low, high, top_t, top = total(pos, w, parts)
-
-    def deliver(value, target):
-        return send(value, [(at(*o), at(*target(k, z))) for (k, z), o in owners.items()])
-
-    def first_core(k, z):
-        return 0 if k < z else 1
-
-    slabs = [
-        own,
-        send(own, [(at(*owners[p]), at(*p, first_core(*p))) for p in ((0, 3), (3, 0))]),
-        deliver(sib, lambda k, z: (k, z, 1 - first_core(k, z))),
-        deliver(low, lambda k, z: (z, k, 0)),
-        deliver(high, lambda k, z: (z, k, 1)),
-        deliver(top_t, lambda k, z: ((k - 1) % groups, z, 1)),
-        deliver(top, lambda k, z: ((z - 1) % groups, k, 1)),
-    ]
-    return tiles(pos, w, gram, slabs)
+    own = total(state[0], parts)
+    w = factor_part(3, 1, state, (own,))[1]
+
+    homes = {(k, z): (k, z, 0 if k < z else 1) for k, z in owners}
+    cross = send(own, [(at(*o), at(*homes[z, k])) for (k, z), o in owners.items()])
+    moved = send(own, [(at(*owners[p]), at(*homes[p])) for p in ((0, 3), (3, 0))])
+    mine, sib, top = merge(pos, w, own, moved, cross)
+    sib = send(sib, [(at(k, z, c), at(k, z, 1 - c)) for k, z, c in homes.values()])
+    top = send(top, [(at(k, z, c), at((k - 1) % groups, z, 1)) for k, z, c in homes.values()])
+    return tiles(pos, w, gram, (mine, sib, top))
 
 
 def general_body(velocity, metric):
-    lo, hi = halos(velocity)
-    x, xt, gram = panel(velocity, lo, hi, metric)
+    _, (x, xt, gram) = start(velocity, metric, False)
     w = inverse_factor(lax.psum(gram, "space"))
     count = lax.axis_size("tm")
     following = lax.ppermute(x[:, :1], "tm", [(i, (i - 1) % count) for i in range(count)])

time: 93.5 us -> 71.8 us (0.77)
  the two profiles are of different devices: /device:TPU:3 before, /device:TPU:17 now
where the time goes in v5:
time: 71.8 us; the launch traced here: 71.4 us
  waiting for transfers between devices  27.4 us (38%)
  starting transfers between devices  24.1 us (34%)
  Pallas kernels  17 us (24%)
  local copies, waits for them, and re-layouts  1.76 us (2%)
  other arithmetic  0.85 us (1%)
    ppermute x15, waiting for transfers between devices, send(): return lax.ppermute(value, axes, pairs)  27.4 us
    ppermute x15, starting transfers between devices, send(): return lax.ppermute(value, axes, pairs)  20.3 us
    pallas_call x3, Pallas kernels, factor_part(): pl.pallas_call(kernel, out_shape=(jax.ShapeDtypeStruct((n, n), F32),) * 2...  11.7 us
    ppermute x1, starting transfers between devices, start(): far = lax.ppermute(jnp.where(odd == 0, head, tail), 'space', outside)  3.68 us
    unnamed x4, local copies, waits for them, and re-layouts  1.66 us
    pallas_call x1, Pallas kernels, tiles(): pl.pallas_call(tiles_kernel, out_shape=jax.ShapeDtypeStruct((n, half), F3...  1.61 us
  transfers between devices with their start and end apart: 17, of which 7 were waited for; matrix products, arithmetic and copies ran while one was open for 0% of the time, Pallas kernels for 17%

profile of v5, /device:TPU:17, one launch (start us, length us, event | category | flops | bytes accessed | tf_op | source)
XLA Modules:
  0.0 71.4 jit_solution(3844951812221991637)
XLA Ops:
  0.0 0.7 %broadcast_select_fusion = (bf16[3,1,256]{2,1,0:T(2,128)(2,1)S(1)}, bf16[3,1,256]{2,1,0:T(2,128)(2,1)S(1)}) fusion(pred[]{:T(512)S(6)} %eq.6, bf16[3,384,256]{2,1,0:T(8,128)(2,1)} %vel_ref.1), kind=kLoop, calls=%fused_computation.1 | loop fusion | flops 1536 | bytes 6145 | tf_op jit(solution)/shard_map/jit(_where)/select_n | solution.py:368
  0.7 3.7 %collective-permute-start.1 = (bf16[3,1,256]{2,1,0:T(2,128)(2,1)S(1)}, bf16[3,1,256]{2,1,0:T(2,128)(2,1)S(1)}, u32[]{:S(2)}, u32[]{:S(2)}) collective-permute-start(bf16[3,1,256]{2,1,0:T(2,128)(2,1)S(1)} %get-tuple-element.49), channel_id=1, source_target_pairs={{4,8},{12,16},{20,24},{8,4},{16,12},{24,20},{5,9},{13,17},{21,25},... | collective-permute-start | bytes 4616 | tf_op jit(solution)/shard_map/ppermute | solution.py:368
  5.3 1.1 %copy-done = bf16[3,384,256]{2,1,0:T(8,128)(2,1)S(1)} copy-done((bf16[3,384,256]{2,1,0:T(8,128)(2,1)S(1)}, bf16[3,384,256]{2,1,0:T(8,128)(2,1)}, u32[]{:S(2)}) %copy-start) | copy-done | bytes 589848
  6.8 1.0 %panel.1 = (bf16[1152,256]{1,0:T(8,128)(2,1)S(1)}, bf16[256,1152]{1,0:T(8,128)(2,1)S(1)}, f32[192,128]{1,0:T(8,128)S(1)}, f32[192,128]{1,0:T(8,128)S(1)}) custom-call(s32[4]{0:T(128)S(1)} %pad_add_fusion.pos_ref, bf16[1152,256]{1,0:T(8,128)(2,1)S(1)} %get-tuple-element.27.x_in_ref, f32[3,8,256]{2,1,0:T(8,128)S(1)} %get-tuple-element.28.head_ref, ...), custom_call_target="tpu_custom_call" | custom-call | flops 150994944 | bytes 1769472 | tf_op jit(solution)/shard_map/panel/pallas_call | solution.py:112
  7.8 2.1 %collective-permute-start.7 = (bf16[1152,256]{1,0:T(8,128)(2,1)S(1)}, bf16[1152,256]{1,0:T(8,128)(2,1)S(1)}, u32[]{:S(2)}, u32[]{:S(2)}) collective-permute-start(bf16[1152,256]{1,0:T(8,128)(2,1)S(1)} %get-tuple-element.32.x_in_ref), channel_id=1, source_target_pairs={{0,1},{1,2},{2,3},{8,9},{9,10},{10,11},{16,17},{17,18},{18,19},{24... | collective-permute-start | bytes 1769480 | tf_op jit(solution)/shard_map/ppermute | solution.py:384
  9.9 1.9 %collective-permute-start.2 = (f32[192,128]{1,0:T(8,128)S(1)}, f32[192,128]{1,0:T(8,128)S(1)}, u32[]{:S(2)}, u32[]{:S(2)}) collective-permute-start(f32[192,128]{1,0:T(8,128)S(1)} %get-tuple-element.31), channel_id=1, source_target_pairs={{0,4},{4,0},{1,5},{5,1},{2,6},{6,2},{3,7},{7,3},{8,12},{12,8},{9,1... | collective-permute-start | bytes 294920 | tf_op jit(solution)/shard_map/ppermute | solution.py:384
  11.9 0.9 %collective-permute-done.2 = f32[192,128]{1,0:T(8,128)S(1)} collective-permute-done((f32[192,128]{1,0:T(8,128)S(1)}, f32[192,128]{1,0:T(8,128)S(1)}, u32[]{:S(2)}, u32[]{:S(2)}) %collective-permute-start.2) | collective-permute-done | bytes 98336 | tf_op jit(solution)/shard_map/ppermute | solution.py:384
  12.8 1.3 %collective-permute-start.5 = (f32[192,128]{1,0:T(8,128)S(1)}, f32[192,128]{1,0:T(8,128)S(1)}, u32[]{:S(2)}, u32[]{:S(2)}) collective-permute-start(f32[192,128]{1,0:T(8,128)S(1)} %add.18), channel_id=1, source_target_pairs={{0,24},{4,28},{1,25},{5,29},{2,26},{6,30},{3,27},{7,31},{8,16},{12... | collective-permute-start | bytes 294920 | tf_op jit(solution)/shard_map/ppermute | solution.py:384
  14.1 1.2 %collective-permute-start.4 = (f32[192,128]{1,0:T(8,128)S(1)}, f32[192,128]{1,0:T(8,128)S(1)}, u32[]{:S(2)}, u32[]{:S(2)}) collective-permute-start(f32[192,128]{1,0:T(8,128)S(1)} %add.18), channel_id=1, source_target_pairs={{0,16},{4,20},{1,17},{5,21},{2,18},{6,22},{3,19},{7,23},{8,24},{12... | collective-permute-start | bytes 294920 | tf_op jit(solution)/shard_map/ppermute | solution.py:384
  15.5 2.3 %collective-permute-done.5 = f32[192,128]{1,0:T(8,128)S(1)} collective-permute-done((f32[192,128]{1,0:T(8,128)S(1)}, f32[192,128]{1,0:T(8,128)S(1)}, u32[]{:S(2)}, u32[]{:S(2)}) %collective-permute-start.5) | collective-permute-done | bytes 98336 | tf_op jit(solution)/shard_map/ppermute | solution.py:384
  17.8 2.8 %collective-permute-done.4 = f32[192,128]{1,0:T(8,128)S(1)} collective-permute-done((f32[192,128]{1,0:T(8,128)S(1)}, f32[192,128]{1,0:T(8,128)S(1)}, u32[]{:S(2)}, u32[]{:S(2)}) %collective-permute-start.4) | collective-permute-done | bytes 98336 | tf_op jit(solution)/shard_map/ppermute | solution.py:384
  20.6 0.6 collective-permute-start.6
  21.3 0.9 %collective-permute-done.6.theirs_ref = f32[192,128]{1,0:T(8,128)S(1)} collective-permute-done((f32[192,128]{1,0:T(8,128)S(1)}, f32[192,128]{1,0:T(8,128)S(1)}, u32[]{:S(2)}, u32[]{:S(2)}) %collective-permute-start.6) | collective-permute-done | bytes 98336 | tf_op jit(solution)/shard_map/ppermute | solution.py:384
  22.2 0.6 gather.1
  22.8 0.7 collective-permute-start.9
  23.6 2.7 %collective-permute-start.8 = (bf16[1152,256]{1,0:T(8,128)(2,1)S(1)}, bf16[1152,256]{1,0:T(8,128)(2,1)S(1)}, u32[]{:S(2)}, u32[]{:S(2)}) collective-permute-start(bf16[1152,256]{1,0:T(8,128)(2,1)S(1)} %get-tuple-element.37.near_ref), channel_id=1, source_target_pairs={{1,2},{2,3},{9,10},{10,11},{17,18},{18,19},{25,26},{26,27},{6,5},{... | collective-permute-start | bytes 1769480 | tf_op jit(solution)/shard_map/ppermute | solution.py:384
  26.3 5.9 %factor.3 = (f32[256,256]{1,0:T(8,128)S(1)}, f32[256,256]{1,0:T(8,128)S(1)}) custom-call(f32[256,256]{1,0:T(8,128)S(1)} %get-tuple-element.33.refs_0_.g_ref), custom_call_target="tpu_custom_call" | custom-call | flops 33554432 | bytes 524288 | tf_op jit(solution)/shard_map/factor/pallas_call | solution.py:222
  32.1 0.9 %collective-permute-done.8.far_ref = bf16[1152,256]{1,0:T(8,128)(2,1)S(1)} collective-permute-done((bf16[1152,256]{1,0:T(8,128)(2,1)S(1)}, bf16[1152,256]{1,0:T(8,128)(2,1)S(1)}, u32[]{:S(2)}, u32[]{:S(2)}) %collective-permute-start.8) | collective-permute-done | bytes 589856 | tf_op jit(solution)/shard_map/ppermute | solution.py:384
  33.0 0.9 %blocks.1 = (f32[256,256]{1,0:T(8,128)S(1)}, f32[256,256]{1,0:T(8,128)S(1)}, f32[256,256]{1,0:T(8,128)S(1)}, f32[256,256]{1,0:T(8,128)S(1)}) custom-call(s32[4]{0:T(128)S(1)} %pad_add_fusion.pos_ref, f32[256,256]{1,0:T(8,128)S(1)} %get-tuple-element.34.after_ref.refs_0_, bf16[256,1152]{1,0:T(8,128)(2,1)S(1)} %get-tuple-element.36.xt_ref, ...), custom_call_target="tpu_custom_call" | custom-call | flops 452984832 | bytes 1048576 | tf_op jit(solution)/shard_map/blocks/pallas_call | solution.py:264
  34.0 0.7 collective-permute-start.10
  34.6 0.7 collective-permute-start.11
  35.3 4.3 %collective-permute-start.12 = (f32[256,256]{1,0:T(8,128)S(1)}, f32[256,256]{1,0:T(8,128)S(1)}, u32[]{:S(2)}, u32[]{:S(2)}) collective-permute-start(f32[256,256]{1,0:T(8,128)S(1)} %get-tuple-element.44), channel_id=1, source_target_pairs={{25,1},{26,2},{10,18},{20,12},{18,10},{19,11},{12,20},{13,21},{11,... | collective-permute-start | bytes 786440 | tf_op jit(solution)/shard_map/ppermute | solution.py:384
  39.6 2.8 %factor.4 = (f32[256,256]{1,0:T(8,128)S(1)}, f32[256,256]{1,0:T(8,128)S(1)}) custom-call(f32[256,256]{1,0:T(8,128)S(1)} %get-tuple-element.34.after_ref.refs_0_, f32[256,256]{1,0:T(8,128)S(1)} %get-tuple-element.35.refs_1_, f32[256,256]{1,0:T(8,128)S(1)} %get-tuple-element.39.refs_2_.refs_0_), custom_call_target="tpu_custom_call" | custom-call | flops 33554432 | bytes 524288 | tf_op jit(solution)/shard_map/factor/pallas_call | solution.py:222
  42.5 1.2 %collective-permute-done.12.refs_3_ = f32[256,256]{1,0:T(8,128)S(1)} collective-permute-done((f32[256,256]{1,0:T(8,128)S(1)}, f32[256,256]{1,0:T(8,128)S(1)}, u32[]{:S(2)}, u32[]{:S(2)}) %collective-permute-start.12) | collective-permute-done | bytes 262176 | tf_op jit(solution)/shard_map/ppermute | solution.py:384
  43.8 0.7 collective-permute-start.14
  44.4 0.7 collective-permute-start.13
  45.1 3.0 %factor.5 = (f32[256,256]{1,0:T(8,128)}, f32[256,256]{1,0:T(8,128)S(1)}) custom-call(f32[256,256]{1,0:T(8,128)S(1)} %get-tuple-element.40.after_ref.refs_0_, f32[256,256]{1,0:T(8,128)S(1)} %get-tuple-element.41.refs_1_, f32[256,256]{1,0:T(8,128)S(1)} %total.1.refs_2_.own_ref), custom_call_target="tpu_custom_call" | custom-call | flops 33554432 | bytes 524288 | tf_op jit(solution)/shard_map/factor/pallas_call | solution.py:222
  48.2 0.7 merge.1
  48.9 1.3 %collective-permute-start.15 = (f32[136,256]{1,0:T(8,128)S(1)}, f32[136,256]{1,0:T(8,128)S(1)}, u32[]{:S(2)}, u32[]{:S(2)}) collective-permute-start(f32[136,256]{1,0:T(8,128)S(1)} %get-tuple-element.47), channel_id=1, source_target_pairs={{1,5},{2,6},{3,7},{12,8},{10,14},{11,15},{20,16},{21,17},{19,23},{... | collective-permute-start | bytes 417800 | tf_op jit(solution)/shard_map/ppermute | solution.py:384
  50.2 1.3 %collective-permute-start.16 = (f32[8,256]{1,0:T(8,128)S(1)}, f32[8,256]{1,0:T(8,128)S(1)}, u32[]{:S(2)}, u32[]{:S(2)}) collective-permute-start(f32[8,256]{1,0:T(8,128)S(1)} %get-tuple-element.48), channel_id=1, source_target_pairs={{1,29},{2,30},{3,31},{12,4},{10,6},{11,7},{20,12},{21,13},{19,15},... | collective-permute-start | bytes 24584 | tf_op jit(solution)/shard_map/ppermute | solution.py:384
  51.5 18.3 %collective-permute-done.16.top_ref = f32[8,256]{1,0:T(8,128)S(1)} collective-permute-done((f32[8,256]{1,0:T(8,128)S(1)}, f32[8,256]{1,0:T(8,128)S(1)}, u32[]{:S(2)}, u32[]{:S(2)}) %collective-permute-start.16) | collective-permute-done | bytes 8224 | tf_op jit(solution)/shard_map/ppermute | solution.py:384
  69.8 1.6 %tiles.1 = f32[256,128]{1,0:T(8,128)} custom-call(s32[4]{0:T(128)S(1)} %pad_add_fusion.pos_ref, f32[256,256]{1,0:T(8,128)S(1)} %get-tuple-element.45.after_ref.w_ref, f32[256,256]{1,0:T(8,128)S(1)} %get-tuple-element.33.refs_0_.g_ref, f32[136,256]{1,0:T(8,128)S(1)} %get-tuple-element.46.own_ref, f32[136,256]{1,0:T(8,128)S(1)} %collective-permute-done.15.sib_ref, ...), custom_call_target="tpu_custom_call" | custom-call | tf_op jit(solution)/shard_map/tiles/pallas_call | solution.py:348
  (21 shorter events, 1.7 us)
Async XLA Ops:
  0.7 6.1 %collective-permute-start.1 = (bf16[3,1,256]{2,1,0:T(2,128)(2,1)S(1)}, bf16[3,1,256]{2,1,0:T(2,128)(2,1)S(1)}, u32[]{:S(2)}, u32[]{:S(2)}) collective-permute-start(bf16[3,1,256]{2,1,0:T(2,128)(2,1)S(1)} %get-tuple-element.49), channel_id=1, source_target_pairs={{4,8},{12,16},{20,24},{8,4},{16,12},{24,20},{5,9},{13,17},{21,25},... | collective-permute-start | bytes 4616 | tf_op jit(solution)/shard_map/ppermute | solution.py:368
  4.4 2.4 %collective-permute-start = (bf16[3,1,256]{2,1,0:T(2,128)(2,1)S(1)}, bf16[3,1,256]{2,1,0:T(2,128)(2,1)S(1)}, u32[]{:S(2)}, u32[]{:S(2)}) collective-permute-start(bf16[3,1,256]{2,1,0:T(2,128)(2,1)S(1)} %get-tuple-element.50), channel_id=1, source_target_pairs={{0,4},{4,0},{8,12},{12,8},{16,20},{20,16},{24,28},{28,24},{1,5},{5... | collective-permute-start | bytes 4616 | tf_op jit(solution)/shard_map/ppermute | solution.py:369
  4.5 0.7 copy-start.1
  5.3 1.1 %copy-start = (bf16[3,384,256]{2,1,0:T(8,128)(2,1)S(1)}, bf16[3,384,256]{2,1,0:T(8,128)(2,1)}, u32[]{:S(2)}) copy-start(bf16[3,384,256]{2,1,0:T(8,128)(2,1)} %vel_ref.1) | copy-start | bytes 1769476
  7.8 14.4 %collective-permute-start.7 = (bf16[1152,256]{1,0:T(8,128)(2,1)S(1)}, bf16[1152,256]{1,0:T(8,128)(2,1)S(1)}, u32[]{:S(2)}, u32[]{:S(2)}) collective-permute-start(bf16[1152,256]{1,0:T(8,128)(2,1)S(1)} %get-tuple-element.32.x_in_ref), channel_id=1, source_target_pairs={{0,1},{1,2},{2,3},{8,9},{9,10},{10,11},{16,17},{17,18},{18,19},{24... | collective-permute-start | bytes 1769480 | tf_op jit(solution)/shard_map/ppermute | solution.py:384
  9.9 2.9 %collective-permute-start.2 = (f32[192,128]{1,0:T(8,128)S(1)}, f32[192,128]{1,0:T(8,128)S(1)}, u32[]{:S(2)}, u32[]{:S(2)}) collective-permute-start(f32[192,128]{1,0:T(8,128)S(1)} %get-tuple-element.31), channel_id=1, source_target_pairs={{0,4},{4,0},{1,5},{5,1},{2,6},{6,2},{3,7},{7,3},{8,12},{12,8},{9,1... | collective-permute-start | bytes 294920 | tf_op jit(solution)/shard_map/ppermute | solution.py:384
  12.8 5.0 %collective-permute-start.5 = (f32[192,128]{1,0:T(8,128)S(1)}, f32[192,128]{1,0:T(8,128)S(1)}, u32[]{:S(2)}, u32[]{:S(2)}) collective-permute-start(f32[192,128]{1,0:T(8,128)S(1)} %add.18), channel_id=1, source_target_pairs={{0,24},{4,28},{1,25},{5,29},{2,26},{6,30},{3,27},{7,31},{8,16},{12... | collective-permute-start | bytes 294920 | tf_op jit(solution)/shard_map/ppermute | solution.py:384
  14.1 6.5 %collective-permute-start.4 = (f32[192,128]{1,0:T(8,128)S(1)}, f32[192,128]{1,0:T(8,128)S(1)}, u32[]{:S(2)}, u32[]{:S(2)}) collective-permute-start(f32[192,128]{1,0:T(8,128)S(1)} %add.18), channel_id=1, source_target_pairs={{0,16},{4,20},{1,17},{5,21},{2,18},{6,22},{3,19},{7,23},{8,24},{12... | collective-permute-start | bytes 294920 | tf_op jit(solution)/shard_map/ppermute | solution.py:384
  15.3 5.3 %collective-permute-start.3 = (f32[192,128]{1,0:T(8,128)S(1)}, f32[192,128]{1,0:T(8,128)S(1)}, u32[]{:S(2)}, u32[]{:S(2)}) collective-permute-start(f32[192,128]{1,0:T(8,128)S(1)} %add.18), channel_id=1, source_target_pairs={{0,8},{4,12},{1,9},{5,13},{2,10},{6,14},{3,11},{7,15},{8,0},{12,4}... | collective-permute-start | bytes 294920 | tf_op jit(solution)/shard_map/ppermute | solution.py:384
  20.6 1.6 %collective-permute-start.6 = (f32[192,128]{1,0:T(8,128)S(1)}, f32[192,128]{1,0:T(8,128)S(1)}, u32[]{:S(2)}, u32[]{:S(2)}) collective-permute-start(f32[192,128]{1,0:T(8,128)S(1)} %add_add_fusion.mine_ref), channel_id=1, source_target_pairs={{0,4},{4,0},{1,5},{5,1},{2,6},{6,2},{3,7},{7,3},{8,12},{12,8},{9,1... | collective-permute-start | bytes 294920 | tf_op jit(solution)/shard_map/ppermute | solution.py:384
  22.8 9.3 %collective-permute-start.9 = (bf16[1152,256]{1,0:T(8,128)(2,1)S(1)}, bf16[1152,256]{1,0:T(8,128)(2,1)S(1)}, u32[]{:S(2)}, u32[]{:S(2)}) collective-permute-start(bf16[1152,256]{1,0:T(8,128)(2,1)S(1)} %get-tuple-element.38), channel_id=1, source_target_pairs={{3,2},{11,10},{19,18},{27,26},{4,5},{12,13},{20,21},{28,29}} | collective-permute-start | bytes 1769480 | tf_op jit(solution)/shard_map/ppermute | solution.py:384
  23.6 9.5 %collective-permute-start.8 = (bf16[1152,256]{1,0:T(8,128)(2,1)S(1)}, bf16[1152,256]{1,0:T(8,128)(2,1)S(1)}, u32[]{:S(2)}, u32[]{:S(2)}) collective-permute-start(bf16[1152,256]{1,0:T(8,128)(2,1)S(1)} %get-tuple-element.37.near_ref), channel_id=1, source_target_pairs={{1,2},{2,3},{9,10},{10,11},{17,18},{18,19},{25,26},{26,27},{6,5},{... | collective-permute-start | bytes 1769480 | tf_op jit(solution)/shard_map/ppermute | solution.py:384
  34.0 8.5 %collective-permute-start.10 = (f32[256,256]{1,0:T(8,128)S(1)}, f32[256,256]{1,0:T(8,128)S(1)}, u32[]{:S(2)}, u32[]{:S(2)}) collective-permute-start(f32[256,256]{1,0:T(8,128)S(1)} %get-tuple-element.42), channel_id=1, source_target_pairs={{9,1},{10,2},{26,18},{4,12},{2,10},{3,11},{28,20},{29,21},{27,19},... | collective-permute-start | bytes 786440 | tf_op jit(solution)/shard_map/ppermute | solution.py:384
  34.6 7.8 %collective-permute-start.11 = (f32[256,256]{1,0:T(8,128)S(1)}, f32[256,256]{1,0:T(8,128)S(1)}, u32[]{:S(2)}, u32[]{:S(2)}) collective-permute-start(f32[256,256]{1,0:T(8,128)S(1)} %get-tuple-element.43), channel_id=1, source_target_pairs={{17,1},{18,2},{2,18},{28,12},{26,10},{27,11},{4,20},{5,21},{3,19},... | collective-permute-start | bytes 786440 | tf_op jit(solution)/shard_map/ppermute | solution.py:384
  35.3 8.4 %collective-permute-start.12 = (f32[256,256]{1,0:T(8,128)S(1)}, f32[256,256]{1,0:T(8,128)S(1)}, u32[]{:S(2)}, u32[]{:S(2)}) collective-permute-start(f32[256,256]{1,0:T(8,128)S(1)} %get-tuple-element.44), channel_id=1, source_target_pairs={{25,1},{26,2},{10,18},{20,12},{18,10},{19,11},{12,20},{13,21},{11,... | collective-permute-start | bytes 786440 | tf_op jit(solution)/shard_map/ppermute | solution.py:384
  43.8 4.4 %collective-permute-start.14 = (f32[256,256]{1,0:T(8,128)S(1)}, f32[256,256]{1,0:T(8,128)S(1)}, u32[]{:S(2)}, u32[]{:S(2)}) collective-permute-start(f32[256,256]{1,0:T(8,128)S(1)} %total.1.refs_2_.own_ref), channel_id=1, source_target_pairs={{1,12},{2,20},{18,28},{12,1},{10,21},{11,29},{20,2},{21,10},{19,30... | collective-permute-start | bytes 786440 | tf_op jit(solution)/shard_map/ppermute | solution.py:384
  44.4 3.7 %collective-permute-start.13 = (f32[256,256]{1,0:T(8,128)S(1)}, f32[256,256]{1,0:T(8,128)S(1)}, u32[]{:S(2)}, u32[]{:S(2)}) collective-permute-start(f32[256,256]{1,0:T(8,128)S(1)} %total.1.refs_2_.own_ref), channel_id=1, source_target_pairs={{18,3},{13,28}} | collective-permute-start | bytes 786440 | tf_op jit(solution)/shard_map/ppermute | solution.py:384
  48.9 20.9 %collective-permute-start.15 = (f32[136,256]{1,0:T(8,128)S(1)}, f32[136,256]{1,0:T(8,128)S(1)}, u32[]{:S(2)}, u32[]{:S(2)}) collective-permute-start(f32[136,256]{1,0:T(8,128)S(1)} %get-tuple-element.47), channel_id=1, source_target_pairs={{1,5},{2,6},{3,7},{12,8},{10,14},{11,15},{20,16},{21,17},{19,23},{... | collective-permute-start | bytes 417800 | tf_op jit(solution)/shard_map/ppermute | solution.py:384
  50.2 19.6 %collective-permute-start.16 = (f32[8,256]{1,0:T(8,128)S(1)}, f32[8,256]{1,0:T(8,128)S(1)}, u32[]{:S(2)}, u32[]{:S(2)}) collective-permute-start(f32[8,256]{1,0:T(8,128)S(1)} %get-tuple-element.48), channel_id=1, source_target_pairs={{1,29},{2,30},{3,31},{12,4},{10,6},{11,7},{20,12},{21,13},{19,15},... | collective-permute-start | bytes 24584 | tf_op jit(solution)/shard_map/ppermute | solution.py:384

commit v6 on v5

--- a/solution.py
+++ b/solution.py
@@ -31,13 +31,24 @@
     return third + center0 * second - center1 * first
 
 
-def interior_kernel(vel_ref, met_ref, x_ref, head_ref, tail_ref):
+def interior_kernel(pos_ref, vel_hbm, met_hbm, x_ref, met_ref, inside_ref, outside_ref, head_ref, tail_ref, vel_ref, row_ref, sems):
     rows, cols = vel_ref.shape[1:]
+    copies = [pltpu.make_async_copy(met_hbm, row_ref, sems.at[3])]
+    copies += [pltpu.make_async_copy(vel_hbm.at[k], vel_ref.at[k], sems.at[k]) for k in range(3)]
+    for copy in copies:
+        copy.start()
+    even = pos_ref[2] == 0
     row = lax.broadcasted_iota(jnp.int32, (rows, cols), 0)
-    metric = met_ref[...]
+    copies[0].wait()
+    metric = jnp.broadcast_to(row_ref[...][None, :], (8, rows)).T[:, 0:1]
+    met_ref[...] = metric
 
     def gradient(k):
+        copies[k + 1].wait()
         field = vel_ref[k].astype(F32)
+        head, tail = field[0:1], field[rows - 1 : rows]
+        inside_ref[k : k + 1] = jnp.where(even, tail, head)
+        outside_ref[k : k + 1] = jnp.where(even, head, tail)
         head_ref[k] = field[:8]
         tail_ref[k] = field[rows - 8 :]
         up = jnp.where(row == rows - 1, 0.0, pltpu.roll(field, rows - 1, 0))
@@ -52,21 +63,30 @@
     x_ref[2 * rows :] = third.astype(BF16)
 
 
-def interior(velocity, metric):
+def interior(pos, velocity, metric):
     _, rows, cols = velocity.shape
+    hbm = pl.BlockSpec(memory_space=pltpu.HBM)
     return pl.pallas_call(
         interior_kernel,
         out_shape=(
             jax.ShapeDtypeStruct((3 * rows, cols), BF16),
+            jax.ShapeDtypeStruct((rows, 1), F32),
+            jax.ShapeDtypeStruct((8, cols), F32),
+            jax.ShapeDtypeStruct((8, cols), F32),
             jax.ShapeDtypeStruct((3, 8, cols), F32),
             jax.ShapeDtypeStruct((3, 8, cols), F32),
         ),
-        in_specs=[VMEM] * 2,
-        out_specs=(VMEM,) * 3,
-        compiler_params=params(),
+        in_specs=[SMEM, hbm, hbm],
+        out_specs=(VMEM,) * 6,
+        scratch_shapes=[
+            pltpu.VMEM((3, rows, cols), BF16),
+            pltpu.VMEM((rows,), F32),
+            pltpu.SemaphoreType.DMA((4,)),
+        ],
+        compiler_params=params(60),
         cost_estimate=cost(30 * rows * cols, 12 * rows * cols),
         name="interior",
-    )(velocity, metric)
+    )(pos, velocity, metric)
 
 
 def panel_kernel(pos_ref, x_in_ref, head_ref, tail_ref, near_ref, far_ref, met_ref, x_ref, xt_ref, *g_refs):
@@ -84,8 +104,8 @@
             x_ref[span] = jnp.where(row == at, value, kept).astype(BF16)
 
     x_ref[...] = x_in_ref[...]
-    lo = [jnp.where(even, far_ref[k].astype(F32), near_ref[k].astype(F32)) for k in range(3)]
-    hi = [jnp.where(even, near_ref[k].astype(F32), far_ref[k].astype(F32)) for k in range(3)]
+    lo = [jnp.where(even, far_ref[k : k + 1], near_ref[k : k + 1]) for k in range(3)]
+    hi = [jnp.where(even, near_ref[k : k + 1], far_ref[k : k + 1]) for k in range(3)]
     low = met_ref[0:1]
     edge(0, lambda k: low * (head_ref[k, 1:2] - lo[k]) * 0.5, [head_ref[k, 0:1] for k in range(2)], 0)
     high = met_ref[rows - 1 : rows]
@@ -121,8 +141,7 @@
     )(pos, x, head, tail, near, far, metric)
 
 
-def gather_kernel(pos_ref, mine_ref, theirs_ref, x_in_ref, near_in_ref, g_ref, x_ref, near_ref):
-    del x_in_ref, near_in_ref, x_ref, near_ref
+def gather_kernel(pos_ref, mine_ref, theirs_ref, g_ref):
     half = mine_ref.shape[1]
     even = pos_ref[2] == 0
     first = jnp.where(even, mine_ref[...], theirs_ref[...])
@@ -134,22 +153,28 @@
     g_ref[0:half, half:] = across.T
 
 
-def gather_gram(pos, mine, theirs, x, near):
+def gather_gram(pos, mine, theirs):
     n = 2 * mine.shape[1]
+    return pl.pallas_call(
+        gather_kernel,
+        out_shape=jax.ShapeDtypeStruct((n, n), F32),
+        in_specs=[SMEM, VMEM, VMEM],
+        out_specs=VMEM,
+        compiler_params=params(),
+        name="gather",
+    )(pos, mine, theirs)
+
+
+def passed(value, after):
     anywhere = pl.BlockSpec(memory_space=pl.ANY)
     return pl.pallas_call(
-        gather_kernel,
-        out_shape=(
-            jax.ShapeDtypeStruct((n, n), F32),
-            jax.ShapeDtypeStruct(x.shape, x.dtype),
-            jax.ShapeDtypeStruct(near.shape, near.dtype),
-        ),
-        in_specs=[SMEM, VMEM, VMEM, anywhere, anywhere],
-        out_specs=(VMEM, anywhere, anywhere),
-        input_output_aliases={3: 1, 4: 2},
-        compiler_params=params(),
-        name="gather",
-    )(pos, mine, theirs, x, near)
+        lambda *refs: None,
+        out_shape=jax.ShapeDtypeStruct(value.shape, value.dtype),
+        in_specs=[anywhere, anywhere],
+        out_specs=anywhere,
+        input_output_aliases={0: 0},
+        name="passed",
+    )(value, after)
 
 
 def leaf_inverse(block):
@@ -234,96 +259,89 @@
     return factor_part(0, gram.shape[0] // LEAF, (gram,))[1]
 
 
-def blocks_kernel(pos_ref, after_ref, xt_ref, near_ref, far_ref, swap_ref, *outs):
+def core_of(chip, group, count):
+    behind = (group - chip + count) % count
+    return jnp.where((behind == 1) | ((behind == 2) & (group > chip)), 0, 1)
+
+
+def blocks_kernel(pos_ref, after_ref, xt_ref, near_ref, far_ref, *outs):
     del after_ref
     chip, group, core = pos_ref[0], pos_ref[1], pos_ref[2]
     count = len(outs)
-
-    def store(block, owner):
-        for m in range(count):
-
-            @pl.when(jnp.bitwise_xor(chip, m) == owner)
-            def _(m=m):
-                outs[m][...] = block
-
     for r, panel_ref in ((1, near_ref), (2, far_ref)):
-        owner = group + jnp.where(core == 0, -r, r)
-
-        @pl.when((owner >= 0) & (owner < count))
+        owner = (group + jnp.where(core == 0, count - r, r)) % count
+
+        @pl.when((r == 1) | (core_of(owner, group, count) == core))
         def _(panel_ref=panel_ref, owner=owner):
-            store(jnp.dot(xt_ref[...], panel_ref[...], preferred_element_type=F32), owner)
-
-    @pl.when(group == jnp.where(core == 0, 2, 1))
-    def _():
-        dims = (((0,), (0,)), ((), ()))
-        store(lax.dot_general(swap_ref[...], far_ref[...], dims, preferred_element_type=F32), group)
-
-
-def blocks(pos, after, xt, near, far, swap, count):
+            block = jnp.dot(xt_ref[...], panel_ref[...], preferred_element_type=F32)
+            for m in range(count):
+
+                @pl.when(jnp.bitwise_xor(chip, m) == owner)
+                def _(m=m):
+                    outs[m][...] = block
+
+
+def blocks(pos, after, xt, near, far, count):
     n = xt.shape[0]
     return pl.pallas_call(
         blocks_kernel,
         out_shape=(jax.ShapeDtypeStruct((n, n), F32),) * count,
-        in_specs=[SMEM, pl.BlockSpec(memory_space=pl.ANY)] + [VMEM] * 4,
+        in_specs=[SMEM, pl.BlockSpec(memory_space=pl.ANY)] + [VMEM] * 3,
         out_specs=(VMEM,) * count,
         compiler_params=params(),
-        cost_estimate=cost(2 * 3 * n * n * xt.shape[1], 4 * count * n * n),
+        cost_estimate=cost(2 * 2 * n * n * xt.shape[1], 4 * count * n * n),
         name="blocks",
-    )(pos, after, xt, near, far, swap)
-
-
-def total_kernel(after_ref, *refs):
-    del after_ref
+    )(pos, after, xt, near, far)
+
+
+def total_kernel(*refs):
     value = refs[0][...]
     for ref in refs[1:-1]:
         value = value + ref[...]
     refs[-1][...] = value
 
 
-def total(after, parts):
+def total(parts):
     n = parts[0].shape[0]
     return pl.pallas_call(
         total_kernel,
         out_shape=jax.ShapeDtypeStruct((n, n), F32),
-        in_specs=[pl.BlockSpec(memory_space=pl.ANY)] + [VMEM] * len(parts),
+        in_specs=[VMEM] * len(parts),
         out_specs=VMEM,
         compiler_params=params(),
         name="total",
-    )(after, *parts)
-
-
-def merge_kernel(pos_ref, after_ref, own_ref, moved_ref, cross_ref, mine_ref, sib_ref, top_ref, t_ref):
-    del after_ref
+    )(*parts)
+
+
+def merge_kernel(pos_ref, own_ref, cross_ref, mine_ref, sib_ref, top_ref, t_ref):
     n = own_ref.shape[0]
     half = n // 2
-    moved = jnp.abs(pos_ref[0] - pos_ref[1]) == 3
-    own = jnp.where(moved, moved_ref[...], own_ref[...])
-    t_ref[0:n] = own.T + cross_ref[...]
+    t_ref[0:n] = own_ref[...].T + cross_ref[...]
     core = pos_ref[2]
     top_ref[...] = t_ref[0:8]
     mine_ref[...] = t_ref[pl.ds(pl.multiple_of(core * half, 8), half + 8)]
     sib_ref[...] = t_ref[pl.ds(pl.multiple_of((1 - core) * half, 8), half + 8)]
 
 
-def merge(pos, after, own, moved, cross):
+def merge(pos, own, cross):
     n = own.shape[0]
     half = n // 2
     return pl.pallas_call(
         merge_kernel,
         out_shape=tuple(jax.ShapeDtypeStruct((r, n), F32) for r in (half + 8, half + 8, 8)),
-        in_specs=[SMEM, pl.BlockSpec(memory_space=pl.ANY)] + [VMEM] * 3,
+        in_specs=[SMEM] + [VMEM] * 2,
         out_specs=(VMEM,) * 3,
         scratch_shapes=[pltpu.VMEM((n + 8, n), F32)],
         compiler_params=params(),
         name="merge",
-    )(pos, after, own, moved, cross)
+    )(pos, own, cross)
 
 
 def tiles_kernel(pos_ref, w_ref, g_ref, own_ref, sib_ref, top_ref, out_ref, p_ref):
     chip, group, core, count = pos_ref[0], pos_ref[1], pos_ref[2], pos_ref[3]
     half = out_ref.shape[1]
     following = jnp.where(chip + 1 == count, 0, chip + 1)
-    owner = jnp.where(chip < group, 0, 1)
+    owner = core_of(chip, group, count)
 
     @pl.when(chip == group)
     def _():
@@ -361,14 +379,13 @@
     space, group = lax.axis_index("space"), lax.axis_index("tm")
     odd = space % 2
     pos = jnp.stack([space // 2, group, odd, lax.axis_size("tm")]).astype(jnp.int32)
-    head, tail = velocity[:, :1], velocity[:, -1:]
+    x, column, inward, outward, head, tail = interior(pos, velocity, metric)
     inside = [(i, i ^ 1) for i in range(count)]
     outside = [(i, i + 1) for i in range(1, count - 1, 2)]
     outside += [(j, i) for i, j in outside]
-    far = lax.ppermute(jnp.where(odd == 0, head, tail), "space", outside)
-    near = lax.ppermute(jnp.where(odd == 0, tail, head), "space", inside)
-    column = metric.reshape(-1, 1)
-    return pos, panel(pos, interior(velocity, column), near, far, column, packed)
+    far = lax.ppermute(outward, "space", outside)
+    near = lax.ppermute(inward, "space", inside)
+    return pos, panel(pos, (x, head, tail), near, far, column, packed)
 
 
 def paired_body(velocity, metric):
@@ -385,11 +402,11 @@
 
     pos, (x, xt, away, mine) = start(velocity, metric, True)
 
-    def hops(group_pairs):
-        pairs = [(at(k, z, 0), at(k, t, 0)) for k in every for z, t in group_pairs]
-        return pairs + [(at(k, 3 - z, 1), at(k, 3 - t, 1)) for k in every for z, t in group_pairs]
-
-    near = send(x, hops([(0, 1), (1, 2), (2, 3)]))
+    def hops(sources):
+        pairs = [(at(k, z, 0), at(k, (z + 1) % groups, 0)) for k in every for z in sources]
+        return pairs + [(at(k, 3 - z, 1), at(k, (2 - z) % groups, 1)) for k in every for z in sources]
+
+    near = send(x, hops(every))
 
     siblings = [(at(k, z, c), at(k, z, 1 - c)) for k in every for z in every for c in cores]
     mine = mine + send(away, siblings)
@@ -399,26 +416,22 @@
     ]
     for other in others:
         mine = mine + other
-    gram, x, near = gather_gram(pos, mine, send(mine, siblings), x, near)
-    state = factor_part(0, 2, (gram,))
-
-    far = send(near, hops([(1, 2), (2, 3)]))
-    swap = send(x, hops([(3, 2)]))
-    parts = list(blocks(pos, state[0], xt, near, far, swap, groups))
-    state = factor_part(2, 1, state, (parts[0],))
-
-    owners = {(k, z): (k, z, 0 if k < z else 1) for k in every for z in every if k != z}
-    owners[0, 3] = (2, 2, 0)
-    owners[3, 0] = (1, 1, 1)
+    gram = gather_gram(pos, mine, send(mine, siblings))
+    state = factor_part(0, 1, (gram,))
+    near = passed(near, state[0])
+    far = send(near, hops((1, 2)))
+    w = factor_part(1, 3, state)[1]
+    parts = list(blocks(pos, w, xt, near, far, groups))
+
+    def holder(k, z):
+        return 0 if (z - k) % groups == 1 or z - k == 2 else 1
+
+    homes = {(k, z): (k, z, holder(k, z)) for k in every for z in every if k != z}
     for m in range(1, groups):
-        parts[m] = send(parts[m], [(at(k ^ m, z, c), at(k, z, c)) for k, z, c in owners.values()])
-    own = total(state[0], parts)
-    w = factor_part(3, 1, state, (own,))[1]
-
-    homes = {(k, z): (k, z, 0 if k < z else 1) for k, z in owners}
-    cross = send(own, [(at(*o), at(*homes[z, k])) for (k, z), o in owners.items()])
-    moved = send(own, [(at(*owners[p]), at(*homes[p])) for p in ((0, 3), (3, 0))])
-    mine, sib, top = merge(pos, w, own, moved, cross)
+        parts[m] = send(parts[m], [(at(k ^ m, z, c), at(k, z, c)) for k, z, c in homes.values()])
+    own = total(parts)
+    cross = send(own, [(at(*home), at(*homes[z, k])) for (k, z), home in homes.items()])
+    mine, sib, top = merge(pos, own, cross)
     sib = send(sib, [(at(k, z, c), at(k, z, 1 - c)) for k, z, c in homes.values()])
     top = send(top, [(at(k, z, c), at((k - 1) % groups, z, 1)) for k, z, c in homes.values()])
     return tiles(pos, w, gram, (mine, sib, top))

time: 71.8 us -> 82.7 us (1.15)
  the two profiles are of different devices: /device:TPU:17 before, /device:TPU:3 now
where the time goes in v6:
time: 82.7 us; the launch traced here: 82.2 us
  waiting for transfers between devices  30 us (36%)
  starting transfers between devices  24.6 us (30%)
  Pallas kernels  20 us (24%)
  local copies, waits for them, and re-layouts  6.74 us (8%)
    ppermute x13, waiting for transfers between devices, send(): return lax.ppermute(value, axes, pairs)  27 us
    ppermute x13, starting transfers between devices, send(): return lax.ppermute(value, axes, pairs)  20.9 us
    pallas_call x2, Pallas kernels, factor_part(): pl.pallas_call(kernel, out_shape=(jax.ShapeDtypeStruct((n, n), F32),) * 2...  11.8 us
    unnamed x18, local copies, waits for them, and re-layouts  6.74 us
    ppermute x1, waiting for transfers between devices, start(): far = lax.ppermute(outward, 'space', outside)  3.03 us
    ppermute x1, starting transfers between devices, start(): far = lax.ppermute(outward, 'space', outside)  3.02 us
    pallas_call x1, Pallas kernels, interior(): pl.pallas_call(interior_kernel, out_shape=(jax.ShapeDtypeStruct((3 * rows...  2.94 us
  transfers between devices with their start and end apart: 15, of which 10 were waited for; matrix products, arithmetic and copies ran while one was open for 0% of the time, Pallas kernels for 15%

profile of v6, /device:TPU:3, one launch (start us, length us, event | category | flops | bytes accessed | tf_op | source)
XLA Modules:
  0.0 82.2 jit_solution(10933708927139085124)
XLA Ops:
  0.7 2.9 %interior.1 = (bf16[1152,256]{1,0:T(8,128)(2,1)}, f32[384,1]{1,0:T(8,128)}, f32[8,256]{1,0:T(8,128)}, f32[8,256]{1,0:T(8,128)}, f32[3,8,256]{2,1,0:T(8,128)}, /*index=5*/f32[3,8,256]{2,1,0:T(8,128)}) custom-call(s32[4]{0:T(128)} %pad_add_fusion.pos_ref, bf16[3,384,256]{2,1,0:T(8,128)(2,1)} %vel_hbm.1, f32[384]{0:T(512)} %met_hbm.1), custom_call_target="tpu_custom_call" | custom-call | flops 2949120 | bytes 1179648 | tf_op jit(solution)/shard_map/interior/pallas_call | solution.py:69
  3.6 0.7 collective-permute-start
  4.3 3.0 %collective-permute-start.1 = (f32[8,256]{1,0:T(8,128)}, f32[8,256]{1,0:T(8,128)S(1)}, u32[]{:S(2)}, u32[]{:S(2)}) collective-permute-start(f32[8,256]{1,0:T(8,128)} %get-tuple-element.29), channel_id=1, source_target_pairs={{4,8},{12,16},{20,24},{8,4},{16,12},{24,20},{5,9},{13,17},{21,25},... | collective-permute-start | bytes 24584 | tf_op jit(solution)/shard_map/ppermute | solution.py:386
  7.4 3.0 %collective-permute-done.1.far_ref = f32[8,256]{1,0:T(8,128)S(1)} collective-permute-done((f32[8,256]{1,0:T(8,128)}, f32[8,256]{1,0:T(8,128)S(1)}, u32[]{:S(2)}, u32[]{:S(2)}) %collective-permute-start.1) | collective-permute-done | bytes 8224 | tf_op jit(solution)/shard_map/ppermute | solution.py:386
  11.1 1.1 %copy-done.4 = bf16[1152,256]{1,0:T(8,128)(2,1)S(1)} copy-done((bf16[1152,256]{1,0:T(8,128)(2,1)S(1)}, bf16[1152,256]{1,0:T(8,128)(2,1)}, u32[]{:S(2)}) %copy-start.4) | copy-done | bytes 589848
  12.1 0.9 %copy-done.5 = f32[384,1]{1,0:T(8,128)S(1)} copy-done((f32[384,1]{1,0:T(8,128)S(1)}, f32[384,1]{1,0:T(8,128)}, u32[]{:S(2)}) %copy-start.5) | copy-done | bytes 1560
  14.5 1.0 %panel.1 = (bf16[1152,256]{1,0:T(8,128)(2,1)S(1)}, bf16[256,1152]{1,0:T(8,128)(2,1)S(1)}, f32[192,128]{1,0:T(8,128)S(1)}, f32[192,128]{1,0:T(8,128)S(1)}) custom-call(s32[4]{0:T(128)S(1)} %copy-done.6, bf16[1152,256]{1,0:T(8,128)(2,1)S(1)} %copy-done.4, f32[3,8,256]{2,1,0:T(8,128)S(1)} %copy-done.7, f32[3,8,256]{2,1,0:T(8,128)S(1)} %copy-done.8, ...), custom_call_target="tpu_custom_call" | custom-call | flops 150994944 | bytes 1769472 | tf_op jit(solution)/shard_map/panel/pallas_call | solution.py:132
  15.5 3.4 %collective-permute-start.7 = (bf16[1152,256]{1,0:T(8,128)(2,1)S(1)}, bf16[1152,256]{1,0:T(8,128)(2,1)S(1)}, u32[]{:S(2)}, u32[]{:S(2)}) collective-permute-start(bf16[1152,256]{1,0:T(8,128)(2,1)S(1)} %get-tuple-element.37), channel_id=1, source_target_pairs={{0,1},{1,2},{2,3},{3,0},{8,9},{9,10},{10,11},{11,8},{16,17},{17,18... | collective-permute-start | bytes 1769480 | tf_op jit(solution)/shard_map/ppermute | solution.py:401
  18.9 1.3 %collective-permute-done.2 = f32[192,128]{1,0:T(8,128)S(1)} collective-permute-done((f32[192,128]{1,0:T(8,128)S(1)}, f32[192,128]{1,0:T(8,128)S(1)}, u32[]{:S(2)}, u32[]{:S(2)}) %collective-permute-start.2) | collective-permute-done | bytes 98336 | tf_op jit(solution)/shard_map/ppermute | solution.py:401
  20.9 2.0 %collective-permute-start.3 = (f32[192,128]{1,0:T(8,128)S(1)}, f32[192,128]{1,0:T(8,128)S(1)}, u32[]{:S(2)}, u32[]{:S(2)}) collective-permute-start(f32[192,128]{1,0:T(8,128)S(1)} %add.18), channel_id=1, source_target_pairs={{0,8},{4,12},{1,9},{5,13},{2,10},{6,14},{3,11},{7,15},{8,0},{12,4}... | collective-permute-start | bytes 294920 | tf_op jit(solution)/shard_map/ppermute | solution.py:401
  22.9 2.5 %collective-permute-done.5 = f32[192,128]{1,0:T(8,128)S(1)} collective-permute-done((f32[192,128]{1,0:T(8,128)S(1)}, f32[192,128]{1,0:T(8,128)S(1)}, u32[]{:S(2)}, u32[]{:S(2)}) %collective-permute-start.5) | collective-permute-done | bytes 98336 | tf_op jit(solution)/shard_map/ppermute | solution.py:401
  25.5 2.0 %collective-permute-done.4 = f32[192,128]{1,0:T(8,128)S(1)} collective-permute-done((f32[192,128]{1,0:T(8,128)S(1)}, f32[192,128]{1,0:T(8,128)S(1)}, u32[]{:S(2)}, u32[]{:S(2)}) %collective-permute-start.4) | collective-permute-done | bytes 98336 | tf_op jit(solution)/shard_map/ppermute | solution.py:401
  27.5 0.8 %collective-permute-start.6 = (f32[192,128]{1,0:T(8,128)S(1)}, f32[192,128]{1,0:T(8,128)S(1)}, u32[]{:S(2)}, u32[]{:S(2)}) collective-permute-start(f32[192,128]{1,0:T(8,128)S(1)} %add_add_fusion.mine_ref), channel_id=1, source_target_pairs={{0,4},{4,0},{1,5},{5,1},{2,6},{6,2},{3,7},{7,3},{8,12},{12,8},{9,1... | collective-permute-start | bytes 294920 | tf_op jit(solution)/shard_map/ppermute | solution.py:401
  28.3 0.9 %collective-permute-done.6.theirs_ref = f32[192,128]{1,0:T(8,128)S(1)} collective-permute-done((f32[192,128]{1,0:T(8,128)S(1)}, f32[192,128]{1,0:T(8,128)S(1)}, u32[]{:S(2)}, u32[]{:S(2)}) %collective-permute-start.6) | collective-permute-done | bytes 98336 | tf_op jit(solution)/shard_map/ppermute | solution.py:401
  29.9 3.0 %factor.2 = (f32[256,256]{1,0:T(8,128)S(1)}, f32[256,256]{1,0:T(8,128)S(1)}) custom-call(f32[256,256]{1,0:T(8,128)S(1)} %gather.1.refs_0_.g_ref), custom_call_target="tpu_custom_call" | custom-call | flops 33554432 | bytes 524288 | tf_op jit(solution)/shard_map/factor/pallas_call | solution.py:247
  33.6 0.8 %copy-done = bf16[1152,256]{1,0:T(8,128)(2,1)} copy-done((bf16[1152,256]{1,0:T(8,128)(2,1)}, bf16[1152,256]{1,0:T(8,128)(2,1)S(1)}, u32[]{:S(2)}) %copy-start) | copy-done | bytes 589848
  34.5 1.4 %collective-permute-start.8 = (bf16[1152,256]{1,0:T(8,128)(2,1)}, bf16[1152,256]{1,0:T(8,128)(2,1)S(1)}, u32[]{:S(2)}, u32[]{:S(2)}) collective-permute-start(bf16[1152,256]{1,0:T(8,128)(2,1)} %passed.1.near_ref), channel_id=1, source_target_pairs={{1,2},{2,3},{9,10},{10,11},{17,18},{18,19},{25,26},{26,27},{6,5},{... | collective-permute-start | bytes 1769480 | tf_op jit(solution)/shard_map/ppermute | solution.py:401
  35.9 8.8 %factor.3 = (f32[256,256]{1,0:T(8,128)}, f32[256,256]{1,0:T(8,128)S(1)}) custom-call(f32[256,256]{1,0:T(8,128)S(1)} %copy-done.3, f32[256,256]{1,0:T(8,128)S(1)} %get-tuple-element.34.refs_1_), custom_call_target="tpu_custom_call" | custom-call | flops 33554432 | bytes 524288 | tf_op jit(solution)/shard_map/factor/pallas_call | solution.py:247
  44.7 0.8 collective-permute-done.8.far_ref
  45.4 1.1 %copy-done.1 = bf16[1152,256]{1,0:T(8,128)(2,1)S(1)} copy-done((bf16[1152,256]{1,0:T(8,128)(2,1)S(1)}, bf16[1152,256]{1,0:T(8,128)(2,1)}, u32[]{:S(2)}) %copy-start.1) | copy-done | bytes 589848
  46.5 1.3 %blocks.1 = (f32[256,256]{1,0:T(8,128)S(1)}, f32[256,256]{1,0:T(8,128)S(1)}, f32[256,256]{1,0:T(8,128)S(1)}, f32[256,256]{1,0:T(8,128)S(1)}) custom-call(s32[4]{0:T(128)S(1)} %copy-done.6, f32[256,256]{1,0:T(8,128)S(1)} %get-tuple-element.35.after_ref.w_ref, bf16[256,1152]{1,0:T(8,128)(2,1)S(1)} %get-tuple-element.36.xt_ref, ...), custom_call_target="tpu_custom_call" | custom-call | flops 301989888 | bytes 1048576 | tf_op jit(solution)/shard_map/blocks/pallas_call | solution.py:286
  47.8 1.3 %collective-permute-start.9 = (f32[256,256]{1,0:T(8,128)S(1)}, f32[256,256]{1,0:T(8,128)S(1)}, u32[]{:S(2)}, u32[]{:S(2)}) collective-permute-start(f32[256,256]{1,0:T(8,128)S(1)} %get-tuple-element.39), channel_id=1, source_target_pairs={{9,1},{10,2},{15,7},{4,12},{2,10},{3,11},{28,20},{29,21},{27,19},{... | collective-permute-start | bytes 786440 | tf_op jit(solution)/shard_map/ppermute | solution.py:401
  49.1 1.3 %collective-permute-start.10 = (f32[256,256]{1,0:T(8,128)S(1)}, f32[256,256]{1,0:T(8,128)S(1)}, u32[]{:S(2)}, u32[]{:S(2)}) collective-permute-start(f32[256,256]{1,0:T(8,128)S(1)} %get-tuple-element.40), channel_id=1, source_target_pairs={{17,1},{18,2},{23,7},{28,12},{26,10},{27,11},{4,20},{5,21},{3,19},... | collective-permute-start | bytes 786440 | tf_op jit(solution)/shard_map/ppermute | solution.py:401
  50.4 2.8 %collective-permute-start.11 = (f32[256,256]{1,0:T(8,128)S(1)}, f32[256,256]{1,0:T(8,128)S(1)}, u32[]{:S(2)}, u32[]{:S(2)}) collective-permute-start(f32[256,256]{1,0:T(8,128)S(1)} %get-tuple-element.41), channel_id=1, source_target_pairs={{25,1},{26,2},{31,7},{20,12},{18,10},{19,11},{12,20},{13,21},{11,1... | collective-permute-start | bytes 786440 | tf_op jit(solution)/shard_map/ppermute | solution.py:401
  53.2 2.3 %collective-permute-done.9.refs_1_ = f32[256,256]{1,0:T(8,128)S(1)} collective-permute-done((f32[256,256]{1,0:T(8,128)S(1)}, f32[256,256]{1,0:T(8,128)S(1)}, u32[]{:S(2)}, u32[]{:S(2)}) %collective-permute-start.9) | collective-permute-done | bytes 262176 | tf_op jit(solution)/shard_map/ppermute | solution.py:401
  55.5 3.5 %collective-permute-done.10.refs_2_ = f32[256,256]{1,0:T(8,128)S(1)} collective-permute-done((f32[256,256]{1,0:T(8,128)S(1)}, f32[256,256]{1,0:T(8,128)S(1)}, u32[]{:S(2)}, u32[]{:S(2)}) %collective-permute-start.10) | collective-permute-done | bytes 262176 | tf_op jit(solution)/shard_map/ppermute | solution.py:401
  59.1 4.0 %collective-permute-start.12 = (f32[256,256]{1,0:T(8,128)S(1)}, f32[256,256]{1,0:T(8,128)S(1)}, u32[]{:S(2)}, u32[]{:S(2)}) collective-permute-start(f32[256,256]{1,0:T(8,128)S(1)} %total.1.own_ref), channel_id=1, source_target_pairs={{1,12},{2,20},{7,24},{12,1},{10,21},{11,29},{20,2},{21,10},{19,30}... | collective-permute-start | bytes 786440 | tf_op jit(solution)/shard_map/ppermute | solution.py:401
  63.0 10.2 %collective-permute-done.12.cross_ref = f32[256,256]{1,0:T(8,128)S(1)} collective-permute-done((f32[256,256]{1,0:T(8,128)S(1)}, f32[256,256]{1,0:T(8,128)S(1)}, u32[]{:S(2)}, u32[]{:S(2)}) %collective-permute-start.12) | collective-permute-done | bytes 262176 | tf_op jit(solution)/shard_map/ppermute | solution.py:401
  74.0 1.3 %collective-permute-start.13 = (f32[136,256]{1,0:T(8,128)S(1)}, f32[136,256]{1,0:T(8,128)S(1)}, u32[]{:S(2)}, u32[]{:S(2)}) collective-permute-start(f32[136,256]{1,0:T(8,128)S(1)} %get-tuple-element.43), channel_id=1, source_target_pairs={{1,5},{2,6},{7,3},{12,8},{10,14},{11,15},{20,16},{21,17},{19,23},{... | collective-permute-start | bytes 417800 | tf_op jit(solution)/shard_map/ppermute | solution.py:401
  75.3 1.9 %collective-permute-start.14 = (f32[8,256]{1,0:T(8,128)S(1)}, f32[8,256]{1,0:T(8,128)S(1)}, u32[]{:S(2)}, u32[]{:S(2)}) collective-permute-start(f32[8,256]{1,0:T(8,128)S(1)} %get-tuple-element.44), channel_id=1, source_target_pairs={{1,29},{2,30},{7,31},{12,4},{10,6},{11,7},{20,12},{21,13},{19,15},... | collective-permute-start | bytes 24584 | tf_op jit(solution)/shard_map/ppermute | solution.py:401
  77.2 3.4 %collective-permute-done.14.top_ref = f32[8,256]{1,0:T(8,128)S(1)} collective-permute-done((f32[8,256]{1,0:T(8,128)S(1)}, f32[8,256]{1,0:T(8,128)S(1)}, u32[]{:S(2)}, u32[]{:S(2)}) %collective-permute-start.14) | collective-permute-done | bytes 8224 | tf_op jit(solution)/shard_map/ppermute | solution.py:401
  80.6 1.6 %tiles.1 = f32[256,128]{1,0:T(8,128)} custom-call(s32[4]{0:T(128)S(1)} %copy-done.6, f32[256,256]{1,0:T(8,128)S(1)} %get-tuple-element.35.after_ref.w_ref, f32[256,256]{1,0:T(8,128)S(1)} %gather.1.refs_0_.g_ref, f32[136,256]{1,0:T(8,128)S(1)} %get-tuple-element.42.own_ref, f32[136,256]{1,0:T(8,128)S(1)} %collective-permute-done.13.sib_ref, ...), custom_call_target="tpu_custom_call" | custom-call | tf_op jit(solution)/shard_map/tiles/pallas_call | solution.py:366
  (29 shorter events, 5.6 us)
Async XLA Ops:
  3.6 3.8 %collective-permute-start = (f32[8,256]{1,0:T(8,128)}, f32[8,256]{1,0:T(8,128)S(1)}, u32[]{:S(2)}, u32[]{:S(2)}) collective-permute-start(f32[8,256]{1,0:T(8,128)} %get-tuple-element.28), channel_id=1, source_target_pairs={{0,4},{4,0},{8,12},{12,8},{16,20},{20,16},{24,28},{28,24},{1,5},{5... | collective-permute-start | bytes 24584 | tf_op jit(solution)/shard_map/ppermute | solution.py:387
  4.3 6.1 %collective-permute-start.1 = (f32[8,256]{1,0:T(8,128)}, f32[8,256]{1,0:T(8,128)S(1)}, u32[]{:S(2)}, u32[]{:S(2)}) collective-permute-start(f32[8,256]{1,0:T(8,128)} %get-tuple-element.29), channel_id=1, source_target_pairs={{4,8},{12,16},{20,24},{8,4},{16,12},{24,20},{5,9},{13,17},{21,25},... | collective-permute-start | bytes 24584 | tf_op jit(solution)/shard_map/ppermute | solution.py:386
  10.4 0.7 copy-start.6
  11.1 1.1 %copy-start.4 = (bf16[1152,256]{1,0:T(8,128)(2,1)S(1)}, bf16[1152,256]{1,0:T(8,128)(2,1)}, u32[]{:S(2)}) copy-start(bf16[1152,256]{1,0:T(8,128)(2,1)} %get-tuple-element.25.x_in_ref) | copy-start | bytes 1769476
  12.1 0.9 %copy-start.5 = (f32[384,1]{1,0:T(8,128)S(1)}, f32[384,1]{1,0:T(8,128)}, u32[]{:S(2)}) copy-start(f32[384,1]{1,0:T(8,128)} %get-tuple-element.30.met_ref) | copy-start | bytes 4612
  13.1 0.7 copy-start.7
  13.8 0.7 copy-start.8
  15.5 18.1 %collective-permute-start.7 = (bf16[1152,256]{1,0:T(8,128)(2,1)S(1)}, bf16[1152,256]{1,0:T(8,128)(2,1)S(1)}, u32[]{:S(2)}, u32[]{:S(2)}) collective-permute-start(bf16[1152,256]{1,0:T(8,128)(2,1)S(1)} %get-tuple-element.37), channel_id=1, source_target_pairs={{0,1},{1,2},{2,3},{3,0},{8,9},{9,10},{10,11},{11,8},{16,17},{17,18... | collective-permute-start | bytes 1769480 | tf_op jit(solution)/shard_map/ppermute | solution.py:401
  18.9 1.3 %collective-permute-start.2 = (f32[192,128]{1,0:T(8,128)S(1)}, f32[192,128]{1,0:T(8,128)S(1)}, u32[]{:S(2)}, u32[]{:S(2)}) collective-permute-start(f32[192,128]{1,0:T(8,128)S(1)} %get-tuple-element.32), channel_id=1, source_target_pairs={{0,4},{4,0},{1,5},{5,1},{2,6},{6,2},{3,7},{7,3},{8,12},{12,8},{9,1... | collective-permute-start | bytes 294920 | tf_op jit(solution)/shard_map/ppermute | solution.py:401
  20.2 5.3 %collective-permute-start.5 = (f32[192,128]{1,0:T(8,128)S(1)}, f32[192,128]{1,0:T(8,128)S(1)}, u32[]{:S(2)}, u32[]{:S(2)}) collective-permute-start(f32[192,128]{1,0:T(8,128)S(1)} %add.18), channel_id=1, source_target_pairs={{0,24},{4,28},{1,25},{5,29},{2,26},{6,30},{3,27},{7,31},{8,16},{12... | collective-permute-start | bytes 294920 | tf_op jit(solution)/shard_map/ppermute | solution.py:401
  20.9 6.5 %collective-permute-start.4 = (f32[192,128]{1,0:T(8,128)S(1)}, f32[192,128]{1,0:T(8,128)S(1)}, u32[]{:S(2)}, u32[]{:S(2)}) collective-permute-start(f32[192,128]{1,0:T(8,128)S(1)} %add.18), channel_id=1, source_target_pairs={{0,16},{4,20},{1,17},{5,21},{2,18},{6,22},{3,19},{7,23},{8,24},{12... | collective-permute-start | bytes 294920 | tf_op jit(solution)/shard_map/ppermute | solution.py:401
  20.9 6.5 %collective-permute-start.3 = (f32[192,128]{1,0:T(8,128)S(1)}, f32[192,128]{1,0:T(8,128)S(1)}, u32[]{:S(2)}, u32[]{:S(2)}) collective-permute-start(f32[192,128]{1,0:T(8,128)S(1)} %add.18), channel_id=1, source_target_pairs={{0,8},{4,12},{1,9},{5,13},{2,10},{6,14},{3,11},{7,15},{8,0},{12,4}... | collective-permute-start | bytes 294920 | tf_op jit(solution)/shard_map/ppermute | solution.py:401
  27.5 1.8 %collective-permute-start.6 = (f32[192,128]{1,0:T(8,128)S(1)}, f32[192,128]{1,0:T(8,128)S(1)}, u32[]{:S(2)}, u32[]{:S(2)}) collective-permute-start(f32[192,128]{1,0:T(8,128)S(1)} %add_add_fusion.mine_ref), channel_id=1, source_target_pairs={{0,4},{4,0},{1,5},{5,1},{2,6},{6,2},{3,7},{7,3},{8,12},{12,8},{9,1... | collective-permute-start | bytes 294920 | tf_op jit(solution)/shard_map/ppermute | solution.py:401
  32.9 0.7 copy-start.2
  33.6 0.8 %copy-start = (bf16[1152,256]{1,0:T(8,128)(2,1)}, bf16[1152,256]{1,0:T(8,128)(2,1)S(1)}, u32[]{:S(2)}) copy-start(bf16[1152,256]{1,0:T(8,128)(2,1)S(1)} %collective-permute-done.7.refs_0_) | copy-start | bytes 1769476
  34.5 1.4 %copy-start.3 = (f32[256,256]{1,0:T(8,128)S(1)}, f32[256,256]{1,0:T(8,128)}, u32[]{:S(2)}) copy-start(f32[256,256]{1,0:T(8,128)} %copy-done.2) | copy-start | bytes 786436
  34.5 11.0 %collective-permute-start.8 = (bf16[1152,256]{1,0:T(8,128)(2,1)}, bf16[1152,256]{1,0:T(8,128)(2,1)S(1)}, u32[]{:S(2)}, u32[]{:S(2)}) collective-permute-start(bf16[1152,256]{1,0:T(8,128)(2,1)} %passed.1.near_ref), channel_id=1, source_target_pairs={{1,2},{2,3},{9,10},{10,11},{17,18},{18,19},{25,26},{26,27},{6,5},{... | collective-permute-start | bytes 1769480 | tf_op jit(solution)/shard_map/ppermute | solution.py:401
  45.4 1.1 %copy-start.1 = (bf16[1152,256]{1,0:T(8,128)(2,1)S(1)}, bf16[1152,256]{1,0:T(8,128)(2,1)}, u32[]{:S(2)}) copy-start(bf16[1152,256]{1,0:T(8,128)(2,1)} %passed.1.near_ref) | copy-start | bytes 1769476
  47.8 7.7 %collective-permute-start.9 = (f32[256,256]{1,0:T(8,128)S(1)}, f32[256,256]{1,0:T(8,128)S(1)}, u32[]{:S(2)}, u32[]{:S(2)}) collective-permute-start(f32[256,256]{1,0:T(8,128)S(1)} %get-tuple-element.39), channel_id=1, source_target_pairs={{9,1},{10,2},{15,7},{4,12},{2,10},{3,11},{28,20},{29,21},{27,19},{... | collective-permute-start | bytes 786440 | tf_op jit(solution)/shard_map/ppermute | solution.py:401
  49.1 9.9 %collective-permute-start.10 = (f32[256,256]{1,0:T(8,128)S(1)}, f32[256,256]{1,0:T(8,128)S(1)}, u32[]{:S(2)}, u32[]{:S(2)}) collective-permute-start(f32[256,256]{1,0:T(8,128)S(1)} %get-tuple-element.40), channel_id=1, source_target_pairs={{17,1},{18,2},{23,7},{28,12},{26,10},{27,11},{4,20},{5,21},{3,19},... | collective-permute-start | bytes 786440 | tf_op jit(solution)/shard_map/ppermute | solution.py:401
  50.4 8.6 %collective-permute-start.11 = (f32[256,256]{1,0:T(8,128)S(1)}, f32[256,256]{1,0:T(8,128)S(1)}, u32[]{:S(2)}, u32[]{:S(2)}) collective-permute-start(f32[256,256]{1,0:T(8,128)S(1)} %get-tuple-element.41), channel_id=1, source_target_pairs={{25,1},{26,2},{31,7},{20,12},{18,10},{19,11},{12,20},{13,21},{11,1... | collective-permute-start | bytes 786440 | tf_op jit(solution)/shard_map/ppermute | solution.py:401
  59.1 14.2 %collective-permute-start.12 = (f32[256,256]{1,0:T(8,128)S(1)}, f32[256,256]{1,0:T(8,128)S(1)}, u32[]{:S(2)}, u32[]{:S(2)}) collective-permute-start(f32[256,256]{1,0:T(8,128)S(1)} %total.1.own_ref), channel_id=1, source_target_pairs={{1,12},{2,20},{7,24},{12,1},{10,21},{11,29},{20,2},{21,10},{19,30}... | collective-permute-start | bytes 786440 | tf_op jit(solution)/shard_map/ppermute | solution.py:401
  74.0 6.6 %collective-permute-start.13 = (f32[136,256]{1,0:T(8,128)S(1)}, f32[136,256]{1,0:T(8,128)S(1)}, u32[]{:S(2)}, u32[]{:S(2)}) collective-permute-start(f32[136,256]{1,0:T(8,128)S(1)} %get-tuple-element.43), channel_id=1, source_target_pairs={{1,5},{2,6},{7,3},{12,8},{10,14},{11,15},{20,16},{21,17},{19,23},{... | collective-permute-start | bytes 417800 | tf_op jit(solution)/shard_map/ppermute | solution.py:401
  75.3 5.3 %collective-permute-start.14 = (f32[8,256]{1,0:T(8,128)S(1)}, f32[8,256]{1,0:T(8,128)S(1)}, u32[]{:S(2)}, u32[]{:S(2)}) collective-permute-start(f32[8,256]{1,0:T(8,128)S(1)} %get-tuple-element.44), channel_id=1, source_target_pairs={{1,29},{2,30},{7,31},{12,4},{10,6},{11,7},{20,12},{21,13},{19,15},... | collective-permute-start | bytes 24584 | tf_op jit(solution)/shard_map/ppermute | solution.py:401

commit v7 on v6

--- a/solution.py
+++ b/solution.py
@@ -31,20 +31,14 @@
     return third + center0 * second - center1 * first
 
 
-def interior_kernel(pos_ref, vel_hbm, met_hbm, x_ref, met_ref, inside_ref, outside_ref, head_ref, tail_ref, vel_ref, row_ref, sems):
+def interior_kernel(pos_ref, vel_ref, row_ref, x_ref, met_ref, inside_ref, outside_ref, head_ref, tail_ref):
     rows, cols = vel_ref.shape[1:]
-    copies = [pltpu.make_async_copy(met_hbm, row_ref, sems.at[3])]
-    copies += [pltpu.make_async_copy(vel_hbm.at[k], vel_ref.at[k], sems.at[k]) for k in range(3)]
-    for copy in copies:
-        copy.start()
     even = pos_ref[2] == 0
     row = lax.broadcasted_iota(jnp.int32, (rows, cols), 0)
-    copies[0].wait()
     metric = jnp.broadcast_to(row_ref[...][None, :], (8, rows)).T[:, 0:1]
     met_ref[...] = metric
 
     def gradient(k):
-        copies[k + 1].wait()
         field = vel_ref[k].astype(F32)
         head, tail = field[0:1], field[rows - 1 : rows]
         inside_ref[k : k + 1] = jnp.where(even, tail, head)
@@ -65,7 +59,6 @@
 
 def interior(pos, velocity, metric):
     _, rows, cols = velocity.shape
-    hbm = pl.BlockSpec(memory_space=pltpu.HBM)
     return pl.pallas_call(
         interior_kernel,
         out_shape=(
@@ -76,14 +69,9 @@
             jax.ShapeDtypeStruct((3, 8, cols), F32),
             jax.ShapeDtypeStruct((3, 8, cols), F32),
         ),
-        in_specs=[SMEM, hbm, hbm],
+        in_specs=[SMEM, VMEM, VMEM],
         out_specs=(VMEM,) * 6,
-        scratch_shapes=[
-            pltpu.VMEM((3, rows, cols), BF16),
-            pltpu.VMEM((rows,), F32),
-            pltpu.SemaphoreType.DMA((4,)),
-        ],
-        compiler_params=params(60),
+        compiler_params=params(),
         cost_estimate=cost(30 * rows * cols, 12 * rows * cols),
         name="interior",
     )(pos, velocity, metric)
@@ -264,77 +252,73 @@
     return jnp.where((behind == 1) | ((behind == 2) & (group > chip)), 0, 1)
 
 
-def blocks_kernel(pos_ref, after_ref, xt_ref, near_ref, far_ref, *outs):
+def block_kernel(after_ref, xt_ref, panel_ref, out_ref):
     del after_ref
-    chip, group, core = pos_ref[0], pos_ref[1], pos_ref[2]
-    count = len(outs)
-    for r, panel_ref in ((1, near_ref), (2, far_ref)):
-        owner = (group + jnp.where(core == 0, count - r, r)) % count
-
-        @pl.when((r == 1) | (core_of(owner, group, count) == core))
-        def _(panel_ref=panel_ref, owner=owner):
-            block = jnp.dot(xt_ref[...], panel_ref[...], preferred_element_type=F32)
-            for m in range(count):
-
-                @pl.when(jnp.bitwise_xor(chip, m) == owner)
-                def _(m=m):
-                    outs[m][...] = block
-
-
-def blocks(pos, after, xt, near, far, count):
+    out_ref[...] = jnp.dot(xt_ref[...], panel_ref[...], preferred_element_type=F32)
+
+
+def pair_block(after, xt, panel):
     n = xt.shape[0]
     return pl.pallas_call(
-        blocks_kernel,
-        out_shape=(jax.ShapeDtypeStruct((n, n), F32),) * count,
-        in_specs=[SMEM, pl.BlockSpec(memory_space=pl.ANY)] + [VMEM] * 3,
-        out_specs=(VMEM,) * count,
-        compiler_params=params(),
-        cost_estimate=cost(2 * 2 * n * n * xt.shape[1], 4 * count * n * n),
-        name="blocks",
-    )(pos, after, xt, near, far)
-
-
-def total_kernel(*refs):
+        block_kernel,
+        out_shape=jax.ShapeDtypeStruct((n, n), F32),
+        in_specs=[pl.BlockSpec(memory_space=pl.ANY)] + [VMEM] * 2,
+        out_specs=VMEM,
+        compiler_params=params(),
+        cost_estimate=cost(2 * n * n * xt.shape[1], 4 * n * n),
+        name="block",
+    )(after, xt, panel)
+
+
+def total_kernel(after_ref, *refs):
+    del after_ref
     value = refs[0][...]
     for ref in refs[1:-1]:
         value = value + ref[...]
     refs[-1][...] = value
 
 
-def total(parts):
+def total(after, parts):
     n = parts[0].shape[0]
     return pl.pallas_call(
         total_kernel,
         out_shape=jax.ShapeDtypeStruct((n, n), F32),
-        in_specs=[VMEM] * len(parts),
+        in_specs=[pl.BlockSpec(memory_space=pl.ANY)] + [VMEM] * len(parts),
         out_specs=VMEM,
         compiler_params=params(),
         name="total",
-    )(*parts)
-
-
-def merge_kernel(pos_ref, own_ref, cross_ref, mine_ref, sib_ref, top_ref, t_ref):
-    n = own_ref.shape[0]
+    )(after, *parts)
+
+
+def merge_kernel(pos_ref, *refs):
+    sums, (mine_ref, sib_ref, top_ref, t_ref) = refs[:4], refs[4:]
+    n = t_ref.shape[0] - 8
     half = n // 2
-    t_ref[0:n] = own_ref[...].T + cross_ref[...]
-    core = pos_ref[2]
+    chip, group, core = pos_ref[0], pos_ref[1], pos_ref[2]
+
+    def put(own_ref, cross_ref):
+        t_ref[0:n] = own_ref[...].T + cross_ref[...]
+
+    distant = jnp.abs(chip - group) == 2
+    pl.when(jnp.logical_not(distant))(lambda: put(*sums[:2]))
+    pl.when(distant)(lambda: put(*sums[2:]))
     top_ref[...] = t_ref[0:8]
     mine_ref[...] = t_ref[pl.ds(pl.multiple_of(core * half, 8), half + 8)]
     sib_ref[...] = t_ref[pl.ds(pl.multiple_of((1 - core) * half, 8), half + 8)]
 
 
-def merge(pos, own, cross):
-    n = own.shape[0]
+def merge(pos, near, far):
+    n = near[0].shape[0]
     half = n // 2
     return pl.pallas_call(
         merge_kernel,
         out_shape=tuple(jax.ShapeDtypeStruct((r, n), F32) for r in (half + 8, half + 8, 8)),
-        in_specs=[SMEM] + [VMEM] * 2,
+        in_specs=[SMEM] + [VMEM] * 4,
         out_specs=(VMEM,) * 3,
         scratch_shapes=[pltpu.VMEM((n + 8, n), F32)],
         compiler_params=params(),
         name="merge",
-    )(pos, own, cross)
+    )(pos, *near, *far)
 
 
 def tiles_kernel(pos_ref, w_ref, g_ref, own_ref, sib_ref, top_ref, out_ref, p_ref):
@@ -420,18 +404,32 @@
     state = factor_part(0, 1, (gram,))
     near = passed(near, state[0])
     far = send(near, hops((1, 2)))
-    w = factor_part(1, 3, state)[1]
-    parts = list(blocks(pos, w, xt, near, far, groups))
 
     def holder(k, z):
         return 0 if (z - k) % groups == 1 or z - k == 2 else 1
 
     homes = {(k, z): (k, z, holder(k, z)) for k in every for z in every if k != z}
-    for m in range(1, groups):
-        parts[m] = send(parts[m], [(at(k ^ m, z, c), at(k, z, c)) for k, z, c in homes.values()])
-    own = total(parts)
-    cross = send(own, [(at(*home), at(*homes[z, k])) for (k, z), home in homes.items()])
-    mine, sib, top = merge(pos, own, cross)
+    far_homes = {pair: home for pair, home in homes.items() if abs(pair[0] - pair[1]) == 2}
+    near_homes = {pair: home for pair, home in homes.items() if pair not in far_homes}
+
+    def gathered(block, group_homes):
+        return [block] + [
+            send(block, [(at(k ^ m, z, c), at(k, z, c)) for k, z, c in group_homes.values()]) for m in range(1, groups)
+        ]
+
+    def exchanged(own, group_homes):
+        return send(own, [(at(*home), at(*homes[z, k])) for (k, z), home in group_homes.items()])
+
+    near_block = pair_block(state[0], xt, near)
+    near_parts = gathered(near_block, near_homes)
+    w = factor_part(1, 3, state, (near_block,))[1]
+    far_block = pair_block(w, xt, far)
+    far_parts = gathered(far_block, far_homes)
+    near_own = total(far_block, near_parts)
+    near_cross = exchanged(near_own, near_homes)
+    far_own = total(far_block, far_parts)
+    far_cross = exchanged(far_own, far_homes)
+    mine, sib, top = merge(pos, (near_own, near_cross), (far_own, far_cross))
     sib = send(sib, [(at(k, z, c), at(k, z, 1 - c)) for k, z, c in homes.values()])
     top = send(top, [(at(k, z, c), at((k - 1) % groups, z, 1)) for k, z, c in homes.values()])
     return tiles(pos, w, gram, (mine, sib, top))

time: 82.7 us -> 77.3 us (0.935)
  the two profiles are of different devices: /device:TPU:3 before, /device:TPU:5 now
where the time goes in v7:
time: 77.3 us; the launch traced here: 75.9 us
  starting transfers between devices  31.6 us (41%)
  waiting for transfers between devices  22.2 us (29%)
  Pallas kernels  17.5 us (23%)
  local copies, waits for them, and re-layouts  4.27 us (6%)
    ppermute x17, starting transfers between devices, send(): return lax.ppermute(value, axes, pairs)  27.8 us
    ppermute x17, waiting for transfers between devices, send(): return lax.ppermute(value, axes, pairs)  19.9 us
    pallas_call x2, Pallas kernels, factor_part(): pl.pallas_call(kernel, out_shape=(jax.ShapeDtypeStruct((n, n), F32),) * 2...  11.8 us
    unnamed x12, local copies, waits for them, and re-layouts  4.27 us
    ppermute x1, starting transfers between devices, start(): far = lax.ppermute(outward, 'space', outside)  3.02 us
    ppermute x1, waiting for transfers between devices, start(): far = lax.ppermute(outward, 'space', outside)  2.22 us
    pallas_call x1, Pallas kernels, tiles(): pl.pallas_call(tiles_kernel, out_shape=jax.ShapeDtypeStruct((n, half), F3...  1.63 us
  transfers between devices with their start and end apart: 19, of which 10 were waited for; matrix products, arithmetic and copies ran while one was open for 0% of the time, Pallas kernels for 17%

profile of v7, /device:TPU:5, one launch (start us, length us, event | category | flops | bytes accessed | tf_op | source)
XLA Modules:
  0.0 75.9 jit_solution(12707096070900181102)
XLA Ops:
  0.7 1.1 %copy-done.4 = bf16[3,384,256]{2,1,0:T(8,128)(2,1)S(1)} copy-done((bf16[3,384,256]{2,1,0:T(8,128)(2,1)S(1)}, bf16[3,384,256]{2,1,0:T(8,128)(2,1)}, u32[]{:S(2)}) %copy-start.4) | copy-done | bytes 589848
  1.7 1.0 %interior.1 = (bf16[1152,256]{1,0:T(8,128)(2,1)S(1)}, f32[384,1]{1,0:T(8,128)S(1)}, f32[8,256]{1,0:T(8,128)S(1)}, f32[8,256]{1,0:T(8,128)S(1)}, f32[3,8,256]{2,1,0:T(8,128)S(1)}, /*index=5*/f32[3,8,256]{2,1,0:T(8,128)S(1)}) custom-call(s32[4]{0:T(128)S(1)} %pad_add_fusion.pos_ref, bf16[3,384,256]{2,1,0:T(8,128)(2,1)S(1)} %copy-done.4, f32[384]{0:T(512)S(1)} %copy-done.5), custom_call_target="tpu_custom_call" | custom-call | flops 2949120 | bytes 1179648 | tf_op jit(solution)/shard_map/interior/pallas_call | solution.py:62
  2.8 0.7 collective-permute-start
  3.5 3.0 %collective-permute-start.1 = (f32[8,256]{1,0:T(8,128)S(1)}, f32[8,256]{1,0:T(8,128)S(1)}, u32[]{:S(2)}, u32[]{:S(2)}) collective-permute-start(f32[8,256]{1,0:T(8,128)S(1)} %get-tuple-element.25), channel_id=1, source_target_pairs={{4,8},{12,16},{20,24},{8,4},{16,12},{24,20},{5,9},{13,17},{21,25},... | collective-permute-start | bytes 24584 | tf_op jit(solution)/shard_map/ppermute | solution.py:370
  6.6 2.2 %collective-permute-done.1.far_ref = f32[8,256]{1,0:T(8,128)S(1)} collective-permute-done((f32[8,256]{1,0:T(8,128)S(1)}, f32[8,256]{1,0:T(8,128)S(1)}, u32[]{:S(2)}, u32[]{:S(2)}) %collective-permute-start.1) | collective-permute-done | bytes 8224 | tf_op jit(solution)/shard_map/ppermute | solution.py:370
  8.8 1.0 %panel.1 = (bf16[1152,256]{1,0:T(8,128)(2,1)S(1)}, bf16[256,1152]{1,0:T(8,128)(2,1)S(1)}, f32[192,128]{1,0:T(8,128)S(1)}, f32[192,128]{1,0:T(8,128)S(1)}) custom-call(s32[4]{0:T(128)S(1)} %pad_add_fusion.pos_ref, bf16[1152,256]{1,0:T(8,128)(2,1)S(1)} %get-tuple-element.21.x_in_ref, f32[3,8,256]{2,1,0:T(8,128)S(1)} %get-tuple-element.22.head_ref, ...), custom_call_target="tpu_custom_call" | custom-call | flops 150994944 | bytes 1769472 | tf_op jit(solution)/shard_map/panel/pallas_call | solution.py:120
  9.8 3.4 %collective-permute-start.7 = (bf16[1152,256]{1,0:T(8,128)(2,1)S(1)}, bf16[1152,256]{1,0:T(8,128)(2,1)S(1)}, u32[]{:S(2)}, u32[]{:S(2)}) collective-permute-start(bf16[1152,256]{1,0:T(8,128)(2,1)S(1)} %get-tuple-element.32), channel_id=1, source_target_pairs={{0,1},{1,2},{2,3},{3,0},{8,9},{9,10},{10,11},{11,8},{16,17},{17,18... | collective-permute-start | bytes 1769480 | tf_op jit(solution)/shard_map/ppermute | solution.py:385
  13.2 1.3 %collective-permute-done.2 = f32[192,128]{1,0:T(8,128)S(1)} collective-permute-done((f32[192,128]{1,0:T(8,128)S(1)}, f32[192,128]{1,0:T(8,128)S(1)}, u32[]{:S(2)}, u32[]{:S(2)}) %collective-permute-start.2) | collective-permute-done | bytes 98336 | tf_op jit(solution)/shard_map/ppermute | solution.py:385
  14.6 2.0 %collective-permute-start.4 = (f32[192,128]{1,0:T(8,128)S(1)}, f32[192,128]{1,0:T(8,128)S(1)}, u32[]{:S(2)}, u32[]{:S(2)}) collective-permute-start(f32[192,128]{1,0:T(8,128)S(1)} %add.18), channel_id=1, source_target_pairs={{0,16},{4,20},{1,17},{5,21},{2,18},{6,22},{3,19},{7,23},{8,24},{12... | collective-permute-start | bytes 294920 | tf_op jit(solution)/shard_map/ppermute | solution.py:385
  17.2 1.6 %collective-permute-done.3 = f32[192,128]{1,0:T(8,128)S(1)} collective-permute-done((f32[192,128]{1,0:T(8,128)S(1)}, f32[192,128]{1,0:T(8,128)S(1)}, u32[]{:S(2)}, u32[]{:S(2)}) %collective-permute-start.3) | collective-permute-done | bytes 98336 | tf_op jit(solution)/shard_map/ppermute | solution.py:385
  19.4 1.9 %collective-permute-done.5 = f32[192,128]{1,0:T(8,128)S(1)} collective-permute-done((f32[192,128]{1,0:T(8,128)S(1)}, f32[192,128]{1,0:T(8,128)S(1)}, u32[]{:S(2)}, u32[]{:S(2)}) %collective-permute-start.5) | collective-permute-done | bytes 98336 | tf_op jit(solution)/shard_map/ppermute | solution.py:385
  21.3 1.6 %collective-permute-start.6 = (f32[192,128]{1,0:T(8,128)S(1)}, f32[192,128]{1,0:T(8,128)S(1)}, u32[]{:S(2)}, u32[]{:S(2)}) collective-permute-start(f32[192,128]{1,0:T(8,128)S(1)} %add_add_fusion.mine_ref), channel_id=1, source_target_pairs={{0,4},{4,0},{1,5},{5,1},{2,6},{6,2},{3,7},{7,3},{8,12},{12,8},{9,1... | collective-permute-start | bytes 294920 | tf_op jit(solution)/shard_map/ppermute | solution.py:385
  22.9 0.9 %collective-permute-done.6.theirs_ref = f32[192,128]{1,0:T(8,128)S(1)} collective-permute-done((f32[192,128]{1,0:T(8,128)S(1)}, f32[192,128]{1,0:T(8,128)S(1)}, u32[]{:S(2)}, u32[]{:S(2)}) %collective-permute-start.6) | collective-permute-done | bytes 98336 | tf_op jit(solution)/shard_map/ppermute | solution.py:385
  24.5 3.0 %factor.2 = (f32[256,256]{1,0:T(8,128)S(1)}, f32[256,256]{1,0:T(8,128)S(1)}) custom-call(f32[256,256]{1,0:T(8,128)S(1)} %gather.1.refs_0_.g_ref), custom_call_target="tpu_custom_call" | custom-call | flops 33554432 | bytes 524288 | tf_op jit(solution)/shard_map/factor/pallas_call | solution.py:235
  27.5 0.7 copy-done.2
  28.2 0.8 %copy-done = bf16[1152,256]{1,0:T(8,128)(2,1)} copy-done((bf16[1152,256]{1,0:T(8,128)(2,1)}, bf16[1152,256]{1,0:T(8,128)(2,1)S(1)}, u32[]{:S(2)}) %copy-start) | copy-done | bytes 589848
  29.1 1.4 %collective-permute-start.8 = (bf16[1152,256]{1,0:T(8,128)(2,1)}, bf16[1152,256]{1,0:T(8,128)(2,1)S(1)}, u32[]{:S(2)}, u32[]{:S(2)}) collective-permute-start(bf16[1152,256]{1,0:T(8,128)(2,1)} %passed.1.panel_ref), channel_id=1, source_target_pairs={{1,2},{2,3},{9,10},{10,11},{17,18},{18,19},{25,26},{26,27},{6,5},{... | collective-permute-start | bytes 1769480 | tf_op jit(solution)/shard_map/ppermute | solution.py:385
  30.5 1.1 %copy-done.1 = bf16[1152,256]{1,0:T(8,128)(2,1)S(1)} copy-done((bf16[1152,256]{1,0:T(8,128)(2,1)S(1)}, bf16[1152,256]{1,0:T(8,128)(2,1)}, u32[]{:S(2)}) %copy-start.1) | copy-done | bytes 589848
  32.6 3.4 %collective-permute-start.11 = (f32[256,256]{1,0:T(8,128)S(1)}, f32[256,256]{1,0:T(8,128)S(1)}, u32[]{:S(2)}, u32[]{:S(2)}) collective-permute-start(f32[256,256]{1,0:T(8,128)S(1)} %block.2.refs_2_.refs_0_), channel_id=1, source_target_pairs={{25,1},{31,7},{20,12},{18,10},{13,21},{11,19},{0,24},{6,30}} | collective-permute-start | bytes 786440 | tf_op jit(solution)/shard_map/ppermute | solution.py:385
  36.7 8.8 %factor.3 = (f32[256,256]{1,0:T(8,128)}, f32[256,256]{1,0:T(8,128)S(1)}) custom-call(f32[256,256]{1,0:T(8,128)S(1)} %copy-done.3, f32[256,256]{1,0:T(8,128)S(1)} %get-tuple-element.30.refs_1_, f32[256,256]{1,0:T(8,128)S(1)} %block.2.refs_2_.refs_0_), custom_call_target="tpu_custom_call" | custom-call | flops 33554432 | bytes 524288 | tf_op jit(solution)/shard_map/factor/pallas_call | solution.py:235
  45.8 1.3 %collective-permute-start.13 = (f32[256,256]{1,0:T(8,128)S(1)}, f32[256,256]{1,0:T(8,128)S(1)}, u32[]{:S(2)}, u32[]{:S(2)}) collective-permute-start(f32[256,256]{1,0:T(8,128)S(1)} %block.3.after_ref.refs_0_), channel_id=1, source_target_pairs={{10,2},{3,11},{28,20},{21,29}} | collective-permute-start | bytes 786440 | tf_op jit(solution)/shard_map/ppermute | solution.py:385
  47.1 1.3 %collective-permute-start.14 = (f32[256,256]{1,0:T(8,128)S(1)}, f32[256,256]{1,0:T(8,128)S(1)}, u32[]{:S(2)}, u32[]{:S(2)}) collective-permute-start(f32[256,256]{1,0:T(8,128)S(1)} %block.3.after_ref.refs_0_), channel_id=1, source_target_pairs={{18,2},{27,11},{4,20},{13,29}} | collective-permute-start | bytes 786440 | tf_op jit(solution)/shard_map/ppermute | solution.py:385
  48.4 1.3 %collective-permute-start.15 = (f32[256,256]{1,0:T(8,128)S(1)}, f32[256,256]{1,0:T(8,128)S(1)}, u32[]{:S(2)}, u32[]{:S(2)}) collective-permute-start(f32[256,256]{1,0:T(8,128)S(1)} %block.3.after_ref.refs_0_), channel_id=1, source_target_pairs={{26,2},{19,11},{12,20},{5,29}} | collective-permute-start | bytes 786440 | tf_op jit(solution)/shard_map/ppermute | solution.py:385
  50.5 2.4 %collective-permute-done.13.refs_1_ = f32[256,256]{1,0:T(8,128)S(1)} collective-permute-done((f32[256,256]{1,0:T(8,128)S(1)}, f32[256,256]{1,0:T(8,128)S(1)}, u32[]{:S(2)}, u32[]{:S(2)}) %collective-permute-start.13) | collective-permute-done | bytes 262176 | tf_op jit(solution)/shard_map/ppermute | solution.py:385
  52.9 4.1 %collective-permute-done.14.refs_2_ = f32[256,256]{1,0:T(8,128)S(1)} collective-permute-done((f32[256,256]{1,0:T(8,128)S(1)}, f32[256,256]{1,0:T(8,128)S(1)}, u32[]{:S(2)}, u32[]{:S(2)}) %collective-permute-start.14) | collective-permute-done | bytes 262176 | tf_op jit(solution)/shard_map/ppermute | solution.py:385
  57.1 6.2 %collective-permute-start.16 = (f32[256,256]{1,0:T(8,128)S(1)}, f32[256,256]{1,0:T(8,128)S(1)}, u32[]{:S(2)}, u32[]{:S(2)}) collective-permute-start(f32[256,256]{1,0:T(8,128)S(1)} %total.3.refs_2_), channel_id=1, source_target_pairs={{2,20},{11,29},{20,2},{29,11}} | collective-permute-start | bytes 786440 | tf_op jit(solution)/shard_map/ppermute | solution.py:385
  63.2 4.0 %collective-permute-done.16.refs_3_ = f32[256,256]{1,0:T(8,128)S(1)} collective-permute-done((f32[256,256]{1,0:T(8,128)S(1)}, f32[256,256]{1,0:T(8,128)S(1)}, u32[]{:S(2)}, u32[]{:S(2)}) %collective-permute-start.16) | collective-permute-done | bytes 262176 | tf_op jit(solution)/shard_map/ppermute | solution.py:385
  67.3 0.7 merge.1
  68.0 1.3 %collective-permute-start.17 = (f32[136,256]{1,0:T(8,128)S(1)}, f32[136,256]{1,0:T(8,128)S(1)}, u32[]{:S(2)}, u32[]{:S(2)}) collective-permute-start(f32[136,256]{1,0:T(8,128)S(1)} %get-tuple-element.35), channel_id=1, source_target_pairs={{1,5},{2,6},{7,3},{12,8},{10,14},{11,15},{20,16},{21,17},{19,23},{... | collective-permute-start | bytes 417800 | tf_op jit(solution)/shard_map/ppermute | solution.py:385
  69.3 1.9 %collective-permute-start.18 = (f32[8,256]{1,0:T(8,128)S(1)}, f32[8,256]{1,0:T(8,128)S(1)}, u32[]{:S(2)}, u32[]{:S(2)}) collective-permute-start(f32[8,256]{1,0:T(8,128)S(1)} %get-tuple-element.36), channel_id=1, source_target_pairs={{1,29},{2,30},{7,31},{12,4},{10,6},{11,7},{20,12},{21,13},{19,15},... | collective-permute-start | bytes 24584 | tf_op jit(solution)/shard_map/ppermute | solution.py:385
  71.2 3.0 %collective-permute-done.18.top_ref = f32[8,256]{1,0:T(8,128)S(1)} collective-permute-done((f32[8,256]{1,0:T(8,128)S(1)}, f32[8,256]{1,0:T(8,128)S(1)}, u32[]{:S(2)}, u32[]{:S(2)}) %collective-permute-start.18) | collective-permute-done | bytes 8224 | tf_op jit(solution)/shard_map/ppermute | solution.py:385
  74.3 1.6 %tiles.1 = f32[256,128]{1,0:T(8,128)} custom-call(s32[4]{0:T(128)S(1)} %pad_add_fusion.pos_ref, f32[256,256]{1,0:T(8,128)S(1)} %get-tuple-element.33.after_ref.w_ref, f32[256,256]{1,0:T(8,128)S(1)} %gather.1.refs_0_.g_ref, f32[136,256]{1,0:T(8,128)S(1)} %get-tuple-element.34.own_ref, f32[136,256]{1,0:T(8,128)S(1)} %collective-permute-done.17.sib_ref, ...), custom_call_target="tpu_custom_call" | custom-call | tf_op jit(solution)/shard_map/tiles/pallas_call | solution.py:350
  (33 shorter events, 5.4 us)
Async XLA Ops:
  0.0 0.7 copy-start.5
  0.7 1.1 %copy-start.4 = (bf16[3,384,256]{2,1,0:T(8,128)(2,1)S(1)}, bf16[3,384,256]{2,1,0:T(8,128)(2,1)}, u32[]{:S(2)}) copy-start(bf16[3,384,256]{2,1,0:T(8,128)(2,1)} %vel_ref.1) | copy-start | bytes 1769476
  2.8 3.8 %collective-permute-start = (f32[8,256]{1,0:T(8,128)S(1)}, f32[8,256]{1,0:T(8,128)S(1)}, u32[]{:S(2)}, u32[]{:S(2)}) collective-permute-start(f32[8,256]{1,0:T(8,128)S(1)} %get-tuple-element.24), channel_id=1, source_target_pairs={{0,4},{4,0},{8,12},{12,8},{16,20},{20,16},{24,28},{28,24},{1,5},{5... | collective-permute-start | bytes 24584 | tf_op jit(solution)/shard_map/ppermute | solution.py:371
  3.5 5.3 %collective-permute-start.1 = (f32[8,256]{1,0:T(8,128)S(1)}, f32[8,256]{1,0:T(8,128)S(1)}, u32[]{:S(2)}, u32[]{:S(2)}) collective-permute-start(f32[8,256]{1,0:T(8,128)S(1)} %get-tuple-element.25), channel_id=1, source_target_pairs={{4,8},{12,16},{20,24},{8,4},{16,12},{24,20},{5,9},{13,17},{21,25},... | collective-permute-start | bytes 24584 | tf_op jit(solution)/shard_map/ppermute | solution.py:370
  9.8 18.5 %collective-permute-start.7 = (bf16[1152,256]{1,0:T(8,128)(2,1)S(1)}, bf16[1152,256]{1,0:T(8,128)(2,1)S(1)}, u32[]{:S(2)}, u32[]{:S(2)}) collective-permute-start(bf16[1152,256]{1,0:T(8,128)(2,1)S(1)} %get-tuple-element.32), channel_id=1, source_target_pairs={{0,1},{1,2},{2,3},{3,0},{8,9},{9,10},{10,11},{11,8},{16,17},{17,18... | collective-permute-start | bytes 1769480 | tf_op jit(solution)/shard_map/ppermute | solution.py:385
  13.2 1.3 %collective-permute-start.2 = (f32[192,128]{1,0:T(8,128)S(1)}, f32[192,128]{1,0:T(8,128)S(1)}, u32[]{:S(2)}, u32[]{:S(2)}) collective-permute-start(f32[192,128]{1,0:T(8,128)S(1)} %get-tuple-element.28), channel_id=1, source_target_pairs={{0,4},{4,0},{1,5},{5,1},{2,6},{6,2},{3,7},{7,3},{8,12},{12,8},{9,1... | collective-permute-start | bytes 294920 | tf_op jit(solution)/shard_map/ppermute | solution.py:385
  14.5 4.3 %collective-permute-start.3 = (f32[192,128]{1,0:T(8,128)S(1)}, f32[192,128]{1,0:T(8,128)S(1)}, u32[]{:S(2)}, u32[]{:S(2)}) collective-permute-start(f32[192,128]{1,0:T(8,128)S(1)} %add.18), channel_id=1, source_target_pairs={{0,8},{4,12},{1,9},{5,13},{2,10},{6,14},{3,11},{7,15},{8,0},{12,4}... | collective-permute-start | bytes 294920 | tf_op jit(solution)/shard_map/ppermute | solution.py:385
  14.6 4.8 %collective-permute-start.4 = (f32[192,128]{1,0:T(8,128)S(1)}, f32[192,128]{1,0:T(8,128)S(1)}, u32[]{:S(2)}, u32[]{:S(2)}) collective-permute-start(f32[192,128]{1,0:T(8,128)S(1)} %add.18), channel_id=1, source_target_pairs={{0,16},{4,20},{1,17},{5,21},{2,18},{6,22},{3,19},{7,23},{8,24},{12... | collective-permute-start | bytes 294920 | tf_op jit(solution)/shard_map/ppermute | solution.py:385
  16.6 4.7 %collective-permute-start.5 = (f32[192,128]{1,0:T(8,128)S(1)}, f32[192,128]{1,0:T(8,128)S(1)}, u32[]{:S(2)}, u32[]{:S(2)}) collective-permute-start(f32[192,128]{1,0:T(8,128)S(1)} %add.18), channel_id=1, source_target_pairs={{0,24},{4,28},{1,25},{5,29},{2,26},{6,30},{3,27},{7,31},{8,16},{12... | collective-permute-start | bytes 294920 | tf_op jit(solution)/shard_map/ppermute | solution.py:385
  21.3 2.6 %collective-permute-start.6 = (f32[192,128]{1,0:T(8,128)S(1)}, f32[192,128]{1,0:T(8,128)S(1)}, u32[]{:S(2)}, u32[]{:S(2)}) collective-permute-start(f32[192,128]{1,0:T(8,128)S(1)} %add_add_fusion.mine_ref), channel_id=1, source_target_pairs={{0,4},{4,0},{1,5},{5,1},{2,6},{6,2},{3,7},{7,3},{8,12},{12,8},{9,1... | collective-permute-start | bytes 294920 | tf_op jit(solution)/shard_map/ppermute | solution.py:385
  27.5 0.7 copy-start.2
  28.2 0.8 %copy-start = (bf16[1152,256]{1,0:T(8,128)(2,1)}, bf16[1152,256]{1,0:T(8,128)(2,1)S(1)}, u32[]{:S(2)}) copy-start(bf16[1152,256]{1,0:T(8,128)(2,1)S(1)} %collective-permute-done.7.refs_0_) | copy-start | bytes 1769476
  29.1 1.4 %copy-start.3 = (f32[256,256]{1,0:T(8,128)S(1)}, f32[256,256]{1,0:T(8,128)}, u32[]{:S(2)}) copy-start(f32[256,256]{1,0:T(8,128)} %copy-done.2) | copy-start | bytes 786436
  29.1 16.4 %collective-permute-start.8 = (bf16[1152,256]{1,0:T(8,128)(2,1)}, bf16[1152,256]{1,0:T(8,128)(2,1)S(1)}, u32[]{:S(2)}, u32[]{:S(2)}) collective-permute-start(bf16[1152,256]{1,0:T(8,128)(2,1)} %passed.1.panel_ref), channel_id=1, source_target_pairs={{1,2},{2,3},{9,10},{10,11},{17,18},{18,19},{25,26},{26,27},{6,5},{... | collective-permute-start | bytes 1769480 | tf_op jit(solution)/shard_map/ppermute | solution.py:385
  30.5 1.1 %copy-start.1 = (bf16[1152,256]{1,0:T(8,128)(2,1)S(1)}, bf16[1152,256]{1,0:T(8,128)(2,1)}, u32[]{:S(2)}) copy-start(bf16[1152,256]{1,0:T(8,128)(2,1)} %passed.1.panel_ref) | copy-start | bytes 1769476
  31.9 16.5 %collective-permute-start.10 = (f32[256,256]{1,0:T(8,128)S(1)}, f32[256,256]{1,0:T(8,128)S(1)}, u32[]{:S(2)}, u32[]{:S(2)}) collective-permute-start(f32[256,256]{1,0:T(8,128)S(1)} %block.2.refs_2_.refs_0_), channel_id=1, source_target_pairs={{17,1},{23,7},{28,12},{26,10},{5,21},{3,19},{8,24},{14,30}} | collective-permute-start | bytes 786440 | tf_op jit(solution)/shard_map/ppermute | solution.py:385
  32.6 17.1 %collective-permute-start.11 = (f32[256,256]{1,0:T(8,128)S(1)}, f32[256,256]{1,0:T(8,128)S(1)}, u32[]{:S(2)}, u32[]{:S(2)}) collective-permute-start(f32[256,256]{1,0:T(8,128)S(1)} %block.2.refs_2_.refs_0_), channel_id=1, source_target_pairs={{25,1},{31,7},{20,12},{18,10},{13,21},{11,19},{0,24},{6,30}} | collective-permute-start | bytes 786440 | tf_op jit(solution)/shard_map/ppermute | solution.py:385
  36.0 13.7 %collective-permute-start.9 = (f32[256,256]{1,0:T(8,128)S(1)}, f32[256,256]{1,0:T(8,128)S(1)}, u32[]{:S(2)}, u32[]{:S(2)}) collective-permute-start(f32[256,256]{1,0:T(8,128)S(1)} %block.2.refs_2_.refs_0_), channel_id=1, source_target_pairs={{9,1},{15,7},{4,12},{2,10},{29,21},{27,19},{16,24},{22,30}} | collective-permute-start | bytes 786440 | tf_op jit(solution)/shard_map/ppermute | solution.py:385
  45.8 7.1 %collective-permute-start.13 = (f32[256,256]{1,0:T(8,128)S(1)}, f32[256,256]{1,0:T(8,128)S(1)}, u32[]{:S(2)}, u32[]{:S(2)}) collective-permute-start(f32[256,256]{1,0:T(8,128)S(1)} %block.3.after_ref.refs_0_), channel_id=1, source_target_pairs={{10,2},{3,11},{28,20},{21,29}} | collective-permute-start | bytes 786440 | tf_op jit(solution)/shard_map/ppermute | solution.py:385
  47.1 9.9 %collective-permute-start.14 = (f32[256,256]{1,0:T(8,128)S(1)}, f32[256,256]{1,0:T(8,128)S(1)}, u32[]{:S(2)}, u32[]{:S(2)}) collective-permute-start(f32[256,256]{1,0:T(8,128)S(1)} %block.3.after_ref.refs_0_), channel_id=1, source_target_pairs={{18,2},{27,11},{4,20},{13,29}} | collective-permute-start | bytes 786440 | tf_op jit(solution)/shard_map/ppermute | solution.py:385
  48.4 8.6 %collective-permute-start.15 = (f32[256,256]{1,0:T(8,128)S(1)}, f32[256,256]{1,0:T(8,128)S(1)}, u32[]{:S(2)}, u32[]{:S(2)}) collective-permute-start(f32[256,256]{1,0:T(8,128)S(1)} %block.3.after_ref.refs_0_), channel_id=1, source_target_pairs={{26,2},{19,11},{12,20},{5,29}} | collective-permute-start | bytes 786440 | tf_op jit(solution)/shard_map/ppermute | solution.py:385
  49.8 13.5 %collective-permute-start.12 = (f32[256,256]{1,0:T(8,128)S(1)}, f32[256,256]{1,0:T(8,128)S(1)}, u32[]{:S(2)}, u32[]{:S(2)}) collective-permute-start(f32[256,256]{1,0:T(8,128)S(1)} %total.2.refs_0_), channel_id=1, source_target_pairs={{1,12},{7,24},{12,1},{10,21},{21,10},{19,30},{24,7},{30,19}} | collective-permute-start | bytes 786440 | tf_op jit(solution)/shard_map/ppermute | solution.py:385
  57.1 10.2 %collective-permute-start.16 = (f32[256,256]{1,0:T(8,128)S(1)}, f32[256,256]{1,0:T(8,128)S(1)}, u32[]{:S(2)}, u32[]{:S(2)}) collective-permute-start(f32[256,256]{1,0:T(8,128)S(1)} %total.3.refs_2_), channel_id=1, source_target_pairs={{2,20},{11,29},{20,2},{29,11}} | collective-permute-start | bytes 786440 | tf_op jit(solution)/shard_map/ppermute | solution.py:385
  68.0 6.3 %collective-permute-start.17 = (f32[136,256]{1,0:T(8,128)S(1)}, f32[136,256]{1,0:T(8,128)S(1)}, u32[]{:S(2)}, u32[]{:S(2)}) collective-permute-start(f32[136,256]{1,0:T(8,128)S(1)} %get-tuple-element.35), channel_id=1, source_target_pairs={{1,5},{2,6},{7,3},{12,8},{10,14},{11,15},{20,16},{21,17},{19,23},{... | collective-permute-start | bytes 417800 | tf_op jit(solution)/shard_map/ppermute | solution.py:385
  69.3 5.0 %collective-permute-start.18 = (f32[8,256]{1,0:T(8,128)S(1)}, f32[8,256]{1,0:T(8,128)S(1)}, u32[]{:S(2)}, u32[]{:S(2)}) collective-permute-start(f32[8,256]{1,0:T(8,128)S(1)} %get-tuple-element.36), channel_id=1, source_target_pairs={{1,29},{2,30},{7,31},{12,4},{10,6},{11,7},{20,12},{21,13},{19,15},... | collective-permute-start | bytes 24584 | tf_op jit(solution)/shard_map/ppermute | solution.py:385

commit v8 on v7

--- a/solution.py
+++ b/solution.py
@@ -31,18 +31,13 @@
     return third + center0 * second - center1 * first
 
 
-def interior_kernel(pos_ref, vel_ref, row_ref, x_ref, met_ref, inside_ref, outside_ref, head_ref, tail_ref):
+def interior_kernel(vel_ref, met_ref, x_ref, head_ref, tail_ref):
     rows, cols = vel_ref.shape[1:]
-    even = pos_ref[2] == 0
     row = lax.broadcasted_iota(jnp.int32, (rows, cols), 0)
-    metric = jnp.broadcast_to(row_ref[...][None, :], (8, rows)).T[:, 0:1]
-    met_ref[...] = metric
+    metric = met_ref[...]
 
     def gradient(k):
         field = vel_ref[k].astype(F32)
-        head, tail = field[0:1], field[rows - 1 : rows]
-        inside_ref[k : k + 1] = jnp.where(even, tail, head)
-        outside_ref[k : k + 1] = jnp.where(even, head, tail)
         head_ref[k] = field[:8]
         tail_ref[k] = field[rows - 8 :]
         up = jnp.where(row == rows - 1, 0.0, pltpu.roll(field, rows - 1, 0))
@@ -57,24 +52,21 @@
     x_ref[2 * rows :] = third.astype(BF16)
 
 
-def interior(pos, velocity, metric):
+def interior(velocity, metric):
     _, rows, cols = velocity.shape
     return pl.pallas_call(
         interior_kernel,
         out_shape=(
             jax.ShapeDtypeStruct((3 * rows, cols), BF16),
-            jax.ShapeDtypeStruct((rows, 1), F32),
-            jax.ShapeDtypeStruct((8, cols), F32),
-            jax.ShapeDtypeStruct((8, cols), F32),
             jax.ShapeDtypeStruct((3, 8, cols), F32),
             jax.ShapeDtypeStruct((3, 8, cols), F32),
         ),
-        in_specs=[SMEM, VMEM, VMEM],
-        out_specs=(VMEM,) * 6,
+        in_specs=[VMEM] * 2,
+        out_specs=(VMEM,) * 3,
         compiler_params=params(),
         cost_estimate=cost(30 * rows * cols, 12 * rows * cols),
         name="interior",
-    )(pos, velocity, metric)
+    )(velocity, metric)
 
 
 def panel_kernel(pos_ref, x_in_ref, head_ref, tail_ref, near_ref, far_ref, met_ref, x_ref, xt_ref, *g_refs):
@@ -92,8 +84,8 @@
             x_ref[span] = jnp.where(row == at, value, kept).astype(BF16)
 
     x_ref[...] = x_in_ref[...]
-    lo = [jnp.where(even, far_ref[k : k + 1], near_ref[k : k + 1]) for k in range(3)]
-    hi = [jnp.where(even, near_ref[k : k + 1], far_ref[k : k + 1]) for k in range(3)]
+    lo = [jnp.where(even, far_ref[k].astype(F32), near_ref[k].astype(F32)) for k in range(3)]
+    hi = [jnp.where(even, near_ref[k].astype(F32), far_ref[k].astype(F32)) for k in range(3)]
     low = met_ref[0:1]
     edge(0, lambda k: low * (head_ref[k, 1:2] - lo[k]) * 0.5, [head_ref[k, 0:1] for k in range(2)], 0)
     high = met_ref[rows - 1 : rows]
@@ -154,13 +146,13 @@
 
 
 def passed(value, after):
-    anywhere = pl.BlockSpec(memory_space=pl.ANY)
     return pl.pallas_call(
         lambda *refs: None,
         out_shape=jax.ShapeDtypeStruct(value.shape, value.dtype),
-        in_specs=[anywhere, anywhere],
-        out_specs=anywhere,
+        in_specs=[VMEM, VMEM],
+        out_specs=VMEM,
         input_output_aliases={0: 0},
+        compiler_params=params(),
         name="passed",
     )(value, after)
 
@@ -290,7 +282,8 @@
     )(after, *parts)
 
 
-def merge_kernel(pos_ref, *refs):
+def merge_kernel(pos_ref, after_ref, *refs):
+    del after_ref
     sums, (mine_ref, sib_ref, top_ref, t_ref) = refs[:4], refs[4:]
     n = t_ref.shape[0] - 8
     half = n // 2
@@ -307,18 +300,18 @@
     sib_ref[...] = t_ref[pl.ds(pl.multiple_of((1 - core) * half, 8), half + 8)]
 
 
-def merge(pos, near, far):
+def merge(pos, after, near, far):
     n = near[0].shape[0]
     half = n // 2
     return pl.pallas_call(
         merge_kernel,
         out_shape=tuple(jax.ShapeDtypeStruct((r, n), F32) for r in (half + 8, half + 8, 8)),
-        in_specs=[SMEM] + [VMEM] * 4,
+        in_specs=[SMEM, pl.BlockSpec(memory_space=pl.ANY)] + [VMEM] * 4,
         out_specs=(VMEM,) * 3,
         scratch_shapes=[pltpu.VMEM((n + 8, n), F32)],
         compiler_params=params(),
         name="merge",
-    )(pos, *near, *far)
+    )(pos, after, *near, *far)
 
 
 def tiles_kernel(pos_ref, w_ref, g_ref, own_ref, sib_ref, top_ref, out_ref, p_ref):
@@ -363,13 +356,14 @@
     space, group = lax.axis_index("space"), lax.axis_index("tm")
     odd = space % 2
     pos = jnp.stack([space // 2, group, odd, lax.axis_size("tm")]).astype(jnp.int32)
-    x, column, inward, outward, head, tail = interior(pos, velocity, metric)
+    head, tail = velocity[:, :1], velocity[:, -1:]
     inside = [(i, i ^ 1) for i in range(count)]
     outside = [(i, i + 1) for i in range(1, count - 1, 2)]
     outside += [(j, i) for i, j in outside]
-    far = lax.ppermute(outward, "space", outside)
-    near = lax.ppermute(inward, "space", inside)
-    return pos, panel(pos, (x, head, tail), near, far, column, packed)
+    far = lax.ppermute(jnp.where(odd == 0, head, tail), "space", outside)
+    near = lax.ppermute(jnp.where(odd == 0, tail, head), "space", inside)
+    column = metric.reshape(-1, 1)
+    return pos, panel(pos, interior(velocity, column), near, far, column, packed)
 
 
 def paired_body(velocity, metric):
@@ -422,14 +416,16 @@
 
     near_block = pair_block(state[0], xt, near)
     near_parts = gathered(near_block, near_homes)
-    w = factor_part(1, 3, state, (near_block,))[1]
-    far_block = pair_block(w, xt, far)
+    state = factor_part(1, 1, state, (near_block,))
+    far_block = pair_block(state[0], xt, far)
     far_parts = gathered(far_block, far_homes)
-    near_own = total(far_block, near_parts)
+    state = factor_part(2, 1, state, (far_block,))
+    near_own = total(state[0], near_parts)
     near_cross = exchanged(near_own, near_homes)
-    far_own = total(far_block, far_parts)
+    far_own = total(state[0], far_parts)
     far_cross = exchanged(far_own, far_homes)
-    mine, sib, top = merge(pos, (near_own, near_cross), (far_own, far_cross))
+    w = factor_part(3, 1, state, (far_own,))[1]
+    mine, sib, top = merge(pos, w, (near_own, near_cross), (far_own, far_cross))
     sib = send(sib, [(at(k, z, c), at(k, z, 1 - c)) for k, z, c in homes.values()])
     top = send(top, [(at(k, z, c), at((k - 1) % groups, z, 1)) for k, z, c in homes.values()])
     return tiles(pos, w, gram, (mine, sib, top))

time: 77.3 us -> 66.3 us (0.86); the launches traced: 75.9 us -> 65.9 us
  waiting for transfers between devices: 22.2 us -> 15.5 us
  local copies, waits for them, and re-layouts: 4.27 us -> 1.76 us
  starting transfers between devices: 31.6 us -> 30.6 us
    ppermute x17, waiting for transfers between devices: 19.9 us -> 15.5 us  [send(): return lax.ppermute(value, axes, pairs)]
    unnamed x12 -> x4, local copies, waits for them, and re-layouts: 4.27 us -> 1.66 us
    ppermute x2, waiting for transfers between devices: 2.22 us -> 0.01 us  [the longest x1 0.01 us: start(): far = lax.ppermute(jnp.where(odd == 0, head, tail), 'space', outside)]
    ppermute x17, starting transfers between devices: 27.8 us -> 26.8 us  [send(): return lax.ppermute(value, axes, pairs)]
    pallas_call x2 -> x4, Pallas kernels: 11.8 us -> 11.8 us  [factor_part(): pl.pallas_call(kernel, out_shape=(jax.ShapeDtypeStruct((n, n), F32),) * 2...]
  transfers between devices with their start and end apart: 19 -> 19, of which waited for: 10 -> 8; matrix products, arithmetic and copies ran while one was open for 0% -> 0% of each run, Pallas kernels for 17% -> 21%
where the time goes in v8:
time: 66.3 us; the launch traced here: 65.9 us
  starting transfers between devices  30.6 us (46%)
  Pallas kernels  16.9 us (25%)
  waiting for transfers between devices  15.5 us (23%)
  local copies, waits for them, and re-layouts  1.76 us (3%)
  other arithmetic  0.85 us (1%)
    ppermute x17, starting transfers between devices, send(): return lax.ppermute(value, axes, pairs)  26.8 us
    ppermute x17, waiting for transfers between devices, send(): return lax.ppermute(value, axes, pairs)  15.5 us
    pallas_call x4, Pallas kernels, factor_part(): pl.pallas_call(kernel, out_shape=(jax.ShapeDtypeStruct((n, n), F32),) * 2...  11.8 us
    ppermute x1, starting transfers between devices, start(): far = lax.ppermute(jnp.where(odd == 0, head, tail), 'space', outside)  3.02 us
    unnamed x4, local copies, waits for them, and re-layouts  1.66 us
    pallas_call x1, Pallas kernels, tiles(): pl.pallas_call(tiles_kernel, out_shape=jax.ShapeDtypeStruct((n, half), F3...  1.62 us
  transfers between devices with their start and end apart: 19, of which 8 were waited for; matrix products, arithmetic and copies ran while one was open for 0% of the time, Pallas kernels for 21%

profile of v8, /device:TPU:5, one launch (start us, length us, event | category | flops | bytes accessed | tf_op | source)
XLA Modules:
  0.0 65.9 jit_solution(11904495396365423681)
XLA Ops:
  0.0 0.7 %broadcast_select_fusion = (bf16[3,1,256]{2,1,0:T(2,128)(2,1)S(1)}, bf16[3,1,256]{2,1,0:T(2,128)(2,1)S(1)}) fusion(pred[]{:T(512)S(6)} %eq.6, bf16[3,384,256]{2,1,0:T(8,128)(2,1)} %vel_ref.1), kind=kLoop, calls=%fused_computation.1 | loop fusion | flops 1536 | bytes 6145 | tf_op jit(solution)/shard_map/jit(_where)/select_n | solution.py:363
  0.7 0.7 %collective-permute-start = (bf16[3,1,256]{2,1,0:T(2,128)(2,1)S(1)}, bf16[3,1,256]{2,1,0:T(2,128)(2,1)S(1)}, u32[]{:S(2)}, u32[]{:S(2)}) collective-permute-start(bf16[3,1,256]{2,1,0:T(2,128)(2,1)S(1)} %get-tuple-element.40), channel_id=1, source_target_pairs={{0,4},{4,0},{8,12},{12,8},{16,20},{20,16},{24,28},{28,24},{1,5},{5... | collective-permute-start | bytes 4616 | tf_op jit(solution)/shard_map/ppermute | solution.py:364
  1.5 3.0 %collective-permute-start.1 = (bf16[3,1,256]{2,1,0:T(2,128)(2,1)S(1)}, bf16[3,1,256]{2,1,0:T(2,128)(2,1)S(1)}, u32[]{:S(2)}, u32[]{:S(2)}) collective-permute-start(bf16[3,1,256]{2,1,0:T(2,128)(2,1)S(1)} %get-tuple-element.39), channel_id=1, source_target_pairs={{4,8},{12,16},{20,24},{8,4},{16,12},{24,20},{5,9},{13,17},{21,25},... | collective-permute-start | bytes 4616 | tf_op jit(solution)/shard_map/ppermute | solution.py:363
  5.3 1.1 %copy-done = bf16[3,384,256]{2,1,0:T(8,128)(2,1)S(1)} copy-done((bf16[3,384,256]{2,1,0:T(8,128)(2,1)S(1)}, bf16[3,384,256]{2,1,0:T(8,128)(2,1)}, u32[]{:S(2)}) %copy-start) | copy-done | bytes 589848
  6.8 1.0 %panel.1 = (bf16[1152,256]{1,0:T(8,128)(2,1)S(1)}, bf16[256,1152]{1,0:T(8,128)(2,1)S(1)}, f32[192,128]{1,0:T(8,128)S(1)}, f32[192,128]{1,0:T(8,128)S(1)}) custom-call(s32[4]{0:T(128)S(1)} %pad_add_fusion.pos_ref, bf16[1152,256]{1,0:T(8,128)(2,1)S(1)} %get-tuple-element.22.x_in_ref, f32[3,8,256]{2,1,0:T(8,128)S(1)} %get-tuple-element.23.head_ref, ...), custom_call_target="tpu_custom_call" | custom-call | flops 150994944 | bytes 1769472 | tf_op jit(solution)/shard_map/panel/pallas_call | solution.py:112
  7.8 3.4 %collective-permute-start.7 = (bf16[1152,256]{1,0:T(8,128)(2,1)S(1)}, bf16[1152,256]{1,0:T(8,128)(2,1)S(1)}, u32[]{:S(2)}, u32[]{:S(2)}) collective-permute-start(bf16[1152,256]{1,0:T(8,128)(2,1)S(1)} %get-tuple-element.30), channel_id=1, source_target_pairs={{0,1},{1,2},{2,3},{3,0},{8,9},{9,10},{10,11},{11,8},{16,17},{17,18... | collective-permute-start | bytes 1769480 | tf_op jit(solution)/shard_map/ppermute | solution.py:379
  11.2 1.3 %collective-permute-done.2 = f32[192,128]{1,0:T(8,128)S(1)} collective-permute-done((f32[192,128]{1,0:T(8,128)S(1)}, f32[192,128]{1,0:T(8,128)S(1)}, u32[]{:S(2)}, u32[]{:S(2)}) %collective-permute-start.2) | collective-permute-done | bytes 98336 | tf_op jit(solution)/shard_map/ppermute | solution.py:379
  12.5 1.7 %collective-permute-start.5 = (f32[192,128]{1,0:T(8,128)S(1)}, f32[192,128]{1,0:T(8,128)S(1)}, u32[]{:S(2)}, u32[]{:S(2)}) collective-permute-start(f32[192,128]{1,0:T(8,128)S(1)} %add.18), channel_id=1, source_target_pairs={{0,24},{4,28},{1,25},{5,29},{2,26},{6,30},{3,27},{7,31},{8,16},{12... | collective-permute-start | bytes 294920 | tf_op jit(solution)/shard_map/ppermute | solution.py:379
  14.2 1.0 %collective-permute-start.3 = (f32[192,128]{1,0:T(8,128)S(1)}, f32[192,128]{1,0:T(8,128)S(1)}, u32[]{:S(2)}, u32[]{:S(2)}) collective-permute-start(f32[192,128]{1,0:T(8,128)S(1)} %add.18), channel_id=1, source_target_pairs={{0,8},{4,12},{1,9},{5,13},{2,10},{6,14},{3,11},{7,15},{8,0},{12,4}... | collective-permute-start | bytes 294920 | tf_op jit(solution)/shard_map/ppermute | solution.py:379
  15.2 2.5 %collective-permute-done.5 = f32[192,128]{1,0:T(8,128)S(1)} collective-permute-done((f32[192,128]{1,0:T(8,128)S(1)}, f32[192,128]{1,0:T(8,128)S(1)}, u32[]{:S(2)}, u32[]{:S(2)}) %collective-permute-start.5) | collective-permute-done | bytes 98336 | tf_op jit(solution)/shard_map/ppermute | solution.py:379
  17.7 2.6 %collective-permute-done.4 = f32[192,128]{1,0:T(8,128)S(1)} collective-permute-done((f32[192,128]{1,0:T(8,128)S(1)}, f32[192,128]{1,0:T(8,128)S(1)}, u32[]{:S(2)}, u32[]{:S(2)}) %collective-permute-start.4) | collective-permute-done | bytes 98336 | tf_op jit(solution)/shard_map/ppermute | solution.py:379
  20.9 0.9 %collective-permute-done.6.theirs_ref = f32[192,128]{1,0:T(8,128)S(1)} collective-permute-done((f32[192,128]{1,0:T(8,128)S(1)}, f32[192,128]{1,0:T(8,128)S(1)}, u32[]{:S(2)}, u32[]{:S(2)}) %collective-permute-start.6) | collective-permute-done | bytes 98336 | tf_op jit(solution)/shard_map/ppermute | solution.py:379
  22.5 3.0 %factor.4 = (f32[256,256]{1,0:T(8,128)S(1)}, f32[256,256]{1,0:T(8,128)S(1)}) custom-call(f32[256,256]{1,0:T(8,128)S(1)} %gather.1.refs_0_.g_ref), custom_call_target="tpu_custom_call" | custom-call | flops 33554432 | bytes 524288 | tf_op jit(solution)/shard_map/factor/pallas_call | solution.py:227
  25.5 1.3 %collective-permute-start.8 = (bf16[1152,256]{1,0:T(8,128)(2,1)S(1)}, bf16[1152,256]{1,0:T(8,128)(2,1)S(1)}, u32[]{:S(2)}, u32[]{:S(2)}) collective-permute-start(bf16[1152,256]{1,0:T(8,128)(2,1)S(1)} %passed.1.panel_ref), channel_id=1, source_target_pairs={{1,2},{2,3},{9,10},{10,11},{17,18},{18,19},{25,26},{26,27},{6,5},{... | collective-permute-start | bytes 1769480 | tf_op jit(solution)/shard_map/ppermute | solution.py:379
  27.2 0.7 %collective-permute-start.12 = (f32[256,256]{1,0:T(8,128)S(1)}, f32[256,256]{1,0:T(8,128)S(1)}, u32[]{:S(2)}, u32[]{:S(2)}) collective-permute-start(f32[256,256]{1,0:T(8,128)S(1)} %block.2.refs_2_.refs_0_), channel_id=1, source_target_pairs={{9,1},{15,7},{4,12},{2,10},{29,21},{27,19},{16,24},{22,30}} | collective-permute-start | bytes 786440 | tf_op jit(solution)/shard_map/ppermute | solution.py:379
  27.8 0.7 %collective-permute-start.13 = (f32[256,256]{1,0:T(8,128)S(1)}, f32[256,256]{1,0:T(8,128)S(1)}, u32[]{:S(2)}, u32[]{:S(2)}) collective-permute-start(f32[256,256]{1,0:T(8,128)S(1)} %block.2.refs_2_.refs_0_), channel_id=1, source_target_pairs={{17,1},{23,7},{28,12},{26,10},{5,21},{3,19},{8,24},{14,30}} | collective-permute-start | bytes 786440 | tf_op jit(solution)/shard_map/ppermute | solution.py:379
  28.5 4.6 %collective-permute-start.14 = (f32[256,256]{1,0:T(8,128)S(1)}, f32[256,256]{1,0:T(8,128)S(1)}, u32[]{:S(2)}, u32[]{:S(2)}) collective-permute-start(f32[256,256]{1,0:T(8,128)S(1)} %block.2.refs_2_.refs_0_), channel_id=1, source_target_pairs={{25,1},{31,7},{20,12},{18,10},{13,21},{11,19},{0,24},{6,30}} | collective-permute-start | bytes 786440 | tf_op jit(solution)/shard_map/ppermute | solution.py:379
  33.1 2.9 %factor.5 = (f32[256,256]{1,0:T(8,128)S(1)}, f32[256,256]{1,0:T(8,128)S(1)}) custom-call(f32[256,256]{1,0:T(8,128)S(1)} %get-tuple-element.27.refs_1_.after_ref.refs_0_, f32[256,256]{1,0:T(8,128)S(1)} %get-tuple-element.28.refs_1_, f32[256,256]{1,0:T(8,128)S(1)} %block.2.refs_2_.refs_0_), custom_call_target="tpu_custom_call" | custom-call | flops 33554432 | bytes 524288 | tf_op jit(solution)/shard_map/factor/pallas_call | solution.py:227
  36.5 1.3 %collective-permute-start.9 = (f32[256,256]{1,0:T(8,128)S(1)}, f32[256,256]{1,0:T(8,128)S(1)}, u32[]{:S(2)}, u32[]{:S(2)}) collective-permute-start(f32[256,256]{1,0:T(8,128)S(1)} %block.3.refs_2_.refs_0_), channel_id=1, source_target_pairs={{10,2},{3,11},{28,20},{21,29}} | collective-permute-start | bytes 786440 | tf_op jit(solution)/shard_map/ppermute | solution.py:379
  37.8 1.3 %collective-permute-start.10 = (f32[256,256]{1,0:T(8,128)S(1)}, f32[256,256]{1,0:T(8,128)S(1)}, u32[]{:S(2)}, u32[]{:S(2)}) collective-permute-start(f32[256,256]{1,0:T(8,128)S(1)} %block.3.refs_2_.refs_0_), channel_id=1, source_target_pairs={{18,2},{27,11},{4,20},{13,29}} | collective-permute-start | bytes 786440 | tf_op jit(solution)/shard_map/ppermute | solution.py:379
  39.1 1.3 %collective-permute-start.11 = (f32[256,256]{1,0:T(8,128)S(1)}, f32[256,256]{1,0:T(8,128)S(1)}, u32[]{:S(2)}, u32[]{:S(2)}) collective-permute-start(f32[256,256]{1,0:T(8,128)S(1)} %block.3.refs_2_.refs_0_), channel_id=1, source_target_pairs={{26,2},{19,11},{12,20},{5,29}} | collective-permute-start | bytes 786440 | tf_op jit(solution)/shard_map/ppermute | solution.py:379
  40.4 2.8 %factor.6 = (f32[256,256]{1,0:T(8,128)S(1)}, f32[256,256]{1,0:T(8,128)S(1)}) custom-call(f32[256,256]{1,0:T(8,128)S(1)} %get-tuple-element.31.after_ref.refs_0_, f32[256,256]{1,0:T(8,128)S(1)} %get-tuple-element.32.refs_1_, f32[256,256]{1,0:T(8,128)S(1)} %block.3.refs_2_.refs_0_), custom_call_target="tpu_custom_call" | custom-call | flops 33554432 | bytes 524288 | tf_op jit(solution)/shard_map/factor/pallas_call | solution.py:227
  43.3 0.7 %collective-permute-start.15 = (f32[256,256]{1,0:T(8,128)S(1)}, f32[256,256]{1,0:T(8,128)S(1)}, u32[]{:S(2)}, u32[]{:S(2)}) collective-permute-start(f32[256,256]{1,0:T(8,128)S(1)} %total.3.refs_0_), channel_id=1, source_target_pairs={{1,12},{7,24},{12,1},{10,21},{21,10},{19,30},{24,7},{30,19}} | collective-permute-start | bytes 786440 | tf_op jit(solution)/shard_map/ppermute | solution.py:379
  44.0 3.7 %collective-permute-done.10.refs_2_ = f32[256,256]{1,0:T(8,128)S(1)} collective-permute-done((f32[256,256]{1,0:T(8,128)S(1)}, f32[256,256]{1,0:T(8,128)S(1)}, u32[]{:S(2)}, u32[]{:S(2)}) %collective-permute-start.10) | collective-permute-done | bytes 262176 | tf_op jit(solution)/shard_map/ppermute | solution.py:379
  47.8 5.2 %collective-permute-start.16 = (f32[256,256]{1,0:T(8,128)S(1)}, f32[256,256]{1,0:T(8,128)S(1)}, u32[]{:S(2)}, u32[]{:S(2)}) collective-permute-start(f32[256,256]{1,0:T(8,128)S(1)} %total.2.refs_2_), channel_id=1, source_target_pairs={{2,20},{11,29},{20,2},{29,11}} | collective-permute-start | bytes 786440 | tf_op jit(solution)/shard_map/ppermute | solution.py:379
  53.0 3.1 %factor.7 = (f32[256,256]{1,0:T(8,128)}, f32[256,256]{1,0:T(8,128)S(1)}) custom-call(f32[256,256]{1,0:T(8,128)S(1)} %get-tuple-element.33.after_ref.refs_0_, f32[256,256]{1,0:T(8,128)S(1)} %get-tuple-element.34.refs_1_, f32[256,256]{1,0:T(8,128)S(1)} %total.2.refs_2_), custom_call_target="tpu_custom_call" | custom-call | flops 33554432 | bytes 524288 | tf_op jit(solution)/shard_map/factor/pallas_call | solution.py:227
  56.0 1.3 %collective-permute-done.16.refs_3_ = f32[256,256]{1,0:T(8,128)S(1)} collective-permute-done((f32[256,256]{1,0:T(8,128)S(1)}, f32[256,256]{1,0:T(8,128)S(1)}, u32[]{:S(2)}, u32[]{:S(2)}) %collective-permute-start.16) | collective-permute-done | bytes 262176 | tf_op jit(solution)/shard_map/ppermute | solution.py:379
  57.3 0.7 %merge.1 = (f32[136,256]{1,0:T(8,128)S(1)}, f32[136,256]{1,0:T(8,128)S(1)}, f32[8,256]{1,0:T(8,128)S(1)}) custom-call(s32[4]{0:T(128)S(1)} %pad_add_fusion.pos_ref, f32[256,256]{1,0:T(8,128)S(1)} %get-tuple-element.35.after_ref.w_ref, f32[256,256]{1,0:T(8,128)S(1)} %total.3.refs_0_, f32[256,256]{1,0:T(8,128)S(1)} %collective-permute-done.15.refs_1_, ...), custom_call_target="tpu_custom_call" | custom-call | tf_op jit(solution)/shard_map/merge/pallas_call | solution.py:306
  58.0 1.3 %collective-permute-start.17 = (f32[136,256]{1,0:T(8,128)S(1)}, f32[136,256]{1,0:T(8,128)S(1)}, u32[]{:S(2)}, u32[]{:S(2)}) collective-permute-start(f32[136,256]{1,0:T(8,128)S(1)} %get-tuple-element.37), channel_id=1, source_target_pairs={{1,5},{2,6},{7,3},{12,8},{10,14},{11,15},{20,16},{21,17},{19,23},{... | collective-permute-start | bytes 417800 | tf_op jit(solution)/shard_map/ppermute | solution.py:379
  59.3 1.9 %collective-permute-start.18 = (f32[8,256]{1,0:T(8,128)S(1)}, f32[8,256]{1,0:T(8,128)S(1)}, u32[]{:S(2)}, u32[]{:S(2)}) collective-permute-start(f32[8,256]{1,0:T(8,128)S(1)} %get-tuple-element.38), channel_id=1, source_target_pairs={{1,29},{2,30},{7,31},{12,4},{10,6},{11,7},{20,12},{21,13},{19,15},... | collective-permute-start | bytes 24584 | tf_op jit(solution)/shard_map/ppermute | solution.py:379
  61.2 3.0 %collective-permute-done.18.top_ref = f32[8,256]{1,0:T(8,128)S(1)} collective-permute-done((f32[8,256]{1,0:T(8,128)S(1)}, f32[8,256]{1,0:T(8,128)S(1)}, u32[]{:S(2)}, u32[]{:S(2)}) %collective-permute-start.18) | collective-permute-done | bytes 8224 | tf_op jit(solution)/shard_map/ppermute | solution.py:379
  64.3 1.6 %tiles.1 = f32[256,128]{1,0:T(8,128)} custom-call(s32[4]{0:T(128)S(1)} %pad_add_fusion.pos_ref, f32[256,256]{1,0:T(8,128)S(1)} %get-tuple-element.35.after_ref.w_ref, f32[256,256]{1,0:T(8,128)S(1)} %gather.1.refs_0_.g_ref, f32[136,256]{1,0:T(8,128)S(1)} %get-tuple-element.36.own_ref, f32[136,256]{1,0:T(8,128)S(1)} %collective-permute-done.17.sib_ref, ...), custom_call_target="tpu_custom_call" | custom-call | tf_op jit(solution)/shard_map/tiles/pallas_call | solution.py:343
  (29 shorter events, 3.3 us)
Async XLA Ops:
  0.7 6.1 %collective-permute-start = (bf16[3,1,256]{2,1,0:T(2,128)(2,1)S(1)}, bf16[3,1,256]{2,1,0:T(2,128)(2,1)S(1)}, u32[]{:S(2)}, u32[]{:S(2)}) collective-permute-start(bf16[3,1,256]{2,1,0:T(2,128)(2,1)S(1)} %get-tuple-element.40), channel_id=1, source_target_pairs={{0,4},{4,0},{8,12},{12,8},{16,20},{20,16},{24,28},{28,24},{1,5},{5... | collective-permute-start | bytes 4616 | tf_op jit(solution)/shard_map/ppermute | solution.py:364
  1.5 5.3 %collective-permute-start.1 = (bf16[3,1,256]{2,1,0:T(2,128)(2,1)S(1)}, bf16[3,1,256]{2,1,0:T(2,128)(2,1)S(1)}, u32[]{:S(2)}, u32[]{:S(2)}) collective-permute-start(bf16[3,1,256]{2,1,0:T(2,128)(2,1)S(1)} %get-tuple-element.39), channel_id=1, source_target_pairs={{4,8},{12,16},{20,24},{8,4},{16,12},{24,20},{5,9},{13,17},{21,25},... | collective-permute-start | bytes 4616 | tf_op jit(solution)/shard_map/ppermute | solution.py:363
  4.5 0.7 %copy-start.1 = (f32[384]{0:T(512)S(1)}, f32[384]{0:T(512)}, u32[]{:S(2)}) copy-start(f32[384]{0:T(512)} %param.3) | copy-start | bytes 4612
  5.3 1.1 %copy-start = (bf16[3,384,256]{2,1,0:T(8,128)(2,1)S(1)}, bf16[3,384,256]{2,1,0:T(8,128)(2,1)}, u32[]{:S(2)}) copy-start(bf16[3,384,256]{2,1,0:T(8,128)(2,1)} %vel_ref.1) | copy-start | bytes 1769476
  7.8 17.7 %collective-permute-start.7 = (bf16[1152,256]{1,0:T(8,128)(2,1)S(1)}, bf16[1152,256]{1,0:T(8,128)(2,1)S(1)}, u32[]{:S(2)}, u32[]{:S(2)}) collective-permute-start(bf16[1152,256]{1,0:T(8,128)(2,1)S(1)} %get-tuple-element.30), channel_id=1, source_target_pairs={{0,1},{1,2},{2,3},{3,0},{8,9},{9,10},{10,11},{11,8},{16,17},{17,18... | collective-permute-start | bytes 1769480 | tf_op jit(solution)/shard_map/ppermute | solution.py:379
  11.2 1.3 %collective-permute-start.2 = (f32[192,128]{1,0:T(8,128)S(1)}, f32[192,128]{1,0:T(8,128)S(1)}, u32[]{:S(2)}, u32[]{:S(2)}) collective-permute-start(f32[192,128]{1,0:T(8,128)S(1)} %get-tuple-element.26), channel_id=1, source_target_pairs={{0,4},{4,0},{1,5},{5,1},{2,6},{6,2},{3,7},{7,3},{8,12},{12,8},{9,1... | collective-permute-start | bytes 294920 | tf_op jit(solution)/shard_map/ppermute | solution.py:379
  12.5 5.2 %collective-permute-start.5 = (f32[192,128]{1,0:T(8,128)S(1)}, f32[192,128]{1,0:T(8,128)S(1)}, u32[]{:S(2)}, u32[]{:S(2)}) collective-permute-start(f32[192,128]{1,0:T(8,128)S(1)} %add.18), channel_id=1, source_target_pairs={{0,24},{4,28},{1,25},{5,29},{2,26},{6,30},{3,27},{7,31},{8,16},{12... | collective-permute-start | bytes 294920 | tf_op jit(solution)/shard_map/ppermute | solution.py:379
  14.2 6.1 %collective-permute-start.4 = (f32[192,128]{1,0:T(8,128)S(1)}, f32[192,128]{1,0:T(8,128)S(1)}, u32[]{:S(2)}, u32[]{:S(2)}) collective-permute-start(f32[192,128]{1,0:T(8,128)S(1)} %add.18), channel_id=1, source_target_pairs={{0,16},{4,20},{1,17},{5,21},{2,18},{6,22},{3,19},{7,23},{8,24},{12... | collective-permute-start | bytes 294920 | tf_op jit(solution)/shard_map/ppermute | solution.py:379
  14.2 6.1 %collective-permute-start.3 = (f32[192,128]{1,0:T(8,128)S(1)}, f32[192,128]{1,0:T(8,128)S(1)}, u32[]{:S(2)}, u32[]{:S(2)}) collective-permute-start(f32[192,128]{1,0:T(8,128)S(1)} %add.18), channel_id=1, source_target_pairs={{0,8},{4,12},{1,9},{5,13},{2,10},{6,14},{3,11},{7,15},{8,0},{12,4}... | collective-permute-start | bytes 294920 | tf_op jit(solution)/shard_map/ppermute | solution.py:379
  20.3 1.5 %collective-permute-start.6 = (f32[192,128]{1,0:T(8,128)S(1)}, f32[192,128]{1,0:T(8,128)S(1)}, u32[]{:S(2)}, u32[]{:S(2)}) collective-permute-start(f32[192,128]{1,0:T(8,128)S(1)} %add_add_fusion.mine_ref), channel_id=1, source_target_pairs={{0,4},{4,0},{1,5},{5,1},{2,6},{6,2},{3,7},{7,3},{8,12},{12,8},{9,1... | collective-permute-start | bytes 294920 | tf_op jit(solution)/shard_map/ppermute | solution.py:379
  25.5 10.6 %collective-permute-start.8 = (bf16[1152,256]{1,0:T(8,128)(2,1)S(1)}, bf16[1152,256]{1,0:T(8,128)(2,1)S(1)}, u32[]{:S(2)}, u32[]{:S(2)}) collective-permute-start(bf16[1152,256]{1,0:T(8,128)(2,1)S(1)} %passed.1.panel_ref), channel_id=1, source_target_pairs={{1,2},{2,3},{9,10},{10,11},{17,18},{18,19},{25,26},{26,27},{6,5},{... | collective-permute-start | bytes 1769480 | tf_op jit(solution)/shard_map/ppermute | solution.py:379
  27.2 11.9 %collective-permute-start.12 = (f32[256,256]{1,0:T(8,128)S(1)}, f32[256,256]{1,0:T(8,128)S(1)}, u32[]{:S(2)}, u32[]{:S(2)}) collective-permute-start(f32[256,256]{1,0:T(8,128)S(1)} %block.2.refs_2_.refs_0_), channel_id=1, source_target_pairs={{9,1},{15,7},{4,12},{2,10},{29,21},{27,19},{16,24},{22,30}} | collective-permute-start | bytes 786440 | tf_op jit(solution)/shard_map/ppermute | solution.py:379
  27.8 15.4 %collective-permute-start.13 = (f32[256,256]{1,0:T(8,128)S(1)}, f32[256,256]{1,0:T(8,128)S(1)}, u32[]{:S(2)}, u32[]{:S(2)}) collective-permute-start(f32[256,256]{1,0:T(8,128)S(1)} %block.2.refs_2_.refs_0_), channel_id=1, source_target_pairs={{17,1},{23,7},{28,12},{26,10},{5,21},{3,19},{8,24},{14,30}} | collective-permute-start | bytes 786440 | tf_op jit(solution)/shard_map/ppermute | solution.py:379
  28.5 14.7 %collective-permute-start.14 = (f32[256,256]{1,0:T(8,128)S(1)}, f32[256,256]{1,0:T(8,128)S(1)}, u32[]{:S(2)}, u32[]{:S(2)}) collective-permute-start(f32[256,256]{1,0:T(8,128)S(1)} %block.2.refs_2_.refs_0_), channel_id=1, source_target_pairs={{25,1},{31,7},{20,12},{18,10},{13,21},{11,19},{0,24},{6,30}} | collective-permute-start | bytes 786440 | tf_op jit(solution)/shard_map/ppermute | solution.py:379
  36.5 7.5 %collective-permute-start.9 = (f32[256,256]{1,0:T(8,128)S(1)}, f32[256,256]{1,0:T(8,128)S(1)}, u32[]{:S(2)}, u32[]{:S(2)}) collective-permute-start(f32[256,256]{1,0:T(8,128)S(1)} %block.3.refs_2_.refs_0_), channel_id=1, source_target_pairs={{10,2},{3,11},{28,20},{21,29}} | collective-permute-start | bytes 786440 | tf_op jit(solution)/shard_map/ppermute | solution.py:379
  37.8 9.9 %collective-permute-start.10 = (f32[256,256]{1,0:T(8,128)S(1)}, f32[256,256]{1,0:T(8,128)S(1)}, u32[]{:S(2)}, u32[]{:S(2)}) collective-permute-start(f32[256,256]{1,0:T(8,128)S(1)} %block.3.refs_2_.refs_0_), channel_id=1, source_target_pairs={{18,2},{27,11},{4,20},{13,29}} | collective-permute-start | bytes 786440 | tf_op jit(solution)/shard_map/ppermute | solution.py:379
  39.1 8.6 %collective-permute-start.11 = (f32[256,256]{1,0:T(8,128)S(1)}, f32[256,256]{1,0:T(8,128)S(1)}, u32[]{:S(2)}, u32[]{:S(2)}) collective-permute-start(f32[256,256]{1,0:T(8,128)S(1)} %block.3.refs_2_.refs_0_), channel_id=1, source_target_pairs={{26,2},{19,11},{12,20},{5,29}} | collective-permute-start | bytes 786440 | tf_op jit(solution)/shard_map/ppermute | solution.py:379
  43.3 12.7 %collective-permute-start.15 = (f32[256,256]{1,0:T(8,128)S(1)}, f32[256,256]{1,0:T(8,128)S(1)}, u32[]{:S(2)}, u32[]{:S(2)}) collective-permute-start(f32[256,256]{1,0:T(8,128)S(1)} %total.3.refs_0_), channel_id=1, source_target_pairs={{1,12},{7,24},{12,1},{10,21},{21,10},{19,30},{24,7},{30,19}} | collective-permute-start | bytes 786440 | tf_op jit(solution)/shard_map/ppermute | solution.py:379
  47.8 9.5 %collective-permute-start.16 = (f32[256,256]{1,0:T(8,128)S(1)}, f32[256,256]{1,0:T(8,128)S(1)}, u32[]{:S(2)}, u32[]{:S(2)}) collective-permute-start(f32[256,256]{1,0:T(8,128)S(1)} %total.2.refs_2_), channel_id=1, source_target_pairs={{2,20},{11,29},{20,2},{29,11}} | collective-permute-start | bytes 786440 | tf_op jit(solution)/shard_map/ppermute | solution.py:379
  58.0 6.3 %collective-permute-start.17 = (f32[136,256]{1,0:T(8,128)S(1)}, f32[136,256]{1,0:T(8,128)S(1)}, u32[]{:S(2)}, u32[]{:S(2)}) collective-permute-start(f32[136,256]{1,0:T(8,128)S(1)} %get-tuple-element.37), channel_id=1, source_target_pairs={{1,5},{2,6},{7,3},{12,8},{10,14},{11,15},{20,16},{21,17},{19,23},{... | collective-permute-start | bytes 417800 | tf_op jit(solution)/shard_map/ppermute | solution.py:379
  59.3 5.0 %collective-permute-start.18 = (f32[8,256]{1,0:T(8,128)S(1)}, f32[8,256]{1,0:T(8,128)S(1)}, u32[]{:S(2)}, u32[]{:S(2)}) collective-permute-start(f32[8,256]{1,0:T(8,128)S(1)} %get-tuple-element.38), channel_id=1, source_target_pairs={{1,29},{2,30},{7,31},{12,4},{10,6},{11,7},{20,12},{21,13},{19,15},... | collective-permute-start | bytes 24584 | tf_op jit(solution)/shard_map/ppermute | solution.py:379

commit v9 on v8

--- a/solution.py
+++ b/solution.py
@@ -244,16 +244,25 @@
     return jnp.where((behind == 1) | ((behind == 2) & (group > chip)), 0, 1)
 
 
+TOP = 14.0
+TAIL = 16
+
+
 def block_kernel(after_ref, xt_ref, panel_ref, out_ref):
     del after_ref
-    out_ref[...] = jnp.dot(xt_ref[...], panel_ref[...], preferred_element_type=F32)
+    n = xt_ref.shape[0]
+    block = jnp.dot(xt_ref[...], panel_ref[...], preferred_element_type=F32)
+    peak = jnp.max(jnp.abs(block), axis=(0, 1), keepdims=True)
+    exponent = jnp.ceil(jnp.log2(jnp.maximum(peak, 1e-30)))
+    out_ref[0:n] = block * jnp.exp2(TOP - exponent)
+    out_ref[n:] = jnp.broadcast_to(exponent, (TAIL, n))
 
 
 def pair_block(after, xt, panel):
     n = xt.shape[0]
     return pl.pallas_call(
         block_kernel,
-        out_shape=jax.ShapeDtypeStruct((n, n), F32),
+        out_shape=jax.ShapeDtypeStruct((n + TAIL, n), F32),
         in_specs=[pl.BlockSpec(memory_space=pl.ANY)] + [VMEM] * 2,
         out_specs=VMEM,
         compiler_params=params(),
@@ -262,24 +271,14 @@
     )(after, xt, panel)
 
 
-def total_kernel(after_ref, *refs):
-    del after_ref
-    value = refs[0][...]
-    for ref in refs[1:-1]:
-        value = value + ref[...]
-    refs[-1][...] = value
-
-
-def total(after, parts):
-    n = parts[0].shape[0]
-    return pl.pallas_call(
-        total_kernel,
-        out_shape=jax.ShapeDtypeStruct((n, n), F32),
-        in_specs=[pl.BlockSpec(memory_space=pl.ANY)] + [VMEM] * len(parts),
-        out_specs=VMEM,
-        compiler_params=params(),
-        name="total",
-    )(after, *parts)
+def total(parts):
+    parts = [part.astype(F32) for part in parts]
+    n = parts[0].shape[1]
+    exponents = [part[n : n + 1, 0:1] for part in parts]
+    value = sum(part[:n] * jnp.exp2(exponent - TOP) for part, exponent in zip(parts, exponents))
+    exponent = functools.reduce(jnp.maximum, exponents) + 2.0
+    packed = jnp.concatenate([value * jnp.exp2(TOP - exponent), jnp.broadcast_to(exponent, (TAIL, n))])
+    return value, packed.astype(jnp.float16)
 
 
 def merge_kernel(pos_ref, after_ref, *refs):
@@ -290,7 +289,7 @@
     chip, group, core = pos_ref[0], pos_ref[1], pos_ref[2]
 
     def put(own_ref, cross_ref):
-        t_ref[0:n] = own_ref[...].T + cross_ref[...]
+        t_ref[0:n] = own_ref[...].T + cross_ref[0:n] * jnp.exp2(cross_ref[n : n + 1, 0:1] - TOP)
 
     distant = jnp.abs(chip - group) == 2
     pl.when(jnp.logical_not(distant))(lambda: put(*sums[:2]))
@@ -407,12 +406,14 @@
     near_homes = {pair: home for pair, home in homes.items() if pair not in far_homes}
 
     def gathered(block, group_homes):
+        half = block.astype(jnp.float16)
         return [block] + [
-            send(block, [(at(k ^ m, z, c), at(k, z, c)) for k, z, c in group_homes.values()]) for m in range(1, groups)
+            send(half, [(at(k ^ m, z, c), at(k, z, c)) for k, z, c in group_homes.values()]) for m in range(1, groups)
         ]
 
-    def exchanged(own, group_homes):
-        return send(own, [(at(*home), at(*homes[z, k])) for (k, z), home in group_homes.items()])
+    def exchanged(packed, group_homes):
+        received = send(packed, [(at(*home), at(*homes[z, k])) for (k, z), home in group_homes.items()])
+        return received.astype(F32)
 
     near_block = pair_block(state[0], xt, near)
     near_parts = gathered(near_block, near_homes)
@@ -420,10 +421,10 @@
     far_block = pair_block(state[0], xt, far)
     far_parts = gathered(far_block, far_homes)
     state = factor_part(2, 1, state, (far_block,))
-    near_own = total(state[0], near_parts)
-    near_cross = exchanged(near_own, near_homes)
-    far_own = total(state[0], far_parts)
-    far_cross = exchanged(far_own, far_homes)
+    near_own, packed = total([passed(near_parts[0], state[0])] + near_parts[1:])
+    near_cross = exchanged(packed, near_homes)
+    far_own, packed = total(far_parts)
+    far_cross = exchanged(packed, far_homes)
     w = factor_part(3, 1, state, (far_own,))[1]
     mine, sib, top = merge(pos, w, (near_own, near_cross), (far_own, far_cross))
     sib = send(sib, [(at(k, z, c), at(k, z, 1 - c)) for k, z, c in homes.values()])

time: 66.3 us -> 76.9 us (1.16)
  between operations: 0.3 us -> 11 us
  local copies, waits for them, and re-layouts: 1.76 us -> 6.12 us
  waiting for transfers between devices: 15.5 us -> 12.3 us
  starting transfers between devices: 30.6 us -> 28.6 us
    slice x0 -> x8, local copies, waits for them, and re-layouts: none -> 4.3 us  [total(): exponents = [part[n:n + 1, 0:1] for part in parts]]
    ppermute x17, waiting for transfers between devices: 15.5 us -> 12.3 us  [send(): return lax.ppermute(value, axes, pairs)]
    ppermute x17, starting transfers between devices: 26.8 us -> 24.8 us  [send(): return lax.ppermute(value, axes, pairs)]
  transfers between devices with their start and end apart: 19 -> 19, of which waited for: 8 -> 6; matrix products, arithmetic and copies ran while one was open for 0% -> 6% of each run, Pallas kernels for 21% -> 17%
where the time goes in v9:
time: 76.9 us; the launch traced here: 76.4 us
  starting transfers between devices  28.6 us (37%)
  Pallas kernels  17.1 us (22%)
  waiting for transfers between devices  12.3 us (16%)
  between operations  11 us (14%)
  local copies, waits for them, and re-layouts  6.12 us (8%)
  other arithmetic  1.24 us (2%)
    ppermute x17, starting transfers between devices, send(): return lax.ppermute(value, axes, pairs)  24.8 us
    ppermute x17, waiting for transfers between devices, send(): return lax.ppermute(value, axes, pairs)  12.3 us
    pallas_call x4, Pallas kernels, factor_part(): pl.pallas_call(kernel, out_shape=(jax.ShapeDtypeStruct((n, n), F32),) * 2...  11.7 us
    slice x8, local copies, waits for them, and re-layouts, total(): exponents = [part[n:n + 1, 0:1] for part in parts]  4.3 us
    ppermute x1, starting transfers between devices, start(): far = lax.ppermute(jnp.where(odd == 0, head, tail), 'space', outside)  3.02 us
    unnamed x4, local copies, waits for them, and re-layouts  1.66 us
    pallas_call x1, Pallas kernels, tiles(): pl.pallas_call(tiles_kernel, out_shape=jax.ShapeDtypeStruct((n, half), F3...  1.62 us
  transfers between devices with their start and end apart: 19, of which 6 were waited for; matrix products, arithmetic and copies ran while one was open for 6% of the time, Pallas kernels for 17%

profile of v9, /device:TPU:5, one launch (start us, length us, event | category | flops | bytes accessed | tf_op | source)
XLA Modules:
  0.0 76.4 jit_solution(4608753633443882432)
XLA Ops:
  0.0 0.7 broadcast_select_fusion
  0.7 0.7 collective-permute-start
  1.5 3.0 %collective-permute-start.1 = (bf16[3,1,256]{2,1,0:T(2,128)(2,1)S(1)}, bf16[3,1,256]{2,1,0:T(2,128)(2,1)S(1)}, u32[]{:S(2)}, u32[]{:S(2)}) collective-permute-start(bf16[3,1,256]{2,1,0:T(2,128)(2,1)S(1)} %get-tuple-element.43), channel_id=1, source_target_pairs={{4,8},{12,16},{20,24},{8,4},{16,12},{24,20},{5,9},{13,17},{21,25},... | collective-permute-start | bytes 4616 | tf_op jit(solution)/shard_map/ppermute | solution.py:362
  5.3 1.1 %copy-done = bf16[3,384,256]{2,1,0:T(8,128)(2,1)S(1)} copy-done((bf16[3,384,256]{2,1,0:T(8,128)(2,1)S(1)}, bf16[3,384,256]{2,1,0:T(8,128)(2,1)}, u32[]{:S(2)}) %copy-start) | copy-done | bytes 589848
  6.8 1.0 %panel.1 = (bf16[1152,256]{1,0:T(8,128)(2,1)S(1)}, bf16[256,1152]{1,0:T(8,128)(2,1)S(1)}, f32[192,128]{1,0:T(8,128)S(1)}, f32[192,128]{1,0:T(8,128)S(1)}) custom-call(s32[4]{0:T(128)S(1)} %pad_add_fusion.pos_ref, bf16[1152,256]{1,0:T(8,128)(2,1)S(1)} %get-tuple-element.22.x_in_ref, f32[3,8,256]{2,1,0:T(8,128)S(1)} %get-tuple-element.23.head_ref, ...), custom_call_target="tpu_custom_call" | custom-call | flops 150994944 | bytes 1769472 | tf_op jit(solution)/shard_map/panel/pallas_call | solution.py:112
  7.8 3.4 %collective-permute-start.7 = (bf16[1152,256]{1,0:T(8,128)(2,1)S(1)}, bf16[1152,256]{1,0:T(8,128)(2,1)S(1)}, u32[]{:S(2)}, u32[]{:S(2)}) collective-permute-start(bf16[1152,256]{1,0:T(8,128)(2,1)S(1)} %get-tuple-element.30), channel_id=1, source_target_pairs={{0,1},{1,2},{2,3},{3,0},{8,9},{9,10},{10,11},{11,8},{16,17},{17,18... | collective-permute-start | bytes 1769480 | tf_op jit(solution)/shard_map/ppermute | solution.py:378
  11.2 1.3 %collective-permute-done.2 = f32[192,128]{1,0:T(8,128)S(1)} collective-permute-done((f32[192,128]{1,0:T(8,128)S(1)}, f32[192,128]{1,0:T(8,128)S(1)}, u32[]{:S(2)}, u32[]{:S(2)}) %collective-permute-start.2) | collective-permute-done | bytes 98336 | tf_op jit(solution)/shard_map/ppermute | solution.py:378
  12.5 1.7 %collective-permute-start.5 = (f32[192,128]{1,0:T(8,128)S(1)}, f32[192,128]{1,0:T(8,128)S(1)}, u32[]{:S(2)}, u32[]{:S(2)}) collective-permute-start(f32[192,128]{1,0:T(8,128)S(1)} %add.54), channel_id=1, source_target_pairs={{0,24},{4,28},{1,25},{5,29},{2,26},{6,30},{3,27},{7,31},{8,16},{12... | collective-permute-start | bytes 294920 | tf_op jit(solution)/shard_map/ppermute | solution.py:378
  14.2 1.0 %collective-permute-start.3 = (f32[192,128]{1,0:T(8,128)S(1)}, f32[192,128]{1,0:T(8,128)S(1)}, u32[]{:S(2)}, u32[]{:S(2)}) collective-permute-start(f32[192,128]{1,0:T(8,128)S(1)} %add.54), channel_id=1, source_target_pairs={{0,8},{4,12},{1,9},{5,13},{2,10},{6,14},{3,11},{7,15},{8,0},{12,4}... | collective-permute-start | bytes 294920 | tf_op jit(solution)/shard_map/ppermute | solution.py:378
  15.2 2.5 %collective-permute-done.5 = f32[192,128]{1,0:T(8,128)S(1)} collective-permute-done((f32[192,128]{1,0:T(8,128)S(1)}, f32[192,128]{1,0:T(8,128)S(1)}, u32[]{:S(2)}, u32[]{:S(2)}) %collective-permute-start.5) | collective-permute-done | bytes 98336 | tf_op jit(solution)/shard_map/ppermute | solution.py:378
  17.7 2.6 %collective-permute-done.4 = f32[192,128]{1,0:T(8,128)S(1)} collective-permute-done((f32[192,128]{1,0:T(8,128)S(1)}, f32[192,128]{1,0:T(8,128)S(1)}, u32[]{:S(2)}, u32[]{:S(2)}) %collective-permute-start.4) | collective-permute-done | bytes 98336 | tf_op jit(solution)/shard_map/ppermute | solution.py:378
  20.9 0.9 %collective-permute-done.6.theirs_ref = f32[192,128]{1,0:T(8,128)S(1)} collective-permute-done((f32[192,128]{1,0:T(8,128)S(1)}, f32[192,128]{1,0:T(8,128)S(1)}, u32[]{:S(2)}, u32[]{:S(2)}) %collective-permute-start.6) | collective-permute-done | bytes 98336 | tf_op jit(solution)/shard_map/ppermute | solution.py:378
  21.8 0.6 gather.1.refs_0_.g_ref
  22.5 3.0 %factor.4 = (f32[256,256]{1,0:T(8,128)S(1)}, f32[256,256]{1,0:T(8,128)S(1)}) custom-call(f32[256,256]{1,0:T(8,128)S(1)} %gather.1.refs_0_.g_ref), custom_call_target="tpu_custom_call" | custom-call | flops 33554432 | bytes 524288 | tf_op jit(solution)/shard_map/factor/pallas_call | solution.py:227
  25.5 1.3 %collective-permute-start.8 = (bf16[1152,256]{1,0:T(8,128)(2,1)S(1)}, bf16[1152,256]{1,0:T(8,128)(2,1)S(1)}, u32[]{:S(2)}, u32[]{:S(2)}) collective-permute-start(bf16[1152,256]{1,0:T(8,128)(2,1)S(1)} %passed.2.panel_ref), channel_id=1, source_target_pairs={{1,2},{2,3},{9,10},{10,11},{17,18},{18,19},{25,26},{26,27},{6,5},{... | collective-permute-start | bytes 1769480 | tf_op jit(solution)/shard_map/ppermute | solution.py:378
  27.3 0.7 collective-permute-start.12
  28.0 0.7 collective-permute-start.13
  28.7 4.6 %collective-permute-start.14 = (f16[272,256]{1,0:T(8,128)(2,1)S(1)}, f16[272,256]{1,0:T(8,128)(2,1)S(1)}, u32[]{:S(2)}, u32[]{:S(2)}) collective-permute-start(f16[272,256]{1,0:T(8,128)(2,1)S(1)} %convert_element_type.36), channel_id=1, source_target_pairs={{25,1},{31,7},{20,12},{18,10},{13,21},{11,19},{0,24},{6,30}} | collective-permute-start | bytes 417800 | tf_op jit(solution)/shard_map/ppermute | solution.py:378
  33.3 2.9 %factor.5 = (f32[256,256]{1,0:T(8,128)S(1)}, f32[256,256]{1,0:T(8,128)S(1)}) custom-call(f32[256,256]{1,0:T(8,128)S(1)} %get-tuple-element.27.refs_1_.after_ref.refs_0_, f32[256,256]{1,0:T(8,128)S(1)} %get-tuple-element.28.refs_1_, f32[272,256]{1,0:T(8,128)S(1)} %block.2.refs_2_.refs_0_), custom_call_target="tpu_custom_call" | custom-call | flops 33554432 | bytes 524288 | tf_op jit(solution)/shard_map/factor/pallas_call | solution.py:227
  40.8 1.3 %collective-permute-start.9 = (f16[272,256]{1,0:T(8,128)(2,1)S(1)}, f16[272,256]{1,0:T(8,128)(2,1)S(1)}, u32[]{:S(2)}, u32[]{:S(2)}) collective-permute-start(f16[272,256]{1,0:T(8,128)(2,1)S(1)} %convert_element_type.32), channel_id=1, source_target_pairs={{10,2},{3,11},{28,20},{21,29}} | collective-permute-start | bytes 417800 | tf_op jit(solution)/shard_map/ppermute | solution.py:378
  42.1 1.3 %collective-permute-start.10 = (f16[272,256]{1,0:T(8,128)(2,1)S(1)}, f16[272,256]{1,0:T(8,128)(2,1)S(1)}, u32[]{:S(2)}, u32[]{:S(2)}) collective-permute-start(f16[272,256]{1,0:T(8,128)(2,1)S(1)} %convert_element_type.32), channel_id=1, source_target_pairs={{18,2},{27,11},{4,20},{13,29}} | collective-permute-start | bytes 417800 | tf_op jit(solution)/shard_map/ppermute | solution.py:378
  43.4 1.3 %collective-permute-start.11 = (f16[272,256]{1,0:T(8,128)(2,1)S(1)}, f16[272,256]{1,0:T(8,128)(2,1)S(1)}, u32[]{:S(2)}, u32[]{:S(2)}) collective-permute-start(f16[272,256]{1,0:T(8,128)(2,1)S(1)} %convert_element_type.32), channel_id=1, source_target_pairs={{26,2},{19,11},{12,20},{5,29}} | collective-permute-start | bytes 417800 | tf_op jit(solution)/shard_map/ppermute | solution.py:378
  44.7 2.8 %factor.6 = (f32[256,256]{1,0:T(8,128)S(1)}, f32[256,256]{1,0:T(8,128)S(1)}) custom-call(f32[256,256]{1,0:T(8,128)S(1)} %get-tuple-element.31.after_ref.refs_0_, f32[256,256]{1,0:T(8,128)S(1)} %get-tuple-element.32.refs_1_, f32[272,256]{1,0:T(8,128)S(1)} %block.3.refs_2_), custom_call_target="tpu_custom_call" | custom-call | flops 33554432 | bytes 524288 | tf_op jit(solution)/shard_map/factor/pallas_call | solution.py:227
  52.2 0.7 collective-permute-start.15
  59.5 3.2 %collective-permute-start.16 = (f16[272,256]{1,0:T(8,128)(2,1)S(1)}, f16[272,256]{1,0:T(8,128)(2,1)S(1)}, u32[]{:S(2)}, u32[]{:S(2)}) collective-permute-start(f16[272,256]{1,0:T(8,128)(2,1)S(1)} %concatenate.7), channel_id=1, source_target_pairs={{2,20},{11,29},{20,2},{29,11}} | collective-permute-start | bytes 417800 | tf_op jit(solution)/shard_map/ppermute | solution.py:378
  62.7 3.0 %factor.7 = (f32[256,256]{1,0:T(8,128)}, f32[256,256]{1,0:T(8,128)S(1)}) custom-call(f32[256,256]{1,0:T(8,128)S(1)} %get-tuple-element.33.refs_0_.refs_1_, f32[256,256]{1,0:T(8,128)S(1)} %get-tuple-element.34.refs_1_, f32[256,256]{1,0:T(8,128)S(1)} %get-tuple-element.40.refs_2_), custom_call_target="tpu_custom_call" | custom-call | flops 33554432 | bytes 524288 | tf_op jit(solution)/shard_map/factor/pallas_call | solution.py:227
  65.8 1.9 %collective-permute-done.16 = f16[272,256]{1,0:T(8,128)(2,1)S(1)} collective-permute-done((f16[272,256]{1,0:T(8,128)(2,1)S(1)}, f16[272,256]{1,0:T(8,128)(2,1)S(1)}, u32[]{:S(2)}, u32[]{:S(2)}) %collective-permute-start.16) | collective-permute-done | bytes 139296 | tf_op jit(solution)/shard_map/ppermute | solution.py:378
  67.7 0.7 merge.1
  68.5 1.3 %collective-permute-start.17 = (f32[136,256]{1,0:T(8,128)S(1)}, f32[136,256]{1,0:T(8,128)S(1)}, u32[]{:S(2)}, u32[]{:S(2)}) collective-permute-start(f32[136,256]{1,0:T(8,128)S(1)} %get-tuple-element.37), channel_id=1, source_target_pairs={{1,5},{2,6},{7,3},{12,8},{10,14},{11,15},{20,16},{21,17},{19,23},{... | collective-permute-start | bytes 417800 | tf_op jit(solution)/shard_map/ppermute | solution.py:378
  69.8 1.9 %collective-permute-start.18 = (f32[8,256]{1,0:T(8,128)S(1)}, f32[8,256]{1,0:T(8,128)S(1)}, u32[]{:S(2)}, u32[]{:S(2)}) collective-permute-start(f32[8,256]{1,0:T(8,128)S(1)} %get-tuple-element.38), channel_id=1, source_target_pairs={{1,29},{2,30},{7,31},{12,4},{10,6},{11,7},{20,12},{21,13},{19,15},... | collective-permute-start | bytes 24584 | tf_op jit(solution)/shard_map/ppermute | solution.py:378
  71.7 3.0 %collective-permute-done.18.top_ref = f32[8,256]{1,0:T(8,128)S(1)} collective-permute-done((f32[8,256]{1,0:T(8,128)S(1)}, f32[8,256]{1,0:T(8,128)S(1)}, u32[]{:S(2)}, u32[]{:S(2)}) %collective-permute-start.18) | collective-permute-done | bytes 8224 | tf_op jit(solution)/shard_map/ppermute | solution.py:378
  74.7 1.6 %tiles.1 = f32[256,128]{1,0:T(8,128)} custom-call(s32[4]{0:T(128)S(1)} %pad_add_fusion.pos_ref, f32[256,256]{1,0:T(8,128)S(1)} %get-tuple-element.35.after_ref.w_ref, f32[256,256]{1,0:T(8,128)S(1)} %gather.1.refs_0_.g_ref, f32[136,256]{1,0:T(8,128)S(1)} %get-tuple-element.36.own_ref, f32[136,256]{1,0:T(8,128)S(1)} %collective-permute-done.17.sib_ref, ...), custom_call_target="tpu_custom_call" | custom-call | tf_op jit(solution)/shard_map/tiles/pallas_call | solution.py:342
  (50 shorter events, 7.5 us)
Async XLA Ops:
  0.7 6.1 %collective-permute-start = (bf16[3,1,256]{2,1,0:T(2,128)(2,1)S(1)}, bf16[3,1,256]{2,1,0:T(2,128)(2,1)S(1)}, u32[]{:S(2)}, u32[]{:S(2)}) collective-permute-start(bf16[3,1,256]{2,1,0:T(2,128)(2,1)S(1)} %get-tuple-element.44), channel_id=1, source_target_pairs={{0,4},{4,0},{8,12},{12,8},{16,20},{20,16},{24,28},{28,24},{1,5},{5... | collective-permute-start | bytes 4616 | tf_op jit(solution)/shard_map/ppermute | solution.py:363
  1.5 5.3 %collective-permute-start.1 = (bf16[3,1,256]{2,1,0:T(2,128)(2,1)S(1)}, bf16[3,1,256]{2,1,0:T(2,128)(2,1)S(1)}, u32[]{:S(2)}, u32[]{:S(2)}) collective-permute-start(bf16[3,1,256]{2,1,0:T(2,128)(2,1)S(1)} %get-tuple-element.43), channel_id=1, source_target_pairs={{4,8},{12,16},{20,24},{8,4},{16,12},{24,20},{5,9},{13,17},{21,25},... | collective-permute-start | bytes 4616 | tf_op jit(solution)/shard_map/ppermute | solution.py:362
  4.5 0.7 copy-start.1
  5.3 1.1 %copy-start = (bf16[3,384,256]{2,1,0:T(8,128)(2,1)S(1)}, bf16[3,384,256]{2,1,0:T(8,128)(2,1)}, u32[]{:S(2)}) copy-start(bf16[3,384,256]{2,1,0:T(8,128)(2,1)} %vel_ref.1) | copy-start | bytes 1769476
  7.8 17.7 %collective-permute-start.7 = (bf16[1152,256]{1,0:T(8,128)(2,1)S(1)}, bf16[1152,256]{1,0:T(8,128)(2,1)S(1)}, u32[]{:S(2)}, u32[]{:S(2)}) collective-permute-start(bf16[1152,256]{1,0:T(8,128)(2,1)S(1)} %get-tuple-element.30), channel_id=1, source_target_pairs={{0,1},{1,2},{2,3},{3,0},{8,9},{9,10},{10,11},{11,8},{16,17},{17,18... | collective-permute-start | bytes 1769480 | tf_op jit(solution)/shard_map/ppermute | solution.py:378
  11.2 1.3 %collective-permute-start.2 = (f32[192,128]{1,0:T(8,128)S(1)}, f32[192,128]{1,0:T(8,128)S(1)}, u32[]{:S(2)}, u32[]{:S(2)}) collective-permute-start(f32[192,128]{1,0:T(8,128)S(1)} %get-tuple-element.26), channel_id=1, source_target_pairs={{0,4},{4,0},{1,5},{5,1},{2,6},{6,2},{3,7},{7,3},{8,12},{12,8},{9,1... | collective-permute-start | bytes 294920 | tf_op jit(solution)/shard_map/ppermute | solution.py:378
  12.5 5.2 %collective-permute-start.5 = (f32[192,128]{1,0:T(8,128)S(1)}, f32[192,128]{1,0:T(8,128)S(1)}, u32[]{:S(2)}, u32[]{:S(2)}) collective-permute-start(f32[192,128]{1,0:T(8,128)S(1)} %add.54), channel_id=1, source_target_pairs={{0,24},{4,28},{1,25},{5,29},{2,26},{6,30},{3,27},{7,31},{8,16},{12... | collective-permute-start | bytes 294920 | tf_op jit(solution)/shard_map/ppermute | solution.py:378
  14.2 6.1 %collective-permute-start.4 = (f32[192,128]{1,0:T(8,128)S(1)}, f32[192,128]{1,0:T(8,128)S(1)}, u32[]{:S(2)}, u32[]{:S(2)}) collective-permute-start(f32[192,128]{1,0:T(8,128)S(1)} %add.54), channel_id=1, source_target_pairs={{0,16},{4,20},{1,17},{5,21},{2,18},{6,22},{3,19},{7,23},{8,24},{12... | collective-permute-start | bytes 294920 | tf_op jit(solution)/shard_map/ppermute | solution.py:378
  14.2 6.1 %collective-permute-start.3 = (f32[192,128]{1,0:T(8,128)S(1)}, f32[192,128]{1,0:T(8,128)S(1)}, u32[]{:S(2)}, u32[]{:S(2)}) collective-permute-start(f32[192,128]{1,0:T(8,128)S(1)} %add.54), channel_id=1, source_target_pairs={{0,8},{4,12},{1,9},{5,13},{2,10},{6,14},{3,11},{7,15},{8,0},{12,4}... | collective-permute-start | bytes 294920 | tf_op jit(solution)/shard_map/ppermute | solution.py:378
  20.3 1.5 %collective-permute-start.6 = (f32[192,128]{1,0:T(8,128)S(1)}, f32[192,128]{1,0:T(8,128)S(1)}, u32[]{:S(2)}, u32[]{:S(2)}) collective-permute-start(f32[192,128]{1,0:T(8,128)S(1)} %add_add_fusion.mine_ref), channel_id=1, source_target_pairs={{0,4},{4,0},{1,5},{5,1},{2,6},{6,2},{3,7},{7,3},{8,12},{12,8},{9,1... | collective-permute-start | bytes 294920 | tf_op jit(solution)/shard_map/ppermute | solution.py:378
  25.5 14.3 %collective-permute-start.8 = (bf16[1152,256]{1,0:T(8,128)(2,1)S(1)}, bf16[1152,256]{1,0:T(8,128)(2,1)S(1)}, u32[]{:S(2)}, u32[]{:S(2)}) collective-permute-start(bf16[1152,256]{1,0:T(8,128)(2,1)S(1)} %passed.2.panel_ref), channel_id=1, source_target_pairs={{1,2},{2,3},{9,10},{10,11},{17,18},{18,19},{25,26},{26,27},{6,5},{... | collective-permute-start | bytes 1769480 | tf_op jit(solution)/shard_map/ppermute | solution.py:378
  27.3 8.9 %collective-permute-start.12 = (f16[272,256]{1,0:T(8,128)(2,1)S(1)}, f16[272,256]{1,0:T(8,128)(2,1)S(1)}, u32[]{:S(2)}, u32[]{:S(2)}) collective-permute-start(f16[272,256]{1,0:T(8,128)(2,1)S(1)} %convert_element_type.36), channel_id=1, source_target_pairs={{9,1},{15,7},{4,12},{2,10},{29,21},{27,19},{16,24},{22,30}} | collective-permute-start | bytes 417800 | tf_op jit(solution)/shard_map/ppermute | solution.py:378
  28.0 8.8 %collective-permute-start.13 = (f16[272,256]{1,0:T(8,128)(2,1)S(1)}, f16[272,256]{1,0:T(8,128)(2,1)S(1)}, u32[]{:S(2)}, u32[]{:S(2)}) collective-permute-start(f16[272,256]{1,0:T(8,128)(2,1)S(1)} %convert_element_type.36), channel_id=1, source_target_pairs={{17,1},{23,7},{28,12},{26,10},{5,21},{3,19},{8,24},{14,30}} | collective-permute-start | bytes 417800 | tf_op jit(solution)/shard_map/ppermute | solution.py:378
  28.7 8.7 %collective-permute-start.14 = (f16[272,256]{1,0:T(8,128)(2,1)S(1)}, f16[272,256]{1,0:T(8,128)(2,1)S(1)}, u32[]{:S(2)}, u32[]{:S(2)}) collective-permute-start(f16[272,256]{1,0:T(8,128)(2,1)S(1)} %convert_element_type.36), channel_id=1, source_target_pairs={{25,1},{31,7},{20,12},{18,10},{13,21},{11,19},{0,24},{6,30}} | collective-permute-start | bytes 417800 | tf_op jit(solution)/shard_map/ppermute | solution.py:378
  40.8 12.0 %collective-permute-start.9 = (f16[272,256]{1,0:T(8,128)(2,1)S(1)}, f16[272,256]{1,0:T(8,128)(2,1)S(1)}, u32[]{:S(2)}, u32[]{:S(2)}) collective-permute-start(f16[272,256]{1,0:T(8,128)(2,1)S(1)} %convert_element_type.32), channel_id=1, source_target_pairs={{10,2},{3,11},{28,20},{21,29}} | collective-permute-start | bytes 417800 | tf_op jit(solution)/shard_map/ppermute | solution.py:378
  42.1 13.4 %collective-permute-start.10 = (f16[272,256]{1,0:T(8,128)(2,1)S(1)}, f16[272,256]{1,0:T(8,128)(2,1)S(1)}, u32[]{:S(2)}, u32[]{:S(2)}) collective-permute-start(f16[272,256]{1,0:T(8,128)(2,1)S(1)} %convert_element_type.32), channel_id=1, source_target_pairs={{18,2},{27,11},{4,20},{13,29}} | collective-permute-start | bytes 417800 | tf_op jit(solution)/shard_map/ppermute | solution.py:378
  43.4 13.9 %collective-permute-start.11 = (f16[272,256]{1,0:T(8,128)(2,1)S(1)}, f16[272,256]{1,0:T(8,128)(2,1)S(1)}, u32[]{:S(2)}, u32[]{:S(2)}) collective-permute-start(f16[272,256]{1,0:T(8,128)(2,1)S(1)} %convert_element_type.32), channel_id=1, source_target_pairs={{26,2},{19,11},{12,20},{5,29}} | collective-permute-start | bytes 417800 | tf_op jit(solution)/shard_map/ppermute | solution.py:378
  52.2 10.5 %collective-permute-start.15 = (f16[272,256]{1,0:T(8,128)(2,1)S(1)}, f16[272,256]{1,0:T(8,128)(2,1)S(1)}, u32[]{:S(2)}, u32[]{:S(2)}) collective-permute-start(f16[272,256]{1,0:T(8,128)(2,1)S(1)} %concatenate.6), channel_id=1, source_target_pairs={{1,12},{7,24},{12,1},{10,21},{21,10},{19,30},{24,7},{30,19}} | collective-permute-start | bytes 417800 | tf_op jit(solution)/shard_map/ppermute | solution.py:378
  59.5 8.2 %collective-permute-start.16 = (f16[272,256]{1,0:T(8,128)(2,1)S(1)}, f16[272,256]{1,0:T(8,128)(2,1)S(1)}, u32[]{:S(2)}, u32[]{:S(2)}) collective-permute-start(f16[272,256]{1,0:T(8,128)(2,1)S(1)} %concatenate.7), channel_id=1, source_target_pairs={{2,20},{11,29},{20,2},{29,11}} | collective-permute-start | bytes 417800 | tf_op jit(solution)/shard_map/ppermute | solution.py:378
  68.5 6.3 %collective-permute-start.17 = (f32[136,256]{1,0:T(8,128)S(1)}, f32[136,256]{1,0:T(8,128)S(1)}, u32[]{:S(2)}, u32[]{:S(2)}) collective-permute-start(f32[136,256]{1,0:T(8,128)S(1)} %get-tuple-element.37), channel_id=1, source_target_pairs={{1,5},{2,6},{7,3},{12,8},{10,14},{11,15},{20,16},{21,17},{19,23},{... | collective-permute-start | bytes 417800 | tf_op jit(solution)/shard_map/ppermute | solution.py:378
  69.8 5.0 %collective-permute-start.18 = (f32[8,256]{1,0:T(8,128)S(1)}, f32[8,256]{1,0:T(8,128)S(1)}, u32[]{:S(2)}, u32[]{:S(2)}) collective-permute-start(f32[8,256]{1,0:T(8,128)S(1)} %get-tuple-element.38), channel_id=1, source_target_pairs={{1,29},{2,30},{7,31},{12,4},{10,6},{11,7},{20,12},{21,13},{19,15},... | collective-permute-start | bytes 24584 | tf_op jit(solution)/shard_map/ppermute | solution.py:378

commit v10 on v9

--- a/solution.py
+++ b/solution.py
@@ -271,13 +271,30 @@
     )(after, xt, panel)
 
 
-def total(parts):
-    parts = [part.astype(F32) for part in parts]
+def total_kernel(after_ref, *refs):
+    del after_ref
+    parts, (value_ref, packed_ref) = refs[:-2], refs[-2:]
+    n = value_ref.shape[0]
+    exponents = [part[n : n + 1] for part in parts]
+    value = parts[0][0:n] * jnp.exp2(exponents[0] - TOP)
+    for part, exponent in zip(parts[1:], exponents[1:]):
+        value = value + part[0:n] * jnp.exp2(exponent - TOP)
+    exponent = functools.reduce(jnp.maximum, exponents) + 2.0
+    value_ref[...] = value
+    packed_ref[0:n] = value * jnp.exp2(TOP - exponent)
+    packed_ref[n:] = jnp.broadcast_to(exponent, (TAIL, n))
+
+
+def total(after, parts):
     n = parts[0].shape[1]
-    exponents = [part[n : n + 1, 0:1] for part in parts]
-    value = sum(part[:n] * jnp.exp2(exponent - TOP) for part, exponent in zip(parts, exponents))
-    exponent = functools.reduce(jnp.maximum, exponents) + 2.0
-    packed = jnp.concatenate([value * jnp.exp2(TOP - exponent), jnp.broadcast_to(exponent, (TAIL, n))])
+    value, packed = pl.pallas_call(
+        total_kernel,
+        out_shape=(jax.ShapeDtypeStruct((n, n), F32), jax.ShapeDtypeStruct((n + TAIL, n), F32)),
+        in_specs=[pl.BlockSpec(memory_space=pl.ANY)] + [VMEM] * len(parts),
+        out_specs=(VMEM,) * 2,
+        compiler_params=params(),
+        name="total",
+    )(after, *[part.astype(F32) for part in parts])
     return value, packed.astype(jnp.float16)
 
 
@@ -289,7 +306,7 @@
     chip, group, core = pos_ref[0], pos_ref[1], pos_ref[2]
 
     def put(own_ref, cross_ref):
-        t_ref[0:n] = own_ref[...].T + cross_ref[0:n] * jnp.exp2(cross_ref[n : n + 1, 0:1] - TOP)
+        t_ref[0:n] = own_ref[...].T + cross_ref[0:n] * jnp.exp2(cross_ref[n : n + 1] - TOP)
 
     distant = jnp.abs(chip - group) == 2
     pl.when(jnp.logical_not(distant))(lambda: put(*sums[:2]))
@@ -421,9 +438,9 @@
     far_block = pair_block(state[0], xt, far)
     far_parts = gathered(far_block, far_homes)
     state = factor_part(2, 1, state, (far_block,))
-    near_own, packed = total([passed(near_parts[0], state[0])] + near_parts[1:])
+    near_own, packed = total(state[0], near_parts)
     near_cross = exchanged(packed, near_homes)
-    far_own, packed = total(far_parts)
+    far_own, packed = total(state[0], far_parts)
     far_cross = exchanged(packed, far_homes)
     w = factor_part(3, 1, state, (far_own,))[1]
     mine, sib, top = merge(pos, w, (near_own, near_cross), (far_own, far_cross))

time: 76.9 us -> 65.1 us (0.85)
  the two profiles are of different devices: /device:TPU:5 before, /device:TPU:3 now
where the time goes in v10:
time: 65.1 us; the launch traced here: 64.7 us
  starting transfers between devices  28.5 us (44%)
  Pallas kernels  17.3 us (27%)
  waiting for transfers between devices  15.6 us (24%)
  local copies, waits for them, and re-layouts  1.76 us (3%)
  other arithmetic  1.09 us (2%)
    ppermute x17, starting transfers between devices, send(): return lax.ppermute(value, axes, pairs)  24.8 us
    ppermute x17, waiting for transfers between devices, send(): return lax.ppermute(value, axes, pairs)  15.2 us
    pallas_call x4, Pallas kernels, factor_part(): pl.pallas_call(kernel, out_shape=(jax.ShapeDtypeStruct((n, n), F32),) * 2...  11.7 us
    ppermute x1, starting transfers between devices, start(): far = lax.ppermute(jnp.where(odd == 0, head, tail), 'space', outside)  3.02 us
    unnamed x4, local copies, waits for them, and re-layouts  1.66 us
    pallas_call x1, Pallas kernels, tiles(): pl.pallas_call(tiles_kernel, out_shape=jax.ShapeDtypeStruct((n, half), F3...  1.62 us
  transfers between devices with their start and end apart: 19, of which 9 were waited for; matrix products, arithmetic and copies ran while one was open for 1% of the time, Pallas kernels for 22%

profile of v10, /device:TPU:3, one launch (start us, length us, event | category | flops | bytes accessed | tf_op | source)
XLA Modules:
  0.0 64.7 jit_solution(2094794462539703217)
XLA Ops:
  0.0 0.7 %broadcast_select_fusion = (bf16[3,1,256]{2,1,0:T(2,128)(2,1)S(1)}, bf16[3,1,256]{2,1,0:T(2,128)(2,1)S(1)}) fusion(pred[]{:T(512)S(6)} %eq.6, bf16[3,384,256]{2,1,0:T(8,128)(2,1)} %vel_ref.1), kind=kLoop, calls=%fused_computation.1 | loop fusion | flops 1536 | bytes 6145 | tf_op jit(solution)/shard_map/jit(_where)/select_n | solution.py:379
  0.7 0.7 %collective-permute-start = (bf16[3,1,256]{2,1,0:T(2,128)(2,1)S(1)}, bf16[3,1,256]{2,1,0:T(2,128)(2,1)S(1)}, u32[]{:S(2)}, u32[]{:S(2)}) collective-permute-start(bf16[3,1,256]{2,1,0:T(2,128)(2,1)S(1)} %get-tuple-element.48), channel_id=1, source_target_pairs={{0,4},{4,0},{8,12},{12,8},{16,20},{20,16},{24,28},{28,24},{1,5},{5... | collective-permute-start | bytes 4616 | tf_op jit(solution)/shard_map/ppermute | solution.py:380
  1.5 3.0 %collective-permute-start.1 = (bf16[3,1,256]{2,1,0:T(2,128)(2,1)S(1)}, bf16[3,1,256]{2,1,0:T(2,128)(2,1)S(1)}, u32[]{:S(2)}, u32[]{:S(2)}) collective-permute-start(bf16[3,1,256]{2,1,0:T(2,128)(2,1)S(1)} %get-tuple-element.47), channel_id=1, source_target_pairs={{4,8},{12,16},{20,24},{8,4},{16,12},{24,20},{5,9},{13,17},{21,25},... | collective-permute-start | bytes 4616 | tf_op jit(solution)/shard_map/ppermute | solution.py:379
  5.3 1.1 %copy-done = bf16[3,384,256]{2,1,0:T(8,128)(2,1)S(1)} copy-done((bf16[3,384,256]{2,1,0:T(8,128)(2,1)S(1)}, bf16[3,384,256]{2,1,0:T(8,128)(2,1)}, u32[]{:S(2)}) %copy-start) | copy-done | bytes 589848
  7.3 1.0 %panel.1 = (bf16[1152,256]{1,0:T(8,128)(2,1)S(1)}, bf16[256,1152]{1,0:T(8,128)(2,1)S(1)}, f32[192,128]{1,0:T(8,128)S(1)}, f32[192,128]{1,0:T(8,128)S(1)}) custom-call(s32[4]{0:T(128)S(1)} %pad_add_fusion.pos_ref, bf16[1152,256]{1,0:T(8,128)(2,1)S(1)} %get-tuple-element.26.x_in_ref, f32[3,8,256]{2,1,0:T(8,128)S(1)} %get-tuple-element.27.head_ref, ...), custom_call_target="tpu_custom_call" | custom-call | flops 150994944 | bytes 1769472 | tf_op jit(solution)/shard_map/panel/pallas_call | solution.py:112
  8.3 3.4 %collective-permute-start.7 = (bf16[1152,256]{1,0:T(8,128)(2,1)S(1)}, bf16[1152,256]{1,0:T(8,128)(2,1)S(1)}, u32[]{:S(2)}, u32[]{:S(2)}) collective-permute-start(bf16[1152,256]{1,0:T(8,128)(2,1)S(1)} %get-tuple-element.34), channel_id=1, source_target_pairs={{0,1},{1,2},{2,3},{3,0},{8,9},{9,10},{10,11},{11,8},{16,17},{17,18... | collective-permute-start | bytes 1769480 | tf_op jit(solution)/shard_map/ppermute | solution.py:395
  11.6 1.3 %collective-permute-done.2 = f32[192,128]{1,0:T(8,128)S(1)} collective-permute-done((f32[192,128]{1,0:T(8,128)S(1)}, f32[192,128]{1,0:T(8,128)S(1)}, u32[]{:S(2)}, u32[]{:S(2)}) %collective-permute-start.2) | collective-permute-done | bytes 98336 | tf_op jit(solution)/shard_map/ppermute | solution.py:395
  13.0 1.0 %collective-permute-start.4 = (f32[192,128]{1,0:T(8,128)S(1)}, f32[192,128]{1,0:T(8,128)S(1)}, u32[]{:S(2)}, u32[]{:S(2)}) collective-permute-start(f32[192,128]{1,0:T(8,128)S(1)} %add.18), channel_id=1, source_target_pairs={{0,16},{4,20},{1,17},{5,21},{2,18},{6,22},{3,19},{7,23},{8,24},{12... | collective-permute-start | bytes 294920 | tf_op jit(solution)/shard_map/ppermute | solution.py:395
  14.1 1.6 %collective-permute-start.5 = (f32[192,128]{1,0:T(8,128)S(1)}, f32[192,128]{1,0:T(8,128)S(1)}, u32[]{:S(2)}, u32[]{:S(2)}) collective-permute-start(f32[192,128]{1,0:T(8,128)S(1)} %add.18), channel_id=1, source_target_pairs={{0,24},{4,28},{1,25},{5,29},{2,26},{6,30},{3,27},{7,31},{8,16},{12... | collective-permute-start | bytes 294920 | tf_op jit(solution)/shard_map/ppermute | solution.py:395
  15.7 1.6 %collective-permute-done.3 = f32[192,128]{1,0:T(8,128)S(1)} collective-permute-done((f32[192,128]{1,0:T(8,128)S(1)}, f32[192,128]{1,0:T(8,128)S(1)}, u32[]{:S(2)}, u32[]{:S(2)}) %collective-permute-start.3) | collective-permute-done | bytes 98336 | tf_op jit(solution)/shard_map/ppermute | solution.py:395
  17.3 1.4 %collective-permute-done.5 = f32[192,128]{1,0:T(8,128)S(1)} collective-permute-done((f32[192,128]{1,0:T(8,128)S(1)}, f32[192,128]{1,0:T(8,128)S(1)}, u32[]{:S(2)}, u32[]{:S(2)}) %collective-permute-start.5) | collective-permute-done | bytes 98336 | tf_op jit(solution)/shard_map/ppermute | solution.py:395
  18.8 1.7 %collective-permute-start.6 = (f32[192,128]{1,0:T(8,128)S(1)}, f32[192,128]{1,0:T(8,128)S(1)}, u32[]{:S(2)}, u32[]{:S(2)}) collective-permute-start(f32[192,128]{1,0:T(8,128)S(1)} %add_add_fusion.mine_ref), channel_id=1, source_target_pairs={{0,4},{4,0},{1,5},{5,1},{2,6},{6,2},{3,7},{7,3},{8,12},{12,8},{9,1... | collective-permute-start | bytes 294920 | tf_op jit(solution)/shard_map/ppermute | solution.py:395
  20.5 0.9 %collective-permute-done.6.theirs_ref = f32[192,128]{1,0:T(8,128)S(1)} collective-permute-done((f32[192,128]{1,0:T(8,128)S(1)}, f32[192,128]{1,0:T(8,128)S(1)}, u32[]{:S(2)}, u32[]{:S(2)}) %collective-permute-start.6) | collective-permute-done | bytes 98336 | tf_op jit(solution)/shard_map/ppermute | solution.py:395
  22.1 3.0 %factor.4 = (f32[256,256]{1,0:T(8,128)S(1)}, f32[256,256]{1,0:T(8,128)S(1)}) custom-call(f32[256,256]{1,0:T(8,128)S(1)} %gather.1.refs_0_.g_ref), custom_call_target="tpu_custom_call" | custom-call | flops 33554432 | bytes 524288 | tf_op jit(solution)/shard_map/factor/pallas_call | solution.py:227
  25.1 1.3 %collective-permute-start.8 = (bf16[1152,256]{1,0:T(8,128)(2,1)S(1)}, bf16[1152,256]{1,0:T(8,128)(2,1)S(1)}, u32[]{:S(2)}, u32[]{:S(2)}) collective-permute-start(bf16[1152,256]{1,0:T(8,128)(2,1)S(1)} %passed.1.panel_ref), channel_id=1, source_target_pairs={{1,2},{2,3},{9,10},{10,11},{17,18},{18,19},{25,26},{26,27},{6,5},{... | collective-permute-start | bytes 1769480 | tf_op jit(solution)/shard_map/ppermute | solution.py:395
  27.0 1.3 %collective-permute-start.12 = (f16[272,256]{1,0:T(8,128)(2,1)S(1)}, f16[272,256]{1,0:T(8,128)(2,1)S(1)}, u32[]{:S(2)}, u32[]{:S(2)}) collective-permute-start(f16[272,256]{1,0:T(8,128)(2,1)S(1)} %convert_element_type.40), channel_id=1, source_target_pairs={{9,1},{15,7},{4,12},{2,10},{29,21},{27,19},{16,24},{22,30}} | collective-permute-start | bytes 417800 | tf_op jit(solution)/shard_map/ppermute | solution.py:395
  28.3 1.3 %collective-permute-start.13 = (f16[272,256]{1,0:T(8,128)(2,1)S(1)}, f16[272,256]{1,0:T(8,128)(2,1)S(1)}, u32[]{:S(2)}, u32[]{:S(2)}) collective-permute-start(f16[272,256]{1,0:T(8,128)(2,1)S(1)} %convert_element_type.40), channel_id=1, source_target_pairs={{17,1},{23,7},{28,12},{26,10},{5,21},{3,19},{8,24},{14,30}} | collective-permute-start | bytes 417800 | tf_op jit(solution)/shard_map/ppermute | solution.py:395
  29.6 1.3 %collective-permute-start.14 = (f16[272,256]{1,0:T(8,128)(2,1)S(1)}, f16[272,256]{1,0:T(8,128)(2,1)S(1)}, u32[]{:S(2)}, u32[]{:S(2)}) collective-permute-start(f16[272,256]{1,0:T(8,128)(2,1)S(1)} %convert_element_type.40), channel_id=1, source_target_pairs={{25,1},{31,7},{20,12},{18,10},{13,21},{11,19},{0,24},{6,30}} | collective-permute-start | bytes 417800 | tf_op jit(solution)/shard_map/ppermute | solution.py:395
  30.9 2.9 %factor.5 = (f32[256,256]{1,0:T(8,128)S(1)}, f32[256,256]{1,0:T(8,128)S(1)}) custom-call(f32[256,256]{1,0:T(8,128)S(1)} %get-tuple-element.31.refs_1_.after_ref.refs_0_, f32[256,256]{1,0:T(8,128)S(1)} %get-tuple-element.32.refs_1_, f32[272,256]{1,0:T(8,128)S(1)} %block.2.refs_2_.refs_0_), custom_call_target="tpu_custom_call" | custom-call | flops 33554432 | bytes 524288 | tf_op jit(solution)/shard_map/factor/pallas_call | solution.py:227
  33.8 2.0 %collective-permute-done.8.panel_ref = bf16[1152,256]{1,0:T(8,128)(2,1)S(1)} collective-permute-done((bf16[1152,256]{1,0:T(8,128)(2,1)S(1)}, bf16[1152,256]{1,0:T(8,128)(2,1)S(1)}, u32[]{:S(2)}, u32[]{:S(2)}) %collective-permute-start.8) | collective-permute-done | bytes 589856 | tf_op jit(solution)/shard_map/ppermute | solution.py:395
  36.3 0.7 %collective-permute-start.9 = (f16[272,256]{1,0:T(8,128)(2,1)S(1)}, f16[272,256]{1,0:T(8,128)(2,1)S(1)}, u32[]{:S(2)}, u32[]{:S(2)}) collective-permute-start(f16[272,256]{1,0:T(8,128)(2,1)S(1)} %convert_element_type.36), channel_id=1, source_target_pairs={{10,2},{3,11},{28,20},{21,29}} | collective-permute-start | bytes 417800 | tf_op jit(solution)/shard_map/ppermute | solution.py:395
  37.0 0.7 %collective-permute-start.10 = (f16[272,256]{1,0:T(8,128)(2,1)S(1)}, f16[272,256]{1,0:T(8,128)(2,1)S(1)}, u32[]{:S(2)}, u32[]{:S(2)}) collective-permute-start(f16[272,256]{1,0:T(8,128)(2,1)S(1)} %convert_element_type.36), channel_id=1, source_target_pairs={{18,2},{27,11},{4,20},{13,29}} | collective-permute-start | bytes 417800 | tf_op jit(solution)/shard_map/ppermute | solution.py:395
  37.6 4.7 %collective-permute-start.11 = (f16[272,256]{1,0:T(8,128)(2,1)S(1)}, f16[272,256]{1,0:T(8,128)(2,1)S(1)}, u32[]{:S(2)}, u32[]{:S(2)}) collective-permute-start(f16[272,256]{1,0:T(8,128)(2,1)S(1)} %convert_element_type.36), channel_id=1, source_target_pairs={{26,2},{19,11},{12,20},{5,29}} | collective-permute-start | bytes 417800 | tf_op jit(solution)/shard_map/ppermute | solution.py:395
  42.4 2.8 %factor.6 = (f32[256,256]{1,0:T(8,128)S(1)}, f32[256,256]{1,0:T(8,128)S(1)}) custom-call(f32[256,256]{1,0:T(8,128)S(1)} %get-tuple-element.35.after_ref.refs_0_, f32[256,256]{1,0:T(8,128)S(1)} %get-tuple-element.36.refs_1_, f32[272,256]{1,0:T(8,128)S(1)} %block.3.refs_2_.refs_0_), custom_call_target="tpu_custom_call" | custom-call | flops 33554432 | bytes 524288 | tf_op jit(solution)/shard_map/factor/pallas_call | solution.py:227
  45.4 1.9 %collective-permute-start.15 = (f16[272,256]{1,0:T(8,128)(2,1)S(1)}, f16[272,256]{1,0:T(8,128)(2,1)S(1)}, u32[]{:S(2)}, u32[]{:S(2)}) collective-permute-start(f16[272,256]{1,0:T(8,128)(2,1)S(1)} %convert_element_type.44), channel_id=1, source_target_pairs={{1,12},{7,24},{12,1},{10,21},{21,10},{19,30},{24,7},{30,19}} | collective-permute-start | bytes 417800 | tf_op jit(solution)/shard_map/ppermute | solution.py:395
  48.2 4.4 %collective-permute-done.15 = f16[272,256]{1,0:T(8,128)(2,1)S(1)} collective-permute-done((f16[272,256]{1,0:T(8,128)(2,1)S(1)}, f16[272,256]{1,0:T(8,128)(2,1)S(1)}, u32[]{:S(2)}, u32[]{:S(2)}) %collective-permute-start.15) | collective-permute-done | bytes 139296 | tf_op jit(solution)/shard_map/ppermute | solution.py:395
  52.6 3.0 %factor.7 = (f32[256,256]{1,0:T(8,128)}, f32[256,256]{1,0:T(8,128)S(1)}) custom-call(f32[256,256]{1,0:T(8,128)S(1)} %get-tuple-element.37.after_ref.refs_0_, f32[256,256]{1,0:T(8,128)S(1)} %get-tuple-element.38.refs_1_, f32[256,256]{1,0:T(8,128)S(1)} %get-tuple-element.39.refs_2_), custom_call_target="tpu_custom_call" | custom-call | flops 33554432 | bytes 524288 | tf_op jit(solution)/shard_map/factor/pallas_call | solution.py:227
  55.7 0.7 %merge.1 = (f32[136,256]{1,0:T(8,128)S(1)}, f32[136,256]{1,0:T(8,128)S(1)}, f32[8,256]{1,0:T(8,128)S(1)}) custom-call(s32[4]{0:T(128)S(1)} %pad_add_fusion.pos_ref, f32[256,256]{1,0:T(8,128)S(1)} %get-tuple-element.40.after_ref.w_ref, f32[256,256]{1,0:T(8,128)S(1)} %get-tuple-element.41.refs_0_, f32[272,256]{1,0:T(8,128)S(1)} %convert_element_type.45.refs_1_, ...), custom_call_target="tpu_custom_call" | custom-call | tf_op jit(solution)/shard_map/merge/pallas_call | solution.py:322
  56.4 1.3 %collective-permute-start.17 = (f32[136,256]{1,0:T(8,128)S(1)}, f32[136,256]{1,0:T(8,128)S(1)}, u32[]{:S(2)}, u32[]{:S(2)}) collective-permute-start(f32[136,256]{1,0:T(8,128)S(1)} %get-tuple-element.45), channel_id=1, source_target_pairs={{1,5},{2,6},{7,3},{12,8},{10,14},{11,15},{20,16},{21,17},{19,23},{... | collective-permute-start | bytes 417800 | tf_op jit(solution)/shard_map/ppermute | solution.py:395
  57.7 1.9 %collective-permute-start.18 = (f32[8,256]{1,0:T(8,128)S(1)}, f32[8,256]{1,0:T(8,128)S(1)}, u32[]{:S(2)}, u32[]{:S(2)}) collective-permute-start(f32[8,256]{1,0:T(8,128)S(1)} %get-tuple-element.46), channel_id=1, source_target_pairs={{1,29},{2,30},{7,31},{12,4},{10,6},{11,7},{20,12},{21,13},{19,15},... | collective-permute-start | bytes 24584 | tf_op jit(solution)/shard_map/ppermute | solution.py:395
  59.7 3.4 %collective-permute-done.18.top_ref = f32[8,256]{1,0:T(8,128)S(1)} collective-permute-done((f32[8,256]{1,0:T(8,128)S(1)}, f32[8,256]{1,0:T(8,128)S(1)}, u32[]{:S(2)}, u32[]{:S(2)}) %collective-permute-start.18) | collective-permute-done | bytes 8224 | tf_op jit(solution)/shard_map/ppermute | solution.py:395
  63.0 1.6 %tiles.1 = f32[256,128]{1,0:T(8,128)} custom-call(s32[4]{0:T(128)S(1)} %pad_add_fusion.pos_ref, f32[256,256]{1,0:T(8,128)S(1)} %get-tuple-element.40.after_ref.w_ref, f32[256,256]{1,0:T(8,128)S(1)} %gather.1.refs_0_.g_ref, f32[136,256]{1,0:T(8,128)S(1)} %get-tuple-element.44.own_ref, f32[136,256]{1,0:T(8,128)S(1)} %collective-permute-done.17.sib_ref, ...), custom_call_target="tpu_custom_call" | custom-call | tf_op jit(solution)/shard_map/tiles/pallas_call | solution.py:359
  (41 shorter events, 4.6 us)
Async XLA Ops:
  0.7 6.1 %collective-permute-start = (bf16[3,1,256]{2,1,0:T(2,128)(2,1)S(1)}, bf16[3,1,256]{2,1,0:T(2,128)(2,1)S(1)}, u32[]{:S(2)}, u32[]{:S(2)}) collective-permute-start(bf16[3,1,256]{2,1,0:T(2,128)(2,1)S(1)} %get-tuple-element.48), channel_id=1, source_target_pairs={{0,4},{4,0},{8,12},{12,8},{16,20},{20,16},{24,28},{28,24},{1,5},{5... | collective-permute-start | bytes 4616 | tf_op jit(solution)/shard_map/ppermute | solution.py:380
  1.5 5.8 %collective-permute-start.1 = (bf16[3,1,256]{2,1,0:T(2,128)(2,1)S(1)}, bf16[3,1,256]{2,1,0:T(2,128)(2,1)S(1)}, u32[]{:S(2)}, u32[]{:S(2)}) collective-permute-start(bf16[3,1,256]{2,1,0:T(2,128)(2,1)S(1)} %get-tuple-element.47), channel_id=1, source_target_pairs={{4,8},{12,16},{20,24},{8,4},{16,12},{24,20},{5,9},{13,17},{21,25},... | collective-permute-start | bytes 4616 | tf_op jit(solution)/shard_map/ppermute | solution.py:379
  4.5 0.7 %copy-start.1 = (f32[384]{0:T(512)S(1)}, f32[384]{0:T(512)}, u32[]{:S(2)}) copy-start(f32[384]{0:T(512)} %param.3) | copy-start | bytes 4612
  5.3 1.1 %copy-start = (bf16[3,384,256]{2,1,0:T(8,128)(2,1)S(1)}, bf16[3,384,256]{2,1,0:T(8,128)(2,1)}, u32[]{:S(2)}) copy-start(bf16[3,384,256]{2,1,0:T(8,128)(2,1)} %vel_ref.1) | copy-start | bytes 1769476
  8.3 16.8 %collective-permute-start.7 = (bf16[1152,256]{1,0:T(8,128)(2,1)S(1)}, bf16[1152,256]{1,0:T(8,128)(2,1)S(1)}, u32[]{:S(2)}, u32[]{:S(2)}) collective-permute-start(bf16[1152,256]{1,0:T(8,128)(2,1)S(1)} %get-tuple-element.34), channel_id=1, source_target_pairs={{0,1},{1,2},{2,3},{3,0},{8,9},{9,10},{10,11},{11,8},{16,17},{17,18... | collective-permute-start | bytes 1769480 | tf_op jit(solution)/shard_map/ppermute | solution.py:395
  11.6 1.3 %collective-permute-start.2 = (f32[192,128]{1,0:T(8,128)S(1)}, f32[192,128]{1,0:T(8,128)S(1)}, u32[]{:S(2)}, u32[]{:S(2)}) collective-permute-start(f32[192,128]{1,0:T(8,128)S(1)} %get-tuple-element.30), channel_id=1, source_target_pairs={{0,4},{4,0},{1,5},{5,1},{2,6},{6,2},{3,7},{7,3},{8,12},{12,8},{9,1... | collective-permute-start | bytes 294920 | tf_op jit(solution)/shard_map/ppermute | solution.py:395
  13.0 4.3 %collective-permute-start.3 = (f32[192,128]{1,0:T(8,128)S(1)}, f32[192,128]{1,0:T(8,128)S(1)}, u32[]{:S(2)}, u32[]{:S(2)}) collective-permute-start(f32[192,128]{1,0:T(8,128)S(1)} %add.18), channel_id=1, source_target_pairs={{0,8},{4,12},{1,9},{5,13},{2,10},{6,14},{3,11},{7,15},{8,0},{12,4}... | collective-permute-start | bytes 294920 | tf_op jit(solution)/shard_map/ppermute | solution.py:395
  13.0 4.3 %collective-permute-start.4 = (f32[192,128]{1,0:T(8,128)S(1)}, f32[192,128]{1,0:T(8,128)S(1)}, u32[]{:S(2)}, u32[]{:S(2)}) collective-permute-start(f32[192,128]{1,0:T(8,128)S(1)} %add.18), channel_id=1, source_target_pairs={{0,16},{4,20},{1,17},{5,21},{2,18},{6,22},{3,19},{7,23},{8,24},{12... | collective-permute-start | bytes 294920 | tf_op jit(solution)/shard_map/ppermute | solution.py:395
  14.1 4.7 %collective-permute-start.5 = (f32[192,128]{1,0:T(8,128)S(1)}, f32[192,128]{1,0:T(8,128)S(1)}, u32[]{:S(2)}, u32[]{:S(2)}) collective-permute-start(f32[192,128]{1,0:T(8,128)S(1)} %add.18), channel_id=1, source_target_pairs={{0,24},{4,28},{1,25},{5,29},{2,26},{6,30},{3,27},{7,31},{8,16},{12... | collective-permute-start | bytes 294920 | tf_op jit(solution)/shard_map/ppermute | solution.py:395
  18.8 2.7 %collective-permute-start.6 = (f32[192,128]{1,0:T(8,128)S(1)}, f32[192,128]{1,0:T(8,128)S(1)}, u32[]{:S(2)}, u32[]{:S(2)}) collective-permute-start(f32[192,128]{1,0:T(8,128)S(1)} %add_add_fusion.mine_ref), channel_id=1, source_target_pairs={{0,4},{4,0},{1,5},{5,1},{2,6},{6,2},{3,7},{7,3},{8,12},{12,8},{9,1... | collective-permute-start | bytes 294920 | tf_op jit(solution)/shard_map/ppermute | solution.py:395
  25.1 10.6 %collective-permute-start.8 = (bf16[1152,256]{1,0:T(8,128)(2,1)S(1)}, bf16[1152,256]{1,0:T(8,128)(2,1)S(1)}, u32[]{:S(2)}, u32[]{:S(2)}) collective-permute-start(bf16[1152,256]{1,0:T(8,128)(2,1)S(1)} %passed.1.panel_ref), channel_id=1, source_target_pairs={{1,2},{2,3},{9,10},{10,11},{17,18},{18,19},{25,26},{26,27},{6,5},{... | collective-permute-start | bytes 1769480 | tf_op jit(solution)/shard_map/ppermute | solution.py:395
  27.0 10.7 %collective-permute-start.12 = (f16[272,256]{1,0:T(8,128)(2,1)S(1)}, f16[272,256]{1,0:T(8,128)(2,1)S(1)}, u32[]{:S(2)}, u32[]{:S(2)}) collective-permute-start(f16[272,256]{1,0:T(8,128)(2,1)S(1)} %convert_element_type.40), channel_id=1, source_target_pairs={{9,1},{15,7},{4,12},{2,10},{29,21},{27,19},{16,24},{22,30}} | collective-permute-start | bytes 417800 | tf_op jit(solution)/shard_map/ppermute | solution.py:395
  28.3 14.1 %collective-permute-start.13 = (f16[272,256]{1,0:T(8,128)(2,1)S(1)}, f16[272,256]{1,0:T(8,128)(2,1)S(1)}, u32[]{:S(2)}, u32[]{:S(2)}) collective-permute-start(f16[272,256]{1,0:T(8,128)(2,1)S(1)} %convert_element_type.40), channel_id=1, source_target_pairs={{17,1},{23,7},{28,12},{26,10},{5,21},{3,19},{8,24},{14,30}} | collective-permute-start | bytes 417800 | tf_op jit(solution)/shard_map/ppermute | solution.py:395
  29.6 12.8 %collective-permute-start.14 = (f16[272,256]{1,0:T(8,128)(2,1)S(1)}, f16[272,256]{1,0:T(8,128)(2,1)S(1)}, u32[]{:S(2)}, u32[]{:S(2)}) collective-permute-start(f16[272,256]{1,0:T(8,128)(2,1)S(1)} %convert_element_type.40), channel_id=1, source_target_pairs={{25,1},{31,7},{20,12},{18,10},{13,21},{11,19},{0,24},{6,30}} | collective-permute-start | bytes 417800 | tf_op jit(solution)/shard_map/ppermute | solution.py:395
  36.3 11.0 %collective-permute-start.9 = (f16[272,256]{1,0:T(8,128)(2,1)S(1)}, f16[272,256]{1,0:T(8,128)(2,1)S(1)}, u32[]{:S(2)}, u32[]{:S(2)}) collective-permute-start(f16[272,256]{1,0:T(8,128)(2,1)S(1)} %convert_element_type.36), channel_id=1, source_target_pairs={{10,2},{3,11},{28,20},{21,29}} | collective-permute-start | bytes 417800 | tf_op jit(solution)/shard_map/ppermute | solution.py:395
  37.0 10.4 %collective-permute-start.10 = (f16[272,256]{1,0:T(8,128)(2,1)S(1)}, f16[272,256]{1,0:T(8,128)(2,1)S(1)}, u32[]{:S(2)}, u32[]{:S(2)}) collective-permute-start(f16[272,256]{1,0:T(8,128)(2,1)S(1)} %convert_element_type.36), channel_id=1, source_target_pairs={{18,2},{27,11},{4,20},{13,29}} | collective-permute-start | bytes 417800 | tf_op jit(solution)/shard_map/ppermute | solution.py:395
  37.6 9.7 %collective-permute-start.11 = (f16[272,256]{1,0:T(8,128)(2,1)S(1)}, f16[272,256]{1,0:T(8,128)(2,1)S(1)}, u32[]{:S(2)}, u32[]{:S(2)}) collective-permute-start(f16[272,256]{1,0:T(8,128)(2,1)S(1)} %convert_element_type.36), channel_id=1, source_target_pairs={{26,2},{19,11},{12,20},{5,29}} | collective-permute-start | bytes 417800 | tf_op jit(solution)/shard_map/ppermute | solution.py:395
  45.4 7.3 %collective-permute-start.15 = (f16[272,256]{1,0:T(8,128)(2,1)S(1)}, f16[272,256]{1,0:T(8,128)(2,1)S(1)}, u32[]{:S(2)}, u32[]{:S(2)}) collective-permute-start(f16[272,256]{1,0:T(8,128)(2,1)S(1)} %convert_element_type.44), channel_id=1, source_target_pairs={{1,12},{7,24},{12,1},{10,21},{21,10},{19,30},{24,7},{30,19}} | collective-permute-start | bytes 417800 | tf_op jit(solution)/shard_map/ppermute | solution.py:395
  47.5 8.2 %collective-permute-start.16 = (f16[272,256]{1,0:T(8,128)(2,1)S(1)}, f16[272,256]{1,0:T(8,128)(2,1)S(1)}, u32[]{:S(2)}, u32[]{:S(2)}) collective-permute-start(f16[272,256]{1,0:T(8,128)(2,1)S(1)} %convert_element_type.46), channel_id=1, source_target_pairs={{2,20},{11,29},{20,2},{29,11}} | collective-permute-start | bytes 417800 | tf_op jit(solution)/shard_map/ppermute | solution.py:395
  56.4 6.6 %collective-permute-start.17 = (f32[136,256]{1,0:T(8,128)S(1)}, f32[136,256]{1,0:T(8,128)S(1)}, u32[]{:S(2)}, u32[]{:S(2)}) collective-permute-start(f32[136,256]{1,0:T(8,128)S(1)} %get-tuple-element.45), channel_id=1, source_target_pairs={{1,5},{2,6},{7,3},{12,8},{10,14},{11,15},{20,16},{21,17},{19,23},{... | collective-permute-start | bytes 417800 | tf_op jit(solution)/shard_map/ppermute | solution.py:395
  57.7 5.3 %collective-permute-start.18 = (f32[8,256]{1,0:T(8,128)S(1)}, f32[8,256]{1,0:T(8,128)S(1)}, u32[]{:S(2)}, u32[]{:S(2)}) collective-permute-start(f32[8,256]{1,0:T(8,128)S(1)} %get-tuple-element.46), channel_id=1, source_target_pairs={{1,29},{2,30},{7,31},{12,4},{10,6},{11,7},{20,12},{21,13},{19,15},... | collective-permute-start | bytes 24584 | tf_op jit(solution)/shard_map/ppermute | solution.py:395

commit v11 on v10

--- a/solution.py
+++ b/solution.py
@@ -13,7 +13,7 @@
 VMEM = pl.BlockSpec(memory_space=pltpu.VMEM)
 SMEM = pl.BlockSpec(memory_space=pltpu.SMEM)
 LEAF = 64
-PIVOTS = 4
+PIVOTS = 8
 
 
 def params(mib=40):
@@ -217,18 +217,21 @@
             w_ref[k:, :] -= mm(u[:, k:], done, ((0,), (0,)))
 
 
-def factor_part(first, leaves, state, after=()):
+def factor_part(first, leaves, state, after=(), unit=False):
     n = state[0].shape[0]
     skip = len(after)
 
     def kernel(*refs):
-        factor_kernel(first, leaves, *refs[: len(state)], *refs[len(state) + skip :])
+        made = refs[len(state) + skip :]
+        factor_kernel(first, leaves, *refs[: len(state)], *made[:2])
+        if unit:
+            made[2][...] = jnp.ones_like(made[2])
 
     return pl.pallas_call(
         kernel,
-        out_shape=(jax.ShapeDtypeStruct((n, n), F32),) * 2,
+        out_shape=(jax.ShapeDtypeStruct((n, n), F32),) * 2 + (jax.ShapeDtypeStruct((8, n), F32),) * unit,
         in_specs=[VMEM] * len(state) + [pl.BlockSpec(memory_space=pl.ANY)] * skip,
-        out_specs=(VMEM,) * 2,
+        out_specs=(VMEM,) * (2 + unit),
         compiler_params=params(),
         cost_estimate=cost(2 * n * n * n, 8 * n * n),
         name="factor",
@@ -429,8 +432,7 @@
         ]
 
     def exchanged(packed, group_homes):
-        received = send(packed, [(at(*home), at(*homes[z, k])) for (k, z), home in group_homes.items()])
-        return received.astype(F32)
+        return send(packed, [(at(*home), at(*homes[z, k])) for (k, z), home in group_homes.items()])
 
     near_block = pair_block(state[0], xt, near)
     near_parts = gathered(near_block, near_homes)
@@ -442,7 +444,8 @@
     near_cross = exchanged(packed, near_homes)
     far_own, packed = total(state[0], far_parts)
     far_cross = exchanged(packed, far_homes)
-    w = factor_part(3, 1, state, (far_own,))[1]
+    _, w, unit = factor_part(3, 1, state, (far_own,), True)
+    near_cross, far_cross = near_cross.astype(F32) * unit[0:1], far_cross.astype(F32)
     mine, sib, top = merge(pos, w, (near_own, near_cross), (far_own, far_cross))
     sib = send(sib, [(at(k, z, c), at(k, z, 1 - c)) for k, z, c in homes.values()])
     top = send(top, [(at(k, z, c), at((k - 1) % groups, z, 1)) for k, z, c in homes.values()])

time: 65.1 us -> 65.9 us (1.012)
  the two profiles are of different devices: /device:TPU:3 before, /device:TPU:5 now
where the time goes in v11:
time: 65.9 us; the launch traced here: 65.1 us
  starting transfers between devices  31.1 us (47%)
  Pallas kernels  15.6 us (24%)
  waiting for transfers between devices  15.1 us (23%)
  local copies, waits for them, and re-layouts  1.77 us (3%)
  other arithmetic  1.09 us (2%)
    ppermute x17, starting transfers between devices, send(): return lax.ppermute(value, axes, pairs)  27.3 us
    ppermute x17, waiting for transfers between devices, send(): return lax.ppermute(value, axes, pairs)  15.1 us
    pallas_call x4, Pallas kernels, factor_part(): pl.pallas_call(kernel, out_shape=(jax.ShapeDtypeStruct((n, n), F32),) * 2...  10.1 us
    ppermute x1, starting transfers between devices, start(): far = lax.ppermute(jnp.where(odd == 0, head, tail), 'space', outside)  3.02 us
    unnamed x4, local copies, waits for them, and re-layouts  1.66 us
    pallas_call x1, Pallas kernels, tiles(): pl.pallas_call(tiles_kernel, out_shape=jax.ShapeDtypeStruct((n, half), F3...  1.62 us
  transfers between devices with their start and end apart: 19, of which 9 were waited for; matrix products, arithmetic and copies ran while one was open for 1% of the time, Pallas kernels for 19%

profile of v11, /device:TPU:5, one launch (start us, length us, event | category | flops | bytes accessed | tf_op | source)
XLA Modules:
  0.0 65.1 jit_solution(6208189046053238742)
XLA Ops:
  0.0 0.7 %broadcast_select_fusion = (bf16[3,1,256]{2,1,0:T(2,128)(2,1)S(1)}, bf16[3,1,256]{2,1,0:T(2,128)(2,1)S(1)}) fusion(pred[]{:T(512)S(6)} %eq.6, bf16[3,384,256]{2,1,0:T(8,128)(2,1)} %vel_ref.1), kind=kLoop, calls=%fused_computation.2 | loop fusion | flops 1536 | bytes 6145 | tf_op jit(solution)/shard_map/jit(_where)/select_n | solution.py:382
  0.7 0.7 %collective-permute-start = (bf16[3,1,256]{2,1,0:T(2,128)(2,1)S(1)}, bf16[3,1,256]{2,1,0:T(2,128)(2,1)S(1)}, u32[]{:S(2)}, u32[]{:S(2)}) collective-permute-start(bf16[3,1,256]{2,1,0:T(2,128)(2,1)S(1)} %get-tuple-element.50), channel_id=1, source_target_pairs={{0,4},{4,0},{8,12},{12,8},{16,20},{20,16},{24,28},{28,24},{1,5},{5... | collective-permute-start | bytes 4616 | tf_op jit(solution)/shard_map/ppermute | solution.py:383
  1.5 3.0 %collective-permute-start.1 = (bf16[3,1,256]{2,1,0:T(2,128)(2,1)S(1)}, bf16[3,1,256]{2,1,0:T(2,128)(2,1)S(1)}, u32[]{:S(2)}, u32[]{:S(2)}) collective-permute-start(bf16[3,1,256]{2,1,0:T(2,128)(2,1)S(1)} %get-tuple-element.49), channel_id=1, source_target_pairs={{4,8},{12,16},{20,24},{8,4},{16,12},{24,20},{5,9},{13,17},{21,25},... | collective-permute-start | bytes 4616 | tf_op jit(solution)/shard_map/ppermute | solution.py:382
  5.3 1.1 %copy-done = bf16[3,384,256]{2,1,0:T(8,128)(2,1)S(1)} copy-done((bf16[3,384,256]{2,1,0:T(8,128)(2,1)S(1)}, bf16[3,384,256]{2,1,0:T(8,128)(2,1)}, u32[]{:S(2)}) %copy-start) | copy-done | bytes 589848
  6.8 1.0 %panel.1 = (bf16[1152,256]{1,0:T(8,128)(2,1)S(1)}, bf16[256,1152]{1,0:T(8,128)(2,1)S(1)}, f32[192,128]{1,0:T(8,128)S(1)}, f32[192,128]{1,0:T(8,128)S(1)}) custom-call(s32[4]{0:T(128)S(1)} %pad_add_fusion.pos_ref, bf16[1152,256]{1,0:T(8,128)(2,1)S(1)} %get-tuple-element.27.x_in_ref, f32[3,8,256]{2,1,0:T(8,128)S(1)} %get-tuple-element.28.head_ref, ...), custom_call_target="tpu_custom_call" | custom-call | flops 150994944 | bytes 1769472 | tf_op jit(solution)/shard_map/panel/pallas_call | solution.py:112
  7.8 3.4 %collective-permute-start.7 = (bf16[1152,256]{1,0:T(8,128)(2,1)S(1)}, bf16[1152,256]{1,0:T(8,128)(2,1)S(1)}, u32[]{:S(2)}, u32[]{:S(2)}) collective-permute-start(bf16[1152,256]{1,0:T(8,128)(2,1)S(1)} %get-tuple-element.35), channel_id=1, source_target_pairs={{0,1},{1,2},{2,3},{3,0},{8,9},{9,10},{10,11},{11,8},{16,17},{17,18... | collective-permute-start | bytes 1769480 | tf_op jit(solution)/shard_map/ppermute | solution.py:398
  11.2 1.3 %collective-permute-done.2 = f32[192,128]{1,0:T(8,128)S(1)} collective-permute-done((f32[192,128]{1,0:T(8,128)S(1)}, f32[192,128]{1,0:T(8,128)S(1)}, u32[]{:S(2)}, u32[]{:S(2)}) %collective-permute-start.2) | collective-permute-done | bytes 98336 | tf_op jit(solution)/shard_map/ppermute | solution.py:398
  12.6 1.9 %collective-permute-start.4 = (f32[192,128]{1,0:T(8,128)S(1)}, f32[192,128]{1,0:T(8,128)S(1)}, u32[]{:S(2)}, u32[]{:S(2)}) collective-permute-start(f32[192,128]{1,0:T(8,128)S(1)} %add.18), channel_id=1, source_target_pairs={{0,16},{4,20},{1,17},{5,21},{2,18},{6,22},{3,19},{7,23},{8,24},{12... | collective-permute-start | bytes 294920 | tf_op jit(solution)/shard_map/ppermute | solution.py:398
  14.5 0.8 %collective-permute-start.5 = (f32[192,128]{1,0:T(8,128)S(1)}, f32[192,128]{1,0:T(8,128)S(1)}, u32[]{:S(2)}, u32[]{:S(2)}) collective-permute-start(f32[192,128]{1,0:T(8,128)S(1)} %add.18), channel_id=1, source_target_pairs={{0,24},{4,28},{1,25},{5,29},{2,26},{6,30},{3,27},{7,31},{8,16},{12... | collective-permute-start | bytes 294920 | tf_op jit(solution)/shard_map/ppermute | solution.py:398
  15.2 1.6 %collective-permute-done.3 = f32[192,128]{1,0:T(8,128)S(1)} collective-permute-done((f32[192,128]{1,0:T(8,128)S(1)}, f32[192,128]{1,0:T(8,128)S(1)}, u32[]{:S(2)}, u32[]{:S(2)}) %collective-permute-start.3) | collective-permute-done | bytes 98336 | tf_op jit(solution)/shard_map/ppermute | solution.py:398
  17.2 1.9 %collective-permute-done.5 = f32[192,128]{1,0:T(8,128)S(1)} collective-permute-done((f32[192,128]{1,0:T(8,128)S(1)}, f32[192,128]{1,0:T(8,128)S(1)}, u32[]{:S(2)}, u32[]{:S(2)}) %collective-permute-start.5) | collective-permute-done | bytes 98336 | tf_op jit(solution)/shard_map/ppermute | solution.py:398
  19.2 1.6 %collective-permute-start.6 = (f32[192,128]{1,0:T(8,128)S(1)}, f32[192,128]{1,0:T(8,128)S(1)}, u32[]{:S(2)}, u32[]{:S(2)}) collective-permute-start(f32[192,128]{1,0:T(8,128)S(1)} %add_add_fusion.mine_ref), channel_id=1, source_target_pairs={{0,4},{4,0},{1,5},{5,1},{2,6},{6,2},{3,7},{7,3},{8,12},{12,8},{9,1... | collective-permute-start | bytes 294920 | tf_op jit(solution)/shard_map/ppermute | solution.py:398
  20.8 0.9 %collective-permute-done.6.theirs_ref = f32[192,128]{1,0:T(8,128)S(1)} collective-permute-done((f32[192,128]{1,0:T(8,128)S(1)}, f32[192,128]{1,0:T(8,128)S(1)}, u32[]{:S(2)}, u32[]{:S(2)}) %collective-permute-start.6) | collective-permute-done | bytes 98336 | tf_op jit(solution)/shard_map/ppermute | solution.py:398
  22.4 2.6 %factor.4 = (f32[256,256]{1,0:T(8,128)S(1)}, f32[256,256]{1,0:T(8,128)S(1)}) custom-call(f32[256,256]{1,0:T(8,128)S(1)} %gather.1.refs_0_.g_ref), custom_call_target="tpu_custom_call" | custom-call | flops 33554432 | bytes 524288 | tf_op jit(solution)/shard_map/factor/pallas_call | solution.py:230
  25.0 1.3 %collective-permute-start.8 = (bf16[1152,256]{1,0:T(8,128)(2,1)S(1)}, bf16[1152,256]{1,0:T(8,128)(2,1)S(1)}, u32[]{:S(2)}, u32[]{:S(2)}) collective-permute-start(bf16[1152,256]{1,0:T(8,128)(2,1)S(1)} %passed.1.panel_ref), channel_id=1, source_target_pairs={{1,2},{2,3},{9,10},{10,11},{17,18},{18,19},{25,26},{26,27},{6,5},{... | collective-permute-start | bytes 1769480 | tf_op jit(solution)/shard_map/ppermute | solution.py:398
  26.8 0.7 %collective-permute-start.12 = (f16[272,256]{1,0:T(8,128)(2,1)S(1)}, f16[272,256]{1,0:T(8,128)(2,1)S(1)}, u32[]{:S(2)}, u32[]{:S(2)}) collective-permute-start(f16[272,256]{1,0:T(8,128)(2,1)S(1)} %convert_element_type.40), channel_id=1, source_target_pairs={{9,1},{15,7},{4,12},{2,10},{29,21},{27,19},{16,24},{22,30}} | collective-permute-start | bytes 417800 | tf_op jit(solution)/shard_map/ppermute | solution.py:398
  28.2 4.0 %collective-permute-start.14 = (f16[272,256]{1,0:T(8,128)(2,1)S(1)}, f16[272,256]{1,0:T(8,128)(2,1)S(1)}, u32[]{:S(2)}, u32[]{:S(2)}) collective-permute-start(f16[272,256]{1,0:T(8,128)(2,1)S(1)} %convert_element_type.40), channel_id=1, source_target_pairs={{25,1},{31,7},{20,12},{18,10},{13,21},{11,19},{0,24},{6,30}} | collective-permute-start | bytes 417800 | tf_op jit(solution)/shard_map/ppermute | solution.py:398
  32.2 2.5 %factor.5 = (f32[256,256]{1,0:T(8,128)S(1)}, f32[256,256]{1,0:T(8,128)S(1)}) custom-call(f32[256,256]{1,0:T(8,128)S(1)} %get-tuple-element.32.refs_1_.after_ref.refs_0_, f32[256,256]{1,0:T(8,128)S(1)} %get-tuple-element.33.refs_1_, f32[272,256]{1,0:T(8,128)S(1)} %block.2.refs_2_.refs_0_), custom_call_target="tpu_custom_call" | custom-call | flops 33554432 | bytes 524288 | tf_op jit(solution)/shard_map/factor/pallas_call | solution.py:230
  34.7 0.9 %collective-permute-done.8.panel_ref = bf16[1152,256]{1,0:T(8,128)(2,1)S(1)} collective-permute-done((bf16[1152,256]{1,0:T(8,128)(2,1)S(1)}, bf16[1152,256]{1,0:T(8,128)(2,1)S(1)}, u32[]{:S(2)}, u32[]{:S(2)}) %collective-permute-start.8) | collective-permute-done | bytes 589856 | tf_op jit(solution)/shard_map/ppermute | solution.py:398
  36.2 1.3 %collective-permute-start.9 = (f16[272,256]{1,0:T(8,128)(2,1)S(1)}, f16[272,256]{1,0:T(8,128)(2,1)S(1)}, u32[]{:S(2)}, u32[]{:S(2)}) collective-permute-start(f16[272,256]{1,0:T(8,128)(2,1)S(1)} %convert_element_type.36), channel_id=1, source_target_pairs={{10,2},{3,11},{28,20},{21,29}} | collective-permute-start | bytes 417800 | tf_op jit(solution)/shard_map/ppermute | solution.py:398
  37.5 1.3 %collective-permute-start.10 = (f16[272,256]{1,0:T(8,128)(2,1)S(1)}, f16[272,256]{1,0:T(8,128)(2,1)S(1)}, u32[]{:S(2)}, u32[]{:S(2)}) collective-permute-start(f16[272,256]{1,0:T(8,128)(2,1)S(1)} %convert_element_type.36), channel_id=1, source_target_pairs={{18,2},{27,11},{4,20},{13,29}} | collective-permute-start | bytes 417800 | tf_op jit(solution)/shard_map/ppermute | solution.py:398
  38.8 1.3 %collective-permute-start.11 = (f16[272,256]{1,0:T(8,128)(2,1)S(1)}, f16[272,256]{1,0:T(8,128)(2,1)S(1)}, u32[]{:S(2)}, u32[]{:S(2)}) collective-permute-start(f16[272,256]{1,0:T(8,128)(2,1)S(1)} %convert_element_type.36), channel_id=1, source_target_pairs={{26,2},{19,11},{12,20},{5,29}} | collective-permute-start | bytes 417800 | tf_op jit(solution)/shard_map/ppermute | solution.py:398
  40.2 2.4 %factor.6 = (f32[256,256]{1,0:T(8,128)S(1)}, f32[256,256]{1,0:T(8,128)S(1)}) custom-call(f32[256,256]{1,0:T(8,128)S(1)} %get-tuple-element.36.after_ref.refs_0_, f32[256,256]{1,0:T(8,128)S(1)} %get-tuple-element.37.refs_1_, f32[272,256]{1,0:T(8,128)S(1)} %block.3.refs_2_.refs_0_), custom_call_target="tpu_custom_call" | custom-call | flops 33554432 | bytes 524288 | tf_op jit(solution)/shard_map/factor/pallas_call | solution.py:230
  43.5 2.0 %collective-permute-done.11 = f16[272,256]{1,0:T(8,128)(2,1)S(1)} collective-permute-done((f16[272,256]{1,0:T(8,128)(2,1)S(1)}, f16[272,256]{1,0:T(8,128)(2,1)S(1)}, u32[]{:S(2)}, u32[]{:S(2)}) %collective-permute-start.11) | collective-permute-done | bytes 139296 | tf_op jit(solution)/shard_map/ppermute | solution.py:398
  45.6 2.6 %factor.7 = (f32[256,256]{1,0:T(8,128)}, f32[256,256]{1,0:T(8,128)S(1)}, f32[8,256]{1,0:T(8,128)S(1)}) custom-call(f32[256,256]{1,0:T(8,128)S(1)} %get-tuple-element.38.after_ref.refs_0_, f32[256,256]{1,0:T(8,128)S(1)} %get-tuple-element.39.refs_1_, f32[256,256]{1,0:T(8,128)S(1)} %get-tuple-element.40.refs_2_), custom_call_target="tpu_custom_call" | custom-call | flops 33554432 | bytes 524288 | tf_op jit(solution)/shard_map/factor/pallas_call | solution.py:230
  48.3 5.2 %collective-permute-start.16 = (f16[272,256]{1,0:T(8,128)(2,1)S(1)}, f16[272,256]{1,0:T(8,128)(2,1)S(1)}, u32[]{:S(2)}, u32[]{:S(2)}) collective-permute-start(f16[272,256]{1,0:T(8,128)(2,1)S(1)} %convert_element_type.46), channel_id=1, source_target_pairs={{2,20},{11,29},{20,2},{29,11}} | collective-permute-start | bytes 417800 | tf_op jit(solution)/shard_map/ppermute | solution.py:398
  53.5 2.9 %collective-permute-done.16 = f16[272,256]{1,0:T(8,128)(2,1)S(1)} collective-permute-done((f16[272,256]{1,0:T(8,128)(2,1)S(1)}, f16[272,256]{1,0:T(8,128)(2,1)S(1)}, u32[]{:S(2)}, u32[]{:S(2)}) %collective-permute-start.16) | collective-permute-done | bytes 139296 | tf_op jit(solution)/shard_map/ppermute | solution.py:398
  56.5 0.7 %merge.1 = (f32[136,256]{1,0:T(8,128)S(1)}, f32[136,256]{1,0:T(8,128)S(1)}, f32[8,256]{1,0:T(8,128)S(1)}) custom-call(s32[4]{0:T(128)S(1)} %pad_add_fusion.pos_ref, f32[256,256]{1,0:T(8,128)S(1)} %get-tuple-element.41.after_ref.w_ref, f32[256,256]{1,0:T(8,128)S(1)} %get-tuple-element.42.refs_0_, f32[272,256]{1,0:T(8,128)S(1)} %convert_multiply_fusion.refs_1_, ...), custom_call_target="tpu_custom_call" | custom-call | tf_op jit(solution)/shard_map/merge/pallas_call | solution.py:325
  57.2 1.3 %collective-permute-start.17 = (f32[136,256]{1,0:T(8,128)S(1)}, f32[136,256]{1,0:T(8,128)S(1)}, u32[]{:S(2)}, u32[]{:S(2)}) collective-permute-start(f32[136,256]{1,0:T(8,128)S(1)} %get-tuple-element.47), channel_id=1, source_target_pairs={{1,5},{2,6},{7,3},{12,8},{10,14},{11,15},{20,16},{21,17},{19,23},{... | collective-permute-start | bytes 417800 | tf_op jit(solution)/shard_map/ppermute | solution.py:398
  58.5 1.9 %collective-permute-start.18 = (f32[8,256]{1,0:T(8,128)S(1)}, f32[8,256]{1,0:T(8,128)S(1)}, u32[]{:S(2)}, u32[]{:S(2)}) collective-permute-start(f32[8,256]{1,0:T(8,128)S(1)} %get-tuple-element.48), channel_id=1, source_target_pairs={{1,29},{2,30},{7,31},{12,4},{10,6},{11,7},{20,12},{21,13},{19,15},... | collective-permute-start | bytes 24584 | tf_op jit(solution)/shard_map/ppermute | solution.py:398
  60.4 3.0 %collective-permute-done.18.top_ref = f32[8,256]{1,0:T(8,128)S(1)} collective-permute-done((f32[8,256]{1,0:T(8,128)S(1)}, f32[8,256]{1,0:T(8,128)S(1)}, u32[]{:S(2)}, u32[]{:S(2)}) %collective-permute-start.18) | collective-permute-done | bytes 8224 | tf_op jit(solution)/shard_map/ppermute | solution.py:398
  63.5 1.6 %tiles.1 = f32[256,128]{1,0:T(8,128)} custom-call(s32[4]{0:T(128)S(1)} %pad_add_fusion.pos_ref, f32[256,256]{1,0:T(8,128)S(1)} %get-tuple-element.41.after_ref.w_ref, f32[256,256]{1,0:T(8,128)S(1)} %gather.1.refs_0_.g_ref, f32[136,256]{1,0:T(8,128)S(1)} %get-tuple-element.46.own_ref, f32[136,256]{1,0:T(8,128)S(1)} %collective-permute-done.17.sib_ref, ...), custom_call_target="tpu_custom_call" | custom-call | tf_op jit(solution)/shard_map/tiles/pallas_call | solution.py:362
  (42 shorter events, 5.1 us)
Async XLA Ops:
  0.7 6.1 %collective-permute-start = (bf16[3,1,256]{2,1,0:T(2,128)(2,1)S(1)}, bf16[3,1,256]{2,1,0:T(2,128)(2,1)S(1)}, u32[]{:S(2)}, u32[]{:S(2)}) collective-permute-start(bf16[3,1,256]{2,1,0:T(2,128)(2,1)S(1)} %get-tuple-element.50), channel_id=1, source_target_pairs={{0,4},{4,0},{8,12},{12,8},{16,20},{20,16},{24,28},{28,24},{1,5},{5... | collective-permute-start | bytes 4616 | tf_op jit(solution)/shard_map/ppermute | solution.py:383
  1.5 5.3 %collective-permute-start.1 = (bf16[3,1,256]{2,1,0:T(2,128)(2,1)S(1)}, bf16[3,1,256]{2,1,0:T(2,128)(2,1)S(1)}, u32[]{:S(2)}, u32[]{:S(2)}) collective-permute-start(bf16[3,1,256]{2,1,0:T(2,128)(2,1)S(1)} %get-tuple-element.49), channel_id=1, source_target_pairs={{4,8},{12,16},{20,24},{8,4},{16,12},{24,20},{5,9},{13,17},{21,25},... | collective-permute-start | bytes 4616 | tf_op jit(solution)/shard_map/ppermute | solution.py:382
  4.5 0.7 %copy-start.1 = (f32[384]{0:T(512)S(1)}, f32[384]{0:T(512)}, u32[]{:S(2)}) copy-start(f32[384]{0:T(512)} %param.3) | copy-start | bytes 4612
  5.3 1.1 %copy-start = (bf16[3,384,256]{2,1,0:T(8,128)(2,1)S(1)}, bf16[3,384,256]{2,1,0:T(8,128)(2,1)}, u32[]{:S(2)}) copy-start(bf16[3,384,256]{2,1,0:T(8,128)(2,1)} %vel_ref.1) | copy-start | bytes 1769476
  7.8 17.2 %collective-permute-start.7 = (bf16[1152,256]{1,0:T(8,128)(2,1)S(1)}, bf16[1152,256]{1,0:T(8,128)(2,1)S(1)}, u32[]{:S(2)}, u32[]{:S(2)}) collective-permute-start(bf16[1152,256]{1,0:T(8,128)(2,1)S(1)} %get-tuple-element.35), channel_id=1, source_target_pairs={{0,1},{1,2},{2,3},{3,0},{8,9},{9,10},{10,11},{11,8},{16,17},{17,18... | collective-permute-start | bytes 1769480 | tf_op jit(solution)/shard_map/ppermute | solution.py:398
  11.2 1.3 %collective-permute-start.2 = (f32[192,128]{1,0:T(8,128)S(1)}, f32[192,128]{1,0:T(8,128)S(1)}, u32[]{:S(2)}, u32[]{:S(2)}) collective-permute-start(f32[192,128]{1,0:T(8,128)S(1)} %get-tuple-element.31), channel_id=1, source_target_pairs={{0,4},{4,0},{1,5},{5,1},{2,6},{6,2},{3,7},{7,3},{8,12},{12,8},{9,1... | collective-permute-start | bytes 294920 | tf_op jit(solution)/shard_map/ppermute | solution.py:398
  12.5 4.3 %collective-permute-start.3 = (f32[192,128]{1,0:T(8,128)S(1)}, f32[192,128]{1,0:T(8,128)S(1)}, u32[]{:S(2)}, u32[]{:S(2)}) collective-permute-start(f32[192,128]{1,0:T(8,128)S(1)} %add.18), channel_id=1, source_target_pairs={{0,8},{4,12},{1,9},{5,13},{2,10},{6,14},{3,11},{7,15},{8,0},{12,4}... | collective-permute-start | bytes 294920 | tf_op jit(solution)/shard_map/ppermute | solution.py:398
  12.6 4.6 %collective-permute-start.4 = (f32[192,128]{1,0:T(8,128)S(1)}, f32[192,128]{1,0:T(8,128)S(1)}, u32[]{:S(2)}, u32[]{:S(2)}) collective-permute-start(f32[192,128]{1,0:T(8,128)S(1)} %add.18), channel_id=1, source_target_pairs={{0,16},{4,20},{1,17},{5,21},{2,18},{6,22},{3,19},{7,23},{8,24},{12... | collective-permute-start | bytes 294920 | tf_op jit(solution)/shard_map/ppermute | solution.py:398
  14.5 4.7 %collective-permute-start.5 = (f32[192,128]{1,0:T(8,128)S(1)}, f32[192,128]{1,0:T(8,128)S(1)}, u32[]{:S(2)}, u32[]{:S(2)}) collective-permute-start(f32[192,128]{1,0:T(8,128)S(1)} %add.18), channel_id=1, source_target_pairs={{0,24},{4,28},{1,25},{5,29},{2,26},{6,30},{3,27},{7,31},{8,16},{12... | collective-permute-start | bytes 294920 | tf_op jit(solution)/shard_map/ppermute | solution.py:398
  19.2 2.6 %collective-permute-start.6 = (f32[192,128]{1,0:T(8,128)S(1)}, f32[192,128]{1,0:T(8,128)S(1)}, u32[]{:S(2)}, u32[]{:S(2)}) collective-permute-start(f32[192,128]{1,0:T(8,128)S(1)} %add_add_fusion.mine_ref), channel_id=1, source_target_pairs={{0,4},{4,0},{1,5},{5,1},{2,6},{6,2},{3,7},{7,3},{8,12},{12,8},{9,1... | collective-permute-start | bytes 294920 | tf_op jit(solution)/shard_map/ppermute | solution.py:398
  25.0 10.6 %collective-permute-start.8 = (bf16[1152,256]{1,0:T(8,128)(2,1)S(1)}, bf16[1152,256]{1,0:T(8,128)(2,1)S(1)}, u32[]{:S(2)}, u32[]{:S(2)}) collective-permute-start(bf16[1152,256]{1,0:T(8,128)(2,1)S(1)} %passed.1.panel_ref), channel_id=1, source_target_pairs={{1,2},{2,3},{9,10},{10,11},{17,18},{18,19},{25,26},{26,27},{6,5},{... | collective-permute-start | bytes 1769480 | tf_op jit(solution)/shard_map/ppermute | solution.py:398
  26.8 11.9 %collective-permute-start.12 = (f16[272,256]{1,0:T(8,128)(2,1)S(1)}, f16[272,256]{1,0:T(8,128)(2,1)S(1)}, u32[]{:S(2)}, u32[]{:S(2)}) collective-permute-start(f16[272,256]{1,0:T(8,128)(2,1)S(1)} %convert_element_type.40), channel_id=1, source_target_pairs={{9,1},{15,7},{4,12},{2,10},{29,21},{27,19},{16,24},{22,30}} | collective-permute-start | bytes 417800 | tf_op jit(solution)/shard_map/ppermute | solution.py:398
  27.5 12.6 %collective-permute-start.13 = (f16[272,256]{1,0:T(8,128)(2,1)S(1)}, f16[272,256]{1,0:T(8,128)(2,1)S(1)}, u32[]{:S(2)}, u32[]{:S(2)}) collective-permute-start(f16[272,256]{1,0:T(8,128)(2,1)S(1)} %convert_element_type.40), channel_id=1, source_target_pairs={{17,1},{23,7},{28,12},{26,10},{5,21},{3,19},{8,24},{14,30}} | collective-permute-start | bytes 417800 | tf_op jit(solution)/shard_map/ppermute | solution.py:398
  28.2 12.0 %collective-permute-start.14 = (f16[272,256]{1,0:T(8,128)(2,1)S(1)}, f16[272,256]{1,0:T(8,128)(2,1)S(1)}, u32[]{:S(2)}, u32[]{:S(2)}) collective-permute-start(f16[272,256]{1,0:T(8,128)(2,1)S(1)} %convert_element_type.40), channel_id=1, source_target_pairs={{25,1},{31,7},{20,12},{18,10},{13,21},{11,19},{0,24},{6,30}} | collective-permute-start | bytes 417800 | tf_op jit(solution)/shard_map/ppermute | solution.py:398
  36.2 7.2 %collective-permute-start.9 = (f16[272,256]{1,0:T(8,128)(2,1)S(1)}, f16[272,256]{1,0:T(8,128)(2,1)S(1)}, u32[]{:S(2)}, u32[]{:S(2)}) collective-permute-start(f16[272,256]{1,0:T(8,128)(2,1)S(1)} %convert_element_type.36), channel_id=1, source_target_pairs={{10,2},{3,11},{28,20},{21,29}} | collective-permute-start | bytes 417800 | tf_op jit(solution)/shard_map/ppermute | solution.py:398
  37.5 6.0 %collective-permute-start.10 = (f16[272,256]{1,0:T(8,128)(2,1)S(1)}, f16[272,256]{1,0:T(8,128)(2,1)S(1)}, u32[]{:S(2)}, u32[]{:S(2)}) collective-permute-start(f16[272,256]{1,0:T(8,128)(2,1)S(1)} %convert_element_type.36), channel_id=1, source_target_pairs={{18,2},{27,11},{4,20},{13,29}} | collective-permute-start | bytes 417800 | tf_op jit(solution)/shard_map/ppermute | solution.py:398
  38.8 6.7 %collective-permute-start.11 = (f16[272,256]{1,0:T(8,128)(2,1)S(1)}, f16[272,256]{1,0:T(8,128)(2,1)S(1)}, u32[]{:S(2)}, u32[]{:S(2)}) collective-permute-start(f16[272,256]{1,0:T(8,128)(2,1)S(1)} %convert_element_type.36), channel_id=1, source_target_pairs={{26,2},{19,11},{12,20},{5,29}} | collective-permute-start | bytes 417800 | tf_op jit(solution)/shard_map/ppermute | solution.py:398
  42.7 10.8 %collective-permute-start.15 = (f16[272,256]{1,0:T(8,128)(2,1)S(1)}, f16[272,256]{1,0:T(8,128)(2,1)S(1)}, u32[]{:S(2)}, u32[]{:S(2)}) collective-permute-start(f16[272,256]{1,0:T(8,128)(2,1)S(1)} %convert_element_type.44), channel_id=1, source_target_pairs={{1,12},{7,24},{12,1},{10,21},{21,10},{19,30},{24,7},{30,19}} | collective-permute-start | bytes 417800 | tf_op jit(solution)/shard_map/ppermute | solution.py:398
  48.3 8.2 %collective-permute-start.16 = (f16[272,256]{1,0:T(8,128)(2,1)S(1)}, f16[272,256]{1,0:T(8,128)(2,1)S(1)}, u32[]{:S(2)}, u32[]{:S(2)}) collective-permute-start(f16[272,256]{1,0:T(8,128)(2,1)S(1)} %convert_element_type.46), channel_id=1, source_target_pairs={{2,20},{11,29},{20,2},{29,11}} | collective-permute-start | bytes 417800 | tf_op jit(solution)/shard_map/ppermute | solution.py:398
  57.2 6.3 %collective-permute-start.17 = (f32[136,256]{1,0:T(8,128)S(1)}, f32[136,256]{1,0:T(8,128)S(1)}, u32[]{:S(2)}, u32[]{:S(2)}) collective-permute-start(f32[136,256]{1,0:T(8,128)S(1)} %get-tuple-element.47), channel_id=1, source_target_pairs={{1,5},{2,6},{7,3},{12,8},{10,14},{11,15},{20,16},{21,17},{19,23},{... | collective-permute-start | bytes 417800 | tf_op jit(solution)/shard_map/ppermute | solution.py:398
  58.5 5.0 %collective-permute-start.18 = (f32[8,256]{1,0:T(8,128)S(1)}, f32[8,256]{1,0:T(8,128)S(1)}, u32[]{:S(2)}, u32[]{:S(2)}) collective-permute-start(f32[8,256]{1,0:T(8,128)S(1)} %get-tuple-element.48), channel_id=1, source_target_pairs={{1,29},{2,30},{7,31},{12,4},{10,6},{11,7},{20,12},{21,13},{19,15},... | collective-permute-start | bytes 24584 | tf_op jit(solution)/shard_map/ppermute | solution.py:398

commit v12 on v10

--- a/solution.py
+++ b/solution.py
@@ -13,7 +13,7 @@
 VMEM = pl.BlockSpec(memory_space=pltpu.VMEM)
 SMEM = pl.BlockSpec(memory_space=pltpu.SMEM)
 LEAF = 64
-PIVOTS = 4
+PIVOTS = 8
 
 
 def params(mib=40):
@@ -248,27 +248,39 @@
 TAIL = 16
 
 
-def block_kernel(after_ref, xt_ref, panel_ref, out_ref):
+def blocks_kernel(pos_ref, after_ref, xt_ref, near_ref, far_ref, *outs):
     del after_ref
+    chip, group, core = pos_ref[0], pos_ref[1], pos_ref[2]
+    count = len(outs)
     n = xt_ref.shape[0]
-    block = jnp.dot(xt_ref[...], panel_ref[...], preferred_element_type=F32)
-    peak = jnp.max(jnp.abs(block), axis=(0, 1), keepdims=True)
-    exponent = jnp.ceil(jnp.log2(jnp.maximum(peak, 1e-30)))
-    out_ref[0:n] = block * jnp.exp2(TOP - exponent)
-    out_ref[n:] = jnp.broadcast_to(exponent, (TAIL, n))
-
-
-def pair_block(after, xt, panel):
+    for r, panel_ref in ((1, near_ref), (2, far_ref)):
+        owner = (group + jnp.where(core == 0, count - r, r)) % count
+
+        @pl.when((r == 1) | (core_of(owner, group, count) == core))
+        def _(panel_ref=panel_ref, owner=owner):
+            block = jnp.dot(xt_ref[...], panel_ref[...], preferred_element_type=F32)
+            peak = jnp.max(jnp.abs(block), axis=(0, 1), keepdims=True)
+            exponent = jnp.ceil(jnp.log2(jnp.maximum(peak, 1e-30)))
+            scaled = block * jnp.exp2(TOP - exponent)
+            for m in range(count):
+
+                @pl.when(jnp.bitwise_xor(chip, m) == owner)
+                def _(m=m):
+                    outs[m][0:n] = scaled
+                    outs[m][n:] = jnp.broadcast_to(exponent, (TAIL, n))
+
+
+def blocks(pos, after, xt, near, far, count):
     n = xt.shape[0]
     return pl.pallas_call(
-        block_kernel,
-        out_shape=jax.ShapeDtypeStruct((n + TAIL, n), F32),
-        in_specs=[pl.BlockSpec(memory_space=pl.ANY)] + [VMEM] * 2,
-        out_specs=VMEM,
-        compiler_params=params(),
-        cost_estimate=cost(2 * n * n * xt.shape[1], 4 * n * n),
-        name="block",
-    )(after, xt, panel)
+        blocks_kernel,
+        out_shape=(jax.ShapeDtypeStruct((n + TAIL, n), F32),) * count,
+        in_specs=[SMEM, pl.BlockSpec(memory_space=pl.ANY)] + [VMEM] * 3,
+        out_specs=(VMEM,) * count,
+        compiler_params=params(),
+        cost_estimate=cost(2 * 2 * n * n * xt.shape[1], 4 * count * n * n),
+        name="blocks",
+    )(pos, after, xt, near, far)
 
 
 def total_kernel(after_ref, *refs):
@@ -298,36 +310,28 @@
     return value, packed.astype(jnp.float16)
 
 
-def merge_kernel(pos_ref, after_ref, *refs):
-    del after_ref
-    sums, (mine_ref, sib_ref, top_ref, t_ref) = refs[:4], refs[4:]
-    n = t_ref.shape[0] - 8
+def merge_kernel(pos_ref, own_ref, cross_ref, mine_ref, sib_ref, top_ref, t_ref):
+    n = own_ref.shape[0]
     half = n // 2
-    chip, group, core = pos_ref[0], pos_ref[1], pos_ref[2]
-
-    def put(own_ref, cross_ref):
-        t_ref[0:n] = own_ref[...].T + cross_ref[0:n] * jnp.exp2(cross_ref[n : n + 1] - TOP)
-
-    distant = jnp.abs(chip - group) == 2
-    pl.when(jnp.logical_not(distant))(lambda: put(*sums[:2]))
-    pl.when(distant)(lambda: put(*sums[2:]))
+    t_ref[0:n] = own_ref[...].T + cross_ref[0:n] * jnp.exp2(cross_ref[n : n + 1] - TOP)
+    core = pos_ref[2]
     top_ref[...] = t_ref[0:8]
     mine_ref[...] = t_ref[pl.ds(pl.multiple_of(core * half, 8), half + 8)]
     sib_ref[...] = t_ref[pl.ds(pl.multiple_of((1 - core) * half, 8), half + 8)]
 
 
-def merge(pos, after, near, far):
-    n = near[0].shape[0]
+def merge(pos, own, cross):
+    n = own.shape[0]
     half = n // 2
     return pl.pallas_call(
         merge_kernel,
         out_shape=tuple(jax.ShapeDtypeStruct((r, n), F32) for r in (half + 8, half + 8, 8)),
-        in_specs=[SMEM, pl.BlockSpec(memory_space=pl.ANY)] + [VMEM] * 4,
+        in_specs=[SMEM] + [VMEM] * 2,
         out_specs=(VMEM,) * 3,
         scratch_shapes=[pltpu.VMEM((n + 8, n), F32)],
         compiler_params=params(),
         name="merge",
-    )(pos, after, *near, *far)
+    )(pos, own, cross)
 
 
 def tiles_kernel(pos_ref, w_ref, g_ref, own_ref, sib_ref, top_ref, out_ref, p_ref):
@@ -419,31 +423,17 @@
         return 0 if (z - k) % groups == 1 or z - k == 2 else 1
 
     homes = {(k, z): (k, z, holder(k, z)) for k in every for z in every if k != z}
-    far_homes = {pair: home for pair, home in homes.items() if abs(pair[0] - pair[1]) == 2}
-    near_homes = {pair: home for pair, home in homes.items() if pair not in far_homes}
-
-    def gathered(block, group_homes):
-        half = block.astype(jnp.float16)
-        return [block] + [
-            send(half, [(at(k ^ m, z, c), at(k, z, c)) for k, z, c in group_homes.values()]) for m in range(1, groups)
-        ]
-
-    def exchanged(packed, group_homes):
-        received = send(packed, [(at(*home), at(*homes[z, k])) for (k, z), home in group_homes.items()])
-        return received.astype(F32)
-
-    near_block = pair_block(state[0], xt, near)
-    near_parts = gathered(near_block, near_homes)
-    state = factor_part(1, 1, state, (near_block,))
-    far_block = pair_block(state[0], xt, far)
-    far_parts = gathered(far_block, far_homes)
-    state = factor_part(2, 1, state, (far_block,))
-    near_own, packed = total(state[0], near_parts)
-    near_cross = exchanged(packed, near_homes)
-    far_own, packed = total(state[0], far_parts)
-    far_cross = exchanged(packed, far_homes)
-    w = factor_part(3, 1, state, (far_own,))[1]
-    mine, sib, top = merge(pos, w, (near_own, near_cross), (far_own, far_cross))
+
+    state = factor_part(1, 2, state)
+    slots = blocks(pos, state[0], xt, near, far, groups)
+    parts = [slots[0]] + [
+        send(slots[m].astype(jnp.float16), [(at(k ^ m, z, c), at(k, z, c)) for k, z, c in homes.values()])
+        for m in range(1, groups)
+    ]
+    w = factor_part(3, 1, state, (slots[0],))[1]
+    own, packed = total(w, parts)
+    cross = send(packed, [(at(*home), at(*homes[z, k])) for (k, z), home in homes.items()])
+    mine, sib, top = merge(pos, own, cross.astype(F32))
     sib = send(sib, [(at(k, z, c), at(k, z, 1 - c)) for k, z, c in homes.values()])
     top = send(top, [(at(k, z, c), at((k - 1) % groups, z, 1)) for k, z, c in homes.values()])
     return tiles(pos, w, gram, (mine, sib, top))

time: 65.1 us -> 67.1 us (1.031)
  the two profiles are of different devices: /device:TPU:3 before, /device:TPU:23 now
where the time goes in v12:
time: 67.1 us; the launch traced here: 66.7 us
  starting transfers between devices  29.8 us (44%)
  waiting for transfers between devices  18.3 us (27%)
  Pallas kernels  15.6 us (23%)
  local copies, waits for them, and re-layouts  1.77 us (3%)
  other arithmetic  1 us (1%)
    ppermute x13, starting transfers between devices, send(): return lax.ppermute(value, axes, pairs)  27.1 us
    ppermute x13, waiting for transfers between devices, send(): return lax.ppermute(value, axes, pairs)  18.3 us
    pallas_call x3, Pallas kernels, factor_part(): pl.pallas_call(kernel, out_shape=(jax.ShapeDtypeStruct((n, n), F32),) * 2...  10.1 us
    ppermute x1, starting transfers between devices, start(): near = lax.ppermute(jnp.where(odd == 0, tail, head), 'space', inside)  2 us
    unnamed x4, local copies, waits for them, and re-layouts  1.67 us
    pallas_call x1, Pallas kernels, tiles(): pl.pallas_call(tiles_kernel, out_shape=jax.ShapeDtypeStruct((n, half), F3...  1.62 us
  transfers between devices with their start and end apart: 15, of which 10 were waited for; matrix products, arithmetic and copies ran while one was open for 0% of the time, Pallas kernels for 17%

profile of v12, /device:TPU:23, one launch (start us, length us, event | category | flops | bytes accessed | tf_op | source)
XLA Modules:
  0.0 66.7 jit_solution(18127926955891228823)
XLA Ops:
  0.0 0.7 %broadcast_select_fusion = (bf16[3,1,256]{2,1,0:T(2,128)(2,1)S(1)}, bf16[3,1,256]{2,1,0:T(2,128)(2,1)S(1)}) fusion(pred[]{:T(512)S(6)} %eq.6, bf16[3,384,256]{2,1,0:T(8,128)(2,1)} %vel_ref.1), kind=kLoop, calls=%fused_computation.1 | loop fusion | flops 1536 | bytes 6145 | tf_op jit(solution)/shard_map/jit(_where)/select_n | solution.py:383
  0.7 0.7 collective-permute-start.1
  1.4 2.0 %collective-permute-start = (bf16[3,1,256]{2,1,0:T(2,128)(2,1)S(1)}, bf16[3,1,256]{2,1,0:T(2,128)(2,1)S(1)}, u32[]{:S(2)}, u32[]{:S(2)}) collective-permute-start(bf16[3,1,256]{2,1,0:T(2,128)(2,1)S(1)} %get-tuple-element.48), channel_id=1, source_target_pairs={{0,4},{4,0},{8,12},{12,8},{16,20},{20,16},{24,28},{28,24},{1,5},{5... | collective-permute-start | bytes 4616 | tf_op jit(solution)/shard_map/ppermute | solution.py:384
  3.5 0.6 copy-done.1
  4.2 1.1 %copy-done = bf16[3,384,256]{2,1,0:T(8,128)(2,1)S(1)} copy-done((bf16[3,384,256]{2,1,0:T(8,128)(2,1)S(1)}, bf16[3,384,256]{2,1,0:T(8,128)(2,1)}, u32[]{:S(2)}) %copy-start) | copy-done | bytes 589848
  5.7 1.0 %panel.1 = (bf16[1152,256]{1,0:T(8,128)(2,1)S(1)}, bf16[256,1152]{1,0:T(8,128)(2,1)S(1)}, f32[192,128]{1,0:T(8,128)S(1)}, f32[192,128]{1,0:T(8,128)S(1)}) custom-call(s32[4]{0:T(128)S(1)} %pad_add_fusion.pos_ref, bf16[1152,256]{1,0:T(8,128)(2,1)S(1)} %get-tuple-element.26.x_in_ref, f32[3,8,256]{2,1,0:T(8,128)S(1)} %get-tuple-element.27.head_ref, ...), custom_call_target="tpu_custom_call" | custom-call | flops 150994944 | bytes 1769472 | tf_op jit(solution)/shard_map/panel/pallas_call | solution.py:112
  6.9 2.0 %collective-permute-start.2 = (f32[192,128]{1,0:T(8,128)S(1)}, f32[192,128]{1,0:T(8,128)S(1)}, u32[]{:S(2)}, u32[]{:S(2)}) collective-permute-start(f32[192,128]{1,0:T(8,128)S(1)} %get-tuple-element.30), channel_id=1, source_target_pairs={{0,4},{4,0},{1,5},{5,1},{2,6},{6,2},{3,7},{7,3},{8,12},{12,8},{9,1... | collective-permute-start | bytes 294920 | tf_op jit(solution)/shard_map/ppermute | solution.py:399
  9.0 0.9 %collective-permute-done.2 = f32[192,128]{1,0:T(8,128)S(1)} collective-permute-done((f32[192,128]{1,0:T(8,128)S(1)}, f32[192,128]{1,0:T(8,128)S(1)}, u32[]{:S(2)}, u32[]{:S(2)}) %collective-permute-start.2) | collective-permute-done | bytes 98336 | tf_op jit(solution)/shard_map/ppermute | solution.py:399
  9.9 1.2 %collective-permute-start.5 = (f32[192,128]{1,0:T(8,128)S(1)}, f32[192,128]{1,0:T(8,128)S(1)}, u32[]{:S(2)}, u32[]{:S(2)}) collective-permute-start(f32[192,128]{1,0:T(8,128)S(1)} %add.18), channel_id=1, source_target_pairs={{0,24},{4,28},{1,25},{5,29},{2,26},{6,30},{3,27},{7,31},{8,16},{12... | collective-permute-start | bytes 294920 | tf_op jit(solution)/shard_map/ppermute | solution.py:399
  11.2 1.2 %collective-permute-start.4 = (f32[192,128]{1,0:T(8,128)S(1)}, f32[192,128]{1,0:T(8,128)S(1)}, u32[]{:S(2)}, u32[]{:S(2)}) collective-permute-start(f32[192,128]{1,0:T(8,128)S(1)} %add.18), channel_id=1, source_target_pairs={{0,16},{4,20},{1,17},{5,21},{2,18},{6,22},{3,19},{7,23},{8,24},{12... | collective-permute-start | bytes 294920 | tf_op jit(solution)/shard_map/ppermute | solution.py:399
  12.6 2.3 %collective-permute-done.5 = f32[192,128]{1,0:T(8,128)S(1)} collective-permute-done((f32[192,128]{1,0:T(8,128)S(1)}, f32[192,128]{1,0:T(8,128)S(1)}, u32[]{:S(2)}, u32[]{:S(2)}) %collective-permute-start.5) | collective-permute-done | bytes 98336 | tf_op jit(solution)/shard_map/ppermute | solution.py:399
  14.9 2.8 %collective-permute-done.4 = f32[192,128]{1,0:T(8,128)S(1)} collective-permute-done((f32[192,128]{1,0:T(8,128)S(1)}, f32[192,128]{1,0:T(8,128)S(1)}, u32[]{:S(2)}, u32[]{:S(2)}) %collective-permute-start.4) | collective-permute-done | bytes 98336 | tf_op jit(solution)/shard_map/ppermute | solution.py:399
  17.7 0.6 collective-permute-start.6
  18.3 0.9 %collective-permute-done.6.theirs_ref = f32[192,128]{1,0:T(8,128)S(1)} collective-permute-done((f32[192,128]{1,0:T(8,128)S(1)}, f32[192,128]{1,0:T(8,128)S(1)}, u32[]{:S(2)}, u32[]{:S(2)}) %collective-permute-start.6) | collective-permute-done | bytes 98336 | tf_op jit(solution)/shard_map/ppermute | solution.py:399
  19.2 0.6 gather.1.refs_0_.g_ref
  19.9 2.6 %factor.3 = (f32[256,256]{1,0:T(8,128)S(1)}, f32[256,256]{1,0:T(8,128)S(1)}) custom-call(f32[256,256]{1,0:T(8,128)S(1)} %gather.1.refs_0_.g_ref), custom_call_target="tpu_custom_call" | custom-call | flops 33554432 | bytes 524288 | tf_op jit(solution)/shard_map/factor/pallas_call | solution.py:227
  22.5 2.1 %collective-permute-start.8 = (bf16[1152,256]{1,0:T(8,128)(2,1)S(1)}, bf16[1152,256]{1,0:T(8,128)(2,1)S(1)}, u32[]{:S(2)}, u32[]{:S(2)}) collective-permute-start(bf16[1152,256]{1,0:T(8,128)(2,1)S(1)} %passed.1.near_ref), channel_id=1, source_target_pairs={{1,2},{2,3},{9,10},{10,11},{17,18},{18,19},{25,26},{26,27},{6,5},{... | collective-permute-start | bytes 1769480 | tf_op jit(solution)/shard_map/ppermute | solution.py:399
  24.6 4.9 %factor.4 = (f32[256,256]{1,0:T(8,128)S(1)}, f32[256,256]{1,0:T(8,128)S(1)}) custom-call(f32[256,256]{1,0:T(8,128)S(1)} %get-tuple-element.31.refs_0_.refs_1_, f32[256,256]{1,0:T(8,128)S(1)} %get-tuple-element.32.refs_1_), custom_call_target="tpu_custom_call" | custom-call | flops 33554432 | bytes 524288 | tf_op jit(solution)/shard_map/factor/pallas_call | solution.py:227
  29.5 1.9 %collective-permute-done.8.far_ref = bf16[1152,256]{1,0:T(8,128)(2,1)S(1)} collective-permute-done((bf16[1152,256]{1,0:T(8,128)(2,1)S(1)}, bf16[1152,256]{1,0:T(8,128)(2,1)S(1)}, u32[]{:S(2)}, u32[]{:S(2)}) %collective-permute-start.8) | collective-permute-done | bytes 589856 | tf_op jit(solution)/shard_map/ppermute | solution.py:399
  31.4 1.1 %blocks.1 = (f32[272,256]{1,0:T(8,128)S(1)}, f32[272,256]{1,0:T(8,128)S(1)}, f32[272,256]{1,0:T(8,128)S(1)}, f32[272,256]{1,0:T(8,128)S(1)}) custom-call(s32[4]{0:T(128)S(1)} %pad_add_fusion.pos_ref, f32[256,256]{1,0:T(8,128)S(1)} %get-tuple-element.33.after_ref.refs_0_, bf16[256,1152]{1,0:T(8,128)(2,1)S(1)} %get-tuple-element.35.xt_ref, ...), custom_call_target="tpu_custom_call" | custom-call | flops 301989888 | bytes 1048576 | tf_op jit(solution)/shard_map/blocks/pallas_call | solution.py:275
  32.5 1.3 %collective-permute-start.11 = (f16[272,256]{1,0:T(8,128)(2,1)S(1)}, f16[272,256]{1,0:T(8,128)(2,1)S(1)}, u32[]{:S(2)}, u32[]{:S(2)}) collective-permute-start(f16[272,256]{1,0:T(8,128)(2,1)S(1)} %convert_element_type.28), channel_id=1, source_target_pairs={{25,1},{26,2},{31,7},{20,12},{18,10},{19,11},{12,20},{13,21},{11,1... | collective-permute-start | bytes 417800 | tf_op jit(solution)/shard_map/ppermute | solution.py:399
  33.8 1.3 %collective-permute-start.10 = (f16[272,256]{1,0:T(8,128)(2,1)S(1)}, f16[272,256]{1,0:T(8,128)(2,1)S(1)}, u32[]{:S(2)}, u32[]{:S(2)}) collective-permute-start(f16[272,256]{1,0:T(8,128)(2,1)S(1)} %convert_element_type.26), channel_id=1, source_target_pairs={{17,1},{18,2},{23,7},{28,12},{26,10},{27,11},{4,20},{5,21},{3,19},... | collective-permute-start | bytes 417800 | tf_op jit(solution)/shard_map/ppermute | solution.py:399
  35.2 1.3 %collective-permute-start.9 = (f16[272,256]{1,0:T(8,128)(2,1)S(1)}, f16[272,256]{1,0:T(8,128)(2,1)S(1)}, u32[]{:S(2)}, u32[]{:S(2)}) collective-permute-start(f16[272,256]{1,0:T(8,128)(2,1)S(1)} %convert_element_type.24), channel_id=1, source_target_pairs={{9,1},{10,2},{15,7},{4,12},{2,10},{3,11},{28,20},{29,21},{27,19},{... | collective-permute-start | bytes 417800 | tf_op jit(solution)/shard_map/ppermute | solution.py:399
  36.5 2.6 %factor.5 = (f32[256,256]{1,0:T(8,128)}, f32[256,256]{1,0:T(8,128)S(1)}) custom-call(f32[256,256]{1,0:T(8,128)S(1)} %get-tuple-element.33.after_ref.refs_0_, f32[256,256]{1,0:T(8,128)S(1)} %get-tuple-element.34.refs_1_, f32[272,256]{1,0:T(8,128)S(1)} %get-tuple-element.37.refs_2_.refs_0_), custom_call_target="tpu_custom_call" | custom-call | flops 33554432 | bytes 524288 | tf_op jit(solution)/shard_map/factor/pallas_call | solution.py:227
  39.4 1.4 %collective-permute-done.10 = f16[272,256]{1,0:T(8,128)(2,1)S(1)} collective-permute-done((f16[272,256]{1,0:T(8,128)(2,1)S(1)}, f16[272,256]{1,0:T(8,128)(2,1)S(1)}, u32[]{:S(2)}, u32[]{:S(2)}) %collective-permute-start.10) | collective-permute-done | bytes 139296 | tf_op jit(solution)/shard_map/ppermute | solution.py:399
  41.1 12.4 %collective-permute-start.12 = (f16[272,256]{1,0:T(8,128)(2,1)S(1)}, f16[272,256]{1,0:T(8,128)(2,1)S(1)}, u32[]{:S(2)}, u32[]{:S(2)}) collective-permute-start(f16[272,256]{1,0:T(8,128)(2,1)S(1)} %convert_element_type.30), channel_id=1, source_target_pairs={{1,12},{2,20},{7,24},{12,1},{10,21},{11,29},{20,2},{21,10},{19,30}... | collective-permute-start | bytes 417800 | tf_op jit(solution)/shard_map/ppermute | solution.py:399
  53.5 3.7 %collective-permute-done.12 = f16[272,256]{1,0:T(8,128)(2,1)S(1)} collective-permute-done((f16[272,256]{1,0:T(8,128)(2,1)S(1)}, f16[272,256]{1,0:T(8,128)(2,1)S(1)}, u32[]{:S(2)}, u32[]{:S(2)}) %collective-permute-start.12) | collective-permute-done | bytes 139296 | tf_op jit(solution)/shard_map/ppermute | solution.py:399
  57.2 0.7 %merge.1 = (f32[136,256]{1,0:T(8,128)S(1)}, f32[136,256]{1,0:T(8,128)S(1)}, f32[8,256]{1,0:T(8,128)S(1)}) custom-call(s32[4]{0:T(128)S(1)} %pad_add_fusion.pos_ref, f32[256,256]{1,0:T(8,128)S(1)} %get-tuple-element.42.own_ref, f32[272,256]{1,0:T(8,128)S(1)} %convert_element_type.31.cross_ref), custom_call_target="tpu_custom_call" | custom-call | tf_op jit(solution)/shard_map/merge/pallas_call | solution.py:326
  57.9 1.3 %collective-permute-start.13 = (f32[136,256]{1,0:T(8,128)S(1)}, f32[136,256]{1,0:T(8,128)S(1)}, u32[]{:S(2)}, u32[]{:S(2)}) collective-permute-start(f32[136,256]{1,0:T(8,128)S(1)} %get-tuple-element.45), channel_id=1, source_target_pairs={{1,5},{2,6},{7,3},{12,8},{10,14},{11,15},{20,16},{21,17},{19,23},{... | collective-permute-start | bytes 417800 | tf_op jit(solution)/shard_map/ppermute | solution.py:399
  59.2 1.9 %collective-permute-start.14 = (f32[8,256]{1,0:T(8,128)S(1)}, f32[8,256]{1,0:T(8,128)S(1)}, u32[]{:S(2)}, u32[]{:S(2)}) collective-permute-start(f32[8,256]{1,0:T(8,128)S(1)} %get-tuple-element.46), channel_id=1, source_target_pairs={{1,29},{2,30},{7,31},{12,4},{10,6},{11,7},{20,12},{21,13},{19,15},... | collective-permute-start | bytes 24584 | tf_op jit(solution)/shard_map/ppermute | solution.py:399
  61.1 3.9 %collective-permute-done.14.top_ref = f32[8,256]{1,0:T(8,128)S(1)} collective-permute-done((f32[8,256]{1,0:T(8,128)S(1)}, f32[8,256]{1,0:T(8,128)S(1)}, u32[]{:S(2)}, u32[]{:S(2)}) %collective-permute-start.14) | collective-permute-done | bytes 8224 | tf_op jit(solution)/shard_map/ppermute | solution.py:399
  65.1 1.6 %tiles.1 = f32[256,128]{1,0:T(8,128)} custom-call(s32[4]{0:T(128)S(1)} %pad_add_fusion.pos_ref, f32[256,256]{1,0:T(8,128)S(1)} %get-tuple-element.38.after_ref.w_ref, f32[256,256]{1,0:T(8,128)S(1)} %gather.1.refs_0_.g_ref, f32[136,256]{1,0:T(8,128)S(1)} %get-tuple-element.44.own_ref, f32[136,256]{1,0:T(8,128)S(1)} %collective-permute-done.13.sib_ref, ...), custom_call_target="tpu_custom_call" | custom-call | tf_op jit(solution)/shard_map/tiles/pallas_call | solution.py:363
  (26 shorter events, 1.8 us)
Async XLA Ops:
  0.7 5.0 %collective-permute-start.1 = (bf16[3,1,256]{2,1,0:T(2,128)(2,1)S(1)}, bf16[3,1,256]{2,1,0:T(2,128)(2,1)S(1)}, u32[]{:S(2)}, u32[]{:S(2)}) collective-permute-start(bf16[3,1,256]{2,1,0:T(2,128)(2,1)S(1)} %get-tuple-element.47), channel_id=1, source_target_pairs={{4,8},{12,16},{20,24},{8,4},{16,12},{24,20},{5,9},{13,17},{21,25},... | collective-permute-start | bytes 4616 | tf_op jit(solution)/shard_map/ppermute | solution.py:383
  1.4 4.3 %collective-permute-start = (bf16[3,1,256]{2,1,0:T(2,128)(2,1)S(1)}, bf16[3,1,256]{2,1,0:T(2,128)(2,1)S(1)}, u32[]{:S(2)}, u32[]{:S(2)}) collective-permute-start(bf16[3,1,256]{2,1,0:T(2,128)(2,1)S(1)} %get-tuple-element.48), channel_id=1, source_target_pairs={{0,4},{4,0},{8,12},{12,8},{16,20},{20,16},{24,28},{28,24},{1,5},{5... | collective-permute-start | bytes 4616 | tf_op jit(solution)/shard_map/ppermute | solution.py:384
  3.4 0.7 %copy-start.1 = (f32[384]{0:T(512)S(1)}, f32[384]{0:T(512)}, u32[]{:S(2)}) copy-start(f32[384]{0:T(512)} %param.3) | copy-start | bytes 4612
  4.2 1.1 %copy-start = (bf16[3,384,256]{2,1,0:T(8,128)(2,1)S(1)}, bf16[3,384,256]{2,1,0:T(8,128)(2,1)}, u32[]{:S(2)}) copy-start(bf16[3,384,256]{2,1,0:T(8,128)(2,1)} %vel_ref.1) | copy-start | bytes 1769476
  6.7 15.8 %collective-permute-start.7 = (bf16[1152,256]{1,0:T(8,128)(2,1)S(1)}, bf16[1152,256]{1,0:T(8,128)(2,1)S(1)}, u32[]{:S(2)}, u32[]{:S(2)}) collective-permute-start(bf16[1152,256]{1,0:T(8,128)(2,1)S(1)} %get-tuple-element.36), channel_id=1, source_target_pairs={{0,1},{1,2},{2,3},{3,0},{8,9},{9,10},{10,11},{11,8},{16,17},{17,18... | collective-permute-start | bytes 1769480 | tf_op jit(solution)/shard_map/ppermute | solution.py:399
  6.9 3.0 %collective-permute-start.2 = (f32[192,128]{1,0:T(8,128)S(1)}, f32[192,128]{1,0:T(8,128)S(1)}, u32[]{:S(2)}, u32[]{:S(2)}) collective-permute-start(f32[192,128]{1,0:T(8,128)S(1)} %get-tuple-element.30), channel_id=1, source_target_pairs={{0,4},{4,0},{1,5},{5,1},{2,6},{6,2},{3,7},{7,3},{8,12},{12,8},{9,1... | collective-permute-start | bytes 294920 | tf_op jit(solution)/shard_map/ppermute | solution.py:399
  9.9 5.0 %collective-permute-start.5 = (f32[192,128]{1,0:T(8,128)S(1)}, f32[192,128]{1,0:T(8,128)S(1)}, u32[]{:S(2)}, u32[]{:S(2)}) collective-permute-start(f32[192,128]{1,0:T(8,128)S(1)} %add.18), channel_id=1, source_target_pairs={{0,24},{4,28},{1,25},{5,29},{2,26},{6,30},{3,27},{7,31},{8,16},{12... | collective-permute-start | bytes 294920 | tf_op jit(solution)/shard_map/ppermute | solution.py:399
  11.2 6.6 %collective-permute-start.4 = (f32[192,128]{1,0:T(8,128)S(1)}, f32[192,128]{1,0:T(8,128)S(1)}, u32[]{:S(2)}, u32[]{:S(2)}) collective-permute-start(f32[192,128]{1,0:T(8,128)S(1)} %add.18), channel_id=1, source_target_pairs={{0,16},{4,20},{1,17},{5,21},{2,18},{6,22},{3,19},{7,23},{8,24},{12... | collective-permute-start | bytes 294920 | tf_op jit(solution)/shard_map/ppermute | solution.py:399
  12.4 5.3 %collective-permute-start.3 = (f32[192,128]{1,0:T(8,128)S(1)}, f32[192,128]{1,0:T(8,128)S(1)}, u32[]{:S(2)}, u32[]{:S(2)}) collective-permute-start(f32[192,128]{1,0:T(8,128)S(1)} %add.18), channel_id=1, source_target_pairs={{0,8},{4,12},{1,9},{5,13},{2,10},{6,14},{3,11},{7,15},{8,0},{12,4}... | collective-permute-start | bytes 294920 | tf_op jit(solution)/shard_map/ppermute | solution.py:399
  17.7 1.5 %collective-permute-start.6 = (f32[192,128]{1,0:T(8,128)S(1)}, f32[192,128]{1,0:T(8,128)S(1)}, u32[]{:S(2)}, u32[]{:S(2)}) collective-permute-start(f32[192,128]{1,0:T(8,128)S(1)} %add_add_fusion.mine_ref), channel_id=1, source_target_pairs={{0,4},{4,0},{1,5},{5,1},{2,6},{6,2},{3,7},{7,3},{8,12},{12,8},{9,1... | collective-permute-start | bytes 294920 | tf_op jit(solution)/shard_map/ppermute | solution.py:399
  22.5 8.9 %collective-permute-start.8 = (bf16[1152,256]{1,0:T(8,128)(2,1)S(1)}, bf16[1152,256]{1,0:T(8,128)(2,1)S(1)}, u32[]{:S(2)}, u32[]{:S(2)}) collective-permute-start(bf16[1152,256]{1,0:T(8,128)(2,1)S(1)} %passed.1.near_ref), channel_id=1, source_target_pairs={{1,2},{2,3},{9,10},{10,11},{17,18},{18,19},{25,26},{26,27},{6,5},{... | collective-permute-start | bytes 1769480 | tf_op jit(solution)/shard_map/ppermute | solution.py:399
  32.5 6.8 %collective-permute-start.11 = (f16[272,256]{1,0:T(8,128)(2,1)S(1)}, f16[272,256]{1,0:T(8,128)(2,1)S(1)}, u32[]{:S(2)}, u32[]{:S(2)}) collective-permute-start(f16[272,256]{1,0:T(8,128)(2,1)S(1)} %convert_element_type.28), channel_id=1, source_target_pairs={{25,1},{26,2},{31,7},{20,12},{18,10},{19,11},{12,20},{13,21},{11,1... | collective-permute-start | bytes 417800 | tf_op jit(solution)/shard_map/ppermute | solution.py:399
  33.8 6.9 %collective-permute-start.10 = (f16[272,256]{1,0:T(8,128)(2,1)S(1)}, f16[272,256]{1,0:T(8,128)(2,1)S(1)}, u32[]{:S(2)}, u32[]{:S(2)}) collective-permute-start(f16[272,256]{1,0:T(8,128)(2,1)S(1)} %convert_element_type.26), channel_id=1, source_target_pairs={{17,1},{18,2},{23,7},{28,12},{26,10},{27,11},{4,20},{5,21},{3,19},... | collective-permute-start | bytes 417800 | tf_op jit(solution)/shard_map/ppermute | solution.py:399
  35.2 5.8 %collective-permute-start.9 = (f16[272,256]{1,0:T(8,128)(2,1)S(1)}, f16[272,256]{1,0:T(8,128)(2,1)S(1)}, u32[]{:S(2)}, u32[]{:S(2)}) collective-permute-start(f16[272,256]{1,0:T(8,128)(2,1)S(1)} %convert_element_type.24), channel_id=1, source_target_pairs={{9,1},{10,2},{15,7},{4,12},{2,10},{3,11},{28,20},{29,21},{27,19},{... | collective-permute-start | bytes 417800 | tf_op jit(solution)/shard_map/ppermute | solution.py:399
  41.1 16.0 %collective-permute-start.12 = (f16[272,256]{1,0:T(8,128)(2,1)S(1)}, f16[272,256]{1,0:T(8,128)(2,1)S(1)}, u32[]{:S(2)}, u32[]{:S(2)}) collective-permute-start(f16[272,256]{1,0:T(8,128)(2,1)S(1)} %convert_element_type.30), channel_id=1, source_target_pairs={{1,12},{2,20},{7,24},{12,1},{10,21},{11,29},{20,2},{21,10},{19,30}... | collective-permute-start | bytes 417800 | tf_op jit(solution)/shard_map/ppermute | solution.py:399
  57.9 7.2 %collective-permute-start.13 = (f32[136,256]{1,0:T(8,128)S(1)}, f32[136,256]{1,0:T(8,128)S(1)}, u32[]{:S(2)}, u32[]{:S(2)}) collective-permute-start(f32[136,256]{1,0:T(8,128)S(1)} %get-tuple-element.45), channel_id=1, source_target_pairs={{1,5},{2,6},{7,3},{12,8},{10,14},{11,15},{20,16},{21,17},{19,23},{... | collective-permute-start | bytes 417800 | tf_op jit(solution)/shard_map/ppermute | solution.py:399
  59.2 5.9 %collective-permute-start.14 = (f32[8,256]{1,0:T(8,128)S(1)}, f32[8,256]{1,0:T(8,128)S(1)}, u32[]{:S(2)}, u32[]{:S(2)}) collective-permute-start(f32[8,256]{1,0:T(8,128)S(1)} %get-tuple-element.46), channel_id=1, source_target_pairs={{1,29},{2,30},{7,31},{12,4},{10,6},{11,7},{20,12},{21,13},{19,15},... | collective-permute-start | bytes 24584 | tf_op jit(solution)/shard_map/ppermute | solution.py:399

commit v13 on v10

--- a/solution.py
+++ b/solution.py
@@ -13,7 +13,7 @@
 VMEM = pl.BlockSpec(memory_space=pltpu.VMEM)
 SMEM = pl.BlockSpec(memory_space=pltpu.SMEM)
 LEAF = 64
-PIVOTS = 4
+PIVOTS = 8
 
 
 def params(mib=40):
@@ -69,7 +69,7 @@
     )(velocity, metric)
 
 
-def panel_kernel(pos_ref, x_in_ref, head_ref, tail_ref, near_ref, far_ref, met_ref, x_ref, xt_ref, *g_refs):
+def edges_kernel(pos_ref, x_in_ref, head_ref, tail_ref, near_ref, far_ref, met_ref, x_ref):
     cols = x_ref.shape[1]
     rows = x_ref.shape[0] // 3
     even = pos_ref[2] == 0
@@ -80,16 +80,19 @@
         third = combine(first, second, third, heads[0], heads[1])
         for k, value in enumerate((first, second, third)):
             span = slice(k * rows + start, k * rows + start + EDGE)
-            kept = x_in_ref[span].astype(F32)
+            kept = x_ref[span].astype(F32)
             x_ref[span] = jnp.where(row == at, value, kept).astype(BF16)
 
-    x_ref[...] = x_in_ref[...]
+    del x_in_ref
     lo = [jnp.where(even, far_ref[k].astype(F32), near_ref[k].astype(F32)) for k in range(3)]
     hi = [jnp.where(even, near_ref[k].astype(F32), far_ref[k].astype(F32)) for k in range(3)]
     low = met_ref[0:1]
     edge(0, lambda k: low * (head_ref[k, 1:2] - lo[k]) * 0.5, [head_ref[k, 0:1] for k in range(2)], 0)
     high = met_ref[rows - 1 : rows]
     edge(rows - EDGE, lambda k: high * (hi[k] - tail_ref[k, 6:7]) * 0.5, [tail_ref[k, 7:8] for k in range(2)], EDGE - 1)
+
+
+def panel_kernel(pos_ref, x_ref, xt_ref, *g_refs):
     xt_ref[...] = x_ref[...].T
     gram = jnp.dot(xt_ref[...], x_ref[...], preferred_element_type=F32)
     if len(g_refs) == 1:
@@ -97,28 +100,41 @@
         return
     away_ref, mine_ref, g_ref = g_refs
     g_ref[...] = gram
+    cols = x_ref.shape[1]
     half = cols // 2
     for ref, core in ((mine_ref, pos_ref[2]), (away_ref, 1 - pos_ref[2])):
         ref[0:half] = jnp.where(core == 0, g_ref[0:half, 0:half], g_ref[half:, half:])
         ref[half:] = jnp.where(core == 0, g_ref[half : half + half // 2, 0:half], g_ref[half + half // 2 :, 0:half])
 
 
-def panel(pos, inner, near, far, metric, packed):
+def edges(pos, inner, near, far, metric):
     x, head, tail = inner
+    return pl.pallas_call(
+        edges_kernel,
+        out_shape=jax.ShapeDtypeStruct(x.shape, BF16),
+        in_specs=[SMEM] + [VMEM] * 6,
+        out_specs=VMEM,
+        input_output_aliases={1: 0},
+        compiler_params=params(),
+        name="edges",
+    )(pos, x, head, tail, near, far, metric)
+
+
+def panel(pos, x, packed):
     height, cols = x.shape
     share = jax.ShapeDtypeStruct((3 * cols // 4, cols // 2), F32)
     whole = jax.ShapeDtypeStruct((cols, cols), F32)
     grams = (share, share) if packed else (whole,)
     return pl.pallas_call(
         panel_kernel,
-        out_shape=(jax.ShapeDtypeStruct((height, cols), BF16), jax.ShapeDtypeStruct((cols, height), BF16)) + grams,
-        in_specs=[SMEM] + [VMEM] * 6,
-        out_specs=(VMEM,) * (2 + len(grams)),
+        out_shape=(jax.ShapeDtypeStruct((cols, height), BF16),) + grams,
+        in_specs=[SMEM, VMEM],
+        out_specs=(VMEM,) * (1 + len(grams)),
         scratch_shapes=[pltpu.VMEM((cols, cols), F32)] if packed else [],
         compiler_params=params(),
         cost_estimate=cost(2 * height * cols * cols, 6 * height * cols),
         name="panel",
-    )(pos, x, head, tail, near, far, metric)
+    )(pos, x)
 
 
 def gather_kernel(pos_ref, mine_ref, theirs_ref, g_ref):
@@ -217,18 +233,27 @@
             w_ref[k:, :] -= mm(u[:, k:], done, ((0,), (0,)))
 
 
-def factor_part(first, leaves, state, after=()):
+def halves(value):
+    high = value.astype(BF16)
+    return high, (value - high.astype(F32)).astype(BF16)
+
+
+def factor_part(first, leaves, state, after=(), split=False):
     n = state[0].shape[0]
     skip = len(after)
 
     def kernel(*refs):
-        factor_kernel(first, leaves, *refs[: len(state)], *refs[len(state) + skip :])
+        made = refs[len(state) + skip :]
+        factor_kernel(first, leaves, *refs[: len(state)], *made[-2:])
+        if split:
+            made[0][...], made[1][...] = halves(made[-1][...])
 
     return pl.pallas_call(
         kernel,
-        out_shape=(jax.ShapeDtypeStruct((n, n), F32),) * 2,
+        out_shape=(jax.ShapeDtypeStruct((n, n), BF16 if split else F32),) * 2,
         in_specs=[VMEM] * len(state) + [pl.BlockSpec(memory_space=pl.ANY)] * skip,
         out_specs=(VMEM,) * 2,
+        scratch_shapes=[pltpu.VMEM((n, n), F32)] * 2 if split else [],
         compiler_params=params(),
         cost_estimate=cost(2 * n * n * n, 8 * n * n),
         name="factor",
@@ -330,7 +355,7 @@
     )(pos, after, *near, *far)
 
 
-def tiles_kernel(pos_ref, w_ref, g_ref, own_ref, sib_ref, top_ref, out_ref, p_ref):
+def tiles_kernel(pos_ref, high_ref, low_ref, g_ref, own_ref, sib_ref, top_ref, out_ref, p_ref):
     chip, group, core, count = pos_ref[0], pos_ref[1], pos_ref[2], pos_ref[3]
     half = out_ref.shape[1]
     following = jnp.where(chip + 1 == count, 0, chip + 1)
@@ -350,21 +375,24 @@
         p_ref[half:] = jnp.where(following == group, g_ref[0:8], top_ref[...])
 
     shifted = pltpu.roll(p_ref[...], half + 7, 0)[:half]
-    out_ref[...] = mm(w_ref[...], shifted, ((1,), (1,)))
+    high, low = halves(shifted)
+    dims = (((1,), (1,)), ((), ()))
+    product = functools.partial(lax.dot_general, dimension_numbers=dims, preferred_element_type=F32)
+    out_ref[...] = product(high_ref[...], high) + (product(high_ref[...], low) + product(low_ref[...], high))
 
 
 def tiles(pos, w, gram, slabs):
-    n = w.shape[0]
+    n = gram.shape[0]
     half = n // 2
     return pl.pallas_call(
         tiles_kernel,
         out_shape=jax.ShapeDtypeStruct((n, half), F32),
-        in_specs=[SMEM] + [VMEM] * 5,
+        in_specs=[SMEM] + [VMEM] * 6,
         out_specs=VMEM,
         scratch_shapes=[pltpu.VMEM((half + 8, n), F32)],
         compiler_params=params(),
         name="tiles",
-    )(pos, w, gram, *slabs)
+    )(pos, *w, gram, *slabs)
 
 
 def start(velocity, metric, packed):
@@ -379,7 +407,8 @@
     far = lax.ppermute(jnp.where(odd == 0, head, tail), "space", outside)
     near = lax.ppermute(jnp.where(odd == 0, tail, head), "space", inside)
     column = metric.reshape(-1, 1)
-    return pos, panel(pos, interior(velocity, column), near, far, column, packed)
+    x = edges(pos, interior(velocity, column), near, far, column)
+    return pos, (x, *panel(pos, x, packed))
 
 
 def paired_body(velocity, metric):
@@ -442,8 +471,8 @@
     near_cross = exchanged(packed, near_homes)
     far_own, packed = total(state[0], far_parts)
     far_cross = exchanged(packed, far_homes)
-    w = factor_part(3, 1, state, (far_own,))[1]
-    mine, sib, top = merge(pos, w, (near_own, near_cross), (far_own, far_cross))
+    w = factor_part(3, 1, state, (far_own, near_cross), True)
+    mine, sib, top = merge(pos, w[0], (near_own, near_cross), (far_own, far_cross))
     sib = send(sib, [(at(k, z, c), at(k, z, 1 - c)) for k, z, c in homes.values()])
     top = send(top, [(at(k, z, c), at((k - 1) % groups, z, 1)) for k, z, c in homes.values()])
     return tiles(pos, w, gram, (mine, sib, top))

time: 65.1 us -> 63.9 us (0.982)
  the two profiles are of different devices: /device:TPU:3 before, /device:TPU:5 now
where the time goes in v13:
time: 63.9 us; the launch traced here: 63 us
  starting transfers between devices  31.9 us (50%)
  Pallas kernels  15.5 us (24%)
  waiting for transfers between devices  12.4 us (19%)
  local copies, waits for them, and re-layouts  1.76 us (3%)
  other arithmetic  1.08 us (2%)
    ppermute x17, starting transfers between devices, send(): return lax.ppermute(value, axes, pairs)  28.2 us
    ppermute x17, waiting for transfers between devices, send(): return lax.ppermute(value, axes, pairs)  12.4 us
    pallas_call x4, Pallas kernels, factor_part(): pl.pallas_call(kernel, out_shape=(jax.ShapeDtypeStruct((n, n), BF16 if sp...  9.52 us
    ppermute x1, starting transfers between devices, start(): far = lax.ppermute(jnp.where(odd == 0, head, tail), 'space', outside)  3.02 us
    unnamed x4, local copies, waits for them, and re-layouts  1.66 us
    pallas_call x1, Pallas kernels, tiles(): pl.pallas_call(tiles_kernel, out_shape=jax.ShapeDtypeStruct((n, half), F3...  1.51 us
  transfers between devices with their start and end apart: 19, of which 8 were waited for; matrix products, arithmetic and copies ran while one was open for 1% of the time, Pallas kernels for 20%

profile of v13, /device:TPU:5, one launch (start us, length us, event | category | flops | bytes accessed | tf_op | source)
XLA Modules:
  0.0 63.0 jit_solution(15524078386179891415)
XLA Ops:
  0.0 0.7 %broadcast_select_fusion = (bf16[3,1,256]{2,1,0:T(2,128)(2,1)S(1)}, bf16[3,1,256]{2,1,0:T(2,128)(2,1)S(1)}) fusion(pred[]{:T(512)S(6)} %eq.6, bf16[3,384,256]{2,1,0:T(8,128)(2,1)} %vel_ref.1), kind=kLoop, calls=%fused_computation.1 | loop fusion | flops 1536 | bytes 6145 | tf_op jit(solution)/shard_map/jit(_where)/select_n | solution.py:407
  0.7 0.7 %collective-permute-start = (bf16[3,1,256]{2,1,0:T(2,128)(2,1)S(1)}, bf16[3,1,256]{2,1,0:T(2,128)(2,1)S(1)}, u32[]{:S(2)}, u32[]{:S(2)}) collective-permute-start(bf16[3,1,256]{2,1,0:T(2,128)(2,1)S(1)} %get-tuple-element.48), channel_id=1, source_target_pairs={{0,4},{4,0},{8,12},{12,8},{16,20},{20,16},{24,28},{28,24},{1,5},{5... | collective-permute-start | bytes 4616 | tf_op jit(solution)/shard_map/ppermute | solution.py:408
  1.5 3.0 %collective-permute-start.1 = (bf16[3,1,256]{2,1,0:T(2,128)(2,1)S(1)}, bf16[3,1,256]{2,1,0:T(2,128)(2,1)S(1)}, u32[]{:S(2)}, u32[]{:S(2)}) collective-permute-start(bf16[3,1,256]{2,1,0:T(2,128)(2,1)S(1)} %get-tuple-element.47), channel_id=1, source_target_pairs={{4,8},{12,16},{20,24},{8,4},{16,12},{24,20},{5,9},{13,17},{21,25},... | collective-permute-start | bytes 4616 | tf_op jit(solution)/shard_map/ppermute | solution.py:407
  5.3 1.1 %copy-done = bf16[3,384,256]{2,1,0:T(8,128)(2,1)S(1)} copy-done((bf16[3,384,256]{2,1,0:T(8,128)(2,1)S(1)}, bf16[3,384,256]{2,1,0:T(8,128)(2,1)}, u32[]{:S(2)}) %copy-start) | copy-done | bytes 589848
  7.5 3.4 %collective-permute-start.7 = (bf16[1152,256]{1,0:T(8,128)(2,1)S(1)}, bf16[1152,256]{1,0:T(8,128)(2,1)S(1)}, u32[]{:S(2)}, u32[]{:S(2)}) collective-permute-start(bf16[1152,256]{1,0:T(8,128)(2,1)S(1)} %edges.1.x_ref), channel_id=1, source_target_pairs={{0,1},{1,2},{2,3},{3,0},{8,9},{9,10},{10,11},{11,8},{16,17},{17,18... | collective-permute-start | bytes 1769480 | tf_op jit(solution)/shard_map/ppermute | solution.py:424
  10.8 0.9 %panel.1 = (bf16[256,1152]{1,0:T(8,128)(2,1)S(1)}, f32[192,128]{1,0:T(8,128)S(1)}, f32[192,128]{1,0:T(8,128)S(1)}) custom-call(s32[4]{0:T(128)S(1)} %pad_add_fusion.pos_ref, bf16[1152,256]{1,0:T(8,128)(2,1)S(1)} %edges.1.x_ref), custom_call_target="tpu_custom_call" | custom-call | flops 150994944 | bytes 1769472 | tf_op jit(solution)/shard_map/panel/pallas_call | solution.py:128
  11.8 1.3 %collective-permute-done.2 = f32[192,128]{1,0:T(8,128)S(1)} collective-permute-done((f32[192,128]{1,0:T(8,128)S(1)}, f32[192,128]{1,0:T(8,128)S(1)}, u32[]{:S(2)}, u32[]{:S(2)}) %collective-permute-start.2) | collective-permute-done | bytes 98336 | tf_op jit(solution)/shard_map/ppermute | solution.py:424
  13.1 1.7 %collective-permute-start.5 = (f32[192,128]{1,0:T(8,128)S(1)}, f32[192,128]{1,0:T(8,128)S(1)}, u32[]{:S(2)}, u32[]{:S(2)}) collective-permute-start(f32[192,128]{1,0:T(8,128)S(1)} %add.18), channel_id=1, source_target_pairs={{0,24},{4,28},{1,25},{5,29},{2,26},{6,30},{3,27},{7,31},{8,16},{12... | collective-permute-start | bytes 294920 | tf_op jit(solution)/shard_map/ppermute | solution.py:424
  14.8 1.0 %collective-permute-start.3 = (f32[192,128]{1,0:T(8,128)S(1)}, f32[192,128]{1,0:T(8,128)S(1)}, u32[]{:S(2)}, u32[]{:S(2)}) collective-permute-start(f32[192,128]{1,0:T(8,128)S(1)} %add.18), channel_id=1, source_target_pairs={{0,8},{4,12},{1,9},{5,13},{2,10},{6,14},{3,11},{7,15},{8,0},{12,4}... | collective-permute-start | bytes 294920 | tf_op jit(solution)/shard_map/ppermute | solution.py:424
  15.9 2.5 %collective-permute-done.5 = f32[192,128]{1,0:T(8,128)S(1)} collective-permute-done((f32[192,128]{1,0:T(8,128)S(1)}, f32[192,128]{1,0:T(8,128)S(1)}, u32[]{:S(2)}, u32[]{:S(2)}) %collective-permute-start.5) | collective-permute-done | bytes 98336 | tf_op jit(solution)/shard_map/ppermute | solution.py:424
  18.4 2.6 %collective-permute-done.4 = f32[192,128]{1,0:T(8,128)S(1)} collective-permute-done((f32[192,128]{1,0:T(8,128)S(1)}, f32[192,128]{1,0:T(8,128)S(1)}, u32[]{:S(2)}, u32[]{:S(2)}) %collective-permute-start.4) | collective-permute-done | bytes 98336 | tf_op jit(solution)/shard_map/ppermute | solution.py:424
  21.5 0.9 %collective-permute-done.6.theirs_ref = f32[192,128]{1,0:T(8,128)S(1)} collective-permute-done((f32[192,128]{1,0:T(8,128)S(1)}, f32[192,128]{1,0:T(8,128)S(1)}, u32[]{:S(2)}, u32[]{:S(2)}) %collective-permute-start.6) | collective-permute-done | bytes 98336 | tf_op jit(solution)/shard_map/ppermute | solution.py:424
  23.1 2.6 %factor.4 = (f32[256,256]{1,0:T(8,128)S(1)}, f32[256,256]{1,0:T(8,128)S(1)}) custom-call(f32[256,256]{1,0:T(8,128)S(1)} %gather.1.refs_0_.g_ref), custom_call_target="tpu_custom_call" | custom-call | flops 33554432 | bytes 524288 | tf_op jit(solution)/shard_map/factor/pallas_call | solution.py:251
  25.7 1.3 %collective-permute-start.8 = (bf16[1152,256]{1,0:T(8,128)(2,1)S(1)}, bf16[1152,256]{1,0:T(8,128)(2,1)S(1)}, u32[]{:S(2)}, u32[]{:S(2)}) collective-permute-start(bf16[1152,256]{1,0:T(8,128)(2,1)S(1)} %passed.1.panel_ref), channel_id=1, source_target_pairs={{1,2},{2,3},{9,10},{10,11},{17,18},{18,19},{25,26},{26,27},{6,5},{... | collective-permute-start | bytes 1769480 | tf_op jit(solution)/shard_map/ppermute | solution.py:424
  27.6 0.7 %collective-permute-start.12 = (f16[272,256]{1,0:T(8,128)(2,1)S(1)}, f16[272,256]{1,0:T(8,128)(2,1)S(1)}, u32[]{:S(2)}, u32[]{:S(2)}) collective-permute-start(f16[272,256]{1,0:T(8,128)(2,1)S(1)} %convert_element_type.40), channel_id=1, source_target_pairs={{9,1},{15,7},{4,12},{2,10},{29,21},{27,19},{16,24},{22,30}} | collective-permute-start | bytes 417800 | tf_op jit(solution)/shard_map/ppermute | solution.py:424
  28.2 0.7 %collective-permute-start.13 = (f16[272,256]{1,0:T(8,128)(2,1)S(1)}, f16[272,256]{1,0:T(8,128)(2,1)S(1)}, u32[]{:S(2)}, u32[]{:S(2)}) collective-permute-start(f16[272,256]{1,0:T(8,128)(2,1)S(1)} %convert_element_type.40), channel_id=1, source_target_pairs={{17,1},{23,7},{28,12},{26,10},{5,21},{3,19},{8,24},{14,30}} | collective-permute-start | bytes 417800 | tf_op jit(solution)/shard_map/ppermute | solution.py:424
  28.9 4.6 %collective-permute-start.14 = (f16[272,256]{1,0:T(8,128)(2,1)S(1)}, f16[272,256]{1,0:T(8,128)(2,1)S(1)}, u32[]{:S(2)}, u32[]{:S(2)}) collective-permute-start(f16[272,256]{1,0:T(8,128)(2,1)S(1)} %convert_element_type.40), channel_id=1, source_target_pairs={{25,1},{31,7},{20,12},{18,10},{13,21},{11,19},{0,24},{6,30}} | collective-permute-start | bytes 417800 | tf_op jit(solution)/shard_map/ppermute | solution.py:424
  33.5 2.5 %factor.5 = (f32[256,256]{1,0:T(8,128)S(1)}, f32[256,256]{1,0:T(8,128)S(1)}) custom-call(f32[256,256]{1,0:T(8,128)S(1)} %get-tuple-element.31.refs_1_.after_ref.refs_0_, f32[256,256]{1,0:T(8,128)S(1)} %get-tuple-element.32.refs_1_, f32[272,256]{1,0:T(8,128)S(1)} %block.2.refs_2_.refs_0_), custom_call_target="tpu_custom_call" | custom-call | flops 33554432 | bytes 524288 | tf_op jit(solution)/shard_map/factor/pallas_call | solution.py:251
  36.9 1.3 %collective-permute-start.9 = (f16[272,256]{1,0:T(8,128)(2,1)S(1)}, f16[272,256]{1,0:T(8,128)(2,1)S(1)}, u32[]{:S(2)}, u32[]{:S(2)}) collective-permute-start(f16[272,256]{1,0:T(8,128)(2,1)S(1)} %convert_element_type.36), channel_id=1, source_target_pairs={{10,2},{3,11},{28,20},{21,29}} | collective-permute-start | bytes 417800 | tf_op jit(solution)/shard_map/ppermute | solution.py:424
  38.2 1.3 %collective-permute-start.10 = (f16[272,256]{1,0:T(8,128)(2,1)S(1)}, f16[272,256]{1,0:T(8,128)(2,1)S(1)}, u32[]{:S(2)}, u32[]{:S(2)}) collective-permute-start(f16[272,256]{1,0:T(8,128)(2,1)S(1)} %convert_element_type.36), channel_id=1, source_target_pairs={{18,2},{27,11},{4,20},{13,29}} | collective-permute-start | bytes 417800 | tf_op jit(solution)/shard_map/ppermute | solution.py:424
  39.5 1.3 %collective-permute-start.11 = (f16[272,256]{1,0:T(8,128)(2,1)S(1)}, f16[272,256]{1,0:T(8,128)(2,1)S(1)}, u32[]{:S(2)}, u32[]{:S(2)}) collective-permute-start(f16[272,256]{1,0:T(8,128)(2,1)S(1)} %convert_element_type.36), channel_id=1, source_target_pairs={{26,2},{19,11},{12,20},{5,29}} | collective-permute-start | bytes 417800 | tf_op jit(solution)/shard_map/ppermute | solution.py:424
  40.9 2.4 %factor.6 = (f32[256,256]{1,0:T(8,128)S(1)}, f32[256,256]{1,0:T(8,128)S(1)}) custom-call(f32[256,256]{1,0:T(8,128)S(1)} %get-tuple-element.34.after_ref.refs_0_, f32[256,256]{1,0:T(8,128)S(1)} %get-tuple-element.35.refs_1_, f32[272,256]{1,0:T(8,128)S(1)} %block.3.refs_2_.refs_0_), custom_call_target="tpu_custom_call" | custom-call | flops 33554432 | bytes 524288 | tf_op jit(solution)/shard_map/factor/pallas_call | solution.py:251
  43.4 0.7 %collective-permute-start.15 = (f16[272,256]{1,0:T(8,128)(2,1)S(1)}, f16[272,256]{1,0:T(8,128)(2,1)S(1)}, u32[]{:S(2)}, u32[]{:S(2)}) collective-permute-start(f16[272,256]{1,0:T(8,128)(2,1)S(1)} %convert_element_type.44), channel_id=1, source_target_pairs={{1,12},{7,24},{12,1},{10,21},{21,10},{19,30},{24,7},{30,19}} | collective-permute-start | bytes 417800 | tf_op jit(solution)/shard_map/ppermute | solution.py:424
  44.2 2.0 %collective-permute-done.11 = f16[272,256]{1,0:T(8,128)(2,1)S(1)} collective-permute-done((f16[272,256]{1,0:T(8,128)(2,1)S(1)}, f16[272,256]{1,0:T(8,128)(2,1)S(1)}, u32[]{:S(2)}, u32[]{:S(2)}) %collective-permute-start.11) | collective-permute-done | bytes 139296 | tf_op jit(solution)/shard_map/ppermute | solution.py:424
  46.3 5.2 %collective-permute-start.16 = (f16[272,256]{1,0:T(8,128)(2,1)S(1)}, f16[272,256]{1,0:T(8,128)(2,1)S(1)}, u32[]{:S(2)}, u32[]{:S(2)}) collective-permute-start(f16[272,256]{1,0:T(8,128)(2,1)S(1)} %convert_element_type.46), channel_id=1, source_target_pairs={{2,20},{11,29},{20,2},{29,11}} | collective-permute-start | bytes 417800 | tf_op jit(solution)/shard_map/ppermute | solution.py:424
  51.6 2.0 %factor.7 = (bf16[256,256]{1,0:T(8,128)(2,1)S(1)}, bf16[256,256]{1,0:T(8,128)(2,1)S(1)}) custom-call(f32[256,256]{1,0:T(8,128)S(1)} %get-tuple-element.36.after_ref.refs_0_, f32[256,256]{1,0:T(8,128)S(1)} %get-tuple-element.37.refs_1_, f32[256,256]{1,0:T(8,128)S(1)} %get-tuple-element.38.refs_2_, f32[272,256]{1,0:T(8,128)S(1)} %convert_element_type.45.refs_3_.refs_1_), custom_call_target="tpu_custom_call" | custom-call | flops 33554432 | bytes 524288 | tf_op jit(solution)/shard_map/factor/pallas_call | solution.py:251
  53.6 0.9 %collective-permute-done.16 = f16[272,256]{1,0:T(8,128)(2,1)S(1)} collective-permute-done((f16[272,256]{1,0:T(8,128)(2,1)S(1)}, f16[272,256]{1,0:T(8,128)(2,1)S(1)}, u32[]{:S(2)}, u32[]{:S(2)}) %collective-permute-start.16) | collective-permute-done | bytes 139296 | tf_op jit(solution)/shard_map/ppermute | solution.py:424
  54.5 0.7 %merge.1 = (f32[136,256]{1,0:T(8,128)S(1)}, f32[136,256]{1,0:T(8,128)S(1)}, f32[8,256]{1,0:T(8,128)S(1)}) custom-call(s32[4]{0:T(128)S(1)} %pad_add_fusion.pos_ref, bf16[256,256]{1,0:T(8,128)(2,1)S(1)} %get-tuple-element.40.after_ref.high_ref, f32[256,256]{1,0:T(8,128)S(1)} %get-tuple-element.42.refs_0_, ...), custom_call_target="tpu_custom_call" | custom-call | tf_op jit(solution)/shard_map/merge/pallas_call | solution.py:347
  55.3 1.3 %collective-permute-start.17 = (f32[136,256]{1,0:T(8,128)S(1)}, f32[136,256]{1,0:T(8,128)S(1)}, u32[]{:S(2)}, u32[]{:S(2)}) collective-permute-start(f32[136,256]{1,0:T(8,128)S(1)} %get-tuple-element.45), channel_id=1, source_target_pairs={{1,5},{2,6},{7,3},{12,8},{10,14},{11,15},{20,16},{21,17},{19,23},{... | collective-permute-start | bytes 417800 | tf_op jit(solution)/shard_map/ppermute | solution.py:424
  56.6 3.2 %collective-permute-start.18 = (f32[8,256]{1,0:T(8,128)S(1)}, f32[8,256]{1,0:T(8,128)S(1)}, u32[]{:S(2)}, u32[]{:S(2)}) collective-permute-start(f32[8,256]{1,0:T(8,128)S(1)} %get-tuple-element.46), channel_id=1, source_target_pairs={{1,29},{2,30},{7,31},{12,4},{10,6},{11,7},{20,12},{21,13},{19,15},... | collective-permute-start | bytes 24584 | tf_op jit(solution)/shard_map/ppermute | solution.py:424
  59.7 1.8 %collective-permute-done.18.top_ref = f32[8,256]{1,0:T(8,128)S(1)} collective-permute-done((f32[8,256]{1,0:T(8,128)S(1)}, f32[8,256]{1,0:T(8,128)S(1)}, u32[]{:S(2)}, u32[]{:S(2)}) %collective-permute-start.18) | collective-permute-done | bytes 8224 | tf_op jit(solution)/shard_map/ppermute | solution.py:424
  61.5 1.5 %tiles.1 = f32[256,128]{1,0:T(8,128)} custom-call(s32[4]{0:T(128)S(1)} %pad_add_fusion.pos_ref, bf16[256,256]{1,0:T(8,128)(2,1)S(1)} %get-tuple-element.40.after_ref.high_ref, bf16[256,256]{1,0:T(8,128)(2,1)S(1)} %get-tuple-element.41.low_ref, f32[256,256]{1,0:T(8,128)S(1)} %gather.1.refs_0_.g_ref, f32[136,256]{1,0:T(8,128)S(1)} %get-tuple-element.44.own_ref, ...), custom_call_target="tpu_custom_call" | custom-call | tf_op jit(solution)/shard_map/tiles/pallas_call | solution.py:387
  (42 shorter events, 4.8 us)
Async XLA Ops:
  0.7 6.1 %collective-permute-start = (bf16[3,1,256]{2,1,0:T(2,128)(2,1)S(1)}, bf16[3,1,256]{2,1,0:T(2,128)(2,1)S(1)}, u32[]{:S(2)}, u32[]{:S(2)}) collective-permute-start(bf16[3,1,256]{2,1,0:T(2,128)(2,1)S(1)} %get-tuple-element.48), channel_id=1, source_target_pairs={{0,4},{4,0},{8,12},{12,8},{16,20},{20,16},{24,28},{28,24},{1,5},{5... | collective-permute-start | bytes 4616 | tf_op jit(solution)/shard_map/ppermute | solution.py:408
  1.5 5.3 %collective-permute-start.1 = (bf16[3,1,256]{2,1,0:T(2,128)(2,1)S(1)}, bf16[3,1,256]{2,1,0:T(2,128)(2,1)S(1)}, u32[]{:S(2)}, u32[]{:S(2)}) collective-permute-start(bf16[3,1,256]{2,1,0:T(2,128)(2,1)S(1)} %get-tuple-element.47), channel_id=1, source_target_pairs={{4,8},{12,16},{20,24},{8,4},{16,12},{24,20},{5,9},{13,17},{21,25},... | collective-permute-start | bytes 4616 | tf_op jit(solution)/shard_map/ppermute | solution.py:407
  4.5 0.7 %copy-start.1 = (f32[384]{0:T(512)S(1)}, f32[384]{0:T(512)}, u32[]{:S(2)}) copy-start(f32[384]{0:T(512)} %param.3) | copy-start | bytes 4612
  5.3 1.1 %copy-start = (bf16[3,384,256]{2,1,0:T(8,128)(2,1)S(1)}, bf16[3,384,256]{2,1,0:T(8,128)(2,1)}, u32[]{:S(2)}) copy-start(bf16[3,384,256]{2,1,0:T(8,128)(2,1)} %vel_ref.1) | copy-start | bytes 1769476
  7.5 18.3 %collective-permute-start.7 = (bf16[1152,256]{1,0:T(8,128)(2,1)S(1)}, bf16[1152,256]{1,0:T(8,128)(2,1)S(1)}, u32[]{:S(2)}, u32[]{:S(2)}) collective-permute-start(bf16[1152,256]{1,0:T(8,128)(2,1)S(1)} %edges.1.x_ref), channel_id=1, source_target_pairs={{0,1},{1,2},{2,3},{3,0},{8,9},{9,10},{10,11},{11,8},{16,17},{17,18... | collective-permute-start | bytes 1769480 | tf_op jit(solution)/shard_map/ppermute | solution.py:424
  11.8 1.4 %collective-permute-start.2 = (f32[192,128]{1,0:T(8,128)S(1)}, f32[192,128]{1,0:T(8,128)S(1)}, u32[]{:S(2)}, u32[]{:S(2)}) collective-permute-start(f32[192,128]{1,0:T(8,128)S(1)} %get-tuple-element.30), channel_id=1, source_target_pairs={{0,4},{4,0},{1,5},{5,1},{2,6},{6,2},{3,7},{7,3},{8,12},{12,8},{9,1... | collective-permute-start | bytes 294920 | tf_op jit(solution)/shard_map/ppermute | solution.py:424
  13.1 5.2 %collective-permute-start.5 = (f32[192,128]{1,0:T(8,128)S(1)}, f32[192,128]{1,0:T(8,128)S(1)}, u32[]{:S(2)}, u32[]{:S(2)}) collective-permute-start(f32[192,128]{1,0:T(8,128)S(1)} %add.18), channel_id=1, source_target_pairs={{0,24},{4,28},{1,25},{5,29},{2,26},{6,30},{3,27},{7,31},{8,16},{12... | collective-permute-start | bytes 294920 | tf_op jit(solution)/shard_map/ppermute | solution.py:424
  14.8 6.1 %collective-permute-start.4 = (f32[192,128]{1,0:T(8,128)S(1)}, f32[192,128]{1,0:T(8,128)S(1)}, u32[]{:S(2)}, u32[]{:S(2)}) collective-permute-start(f32[192,128]{1,0:T(8,128)S(1)} %add.18), channel_id=1, source_target_pairs={{0,16},{4,20},{1,17},{5,21},{2,18},{6,22},{3,19},{7,23},{8,24},{12... | collective-permute-start | bytes 294920 | tf_op jit(solution)/shard_map/ppermute | solution.py:424
  14.8 6.1 %collective-permute-start.3 = (f32[192,128]{1,0:T(8,128)S(1)}, f32[192,128]{1,0:T(8,128)S(1)}, u32[]{:S(2)}, u32[]{:S(2)}) collective-permute-start(f32[192,128]{1,0:T(8,128)S(1)} %add.18), channel_id=1, source_target_pairs={{0,8},{4,12},{1,9},{5,13},{2,10},{6,14},{3,11},{7,15},{8,0},{12,4}... | collective-permute-start | bytes 294920 | tf_op jit(solution)/shard_map/ppermute | solution.py:424
  21.0 1.5 %collective-permute-start.6 = (f32[192,128]{1,0:T(8,128)S(1)}, f32[192,128]{1,0:T(8,128)S(1)}, u32[]{:S(2)}, u32[]{:S(2)}) collective-permute-start(f32[192,128]{1,0:T(8,128)S(1)} %add_add_fusion.mine_ref), channel_id=1, source_target_pairs={{0,4},{4,0},{1,5},{5,1},{2,6},{6,2},{3,7},{7,3},{8,12},{12,8},{9,1... | collective-permute-start | bytes 294920 | tf_op jit(solution)/shard_map/ppermute | solution.py:424
  25.7 10.6 %collective-permute-start.8 = (bf16[1152,256]{1,0:T(8,128)(2,1)S(1)}, bf16[1152,256]{1,0:T(8,128)(2,1)S(1)}, u32[]{:S(2)}, u32[]{:S(2)}) collective-permute-start(bf16[1152,256]{1,0:T(8,128)(2,1)S(1)} %passed.1.panel_ref), channel_id=1, source_target_pairs={{1,2},{2,3},{9,10},{10,11},{17,18},{18,19},{25,26},{26,27},{6,5},{... | collective-permute-start | bytes 1769480 | tf_op jit(solution)/shard_map/ppermute | solution.py:424
  27.6 11.9 %collective-permute-start.12 = (f16[272,256]{1,0:T(8,128)(2,1)S(1)}, f16[272,256]{1,0:T(8,128)(2,1)S(1)}, u32[]{:S(2)}, u32[]{:S(2)}) collective-permute-start(f16[272,256]{1,0:T(8,128)(2,1)S(1)} %convert_element_type.40), channel_id=1, source_target_pairs={{9,1},{15,7},{4,12},{2,10},{29,21},{27,19},{16,24},{22,30}} | collective-permute-start | bytes 417800 | tf_op jit(solution)/shard_map/ppermute | solution.py:424
  28.2 12.6 %collective-permute-start.13 = (f16[272,256]{1,0:T(8,128)(2,1)S(1)}, f16[272,256]{1,0:T(8,128)(2,1)S(1)}, u32[]{:S(2)}, u32[]{:S(2)}) collective-permute-start(f16[272,256]{1,0:T(8,128)(2,1)S(1)} %convert_element_type.40), channel_id=1, source_target_pairs={{17,1},{23,7},{28,12},{26,10},{5,21},{3,19},{8,24},{14,30}} | collective-permute-start | bytes 417800 | tf_op jit(solution)/shard_map/ppermute | solution.py:424
  28.9 12.0 %collective-permute-start.14 = (f16[272,256]{1,0:T(8,128)(2,1)S(1)}, f16[272,256]{1,0:T(8,128)(2,1)S(1)}, u32[]{:S(2)}, u32[]{:S(2)}) collective-permute-start(f16[272,256]{1,0:T(8,128)(2,1)S(1)} %convert_element_type.40), channel_id=1, source_target_pairs={{25,1},{31,7},{20,12},{18,10},{13,21},{11,19},{0,24},{6,30}} | collective-permute-start | bytes 417800 | tf_op jit(solution)/shard_map/ppermute | solution.py:424
  36.9 7.2 %collective-permute-start.9 = (f16[272,256]{1,0:T(8,128)(2,1)S(1)}, f16[272,256]{1,0:T(8,128)(2,1)S(1)}, u32[]{:S(2)}, u32[]{:S(2)}) collective-permute-start(f16[272,256]{1,0:T(8,128)(2,1)S(1)} %convert_element_type.36), channel_id=1, source_target_pairs={{10,2},{3,11},{28,20},{21,29}} | collective-permute-start | bytes 417800 | tf_op jit(solution)/shard_map/ppermute | solution.py:424
  38.2 6.0 %collective-permute-start.10 = (f16[272,256]{1,0:T(8,128)(2,1)S(1)}, f16[272,256]{1,0:T(8,128)(2,1)S(1)}, u32[]{:S(2)}, u32[]{:S(2)}) collective-permute-start(f16[272,256]{1,0:T(8,128)(2,1)S(1)} %convert_element_type.36), channel_id=1, source_target_pairs={{18,2},{27,11},{4,20},{13,29}} | collective-permute-start | bytes 417800 | tf_op jit(solution)/shard_map/ppermute | solution.py:424
  39.5 6.7 %collective-permute-start.11 = (f16[272,256]{1,0:T(8,128)(2,1)S(1)}, f16[272,256]{1,0:T(8,128)(2,1)S(1)}, u32[]{:S(2)}, u32[]{:S(2)}) collective-permute-start(f16[272,256]{1,0:T(8,128)(2,1)S(1)} %convert_element_type.36), channel_id=1, source_target_pairs={{26,2},{19,11},{12,20},{5,29}} | collective-permute-start | bytes 417800 | tf_op jit(solution)/shard_map/ppermute | solution.py:424
  43.4 8.1 %collective-permute-start.15 = (f16[272,256]{1,0:T(8,128)(2,1)S(1)}, f16[272,256]{1,0:T(8,128)(2,1)S(1)}, u32[]{:S(2)}, u32[]{:S(2)}) collective-permute-start(f16[272,256]{1,0:T(8,128)(2,1)S(1)} %convert_element_type.44), channel_id=1, source_target_pairs={{1,12},{7,24},{12,1},{10,21},{21,10},{19,30},{24,7},{30,19}} | collective-permute-start | bytes 417800 | tf_op jit(solution)/shard_map/ppermute | solution.py:424
  46.3 8.2 %collective-permute-start.16 = (f16[272,256]{1,0:T(8,128)(2,1)S(1)}, f16[272,256]{1,0:T(8,128)(2,1)S(1)}, u32[]{:S(2)}, u32[]{:S(2)}) collective-permute-start(f16[272,256]{1,0:T(8,128)(2,1)S(1)} %convert_element_type.46), channel_id=1, source_target_pairs={{2,20},{11,29},{20,2},{29,11}} | collective-permute-start | bytes 417800 | tf_op jit(solution)/shard_map/ppermute | solution.py:424
  55.3 6.3 %collective-permute-start.17 = (f32[136,256]{1,0:T(8,128)S(1)}, f32[136,256]{1,0:T(8,128)S(1)}, u32[]{:S(2)}, u32[]{:S(2)}) collective-permute-start(f32[136,256]{1,0:T(8,128)S(1)} %get-tuple-element.45), channel_id=1, source_target_pairs={{1,5},{2,6},{7,3},{12,8},{10,14},{11,15},{20,16},{21,17},{19,23},{... | collective-permute-start | bytes 417800 | tf_op jit(solution)/shard_map/ppermute | solution.py:424
  56.6 5.0 %collective-permute-start.18 = (f32[8,256]{1,0:T(8,128)S(1)}, f32[8,256]{1,0:T(8,128)S(1)}, u32[]{:S(2)}, u32[]{:S(2)}) collective-permute-start(f32[8,256]{1,0:T(8,128)S(1)} %get-tuple-element.46), channel_id=1, source_target_pairs={{1,29},{2,30},{7,31},{12,4},{10,6},{11,7},{20,12},{21,13},{19,15},... | collective-permute-start | bytes 24584 | tf_op jit(solution)/shard_map/ppermute | solution.py:424

commit v14 on v13

--- a/solution.py
+++ b/solution.py
@@ -323,20 +323,50 @@
     return value, packed.astype(jnp.float16)
 
 
+def paired_sums(pos_ref, refs, put):
+    distant = jnp.abs(pos_ref[0] - pos_ref[1]) == 2
+    pl.when(jnp.logical_not(distant))(lambda: put(*refs[:2]))
+    pl.when(distant)(lambda: put(*refs[2:4]))
+
+
+def unscaled(ref, rows, n):
+    return ref[0:rows] * jnp.exp2(ref[n : n + 1] - TOP)
+
+
+def first_kernel(pos_ref, after_ref, *refs):
+    del after_ref
+    top_ref = refs[4]
+    n = top_ref.shape[1]
+
+    def put(own_ref, cross_ref):
+        top_ref[...] = own_ref[:, 0:128].T[0:8] + unscaled(cross_ref, 8, n)
+
+    paired_sums(pos_ref, refs, put)
+
+
+def first_rows(pos, after, near, far):
+    n = near[0].shape[0]
+    return pl.pallas_call(
+        first_kernel,
+        out_shape=jax.ShapeDtypeStruct((8, n), F32),
+        in_specs=[SMEM, pl.BlockSpec(memory_space=pl.ANY)] + [VMEM] * 4,
+        out_specs=VMEM,
+        compiler_params=params(),
+        name="first",
+    )(pos, after, *near, *far)
+
+
 def merge_kernel(pos_ref, after_ref, *refs):
     del after_ref
-    sums, (mine_ref, sib_ref, top_ref, t_ref) = refs[:4], refs[4:]
+    mine_ref, sib_ref, t_ref = refs[4:]
     n = t_ref.shape[0] - 8
     half = n // 2
-    chip, group, core = pos_ref[0], pos_ref[1], pos_ref[2]
+    core = pos_ref[2]
 
     def put(own_ref, cross_ref):
-        t_ref[0:n] = own_ref[...].T + cross_ref[0:n] * jnp.exp2(cross_ref[n : n + 1] - TOP)
-
-    distant = jnp.abs(chip - group) == 2
-    pl.when(jnp.logical_not(distant))(lambda: put(*sums[:2]))
-    pl.when(distant)(lambda: put(*sums[2:]))
-    top_ref[...] = t_ref[0:8]
+        t_ref[0:n] = own_ref[...].T + unscaled(cross_ref, n, n)
+
+    paired_sums(pos_ref, refs, put)
     mine_ref[...] = t_ref[pl.ds(pl.multiple_of(core * half, 8), half + 8)]
     sib_ref[...] = t_ref[pl.ds(pl.multiple_of((1 - core) * half, 8), half + 8)]
 
@@ -346,9 +376,9 @@
     half = n // 2
     return pl.pallas_call(
         merge_kernel,
-        out_shape=tuple(jax.ShapeDtypeStruct((r, n), F32) for r in (half + 8, half + 8, 8)),
+        out_shape=(jax.ShapeDtypeStruct((half + 8, n), F32),) * 2,
         in_specs=[SMEM, pl.BlockSpec(memory_space=pl.ANY)] + [VMEM] * 4,
-        out_specs=(VMEM,) * 3,
+        out_specs=(VMEM,) * 2,
         scratch_shapes=[pltpu.VMEM((n + 8, n), F32)],
         compiler_params=params(),
         name="merge",
@@ -454,7 +484,7 @@
     def gathered(block, group_homes):
         half = block.astype(jnp.float16)
         return [block] + [
-            send(half, [(at(k ^ m, z, c), at(k, z, c)) for k, z, c in group_homes.values()]) for m in range(1, groups)
+            send(half, [(at(k ^ m, z, c), at(k, z, c)) for k, z, c in group_homes.values()]) for m in reversed(range(1, groups))
         ]
 
     def exchanged(packed, group_homes):
@@ -472,7 +502,9 @@
     far_own, packed = total(state[0], far_parts)
     far_cross = exchanged(packed, far_homes)
     w = factor_part(3, 1, state, (far_own, near_cross), True)
-    mine, sib, top = merge(pos, w[0], (near_own, near_cross), (far_own, far_cross))
+    near_pair, far_pair = (near_own, near_cross), (far_own, far_cross)
+    top = first_rows(pos, w[0], near_pair, far_pair)
+    mine, sib = merge(pos, top, near_pair, far_pair)
     sib = send(sib, [(at(k, z, c), at(k, z, 1 - c)) for k, z, c in homes.values()])
     top = send(top, [(at(k, z, c), at((k - 1) % groups, z, 1)) for k, z, c in homes.values()])
     return tiles(pos, w, gram, (mine, sib, top))

time: 63.9 us -> 65.3 us (1.022)
  the two profiles are of different devices: /device:TPU:5 before, /device:TPU:13 now
where the time goes in v14:
time: 65.3 us; the launch traced here: 64.9 us
  starting transfers between devices  32.7 us (50%)
  Pallas kernels  16.1 us (25%)
  waiting for transfers between devices  12.8 us (20%)
  local copies, waits for them, and re-layouts  1.76 us (3%)
  other arithmetic  1.09 us (2%)
    ppermute x17, starting transfers between devices, send(): return lax.ppermute(value, axes, pairs)  28.9 us
    ppermute x17, waiting for transfers between devices, send(): return lax.ppermute(value, axes, pairs)  12.8 us
    pallas_call x4, Pallas kernels, factor_part(): pl.pallas_call(kernel, out_shape=(jax.ShapeDtypeStruct((n, n), BF16 if sp...  9.53 us
    ppermute x1, starting transfers between devices, start(): far = lax.ppermute(jnp.where(odd == 0, head, tail), 'space', outside)  3.02 us
    unnamed x4, local copies, waits for them, and re-layouts  1.66 us
    pallas_call x1, Pallas kernels, tiles(): pl.pallas_call(tiles_kernel, out_shape=jax.ShapeDtypeStruct((n, half), F3...  1.51 us
  transfers between devices with their start and end apart: 19, of which 6 were waited for; matrix products, arithmetic and copies ran while one was open for 1% of the time, Pallas kernels for 20%

profile of v14, /device:TPU:13, one launch (start us, length us, event | category | flops | bytes accessed | tf_op | source)
XLA Modules:
  0.0 64.9 jit_solution(11193382829758528477)
XLA Ops:
  0.0 0.7 %broadcast_select_fusion = (bf16[3,1,256]{2,1,0:T(2,128)(2,1)S(1)}, bf16[3,1,256]{2,1,0:T(2,128)(2,1)S(1)}) fusion(pred[]{:T(512)S(6)} %eq.6, bf16[3,384,256]{2,1,0:T(8,128)(2,1)} %vel_ref.1), kind=kLoop, calls=%fused_computation.1 | loop fusion | flops 1536 | bytes 6145 | tf_op jit(solution)/shard_map/jit(_where)/select_n | solution.py:437
  0.7 0.7 %collective-permute-start = (bf16[3,1,256]{2,1,0:T(2,128)(2,1)S(1)}, bf16[3,1,256]{2,1,0:T(2,128)(2,1)S(1)}, u32[]{:S(2)}, u32[]{:S(2)}) collective-permute-start(bf16[3,1,256]{2,1,0:T(2,128)(2,1)S(1)} %get-tuple-element.46), channel_id=1, source_target_pairs={{0,4},{4,0},{8,12},{12,8},{16,20},{20,16},{24,28},{28,24},{1,5},{5... | collective-permute-start | bytes 4616 | tf_op jit(solution)/shard_map/ppermute | solution.py:438
  1.5 3.0 %collective-permute-start.1 = (bf16[3,1,256]{2,1,0:T(2,128)(2,1)S(1)}, bf16[3,1,256]{2,1,0:T(2,128)(2,1)S(1)}, u32[]{:S(2)}, u32[]{:S(2)}) collective-permute-start(bf16[3,1,256]{2,1,0:T(2,128)(2,1)S(1)} %get-tuple-element.45), channel_id=1, source_target_pairs={{4,8},{12,16},{20,24},{8,4},{16,12},{24,20},{5,9},{13,17},{21,25},... | collective-permute-start | bytes 4616 | tf_op jit(solution)/shard_map/ppermute | solution.py:437
  5.3 1.1 %copy-done = bf16[3,384,256]{2,1,0:T(8,128)(2,1)S(1)} copy-done((bf16[3,384,256]{2,1,0:T(8,128)(2,1)S(1)}, bf16[3,384,256]{2,1,0:T(8,128)(2,1)}, u32[]{:S(2)}) %copy-start) | copy-done | bytes 589848
  7.7 0.9 %panel.1 = (bf16[256,1152]{1,0:T(8,128)(2,1)S(1)}, f32[192,128]{1,0:T(8,128)S(1)}, f32[192,128]{1,0:T(8,128)S(1)}) custom-call(s32[4]{0:T(128)S(1)} %pad_add_fusion.pos_ref, bf16[1152,256]{1,0:T(8,128)(2,1)S(1)} %edges.1.x_ref), custom_call_target="tpu_custom_call" | custom-call | flops 150994944 | bytes 1769472 | tf_op jit(solution)/shard_map/panel/pallas_call | solution.py:128
  8.6 2.0 %collective-permute-start.2 = (f32[192,128]{1,0:T(8,128)S(1)}, f32[192,128]{1,0:T(8,128)S(1)}, u32[]{:S(2)}, u32[]{:S(2)}) collective-permute-start(f32[192,128]{1,0:T(8,128)S(1)} %get-tuple-element.29), channel_id=1, source_target_pairs={{0,4},{4,0},{1,5},{5,1},{2,6},{6,2},{3,7},{7,3},{8,12},{12,8},{9,1... | collective-permute-start | bytes 294920 | tf_op jit(solution)/shard_map/ppermute | solution.py:454
  10.6 0.9 %collective-permute-done.2 = f32[192,128]{1,0:T(8,128)S(1)} collective-permute-done((f32[192,128]{1,0:T(8,128)S(1)}, f32[192,128]{1,0:T(8,128)S(1)}, u32[]{:S(2)}, u32[]{:S(2)}) %collective-permute-start.2) | collective-permute-done | bytes 98336 | tf_op jit(solution)/shard_map/ppermute | solution.py:454
  11.8 1.2 %collective-permute-start.4 = (f32[192,128]{1,0:T(8,128)S(1)}, f32[192,128]{1,0:T(8,128)S(1)}, u32[]{:S(2)}, u32[]{:S(2)}) collective-permute-start(f32[192,128]{1,0:T(8,128)S(1)} %add.18), channel_id=1, source_target_pairs={{0,16},{4,20},{1,17},{5,21},{2,18},{6,22},{3,19},{7,23},{8,24},{12... | collective-permute-start | bytes 294920 | tf_op jit(solution)/shard_map/ppermute | solution.py:454
  13.1 1.2 %collective-permute-start.3 = (f32[192,128]{1,0:T(8,128)S(1)}, f32[192,128]{1,0:T(8,128)S(1)}, u32[]{:S(2)}, u32[]{:S(2)}) collective-permute-start(f32[192,128]{1,0:T(8,128)S(1)} %add.18), channel_id=1, source_target_pairs={{0,8},{4,12},{1,9},{5,13},{2,10},{6,14},{3,11},{7,15},{8,0},{12,4}... | collective-permute-start | bytes 294920 | tf_op jit(solution)/shard_map/ppermute | solution.py:454
  14.2 2.3 %collective-permute-done.5 = f32[192,128]{1,0:T(8,128)S(1)} collective-permute-done((f32[192,128]{1,0:T(8,128)S(1)}, f32[192,128]{1,0:T(8,128)S(1)}, u32[]{:S(2)}, u32[]{:S(2)}) %collective-permute-start.5) | collective-permute-done | bytes 98336 | tf_op jit(solution)/shard_map/ppermute | solution.py:454
  16.6 1.3 %collective-permute-done.4 = f32[192,128]{1,0:T(8,128)S(1)} collective-permute-done((f32[192,128]{1,0:T(8,128)S(1)}, f32[192,128]{1,0:T(8,128)S(1)}, u32[]{:S(2)}, u32[]{:S(2)}) %collective-permute-start.4) | collective-permute-done | bytes 98336 | tf_op jit(solution)/shard_map/ppermute | solution.py:454
  17.9 1.3 %collective-permute-start.6 = (f32[192,128]{1,0:T(8,128)S(1)}, f32[192,128]{1,0:T(8,128)S(1)}, u32[]{:S(2)}, u32[]{:S(2)}) collective-permute-start(f32[192,128]{1,0:T(8,128)S(1)} %add_add_fusion.mine_ref), channel_id=1, source_target_pairs={{0,4},{4,0},{1,5},{5,1},{2,6},{6,2},{3,7},{7,3},{8,12},{12,8},{9,1... | collective-permute-start | bytes 294920 | tf_op jit(solution)/shard_map/ppermute | solution.py:454
  19.3 0.9 %collective-permute-done.6.theirs_ref = f32[192,128]{1,0:T(8,128)S(1)} collective-permute-done((f32[192,128]{1,0:T(8,128)S(1)}, f32[192,128]{1,0:T(8,128)S(1)}, u32[]{:S(2)}, u32[]{:S(2)}) %collective-permute-start.6) | collective-permute-done | bytes 98336 | tf_op jit(solution)/shard_map/ppermute | solution.py:454
  20.8 2.6 %factor.4 = (f32[256,256]{1,0:T(8,128)S(1)}, f32[256,256]{1,0:T(8,128)S(1)}) custom-call(f32[256,256]{1,0:T(8,128)S(1)} %gather.1.refs_0_.g_ref), custom_call_target="tpu_custom_call" | custom-call | flops 33554432 | bytes 524288 | tf_op jit(solution)/shard_map/factor/pallas_call | solution.py:251
  23.5 4.3 %collective-permute-start.8 = (bf16[1152,256]{1,0:T(8,128)(2,1)S(1)}, bf16[1152,256]{1,0:T(8,128)(2,1)S(1)}, u32[]{:S(2)}, u32[]{:S(2)}) collective-permute-start(bf16[1152,256]{1,0:T(8,128)(2,1)S(1)} %passed.1.panel_ref), channel_id=1, source_target_pairs={{1,2},{2,3},{9,10},{10,11},{17,18},{18,19},{25,26},{26,27},{6,5},{... | collective-permute-start | bytes 1769480 | tf_op jit(solution)/shard_map/ppermute | solution.py:454
  28.3 1.3 %collective-permute-start.12 = (f16[272,256]{1,0:T(8,128)(2,1)S(1)}, f16[272,256]{1,0:T(8,128)(2,1)S(1)}, u32[]{:S(2)}, u32[]{:S(2)}) collective-permute-start(f16[272,256]{1,0:T(8,128)(2,1)S(1)} %convert_element_type.40), channel_id=1, source_target_pairs={{25,1},{31,7},{20,12},{18,10},{13,21},{11,19},{0,24},{6,30}} | collective-permute-start | bytes 417800 | tf_op jit(solution)/shard_map/ppermute | solution.py:454
  29.6 1.3 %collective-permute-start.13 = (f16[272,256]{1,0:T(8,128)(2,1)S(1)}, f16[272,256]{1,0:T(8,128)(2,1)S(1)}, u32[]{:S(2)}, u32[]{:S(2)}) collective-permute-start(f16[272,256]{1,0:T(8,128)(2,1)S(1)} %convert_element_type.40), channel_id=1, source_target_pairs={{17,1},{23,7},{28,12},{26,10},{5,21},{3,19},{8,24},{14,30}} | collective-permute-start | bytes 417800 | tf_op jit(solution)/shard_map/ppermute | solution.py:454
  30.9 1.3 %collective-permute-start.14 = (f16[272,256]{1,0:T(8,128)(2,1)S(1)}, f16[272,256]{1,0:T(8,128)(2,1)S(1)}, u32[]{:S(2)}, u32[]{:S(2)}) collective-permute-start(f16[272,256]{1,0:T(8,128)(2,1)S(1)} %convert_element_type.40), channel_id=1, source_target_pairs={{9,1},{15,7},{4,12},{2,10},{29,21},{27,19},{16,24},{22,30}} | collective-permute-start | bytes 417800 | tf_op jit(solution)/shard_map/ppermute | solution.py:454
  32.2 2.5 %factor.5 = (f32[256,256]{1,0:T(8,128)S(1)}, f32[256,256]{1,0:T(8,128)S(1)}) custom-call(f32[256,256]{1,0:T(8,128)S(1)} %get-tuple-element.30.refs_1_.after_ref.refs_0_, f32[256,256]{1,0:T(8,128)S(1)} %get-tuple-element.31.refs_1_, f32[272,256]{1,0:T(8,128)S(1)} %block.2.refs_2_.refs_0_), custom_call_target="tpu_custom_call" | custom-call | flops 33554432 | bytes 524288 | tf_op jit(solution)/shard_map/factor/pallas_call | solution.py:251
  35.3 0.7 %collective-permute-start.9 = (f16[272,256]{1,0:T(8,128)(2,1)S(1)}, f16[272,256]{1,0:T(8,128)(2,1)S(1)}, u32[]{:S(2)}, u32[]{:S(2)}) collective-permute-start(f16[272,256]{1,0:T(8,128)(2,1)S(1)} %convert_element_type.36), channel_id=1, source_target_pairs={{26,2},{19,11},{12,20},{5,29}} | collective-permute-start | bytes 417800 | tf_op jit(solution)/shard_map/ppermute | solution.py:454
  36.0 0.7 %collective-permute-start.10 = (f16[272,256]{1,0:T(8,128)(2,1)S(1)}, f16[272,256]{1,0:T(8,128)(2,1)S(1)}, u32[]{:S(2)}, u32[]{:S(2)}) collective-permute-start(f16[272,256]{1,0:T(8,128)(2,1)S(1)} %convert_element_type.36), channel_id=1, source_target_pairs={{18,2},{27,11},{4,20},{13,29}} | collective-permute-start | bytes 417800 | tf_op jit(solution)/shard_map/ppermute | solution.py:454
  36.6 5.2 %collective-permute-start.11 = (f16[272,256]{1,0:T(8,128)(2,1)S(1)}, f16[272,256]{1,0:T(8,128)(2,1)S(1)}, u32[]{:S(2)}, u32[]{:S(2)}) collective-permute-start(f16[272,256]{1,0:T(8,128)(2,1)S(1)} %convert_element_type.36), channel_id=1, source_target_pairs={{10,2},{3,11},{28,20},{21,29}} | collective-permute-start | bytes 417800 | tf_op jit(solution)/shard_map/ppermute | solution.py:454
  42.0 2.4 %factor.6 = (f32[256,256]{1,0:T(8,128)S(1)}, f32[256,256]{1,0:T(8,128)S(1)}) custom-call(f32[256,256]{1,0:T(8,128)S(1)} %get-tuple-element.33.after_ref.refs_0_, f32[256,256]{1,0:T(8,128)S(1)} %get-tuple-element.34.refs_1_, f32[272,256]{1,0:T(8,128)S(1)} %block.3.refs_2_.refs_0_), custom_call_target="tpu_custom_call" | custom-call | flops 33554432 | bytes 524288 | tf_op jit(solution)/shard_map/factor/pallas_call | solution.py:251
  44.5 4.0 %collective-permute-start.15 = (f16[272,256]{1,0:T(8,128)(2,1)S(1)}, f16[272,256]{1,0:T(8,128)(2,1)S(1)}, u32[]{:S(2)}, u32[]{:S(2)}) collective-permute-start(f16[272,256]{1,0:T(8,128)(2,1)S(1)} %convert_element_type.44), channel_id=1, source_target_pairs={{1,12},{7,24},{12,1},{10,21},{21,10},{19,30},{24,7},{30,19}} | collective-permute-start | bytes 417800 | tf_op jit(solution)/shard_map/ppermute | solution.py:454
  48.8 0.7 %collective-permute-start.16 = (f16[272,256]{1,0:T(8,128)(2,1)S(1)}, f16[272,256]{1,0:T(8,128)(2,1)S(1)}, u32[]{:S(2)}, u32[]{:S(2)}) collective-permute-start(f16[272,256]{1,0:T(8,128)(2,1)S(1)} %convert_element_type.46), channel_id=1, source_target_pairs={{2,20},{11,29},{20,2},{29,11}} | collective-permute-start | bytes 417800 | tf_op jit(solution)/shard_map/ppermute | solution.py:454
  49.5 4.7 %collective-permute-done.15 = f16[272,256]{1,0:T(8,128)(2,1)S(1)} collective-permute-done((f16[272,256]{1,0:T(8,128)(2,1)S(1)}, f16[272,256]{1,0:T(8,128)(2,1)S(1)}, u32[]{:S(2)}, u32[]{:S(2)}) %collective-permute-start.15) | collective-permute-done | bytes 139296 | tf_op jit(solution)/shard_map/ppermute | solution.py:454
  54.2 2.0 %factor.7 = (bf16[256,256]{1,0:T(8,128)(2,1)S(1)}, bf16[256,256]{1,0:T(8,128)(2,1)S(1)}) custom-call(f32[256,256]{1,0:T(8,128)S(1)} %get-tuple-element.35.after_ref.refs_0_, f32[256,256]{1,0:T(8,128)S(1)} %get-tuple-element.36.refs_1_, f32[256,256]{1,0:T(8,128)S(1)} %get-tuple-element.37.refs_2_, f32[272,256]{1,0:T(8,128)S(1)} %convert_element_type.45.refs_3_.refs_1_), custom_call_target="tpu_custom_call" | custom-call | flops 33554432 | bytes 524288 | tf_op jit(solution)/shard_map/factor/pallas_call | solution.py:251
  56.9 0.7 %merge.1 = (f32[136,256]{1,0:T(8,128)S(1)}, f32[136,256]{1,0:T(8,128)S(1)}) custom-call(s32[4]{0:T(128)S(1)} %pad_add_fusion.pos_ref, f32[8,256]{1,0:T(8,128)S(1)} %first.1.after_ref, f32[256,256]{1,0:T(8,128)S(1)} %get-tuple-element.41.refs_0_, f32[272,256]{1,0:T(8,128)S(1)} %convert_element_type.45.refs_3_.refs_1_, ...), custom_call_target="tpu_custom_call" | custom-call | tf_op jit(solution)/shard_map/merge/pallas_call | solution.py:377
  57.6 1.3 %collective-permute-start.17 = (f32[136,256]{1,0:T(8,128)S(1)}, f32[136,256]{1,0:T(8,128)S(1)}, u32[]{:S(2)}, u32[]{:S(2)}) collective-permute-start(f32[136,256]{1,0:T(8,128)S(1)} %get-tuple-element.44), channel_id=1, source_target_pairs={{1,5},{2,6},{7,3},{12,8},{10,14},{11,15},{20,16},{21,17},{19,23},{... | collective-permute-start | bytes 417800 | tf_op jit(solution)/shard_map/ppermute | solution.py:454
  58.9 1.9 %collective-permute-start.18 = (f32[8,256]{1,0:T(8,128)S(1)}, f32[8,256]{1,0:T(8,128)S(1)}, u32[]{:S(2)}, u32[]{:S(2)}) collective-permute-start(f32[8,256]{1,0:T(8,128)S(1)} %first.1.after_ref), channel_id=1, source_target_pairs={{1,29},{2,30},{7,31},{12,4},{10,6},{11,7},{20,12},{21,13},{19,15},... | collective-permute-start | bytes 24584 | tf_op jit(solution)/shard_map/ppermute | solution.py:454
  60.9 2.5 %collective-permute-done.18.top_ref = f32[8,256]{1,0:T(8,128)S(1)} collective-permute-done((f32[8,256]{1,0:T(8,128)S(1)}, f32[8,256]{1,0:T(8,128)S(1)}, u32[]{:S(2)}, u32[]{:S(2)}) %collective-permute-start.18) | collective-permute-done | bytes 8224 | tf_op jit(solution)/shard_map/ppermute | solution.py:454
  63.3 1.5 %tiles.1 = f32[256,128]{1,0:T(8,128)} custom-call(s32[4]{0:T(128)S(1)} %pad_add_fusion.pos_ref, bf16[256,256]{1,0:T(8,128)(2,1)S(1)} %get-tuple-element.39.after_ref.high_ref, bf16[256,256]{1,0:T(8,128)(2,1)S(1)} %get-tuple-element.40.low_ref, f32[256,256]{1,0:T(8,128)S(1)} %gather.1.refs_0_.g_ref, f32[136,256]{1,0:T(8,128)S(1)} %get-tuple-element.43.own_ref, ...), custom_call_target="tpu_custom_call" | custom-call | tf_op jit(solution)/shard_map/tiles/pallas_call | solution.py:417
  (43 shorter events, 5.1 us)
Async XLA Ops:
  0.7 6.1 %collective-permute-start = (bf16[3,1,256]{2,1,0:T(2,128)(2,1)S(1)}, bf16[3,1,256]{2,1,0:T(2,128)(2,1)S(1)}, u32[]{:S(2)}, u32[]{:S(2)}) collective-permute-start(bf16[3,1,256]{2,1,0:T(2,128)(2,1)S(1)} %get-tuple-element.46), channel_id=1, source_target_pairs={{0,4},{4,0},{8,12},{12,8},{16,20},{20,16},{24,28},{28,24},{1,5},{5... | collective-permute-start | bytes 4616 | tf_op jit(solution)/shard_map/ppermute | solution.py:438
  1.5 5.3 %collective-permute-start.1 = (bf16[3,1,256]{2,1,0:T(2,128)(2,1)S(1)}, bf16[3,1,256]{2,1,0:T(2,128)(2,1)S(1)}, u32[]{:S(2)}, u32[]{:S(2)}) collective-permute-start(bf16[3,1,256]{2,1,0:T(2,128)(2,1)S(1)} %get-tuple-element.45), channel_id=1, source_target_pairs={{4,8},{12,16},{20,24},{8,4},{16,12},{24,20},{5,9},{13,17},{21,25},... | collective-permute-start | bytes 4616 | tf_op jit(solution)/shard_map/ppermute | solution.py:437
  4.5 0.7 %copy-start.1 = (f32[384]{0:T(512)S(1)}, f32[384]{0:T(512)}, u32[]{:S(2)}) copy-start(f32[384]{0:T(512)} %param.3) | copy-start | bytes 4612
  5.3 1.1 %copy-start = (bf16[3,384,256]{2,1,0:T(8,128)(2,1)S(1)}, bf16[3,384,256]{2,1,0:T(8,128)(2,1)}, u32[]{:S(2)}) copy-start(bf16[3,384,256]{2,1,0:T(8,128)(2,1)} %vel_ref.1) | copy-start | bytes 1769476
  7.5 16.0 %collective-permute-start.7 = (bf16[1152,256]{1,0:T(8,128)(2,1)S(1)}, bf16[1152,256]{1,0:T(8,128)(2,1)S(1)}, u32[]{:S(2)}, u32[]{:S(2)}) collective-permute-start(bf16[1152,256]{1,0:T(8,128)(2,1)S(1)} %edges.1.x_ref), channel_id=1, source_target_pairs={{0,1},{1,2},{2,3},{3,0},{8,9},{9,10},{10,11},{11,8},{16,17},{17,18... | collective-permute-start | bytes 1769480 | tf_op jit(solution)/shard_map/ppermute | solution.py:454
  8.6 2.9 %collective-permute-start.2 = (f32[192,128]{1,0:T(8,128)S(1)}, f32[192,128]{1,0:T(8,128)S(1)}, u32[]{:S(2)}, u32[]{:S(2)}) collective-permute-start(f32[192,128]{1,0:T(8,128)S(1)} %get-tuple-element.29), channel_id=1, source_target_pairs={{0,4},{4,0},{1,5},{5,1},{2,6},{6,2},{3,7},{7,3},{8,12},{12,8},{9,1... | collective-permute-start | bytes 294920 | tf_op jit(solution)/shard_map/ppermute | solution.py:454
  11.5 5.0 %collective-permute-start.5 = (f32[192,128]{1,0:T(8,128)S(1)}, f32[192,128]{1,0:T(8,128)S(1)}, u32[]{:S(2)}, u32[]{:S(2)}) collective-permute-start(f32[192,128]{1,0:T(8,128)S(1)} %add.18), channel_id=1, source_target_pairs={{0,24},{4,28},{1,25},{5,29},{2,26},{6,30},{3,27},{7,31},{8,16},{12... | collective-permute-start | bytes 294920 | tf_op jit(solution)/shard_map/ppermute | solution.py:454
  11.8 6.0 %collective-permute-start.4 = (f32[192,128]{1,0:T(8,128)S(1)}, f32[192,128]{1,0:T(8,128)S(1)}, u32[]{:S(2)}, u32[]{:S(2)}) collective-permute-start(f32[192,128]{1,0:T(8,128)S(1)} %add.18), channel_id=1, source_target_pairs={{0,16},{4,20},{1,17},{5,21},{2,18},{6,22},{3,19},{7,23},{8,24},{12... | collective-permute-start | bytes 294920 | tf_op jit(solution)/shard_map/ppermute | solution.py:454
  13.1 4.8 %collective-permute-start.3 = (f32[192,128]{1,0:T(8,128)S(1)}, f32[192,128]{1,0:T(8,128)S(1)}, u32[]{:S(2)}, u32[]{:S(2)}) collective-permute-start(f32[192,128]{1,0:T(8,128)S(1)} %add.18), channel_id=1, source_target_pairs={{0,8},{4,12},{1,9},{5,13},{2,10},{6,14},{3,11},{7,15},{8,0},{12,4}... | collective-permute-start | bytes 294920 | tf_op jit(solution)/shard_map/ppermute | solution.py:454
  17.9 2.3 %collective-permute-start.6 = (f32[192,128]{1,0:T(8,128)S(1)}, f32[192,128]{1,0:T(8,128)S(1)}, u32[]{:S(2)}, u32[]{:S(2)}) collective-permute-start(f32[192,128]{1,0:T(8,128)S(1)} %add_add_fusion.mine_ref), channel_id=1, source_target_pairs={{0,4},{4,0},{1,5},{5,1},{2,6},{6,2},{3,7},{7,3},{8,12},{12,8},{9,1... | collective-permute-start | bytes 294920 | tf_op jit(solution)/shard_map/ppermute | solution.py:454
  23.5 11.3 %collective-permute-start.8 = (bf16[1152,256]{1,0:T(8,128)(2,1)S(1)}, bf16[1152,256]{1,0:T(8,128)(2,1)S(1)}, u32[]{:S(2)}, u32[]{:S(2)}) collective-permute-start(bf16[1152,256]{1,0:T(8,128)(2,1)S(1)} %passed.1.panel_ref), channel_id=1, source_target_pairs={{1,2},{2,3},{9,10},{10,11},{17,18},{18,19},{25,26},{26,27},{6,5},{... | collective-permute-start | bytes 1769480 | tf_op jit(solution)/shard_map/ppermute | solution.py:454
  28.3 8.3 %collective-permute-start.12 = (f16[272,256]{1,0:T(8,128)(2,1)S(1)}, f16[272,256]{1,0:T(8,128)(2,1)S(1)}, u32[]{:S(2)}, u32[]{:S(2)}) collective-permute-start(f16[272,256]{1,0:T(8,128)(2,1)S(1)} %convert_element_type.40), channel_id=1, source_target_pairs={{25,1},{31,7},{20,12},{18,10},{13,21},{11,19},{0,24},{6,30}} | collective-permute-start | bytes 417800 | tf_op jit(solution)/shard_map/ppermute | solution.py:454
  29.6 12.3 %collective-permute-start.13 = (f16[272,256]{1,0:T(8,128)(2,1)S(1)}, f16[272,256]{1,0:T(8,128)(2,1)S(1)}, u32[]{:S(2)}, u32[]{:S(2)}) collective-permute-start(f16[272,256]{1,0:T(8,128)(2,1)S(1)} %convert_element_type.40), channel_id=1, source_target_pairs={{17,1},{23,7},{28,12},{26,10},{5,21},{3,19},{8,24},{14,30}} | collective-permute-start | bytes 417800 | tf_op jit(solution)/shard_map/ppermute | solution.py:454
  30.9 11.0 %collective-permute-start.14 = (f16[272,256]{1,0:T(8,128)(2,1)S(1)}, f16[272,256]{1,0:T(8,128)(2,1)S(1)}, u32[]{:S(2)}, u32[]{:S(2)}) collective-permute-start(f16[272,256]{1,0:T(8,128)(2,1)S(1)} %convert_element_type.40), channel_id=1, source_target_pairs={{9,1},{15,7},{4,12},{2,10},{29,21},{27,19},{16,24},{22,30}} | collective-permute-start | bytes 417800 | tf_op jit(solution)/shard_map/ppermute | solution.py:454
  35.3 13.3 %collective-permute-start.9 = (f16[272,256]{1,0:T(8,128)(2,1)S(1)}, f16[272,256]{1,0:T(8,128)(2,1)S(1)}, u32[]{:S(2)}, u32[]{:S(2)}) collective-permute-start(f16[272,256]{1,0:T(8,128)(2,1)S(1)} %convert_element_type.36), channel_id=1, source_target_pairs={{26,2},{19,11},{12,20},{5,29}} | collective-permute-start | bytes 417800 | tf_op jit(solution)/shard_map/ppermute | solution.py:454
  36.0 12.6 %collective-permute-start.10 = (f16[272,256]{1,0:T(8,128)(2,1)S(1)}, f16[272,256]{1,0:T(8,128)(2,1)S(1)}, u32[]{:S(2)}, u32[]{:S(2)}) collective-permute-start(f16[272,256]{1,0:T(8,128)(2,1)S(1)} %convert_element_type.36), channel_id=1, source_target_pairs={{18,2},{27,11},{4,20},{13,29}} | collective-permute-start | bytes 417800 | tf_op jit(solution)/shard_map/ppermute | solution.py:454
  36.6 12.0 %collective-permute-start.11 = (f16[272,256]{1,0:T(8,128)(2,1)S(1)}, f16[272,256]{1,0:T(8,128)(2,1)S(1)}, u32[]{:S(2)}, u32[]{:S(2)}) collective-permute-start(f16[272,256]{1,0:T(8,128)(2,1)S(1)} %convert_element_type.36), channel_id=1, source_target_pairs={{10,2},{3,11},{28,20},{21,29}} | collective-permute-start | bytes 417800 | tf_op jit(solution)/shard_map/ppermute | solution.py:454
  44.5 9.7 %collective-permute-start.15 = (f16[272,256]{1,0:T(8,128)(2,1)S(1)}, f16[272,256]{1,0:T(8,128)(2,1)S(1)}, u32[]{:S(2)}, u32[]{:S(2)}) collective-permute-start(f16[272,256]{1,0:T(8,128)(2,1)S(1)} %convert_element_type.44), channel_id=1, source_target_pairs={{1,12},{7,24},{12,1},{10,21},{21,10},{19,30},{24,7},{30,19}} | collective-permute-start | bytes 417800 | tf_op jit(solution)/shard_map/ppermute | solution.py:454
  48.8 7.5 %collective-permute-start.16 = (f16[272,256]{1,0:T(8,128)(2,1)S(1)}, f16[272,256]{1,0:T(8,128)(2,1)S(1)}, u32[]{:S(2)}, u32[]{:S(2)}) collective-permute-start(f16[272,256]{1,0:T(8,128)(2,1)S(1)} %convert_element_type.46), channel_id=1, source_target_pairs={{2,20},{11,29},{20,2},{29,11}} | collective-permute-start | bytes 417800 | tf_op jit(solution)/shard_map/ppermute | solution.py:454
  57.6 5.7 %collective-permute-start.17 = (f32[136,256]{1,0:T(8,128)S(1)}, f32[136,256]{1,0:T(8,128)S(1)}, u32[]{:S(2)}, u32[]{:S(2)}) collective-permute-start(f32[136,256]{1,0:T(8,128)S(1)} %get-tuple-element.44), channel_id=1, source_target_pairs={{1,5},{2,6},{7,3},{12,8},{10,14},{11,15},{20,16},{21,17},{19,23},{... | collective-permute-start | bytes 417800 | tf_op jit(solution)/shard_map/ppermute | solution.py:454
  58.9 4.4 %collective-permute-start.18 = (f32[8,256]{1,0:T(8,128)S(1)}, f32[8,256]{1,0:T(8,128)S(1)}, u32[]{:S(2)}, u32[]{:S(2)}) collective-permute-start(f32[8,256]{1,0:T(8,128)S(1)} %first.1.after_ref), channel_id=1, source_target_pairs={{1,29},{2,30},{7,31},{12,4},{10,6},{11,7},{20,12},{21,13},{19,15},... | collective-permute-start | bytes 24584 | tf_op jit(solution)/shard_map/ppermute | solution.py:454
